TPU v7x, 32 devices: a whole 2x2x4 slice. The times are simulated.
32 devices in a mesh: dp: 8 (over z, x), mp: 4 (over y, core).
Axes of the slice: x: 2, y: 2, z: 4, core: 2. Of those that a mesh axis runs over, the one named last changes fastest.
Arguments:
- titles: bfloat16 [2048, 768], P('dp')
- w_attn_in: bfloat16 [3, 768, 768], P(None, None, 'mp')
- w_attn_out: bfloat16 [768, 768], P('mp'), may hold values from -0.21875 to 0.21875
- w_ffn_in: bfloat16 [768, 3072], P(None, 'mp'), may hold values from -0.21875 to 0.21875
- w_ffn_out: bfloat16 [3072, 768], P('mp'), may hold values from -0.109375 to 0.109375
- gains: float32 [2, 768], replicated, may hold values from 0.5 to 1.5
- node_table: bfloat16 [4096, 768], P('dp')
- w_graph: bfloat16 [3, 768, 768], P(None, None, 'mp')
- title_nodes: int32 [16], P('dp'), may hold values from 0 to 511, as said below
- send_ids: int32 [8, 8, 256], P('dp'), may hold values from 0 to 511
- tile_cols: int32 [32, 6], P('dp'), may hold values from 0 to 19, as said below
- nbr_slots: int32 [4096, 16], P('dp'), may hold values from 0 to 767
Outputs:
- encoded: bfloat16 [2048, 768], P('dp')
- graph_out: bfloat16 [4096, 768], P('dp', 'mp')
Inputs may be any that keep to these rules, and one draw needn't show every extreme that they name: `title_nodes`: within each partition the 2 entries are distinct local node indices. `send_ids`: entries are local node indices of the owner partition. `tile_cols`: the entries of one row are distinct; entry 0 of local row tile r is r.
All inputs are finite; a program needn't handle non-finite values.
Results may differ from a plain program's by a relative error of at most 0.02.
Values may be sent and summed in bfloat16 or wider, within the bound.
No kernel may reach another device: no remote copies, remote signals or barrier semaphores. Data moves between devices by JAX's collectives and lax.ppermute only.
A program may use at most 64 MiB of HBM per device.

v0:
```python
import jax
import jax.numpy as jnp
from jax import lax
from jax.sharding import PartitionSpec as P

SEQ = 128
TILE = 128
DEG = 16
TPR = 6
HD = 64
GHD = 96


eps_norm = 1e-06


def layer_norm(values, gain):
    mean = jnp.mean(values, axis=-1, keepdims=True)
    centred = values - mean
    var = jnp.mean(centred * centred, axis=-1, keepdims=True)
    return centred * lax.rsqrt(var + eps_norm) * gain


def local(
    titles,
    w_attn_in,
    w_attn_out,
    w_ffn_in,
    w_ffn_out,
    gains,
    node_table,
    w_graph,
    title_nodes,
    send_ids,
    tile_cols,
    nbr_slots,
):
    bf = jnp.bfloat16
    f32 = jnp.float32
    tok_rows = titles.shape[0]
    width = titles.shape[1]
    local_cols = w_attn_in.shape[2]
    query = jnp.dot(titles, w_attn_in[0], preferred_element_type=f32).astype(bf)
    keyed = jnp.dot(titles, w_attn_in[1], preferred_element_type=f32).astype(bf)
    valued = jnp.dot(titles, w_attn_in[2], preferred_element_type=f32).astype(bf)
    query = query.reshape(-1, SEQ, local_cols // HD, HD)
    keyed = keyed.reshape(-1, SEQ, local_cols // HD, HD)
    valued = valued.reshape(-1, SEQ, local_cols // HD, HD)
    scores = jnp.einsum("bqhd,bkhd->bhqk", query, keyed, preferred_element_type=f32) / jnp.sqrt(
        f32(HD)
    )
    probs = jax.nn.softmax(scores, axis=-1).astype(bf)
    context = jnp.einsum("bhqk,bkhd->bqhd", probs, valued, preferred_element_type=f32).astype(bf)
    context = context.reshape(tok_rows, local_cols)
    attn_terms = jnp.dot(context, w_attn_out, preferred_element_type=f32)
    attn = lax.psum(attn_terms.astype(jnp.bfloat16), "mp").astype(jnp.float32)
    hidden_one = layer_norm(titles.astype(f32) + attn, gains[0]).astype(bf)
    inner = jax.nn.gelu(
        jnp.dot(hidden_one, w_ffn_in, preferred_element_type=f32), approximate=False
    ).astype(bf)
    ffn_terms = jnp.dot(inner, w_ffn_out, preferred_element_type=f32)
    ffn = lax.psum(ffn_terms.astype(jnp.bfloat16), "mp").astype(jnp.float32)
    encoded = layer_norm(hidden_one.astype(f32) + ffn, gains[1]).astype(bf)
    first_tokens = encoded.reshape(-1, SEQ, width)[:, 0]
    features = node_table.at[title_nodes].set(first_tokens)
    graph_q = jnp.dot(features, w_graph[0], preferred_element_type=f32).astype(bf)
    graph_k = jnp.dot(features, w_graph[1], preferred_element_type=f32).astype(bf)
    graph_v = jnp.dot(features, w_graph[2], preferred_element_type=f32).astype(bf)
    send_rows = send_ids[0]
    remote_feat = lax.all_to_all(
        features[send_rows], "dp", split_axis=0, concat_axis=0, tiled=True
    ).reshape(-1, width)
    remote_k = jnp.dot(remote_feat, w_graph[1], preferred_element_type=f32).astype(bf)
    remote_v = jnp.dot(remote_feat, w_graph[2], preferred_element_type=f32).astype(bf)
    node_rows = node_table.shape[0]
    row_tiles = node_rows // TILE
    key_rows = jnp.concatenate([graph_k, remote_k], axis=0).reshape(-1, TILE, local_cols)
    value_rows = jnp.concatenate([graph_v, remote_v], axis=0).reshape(-1, TILE, local_cols)
    local_heads = local_cols // GHD
    key_tiles = key_rows[tile_cols].reshape(row_tiles, TPR * TILE, local_heads, GHD)
    value_tiles = value_rows[tile_cols].reshape(row_tiles, TPR * TILE, local_heads, GHD)
    queries = graph_q.reshape(row_tiles, TILE, local_heads, GHD)
    scores_g = jnp.einsum(
        "rqhd,rkhd->rhqk", queries, key_tiles, preferred_element_type=f32
    ) / jnp.sqrt(f32(GHD))
    columns = jnp.arange(TPR * TILE, dtype=jnp.int32)
    own_pos = jnp.arange(TILE, dtype=jnp.int32)
    slots = nbr_slots.reshape(row_tiles, TILE, DEG)
    edges_init = jnp.broadcast_to(
        columns[None, None, :] == own_pos[None, :, None], (row_tiles, TILE, TPR * TILE)
    )

    def add_edge(edge_index, edges):
        chosen = lax.dynamic_index_in_dim(slots, edge_index, 2, keepdims=True)
        return edges | (chosen == columns)

    edges = lax.fori_loop(0, DEG, add_edge, edges_init)[:, None, :, :]
    masked = jnp.where(edges, scores_g, -jnp.inf)
    top = jnp.max(masked, axis=-1, keepdims=True)
    expo = jnp.where(edges, jnp.exp(masked - top), 0.0)
    weights = (expo / jnp.sum(expo, axis=-1, keepdims=True)).astype(bf)
    graph_out = jnp.einsum("rhqk,rkhd->rqhd", weights, value_tiles, preferred_element_type=f32)
    return (encoded, graph_out.reshape(node_rows, local_cols).astype(bf))


def solution(mesh):
    in_specs = (
        P("dp", None),
        P(None, None, "mp"),
        P("mp", None),
        P(None, "mp"),
        P("mp", None),
        P(),
        P("dp", None),
        P(None, None, "mp"),
        P("dp"),
        P("dp", None, None),
        P("dp", None),
        P("dp", None),
    )
    out_specs = (P("dp", None), P("dp", "mp"))
    return jax.shard_map(local, mesh=mesh, in_specs=in_specs, out_specs=out_specs, check_vma=False)
```

profile of v0, /device:TPU:0, one launch (start us, length us, event | category | flops | bytes accessed | tf_op | source)
XLA Modules:
  0.0 214.5 jit_solution(10044577756972755472)
XLA Ops:
  7.2 0.0 all-reduce.3.cloned.1.call-start
  7.2 1.5 convolution_convert_fusion.9
  8.8 0.3 convolution_convert_fusion.7
  9.1 0.3 convolution_convert_fusion.8
  9.5 0.3 fusion.129
  9.9 0.3 convolution_multiply_fusion
  10.2 0.2 fusion.21
  10.4 0.1 copy.24
  10.5 1.0 convolution_convert_fusion.3
  11.6 0.0 all-reduce.3.cloned.1.call-update
  11.6 0.0 all-reduce.5.cloned.1.call-start
  11.7 0.1 reshape.137
  11.9 35.1 %all-reduce.3.cloned.1.call-done = bf16[256,768]{1,0:T(8,128)(2,1)} async-done(((bf16[256,768]{1,0:T(8,128)(2,1)}), bf16[256,768]{1,0:T(8,128)(2,1)}) %all-reduce.3.cloned.1.call-update) | async-done | bytes 393232 | tf_op jit(solution)/shard_map/psum | solution.py:56
  47.1 1.2 fusion.33
  48.2 1.2 multiply_reduce_fusion.1
  49.5 1.2 multiply_convert_fusion.1
  50.7 4.5 %convolution_convert_fusion.2 = bf16[256,768]{1,0:T(8,128)(2,1)} fusion(bf16[768,768]{1,0:T(8,128)(2,1)S(1)} %copy-done, bf16[256,768]{1,0:T(8,128)(2,1)S(1)} %multiply_convert_fusion.1, bf16[768,768]{1,0:T(8,128)(2,1)} %param.17), kind=kOutput, calls=%fused_computation.21 | convolution fusion | flops 616955904 | bytes 3145728 | tf_op jit(solution)/shard_map/dot_general | solution.py:61
  55.2 0.0 all-reduce.5.cloned.1.call-update
  55.3 32.7 %all-reduce.5.cloned.1.call-done = bf16[256,768]{1,0:T(8,128)(2,1)} async-done(((bf16[256,768]{1,0:T(8,128)(2,1)}), bf16[256,768]{1,0:T(8,128)(2,1)}) %all-reduce.5.cloned.1.call-update) | async-done | bytes 393232 | tf_op jit(solution)/shard_map/psum | solution.py:62
  88.0 1.2 fusion.35
  89.2 1.2 multiply_reduce_fusion
  90.5 1.2 multiply_convert_fusion
  91.7 0.7 copy-done.5
  92.4 1.1 scatter_custom_fusion
  93.5 9.4 %gather_fusion = bf16[2048,768]{1,0:T(8,128)(2,1)} fusion(bf16[512,768]{1,0:T(8,128)(2,1)S(1)} %scatter_custom_fusion, s32[2048]{0:T(1024)S(1)} %broadcast_clamp_fusion), kind=kCustom, calls=%fused_computation | custom fusion | bytes 6299648 | tf_op jit(solution)/shard_map/gather | solution.py:71
  103.0 5.5 %all-to-all-start = ((bf16[8,256,768]{2,1,0:T(8,128)(2,1)}), bf16[8,256,768]{2,1,0:T(8,128)(2,1)}, u32[]{:S(2)}, u32[]{:S(2)}) async-start(bf16[8,256,768]{2,1,0:T(8,128)(2,1)} %bitcast.94), calls=%async_computation | async-start | bytes 6291456 | tf_op jit(solution)/shard_map/all_to_all | solution.py:70
  108.5 0.1 broadcast_in_dim.47
  108.6 11.2 %while.14 = (s32[]{:T(128)}, pred[4,128,768]{2,1,0:T(8,128)(4,1)S(1)}, s32[4,128,16]{1,0,2:T(4,128)S(1)}, s32[]{:T(128)}) while((s32[]{:T(128)}, pred[4,128,768]{2,1,0:T(8,128)(4,1)S(1)}, s32[4,128,16]{1,0,2:T(4,128)S(1)}, s32[]{:T(128)}) %tuple.37), condition=%wide.region_10.11_spmd.clone, body=%wide.region_9.10_spmd.clone.sunk | while | flops 786434 | bytes 792641 | solution.py:97
  108.6 0.7 fusion.151
  109.3 0.7 fusion.151
  110.0 0.7 fusion.151
  110.7 0.7 fusion.151
  111.4 0.7 fusion.151
  112.1 0.7 fusion.151
  112.8 0.7 fusion.151
  113.5 0.7 fusion.151
  114.2 0.7 fusion.151
  114.9 0.7 fusion.151
  115.6 0.7 fusion.151
  116.3 0.7 fusion.151
  117.0 0.7 fusion.151
  117.7 0.7 fusion.151
  118.4 0.7 fusion.151
  119.1 0.7 fusion.151
  119.8 1.4 convolution_convert_fusion.5
  121.2 0.7 reshape.124
  121.9 1.4 convolution_convert_fusion.4
  123.3 2.1 convolution_convert_fusion.6
  125.3 52.9 %all-to-all-done = bf16[8,256,768]{2,1,0:T(8,128)(2,1)} async-done(((bf16[8,256,768]{2,1,0:T(8,128)(2,1)}), bf16[8,256,768]{2,1,0:T(8,128)(2,1)}, u32[]{:S(2)}, u32[]{:S(2)}) %all-to-all-start) | async-done | bytes 3145760 | tf_op jit(solution)/shard_map/all_to_all | solution.py:70
  178.2 3.1 %convolution_convert_fusion = bf16[2048,192]{0,1:T(8,128)(2,1)S(1)} fusion(bf16[2048,768]{1,0:T(8,128)(2,1)} %bitcast.9, bf16[3,768,192]{1,2,0:T(8,128)(2,1)} %param.21), kind=kOutput, calls=%fused_computation.13 | convolution fusion | flops 604372992 | bytes 4227072 | tf_op jit(solution)/shard_map/dot_general | solution.py:73
  181.3 3.1 %convolution_convert_fusion.1 = bf16[2048,192]{0,1:T(8,128)(2,1)S(1)} fusion(bf16[2048,768]{1,0:T(8,128)(2,1)} %bitcast.9, bf16[3,768,192]{1,2,0:T(8,128)(2,1)} %param.21), kind=kOutput, calls=%fused_computation.14 | convolution fusion | flops 604372992 | bytes 4227072 | tf_op jit(solution)/shard_map/dot_general | solution.py:74
  184.4 0.3 copy_bitcast_fusion
  184.6 1.7 gather_fusion.2
  186.4 3.1 %copy.29 = bf16[24,128,192]{1,0,2:T(8,128)(2,1)} copy(bf16[24,128,192]{1,2,0:T(8,128)(2,1)} %gather_fusion.2) | data formatting | bytes 2359296 | tf_op jit(solution)/shard_map/gather | solution.py:80
  189.4 2.6 %reshape.126 = bf16[4,768,2,96]{1,0,3,2:T(4,128)(2,1)S(1)} reshape(bf16[24,128,192]{1,0,2:T(8,128)(2,1)} %copy.29) | data formatting | bytes 2359296 | tf_op jit(solution)/shard_map/reshape | solution.py:80
  192.0 2.2 %copy_bitcast_fusion.1 = bf16[20,128,192]{1,2,0:T(8,128)(2,1)} fusion(bf16[2048,192]{0,1:T(8,128)(2,1)S(1)} %convolution_convert_fusion.1, bf16[512,192]{0,1:T(8,128)(2,1)} %convolution_convert_fusion.6), kind=kLoop, calls=%fused_computation.40 | loop fusion | flops 1966080 | bytes 1966080 | tf_op jit(solution)/shard_map/reshape | solution.py:78
  194.2 2.9 %gather_fusion.1 = bf16[24,128,192]{1,2,0:T(8,128)(2,1)} fusion(bf16[20,128,192]{1,2,0:T(8,128)(2,1)} %copy_bitcast_fusion.1, s32[1024]{0:T(1024)S(1)} %pad_clamp_fusion), kind=kCustom, calls=%fused_computation.1 | custom fusion | bytes 2359392 | tf_op jit(solution)/shard_map/gather | solution.py:81
  197.2 3.1 %copy.27 = bf16[24,128,192]{1,0,2:T(8,128)(2,1)} copy(bf16[24,128,192]{1,2,0:T(8,128)(2,1)} %gather_fusion.1) | data formatting | bytes 2359296 | tf_op jit(solution)/shard_map/gather | solution.py:81
  200.3 3.4 %reshape.122 = bf16[4,768,2,96]{1,0,3,2:T(4,128)(2,1)} reshape(bf16[24,128,192]{1,0,2:T(8,128)(2,1)} %copy.27) | data formatting | bytes 2359296 | tf_op jit(solution)/shard_map/reshape | solution.py:81
  203.7 0.6 fusion.13
  204.3 1.7 fusion.134
  206.0 0.7 fusion.18
  206.7 0.2 copy.33
  206.9 0.7 copy.74
  (58 shorter events, 0.4 us)
Async XLA Ops:
  7.2 43.5 %copy-start = (bf16[768,768]{1,0:T(8,128)(2,1)S(1)}, bf16[768,768]{1,0:T(8,128)(2,1)}, u32[]{:S(2)}) copy-start(bf16[768,768]{1,0:T(8,128)(2,1)} %param.18) | copy-start | bytes 3538948
  7.2 1.6 copy-start.2
  7.2 1.6 copy-start.11
  7.2 39.9 %all-reduce.3.cloned.1.call-start = ((), (), s32[]{:S(2)}) async-start(), calls=%async_computation.1 | async-start | bytes 786432 | tf_op jit(solution)/shard_map/psum | solution.py:56
  9.4 1.1 copy-start.6
  9.8 1.9 copy-start.10
  9.8 2.0 copy-start.8
  9.8 2.0 copy-start.9
  9.9 2.0 copy-start.7
  11.6 76.4 %all-reduce.5.cloned.1.call-start = ((), (), s32[]{:S(2)}) async-start(), calls=%async_computation.2 | async-start | bytes 786432 | tf_op jit(solution)/shard_map/psum | solution.py:62
  50.7 4.5 %copy-start.12 = (s32[2]{0:T(128)S(1)}, s32[2]{0:T(128)}, u32[]{:S(2)}) copy-start(s32[2]{0:T(128)} %param.22) | copy-start | bytes 28
  55.2 37.2 %copy-start.1 = (bf16[512,768]{1,0:T(8,128)(2,1)S(1)}, bf16[512,768]{1,0:T(8,128)(2,1)}, u32[]{:S(2)}) copy-start(bf16[512,768]{1,0:T(8,128)(2,1)} %param.20) | copy-start | bytes 2359300
  91.6 0.7 copy-start.5
  103.0 75.2 %all-to-all-start = ((bf16[8,256,768]{2,1,0:T(8,128)(2,1)}), bf16[8,256,768]{2,1,0:T(8,128)(2,1)}, u32[]{:S(2)}, u32[]{:S(2)}) async-start(bf16[8,256,768]{2,1,0:T(8,128)(2,1)} %bitcast.94), calls=%async_computation | async-start | bytes 6291456 | tf_op jit(solution)/shard_map/all_to_all | solution.py:70
  197.2 6.5 %copy-start.3 = (bf16[4,128,2,96]{1,0,3,2:T(4,128)(2,1)S(1)}, bf16[4,128,2,96]{1,0,3,2:T(4,128)(2,1)}, u32[]{:S(2)}) copy-start(bf16[4,128,2,96]{1,0,3,2:T(4,128)(2,1)} %reshape.124) | copy-start | bytes 589828
  204.3 1.7 copy-start.4
Sparse Core Ops, SparseCore 0:
  11.7 35.2 all-reduce.2
  55.4 32.6 all-reduce.4
where the time goes:
time: 215 us; the launch traced here: 214 us
  waiting for transfers between devices  121 us (56%)
  local copies, waits for them, and re-layouts  30.4 us (14%)
  other arithmetic  22.1 us (10%)
  matrix products  20.8 us (10%)
  between operations  14.4 us (7%)
  starting transfers between devices  5.59 us (3%)
    all_to_all x1, waiting for transfers between devices, local(): lax.all_to_all(features[send_rows], 'dp', split_axis=0, concat_axis=0, ti...  52.9 us
    psum x1, waiting for transfers between devices, local(): attn = lax.psum(attn_terms.astype(jnp.bfloat16), 'mp').astype(jnp.float32)  35.1 us
    psum x1, waiting for transfers between devices, local(): ffn = lax.psum(ffn_terms.astype(jnp.bfloat16), 'mp').astype(jnp.float32)  32.7 us
    or x16, other arithmetic, add_edge(): return edges | (chosen == columns)  10.7 us
    gather x1, local copies, waits for them, and re-layouts, local(): features[send_rows]  9.44 us
    gather x2, local copies, waits for them, and re-layouts, local(): value_rows[tile_cols].reshape(row_tiles, TPR * TILE, local_heads, GHD)  6.07 us
    all_to_all x1, starting transfers between devices, local(): lax.all_to_all(features[send_rows], 'dp', split_axis=0, concat_axis=0, ti...  5.51 us
    gather x2, local copies, waits for them, and re-layouts, local(): key_rows[tile_cols].reshape(row_tiles, TPR * TILE, local_heads, GHD)  4.83 us
  transfers between devices with their start and end apart: 3, of which 3 were waited for; matrix products, arithmetic and copies ran while one was open for 8% of the time, Pallas kernels for 0%

commit v1 on v0

v1 whole, which is shorter than its diff:
```python
import jax
import jax.numpy as jnp
from jax import lax
from jax.experimental import pallas as pl
from jax.experimental.pallas import tpu as pltpu
from jax.sharding import PartitionSpec as P

SEQ = 128
TILE = 128
DEG = 16
TPR = 6
HD = 64
GHD = 96

eps_norm = 1e-06
bf = jnp.bfloat16
f32 = jnp.float32

VMEM = pl.BlockSpec(memory_space=pltpu.VMEM)
SMEM = pl.BlockSpec(memory_space=pltpu.SMEM)
NT = (((1,), (1,)), ((), ()))


def call(kernel, outs, args, smem=(), scratch=(), flops=0, name=None):
    specs = [SMEM if i in smem else VMEM for i in range(len(args))]
    nbytes = sum(a.size * a.dtype.itemsize for a in args)
    return pl.pallas_call(
        kernel,
        out_shape=outs,
        in_specs=specs,
        out_specs=jax.tree.map(lambda _: VMEM, outs),
        scratch_shapes=list(scratch),
        compiler_params=pltpu.CompilerParams(vmem_limit_bytes=40 * 1024 * 1024),
        cost_estimate=pl.CostEstimate(flops=flops, bytes_accessed=nbytes, transcendentals=0),
        name=name,
    )(*args)


def shape(dims, dtype):
    return jax.ShapeDtypeStruct(dims, dtype)


def dot(a, b):
    return jnp.dot(a, b, preferred_element_type=f32)


def dot_nt(a, b):
    return lax.dot_general(a, b, NT, preferred_element_type=f32)


def layer_norm(values, gain):
    mean = jnp.mean(values, axis=-1, keepdims=True)
    centred = values - mean
    var = jnp.mean(centred * centred, axis=-1, keepdims=True)
    return centred * lax.rsqrt(var + eps_norm) * gain


def send_kernel(table_ref, w_ref, ids_ref, sent_ref, kv_ref, q_ref):
    table = table_ref[...]
    cols = w_ref.shape[2]
    kv_ref[:, :cols] = dot(table, w_ref[1]).astype(bf)
    kv_ref[:, cols:] = dot(table, w_ref[2]).astype(bf)
    kv = kv_ref[...]
    nodes = table.shape[0]
    ids = ids_ref[...].astype(f32).T.astype(jnp.int32)
    for tile in range(ids.shape[1]):
        lanes = lax.broadcasted_iota(jnp.int32, (TILE, nodes), 1)
        hot = jnp.where(lanes == ids[:, tile : tile + 1], 1.0, 0.0).astype(bf)
        sent_ref[tile * TILE : (tile + 1) * TILE, :] = dot(hot, kv).astype(bf)
    q_ref[...] = dot(table, w_ref[0]).astype(bf)


def mask_kernel(slots_ref, mask_ref):
    rows = slots_ref.shape[0]
    for tile in range(rows // TILE):
        slots = slots_ref[tile * TILE : (tile + 1) * TILE, :]
        lanes = lax.broadcasted_iota(jnp.int32, (TILE, TPR * TILE), 1)
        edges = lanes == lax.broadcasted_iota(jnp.int32, (TILE, TPR * TILE), 0)
        for edge in range(DEG):
            edges = edges | (lanes == slots[:, edge : edge + 1])
        mask_ref[tile * TILE : (tile + 1) * TILE, :] = jnp.where(edges, 1.0, 0.0).astype(bf)


def attn_kernel(who_ref, titles_ref, w_in_ref, w_out_ref, *refs):
    outs, total = refs[:-1], refs[-1]
    titles = titles_ref[...]
    q = dot(titles, w_in_ref[0]).astype(bf)
    k = dot(titles, w_in_ref[1]).astype(bf)
    v = dot(titles, w_in_ref[2]).astype(bf)
    cols = q.shape[1]
    heads = cols // HD
    lanes = lax.broadcasted_iota(jnp.int32, (SEQ, cols), 1) // HD
    for title in range(titles.shape[0] // SEQ):
        rows = slice(title * SEQ, (title + 1) * SEQ)
        qt, kt, vt = q[rows], k[rows], v[rows]
        stacked = jnp.concatenate(
            [jnp.where(lanes == h, qt, jnp.zeros_like(qt)) for h in range(heads)], axis=0
        )
        scores = dot_nt(stacked, kt) * (1.0 / HD**0.5)
        expo = jnp.exp(scores - jnp.max(scores, axis=-1, keepdims=True))
        probs = (expo / jnp.sum(expo, axis=-1, keepdims=True)).astype(bf)
        mixed = dot(probs, vt)
        context = mixed[:SEQ]
        for h in range(1, heads):
            context = jnp.where(lanes == h, mixed[h * SEQ : (h + 1) * SEQ], context)
        total[rows, :] = dot(context.astype(bf), w_out_ref[...])
    chunk = outs[0].shape[0]
    for step, out in enumerate(outs):
        out[...] = total[pl.ds(pl.multiple_of(who_ref[step] * chunk, chunk), chunk), :].astype(out.dtype)


def norm_one_kernel(who_ref, titles_ref, gains_ref, own_ref, *refs):
    parts, out = refs[:-1], refs[-1]
    chunk = own_ref.shape[0]
    total = own_ref[...]
    for part in parts:
        total = total + part[...].astype(f32)
    base = titles_ref[pl.ds(pl.multiple_of(who_ref[0] * chunk, chunk), chunk), :].astype(f32)
    out[...] = layer_norm(base + total, gains_ref[0:1, :]).astype(bf)


def gelu(x):
    return 0.5 * x * (1.0 + lax.erf(x * (0.5**0.5)))


def ffn_kernel(w_in_ref, w_out_ref, *refs):
    count = len(refs) // 2
    ins, outs = refs[:count], refs[count:]
    chunk = ins[0].shape[0]
    hidden = jnp.concatenate([ref[...] for ref in ins], axis=0)
    inner = gelu(dot(hidden, w_in_ref[...])).astype(bf)
    total = dot(inner, w_out_ref[...])
    for step, out in enumerate(outs):
        out[...] = total[step * chunk : (step + 1) * chunk].astype(out.dtype)


def norm_two_kernel(hidden_ref, gains_ref, own_ref, *refs):
    parts, out, first = refs[:-2], refs[-2], refs[-1]
    total = own_ref[...]
    for part in parts:
        total = total + part[...].astype(f32)
    done = layer_norm(hidden_ref[...].astype(f32) + total, gains_ref[1:2, :]).astype(bf)
    out[...] = done
    first[...] = done[0:1]


def place_kernel(who_ref, *refs):
    chunks, out = refs[:-1], refs[-1]
    chunk = chunks[0].shape[0]
    for step, ref in enumerate(chunks):
        out[pl.ds(pl.multiple_of(who_ref[step] * chunk, chunk), chunk), :] = ref[...]


def graph_kernel(
    cols_ref, nodes_ref, place_ref, q_ref, kv_ref, far_ref, codes_ref, firsts_ref, w_ref, mask_ref,
    out_ref, k_all, v_all,
):
    cols = q_ref.shape[1]
    firsts = firsts_ref[...]
    count = firsts.shape[0]
    first_kv = jnp.concatenate([dot(firsts, w_ref[1]), dot(firsts, w_ref[2])], axis=1).astype(bf)
    first_q = dot(firsts, w_ref[0]).astype(bf)
    codes = codes_ref[...].astype(f32).T.astype(jnp.int32)
    nodes = q_ref.shape[0]
    row_tiles = nodes // TILE
    lanes = lax.broadcasted_iota(jnp.int32, (TILE, count), 1)
    sub = lax.broadcasted_iota(jnp.int32, (TILE, 1), 0)

    def own_code(tile):
        code = jnp.full((TILE, 1), -1, jnp.int32)
        for title in range(nodes_ref.shape[0]):
            code = jnp.where(sub + tile * TILE == nodes_ref[title], place_ref[title], code)
        return code

    for tile in range(row_tiles + far_ref.shape[0] // TILE):
        if tile < row_tiles:
            code = own_code(tile)
            rows = kv_ref[tile * TILE : (tile + 1) * TILE, :]
        else:
            far = tile - row_tiles
            code = codes[:, far : far + 1]
            rows = far_ref[far * TILE : (far + 1) * TILE, :]
        hot = jnp.where(lanes == code, 1.0, 0.0).astype(bf)
        fixed = jnp.where(code >= 0, dot(hot, first_kv), rows.astype(f32)).astype(bf)
        k_all[tile * TILE : (tile + 1) * TILE, :] = fixed[:, :cols]
        v_all[tile * TILE : (tile + 1) * TILE, :] = fixed[:, cols:]

    heads = cols // GHD
    head_of = lax.broadcasted_iota(jnp.int32, (TILE, cols), 1) // GHD
    for tile in range(row_tiles):
        code = own_code(tile)
        hot = jnp.where(lanes == code, 1.0, 0.0).astype(bf)
        rows = q_ref[tile * TILE : (tile + 1) * TILE, :].astype(f32)
        q = jnp.where(code >= 0, dot(hot, first_q), rows)
        stacked = jnp.concatenate(
            [jnp.where(head_of == h, q, 0.0) for h in range(heads)], axis=0
        ).astype(bf)
        starts = [pl.multiple_of(cols_ref[tile, c] * TILE, TILE) for c in range(TPR)]
        scores = jnp.concatenate(
            [dot_nt(stacked, k_all[pl.ds(start, TILE), :]) for start in starts], axis=1
        ) * (1.0 / GHD**0.5)
        mask = mask_ref[tile * TILE : (tile + 1) * TILE, :].astype(f32)
        mask = jnp.concatenate([mask] * heads, axis=0) > 0.5
        masked = jnp.where(mask, scores, -jnp.inf)
        expo = jnp.exp(masked - jnp.max(masked, axis=-1, keepdims=True))
        weights = (expo / jnp.sum(expo, axis=-1, keepdims=True)).astype(bf)
        mixed = jnp.zeros((heads * TILE, cols), f32)
        for c, start in enumerate(starts):
            mixed = mixed + dot(weights[:, c * TILE : (c + 1) * TILE], v_all[pl.ds(start, TILE), :])
        out = mixed[:TILE]
        for h in range(1, heads):
            out = jnp.where(head_of == h, mixed[h * TILE : (h + 1) * TILE], out)
        out_ref[tile * TILE : (tile + 1) * TILE, :] = out.astype(bf)


def local(

    titles,
    w_attn_in,
    w_attn_out,
    w_ffn_in,
    w_ffn_out,
    gains,
    node_table,
    w_graph,
    title_nodes,
    send_ids,
    tile_cols,
    nbr_slots,
):
    tok_rows, width = titles.shape
    nodes = node_table.shape[0]
    cols = w_graph.shape[2]
    mp = lax.axis_size("mp")
    dp = lax.axis_size("dp")
    me_mp = lax.axis_index("mp").astype(jnp.int32)
    me_dp = lax.axis_index("dp").astype(jnp.int32)
    who = me_mp ^ jnp.arange(mp, dtype=jnp.int32)
    chunk = tok_rows // mp
    per_part = title_nodes.shape[0]
    fetch = send_ids.shape[2]

    def swap(value, step):
        return lax.ppermute(value, "mp", [(i, i ^ step) for i in range(mp)])

    ids = send_ids.reshape(-1, TILE)
    sent, kv, q = call(
        send_kernel,
        (shape((dp * fetch, 2 * cols), bf), shape((nodes, 2 * cols), bf), shape((nodes, cols), bf)),
        (node_table, w_graph, ids),
        flops=2 * nodes * width * 3 * cols + 2 * dp * fetch * nodes * 2 * cols,
        name="send",
    )
    far = lax.all_to_all(
        sent.reshape(dp, fetch, 2 * cols), "dp", split_axis=0, concat_axis=0, tiled=True
    ).reshape(dp * fetch, 2 * cols)
    titles_at = jnp.arange(per_part, dtype=jnp.int32) * SEQ // chunk
    place = me_dp * mp + titles_at
    code = jnp.full(send_ids.shape[1:], -1, jnp.int32)
    for title in range(per_part):
        code = jnp.where(send_ids[0] == title_nodes[title], place[title], code)
    codes = lax.all_to_all(code, "dp", split_axis=0, concat_axis=0, tiled=True).reshape(-1, TILE)

    terms = call(
        attn_kernel,
        tuple(shape((chunk, width), bf if step else f32) for step in range(mp)),
        (who, titles, w_attn_in, w_attn_out),
        smem=(0,),
        scratch=[pltpu.VMEM((tok_rows, width), f32)],
        flops=2 * tok_rows * width * 4 * w_attn_in.shape[2],
        name="attn",
    )
    parts = [swap(terms[step], step) for step in range(1, mp)]
    hidden = call(
        norm_one_kernel,
        shape((chunk, width), bf),
        (who, titles, gains, terms[0], *parts),
        smem=(0,),
        name="norm_one",
    )
    hiddens = [hidden] + [swap(hidden, step) for step in range(1, mp)]
    terms = call(
        ffn_kernel,
        tuple(shape((chunk, width), bf if step else f32) for step in range(mp)),
        (w_ffn_in, w_ffn_out, *hiddens),
        flops=4 * tok_rows * width * w_ffn_in.shape[1],
        name="ffn",
    )
    parts = [swap(terms[step], step) for step in range(1, mp)]
    done, first = call(
        norm_two_kernel,
        (shape((chunk, width), bf), shape((1, width), bf)),
        (hidden, gains, terms[0], *parts),
        name="norm_two",
    )
    firsts = lax.all_to_all(
        jnp.broadcast_to(first, (dp * mp, width)), ("dp", "mp"), split_axis=0, concat_axis=0, tiled=True
    )
    dones = [done] + [swap(done, step) for step in range(1, mp)]
    encoded = call(
        place_kernel, shape((tok_rows, width), bf), (who, *dones), smem=(0,), name="place"
    )

    mask = call(mask_kernel, shape((nodes, TPR * TILE), bf), (nbr_slots,), flops=10**9, name="mask")
    graph_out = call(
        graph_kernel,
        shape((nodes, cols), bf),
        (tile_cols, title_nodes, place, q, kv, far, codes, firsts, w_graph, mask),
        smem=(0, 1, 2),
        scratch=[
            pltpu.VMEM((nodes + dp * fetch, cols), bf),
            pltpu.VMEM((nodes + dp * fetch, cols), bf),
        ],
        flops=10**9,
        name="graph",
    )
    return (encoded, graph_out)


def solution(mesh):
    in_specs = (
        P("dp", None),
        P(None, None, "mp"),
        P("mp", None),
        P(None, "mp"),
        P("mp", None),
        P(),
        P("dp", None),
        P(None, None, "mp"),
        P("dp"),
        P("dp", None, None),
        P("dp", None),
        P("dp", None),
    )
    out_specs = (P("dp", None), P("dp", "mp"))
    return jax.shard_map(
        local, mesh=mesh, in_specs=in_specs, out_specs=out_specs, check_vma=False
    )
```

time: 215 us -> 104 us (0.48)
  waiting for transfers between devices: 121 us -> 41.6 us
  matrix products: 20.8 us -> 0 us
  other arithmetic: 22.1 us -> 4.02 us
  Pallas kernels: 0 us -> 17.8 us
  starting transfers between devices: 5.59 us -> 22.2 us
  local copies, waits for them, and re-layouts: 30.4 us -> 16.6 us
  between operations: 14.4 us -> 0.96 us
    psum x2 -> x0, waiting for transfers between devices: 67.9 us -> none  [the longest x1 35.1 us: local(): attn = lax.psum(attn_terms.astype(jnp.bfloat16), 'mp').astype(jnp.float32)]
    dot_general x14 -> x0, matrix products: 20.5 us -> none  [the longest x1 4.5 us: local(): ffn_terms = jnp.dot(inner, w_ffn_out, preferred_element_type=f32)]
    gather x5 -> x0, local copies, waits for them, and re-layouts: 20.3 us -> none  [the longest x1 9.44 us: local(): features[send_rows]]
    all_to_all x1 -> x3, waiting for transfers between devices: 52.9 us -> 32.6 us  [the longest x1 27.4 us: local(): lax.all_to_all(sent.reshape(dp, fetch, 2 * cols), 'dp', split_axis=0, con...]
    pallas_call x0 -> x8, Pallas kernels: none -> 17.8 us  [call(): pl.pallas_call(kernel, out_shape=outs, in_specs=specs, out_specs=jax.tree...]
    unnamed x28 -> x55, local copies, waits for them, and re-layouts: 1.52 us -> 14.9 us
    or x16 -> x0, other arithmetic: 10.7 us -> none  [add_edge(): return edges | (chosen == columns)]
    ppermute x0 -> x12, starting transfers between devices: none -> 9.25 us  [swap(): return lax.ppermute(value, 'mp', [(i, i ^ step) for i in range(mp)])]
  transfers between devices with their start and end apart: 3 -> 15, of which waited for: 3 -> 7; matrix products, arithmetic and copies ran while one was open for 8% -> 8% of each run, Pallas kernels for 0% -> 6%
where the time goes in v1:
time: 104 us; the launch traced here: 103 us
  waiting for transfers between devices  41.6 us (40%)
  starting transfers between devices  22.2 us (21%)
  Pallas kernels  17.8 us (17%)
  local copies, waits for them, and re-layouts  16.6 us (16%)
  other arithmetic  4.02 us (4%)
    all_to_all x1, waiting for transfers between devices, local(): lax.all_to_all(sent.reshape(dp, fetch, 2 * cols), 'dp', split_axis=0, con...  27.4 us
    pallas_call x8, Pallas kernels, call(): pl.pallas_call(kernel, out_shape=outs, in_specs=specs, out_specs=jax.tree...  17.8 us
    unnamed x55, local copies, waits for them, and re-layouts  14.9 us
    ppermute x12, starting transfers between devices, swap(): return lax.ppermute(value, 'mp', [(i, i ^ step) for i in range(mp)])  9.25 us
    ppermute x12, waiting for transfers between devices, swap(): return lax.ppermute(value, 'mp', [(i, i ^ step) for i in range(mp)])  9.02 us
    all_to_all x1, starting transfers between devices, local(): lax.all_to_all(code, 'dp', split_axis=0, concat_axis=0, tiled=True)  5.78 us
    all_to_all x1, starting transfers between devices, local(): lax.all_to_all(sent.reshape(dp, fetch, 2 * cols), 'dp', split_axis=0, con...  3.76 us
    all_to_all x1, starting transfers between devices, local(): lax.all_to_all(jnp.broadcast_to(first, (dp * mp, width)), ('dp', 'mp'), s...  3.38 us
  transfers between devices with their start and end apart: 15, of which 7 were waited for; matrix products, arithmetic and copies ran while one was open for 8% of the time, Pallas kernels for 6%

profile of v1, /device:TPU:0, one launch (start us, length us, event | category | flops | bytes accessed | tf_op | source)
XLA Modules:
  0.0 103.2 jit_solution(15583392413585590659)
XLA Ops:
  0.7 1.6 %copy.26.w_in_ref = bf16[3,768,192]{2,1,0:T(8,128)(2,1)S(1)} copy(bf16[3,768,192]{1,2,0:T(8,128)(2,1)} %param.13) | data formatting | bytes 1769472 | tf_op args[1]
  2.3 0.0 copy-start.11
  2.3 0.0 copy-start.12
  2.3 0.0 copy-start.2
  2.3 2.2 %attn.1 = (f32[64,768]{1,0:T(8,128)S(1)}, bf16[64,768]{1,0:T(8,128)(2,1)S(1)}, bf16[64,768]{1,0:T(8,128)(2,1)S(1)}, bf16[64,768]{1,0:T(8,128)(2,1)S(1)}) custom-call(s32[4]{0:T(128)S(1)} %iota_xor_fusion.who_ref, bf16[256,768]{1,0:T(8,128)(2,1)S(1)} %copy-done.1, bf16[3,768,192]{2,1,0:T(8,128)(2,1)S(1)} %copy.26.w_in_ref, bf16[192,768]{1,0:T(8,128)(2,1)S(1)} %copy-done.6), custom_call_target="tpu_custom_call" | custom-call | flops 301989888 | bytes 1572880 | tf_op jit(solution)/shard_map/attn/pallas_call | solution.py:27
  4.6 0.5 collective-permute-start
  5.1 2.6 %collective-permute-start.1 = (bf16[64,768]{1,0:T(8,128)(2,1)S(1)}, bf16[64,768]{1,0:T(8,128)(2,1)S(1)}, u32[]{:S(2)}, u32[]{:S(2)}) collective-permute-start(bf16[64,768]{1,0:T(8,128)(2,1)S(1)} %get-tuple-element.17), channel_id=1, source_target_pairs={{0,2},{1,3},{2,0},{3,1},{4,6},{5,7},{6,4},{7,5},{8,10},{9,11},{10,... | collective-permute-start | bytes 294920 | tf_op jit(solution)/shard_map/ppermute | solution.py:244
  7.7 0.1 collective-permute-start.2
  7.8 0.6 fusion.3
  8.4 0.0 collective-permute-done.refs_0_
  8.4 3.0 %collective-permute-done.1.refs_1_ = bf16[64,768]{1,0:T(8,128)(2,1)S(1)} collective-permute-done((bf16[64,768]{1,0:T(8,128)(2,1)S(1)}, bf16[64,768]{1,0:T(8,128)(2,1)S(1)}, u32[]{:S(2)}, u32[]{:S(2)}) %collective-permute-start.1) | collective-permute-done | bytes 98336 | tf_op jit(solution)/shard_map/ppermute | solution.py:244
  11.3 1.6 %collective-permute-done.2.refs_2_ = bf16[64,768]{1,0:T(8,128)(2,1)S(1)} collective-permute-done((bf16[64,768]{1,0:T(8,128)(2,1)S(1)}, bf16[64,768]{1,0:T(8,128)(2,1)S(1)}, u32[]{:S(2)}, u32[]{:S(2)}) %collective-permute-start.2) | collective-permute-done | bytes 98336 | tf_op jit(solution)/shard_map/ppermute | solution.py:244
  12.9 0.8 norm_one.1.refs_0_.hidden_ref
  13.7 0.2 collective-permute-start.3
  13.9 1.7 %collective-permute-start.4 = (bf16[64,768]{1,0:T(8,128)(2,1)S(1)}, bf16[64,768]{1,0:T(8,128)(2,1)S(1)}, u32[]{:S(2)}, u32[]{:S(2)}) collective-permute-start(bf16[64,768]{1,0:T(8,128)(2,1)S(1)} %norm_one.1.refs_0_.hidden_ref), channel_id=1, source_target_pairs={{0,2},{1,3},{2,0},{3,1},{4,6},{5,7},{6,4},{7,5},{8,10},{9,11},{10,... | collective-permute-start | bytes 294920 | tf_op jit(solution)/shard_map/ppermute | solution.py:244
  15.6 0.0 collective-permute-start.5
  15.6 0.6 fusion.2
  16.3 0.0 collective-permute-done.3.refs_1_
  16.3 3.1 %collective-permute-done.4.refs_2_ = bf16[64,768]{1,0:T(8,128)(2,1)S(1)} collective-permute-done((bf16[64,768]{1,0:T(8,128)(2,1)S(1)}, bf16[64,768]{1,0:T(8,128)(2,1)S(1)}, u32[]{:S(2)}, u32[]{:S(2)}) %collective-permute-start.4) | collective-permute-done | bytes 98336 | tf_op jit(solution)/shard_map/ppermute | solution.py:244
  19.3 1.4 %collective-permute-done.5.refs_3_ = bf16[64,768]{1,0:T(8,128)(2,1)S(1)} collective-permute-done((bf16[64,768]{1,0:T(8,128)(2,1)S(1)}, bf16[64,768]{1,0:T(8,128)(2,1)S(1)}, u32[]{:S(2)}, u32[]{:S(2)}) %collective-permute-start.5) | collective-permute-done | bytes 98336 | tf_op jit(solution)/shard_map/ppermute | solution.py:244
  20.7 1.3 %copy-done.3 = bf16[768,768]{1,0:T(8,128)(2,1)S(1)} copy-done((bf16[768,768]{1,0:T(8,128)(2,1)S(1)}, bf16[768,768]{1,0:T(8,128)(2,1)}, u32[]{:S(2)}) %copy-start.3) | copy-done | bytes 1179672
  22.0 0.9 ffn.1
  22.9 0.3 collective-permute-start.6
  23.2 1.6 %collective-permute-start.7 = (bf16[64,768]{1,0:T(8,128)(2,1)S(1)}, bf16[64,768]{1,0:T(8,128)(2,1)S(1)}, u32[]{:S(2)}, u32[]{:S(2)}) collective-permute-start(bf16[64,768]{1,0:T(8,128)(2,1)S(1)} %get-tuple-element.21), channel_id=1, source_target_pairs={{0,2},{1,3},{2,0},{3,1},{4,6},{5,7},{6,4},{7,5},{8,10},{9,11},{10,... | collective-permute-start | bytes 294920 | tf_op jit(solution)/shard_map/ppermute | solution.py:244
  24.7 0.1 collective-permute-start.8
  24.8 3.1 %fusion = s32[8,1,256]{2,1,0:T(1,128)} fusion(s32[1,8,256]{2,1,0:T(8,128)S(1)} %copy-done.23, s32[]{:T(128)} %bitcast.5, s32[]{:T(128)} %bitcast.4, s32[]{:T(128)} %bitcast.3, s32[]{:T(128)} %bitcast.2), kind=kLoop, calls=%fused_computation.3 | loop fusion | flops 8192 | bytes 16400 | tf_op jit(solution)/shard_map/jit(_where)/select_n | solution.py:261
  27.9 5.8 %all-to-all-start.1 = ((s32[8,1,256]{2,1,0:T(1,128)}), s32[8,1,256]{2,1,0:T(1,128)S(1)}, u32[]{:S(2)}, u32[]{:S(2)}) async-start(s32[8,1,256]{2,1,0:T(1,128)} %fusion), calls=%async_computation.1 | async-start | bytes 16384 | tf_op jit(solution)/shard_map/all_to_all | solution.py:262
  33.7 0.0 copy-start.19
  33.7 1.6 %copy.27.w_ref = bf16[3,768,192]{2,1,0:T(8,128)(2,1)S(1)} copy(bf16[3,768,192]{1,2,0:T(8,128)(2,1)} %param.19) | data formatting | bytes 1769472 | tf_op args[7]
  35.3 0.0 collective-permute-done.6.refs_0_
  35.3 0.0 collective-permute-done.7.refs_1_
  35.3 0.2 norm_two.1
  35.6 0.1 broadcast_in_dim.18
  35.7 0.5 broadcast.68
  36.2 0.9 reduce.1
  37.1 0.6 reshape.64
  37.7 2.5 %all-to-all-done.1 = s32[8,1,256]{2,1,0:T(1,128)S(1)} async-done(((s32[8,1,256]{2,1,0:T(1,128)}), s32[8,1,256]{2,1,0:T(1,128)S(1)}, u32[]{:S(2)}, u32[]{:S(2)}) %all-to-all-start.1) | async-done | bytes 8224 | tf_op jit(solution)/shard_map/all_to_all | solution.py:262
  40.2 3.4 %all-to-all-start.2 = ((bf16[32,2,384]{2,1,0:T(2,128)(2,1)}), bf16[32,2,384]{2,1,0:T(2,128)(2,1)S(1)}, u32[]{:S(2)}, u32[]{:S(2)}) async-start(bf16[32,2,384]{2,1,0:T(2,128)(2,1)} %reshape.64), calls=%async_computation.2 | async-start | bytes 98304 | tf_op jit(solution)/shard_map/all_to_all | solution.py:296
  43.6 2.6 %send.1 = (bf16[2048,384]{1,0:T(8,128)(2,1)S(1)}, bf16[512,384]{1,0:T(8,128)(2,1)S(1)}, bf16[512,192]{1,0:T(8,128)(2,1)S(1)}) custom-call(bf16[512,768]{1,0:T(8,128)(2,1)S(1)} %copy-done.19, bf16[3,768,192]{2,1,0:T(8,128)(2,1)S(1)} %copy.27.w_ref, s32[16,128]{1,0:T(8,128)S(1)} %reshape.59.ids_ref), custom_call_target="tpu_custom_call" | custom-call | flops 1258291200 | bytes 1679360 | tf_op jit(solution)/shard_map/send/pallas_call | solution.py:27
  46.3 1.2 %copy-done = bf16[2048,384]{1,0:T(8,128)(2,1)} copy-done((bf16[2048,384]{1,0:T(8,128)(2,1)}, bf16[2048,384]{1,0:T(8,128)(2,1)S(1)}, u32[]{:S(2)}) %copy-start) | copy-done | bytes 1572888
  47.5 0.7 copy-done.7
  48.2 2.8 %all-to-all-done.2 = bf16[32,2,384]{2,1,0:T(2,128)(2,1)S(1)} async-done(((bf16[32,2,384]{2,1,0:T(2,128)(2,1)}), bf16[32,2,384]{2,1,0:T(2,128)(2,1)S(1)}, u32[]{:S(2)}, u32[]{:S(2)}) %all-to-all-start.2) | async-done | bytes 49184 | tf_op jit(solution)/shard_map/all_to_all | solution.py:296
  50.9 0.6 copy-done.20
  51.6 3.8 %all-to-all-start = ((bf16[8,256,384]{2,1,0:T(8,128)(2,1)}), bf16[8,256,384]{2,1,0:T(8,128)(2,1)S(1)}, u32[]{:S(2)}, u32[]{:S(2)}) async-start(bf16[8,256,384]{2,1,0:T(8,128)(2,1)} %bitcast.13), calls=%async_computation | async-start | bytes 3145728 | tf_op jit(solution)/shard_map/all_to_all | solution.py:254
  55.3 0.8 collective-permute-start.10
  56.1 0.8 collective-permute-start.11
  56.9 0.7 collective-permute-start.9
  57.5 0.1 copy.30.slots_ref
  57.7 0.0 copy-start.21
  57.7 4.1 %mask.1.mask_ref = bf16[512,768]{1,0:T(8,128)(2,1)S(1)} custom-call(s32[512,16]{1,0:T(8,128)S(1)} %copy.30.slots_ref), custom_call_target="tpu_custom_call" | custom-call | flops 1000000000 | bytes 32768 | tf_op jit(solution)/shard_map/mask/pallas_call | solution.py:27
  61.8 0.9 copy-done.4
  62.8 0.0 collective-permute-done.10.refs_2_
  62.8 0.0 collective-permute-done.11.refs_3_
  62.8 0.7 copy-done.17
  63.5 1.8 %place.1 = bf16[256,768]{1,0:T(8,128)(2,1)} custom-call(s32[4]{0:T(128)S(1)} %copy-done.17, bf16[64,768]{1,0:T(8,128)(2,1)S(1)} %get-tuple-element.23.refs_0_, bf16[64,768]{1,0:T(8,128)(2,1)} %collective-permute-done.9.refs_1_, bf16[64,768]{1,0:T(8,128)(2,1)} %collective-permute-done.10.refs_2_, bf16[64,768]{1,0:T(8,128)(2,1)} %collective-permute-done.11.refs_3_), custom_call_target="tpu_custom_call" | custom-call | bytes 393232 | tf_op jit(solution)/shard_map/place/pallas_call | solution.py:27
  65.3 27.4 %all-to-all-done = bf16[8,256,384]{2,1,0:T(8,128)(2,1)S(1)} async-done(((bf16[8,256,384]{2,1,0:T(8,128)(2,1)}), bf16[8,256,384]{2,1,0:T(8,128)(2,1)S(1)}, u32[]{:S(2)}, u32[]{:S(2)}) %all-to-all-start) | async-done | bytes 1572896 | tf_op jit(solution)/shard_map/all_to_all | solution.py:254
  92.6 1.1 %copy-done.5 = bf16[512,768]{1,0:T(8,128)(2,1)S(1)} copy-done((bf16[512,768]{1,0:T(8,128)(2,1)S(1)}, bf16[512,768]{1,0:T(8,128)(2,1)}, u32[]{:S(2)}) %copy-start.5) | copy-done | bytes 786456
  93.8 0.9 copy-done.8
  94.7 0.7 copy-done.10
  95.4 0.7 copy-done.13
  96.1 0.6 copy-done.15
  96.7 0.7 copy-done.18
  97.3 5.1 %graph.1 = bf16[512,192]{1,0:T(8,128)(2,1)S(1)} custom-call(s32[4,6]{1,0:T(4,128)S(1)} %copy-done.18, s32[2]{0:T(128)S(1)} %copy-done.13, s32[2]{0:T(128)S(1)} %copy-done.15, bf16[512,192]{1,0:T(8,128)(2,1)S(1)} %copy-done.8, bf16[512,384]{1,0:T(8,128)(2,1)S(1)} %get-tuple-element.25.kv_ref, bf16[2048,384]{1,0:T(8,128)(2,1)S(1)} %bitcast.12, ...), custom_call_target="tpu_custom_call" | custom-call | flops 1000000000 | bytes 3891312 | tf_op jit(solution)/shard_map/graph/pallas_call | solution.py:27
  102.4 0.8 copy.32
  (39 shorter events, 0.2 us)
Async XLA Ops:
  0.6 1.6 %copy-start.1 = (bf16[256,768]{1,0:T(8,128)(2,1)S(1)}, bf16[256,768]{1,0:T(8,128)(2,1)}, u32[]{:S(2)}) copy-start(bf16[256,768]{1,0:T(8,128)(2,1)} %titles_ref.3) | copy-start | bytes 1179652
  0.6 1.6 %copy-start.6 = (bf16[192,768]{1,0:T(8,128)(2,1)S(1)}, bf16[192,768]{1,0:T(8,128)(2,1)}, u32[]{:S(2)}) copy-start(bf16[192,768]{1,0:T(8,128)(2,1)} %w_out_ref.2) | copy-start | bytes 884740
  0.7 12.3 %copy-start.16 = (s32[4]{0:T(128)}, s32[4]{0:T(128)S(1)}, u32[]{:S(2)}) copy-start(s32[4]{0:T(128)S(1)} %iota_xor_fusion.who_ref) | copy-start | bytes 52
  2.3 10.6 %copy-start.11 = (f32[2,768]{1,0:T(2,128)S(1)}, f32[2,768]{1,0:T(2,128)}, u32[]{:S(2)}) copy-start(f32[2,768]{1,0:T(2,128)} %gains_ref.3) | copy-start | bytes 18436
  2.3 13.3 %copy-start.12 = (s32[2]{0:T(128)S(1)}, s32[2]{0:T(128)}, u32[]{:S(2)}) copy-start(s32[2]{0:T(128)} %nodes_ref.1) | copy-start | bytes 28
  2.3 18.4 %copy-start.2 = (bf16[768,768]{1,0:T(8,128)(2,1)S(1)}, bf16[768,768]{1,0:T(8,128)(2,1)}, u32[]{:S(2)}) copy-start(bf16[768,768]{1,0:T(8,128)(2,1)} %w_in_ref.2) | copy-start | bytes 3538948
  4.6 3.8 %collective-permute-start = (bf16[64,768]{1,0:T(8,128)(2,1)S(1)}, bf16[64,768]{1,0:T(8,128)(2,1)S(1)}, u32[]{:S(2)}, u32[]{:S(2)}) collective-permute-start(bf16[64,768]{1,0:T(8,128)(2,1)S(1)} %get-tuple-element.16), channel_id=1, source_target_pairs={{0,1},{1,0},{2,3},{3,2},{4,5},{5,4},{6,7},{7,6},{8,9},{9,8},{10,11... | collective-permute-start | bytes 294920 | tf_op jit(solution)/shard_map/ppermute | solution.py:244
  5.1 6.2 %collective-permute-start.1 = (bf16[64,768]{1,0:T(8,128)(2,1)S(1)}, bf16[64,768]{1,0:T(8,128)(2,1)S(1)}, u32[]{:S(2)}, u32[]{:S(2)}) collective-permute-start(bf16[64,768]{1,0:T(8,128)(2,1)S(1)} %get-tuple-element.17), channel_id=1, source_target_pairs={{0,2},{1,3},{2,0},{3,1},{4,6},{5,7},{6,4},{7,5},{8,10},{9,11},{10,... | collective-permute-start | bytes 294920 | tf_op jit(solution)/shard_map/ppermute | solution.py:244
  7.7 5.2 %collective-permute-start.2 = (bf16[64,768]{1,0:T(8,128)(2,1)S(1)}, bf16[64,768]{1,0:T(8,128)(2,1)S(1)}, u32[]{:S(2)}, u32[]{:S(2)}) collective-permute-start(bf16[64,768]{1,0:T(8,128)(2,1)S(1)} %get-tuple-element.18), channel_id=1, source_target_pairs={{0,3},{1,2},{2,1},{3,0},{4,7},{5,6},{6,5},{7,4},{8,11},{9,10},{10,... | collective-permute-start | bytes 294920 | tf_op jit(solution)/shard_map/ppermute | solution.py:244
  7.8 11.6 %copy-start.14 = (s32[2]{0:T(128)}, s32[2]{0:T(128)S(1)}, u32[]{:S(2)}) copy-start(s32[2]{0:T(128)S(1)} %fusion.1.place_ref) | copy-start | bytes 28
  13.7 2.6 %collective-permute-start.3 = (bf16[64,768]{1,0:T(8,128)(2,1)S(1)}, bf16[64,768]{1,0:T(8,128)(2,1)S(1)}, u32[]{:S(2)}, u32[]{:S(2)}) collective-permute-start(bf16[64,768]{1,0:T(8,128)(2,1)S(1)} %norm_one.1.refs_0_.hidden_ref), channel_id=1, source_target_pairs={{0,1},{1,0},{2,3},{3,2},{4,5},{5,4},{6,7},{7,6},{8,9},{9,8},{10,11... | collective-permute-start | bytes 294920 | tf_op jit(solution)/shard_map/ppermute | solution.py:244
  13.9 5.5 %collective-permute-start.4 = (bf16[64,768]{1,0:T(8,128)(2,1)S(1)}, bf16[64,768]{1,0:T(8,128)(2,1)S(1)}, u32[]{:S(2)}, u32[]{:S(2)}) collective-permute-start(bf16[64,768]{1,0:T(8,128)(2,1)S(1)} %norm_one.1.refs_0_.hidden_ref), channel_id=1, source_target_pairs={{0,2},{1,3},{2,0},{3,1},{4,6},{5,7},{6,4},{7,5},{8,10},{9,11},{10,... | collective-permute-start | bytes 294920 | tf_op jit(solution)/shard_map/ppermute | solution.py:244
  15.6 5.1 %collective-permute-start.5 = (bf16[64,768]{1,0:T(8,128)(2,1)S(1)}, bf16[64,768]{1,0:T(8,128)(2,1)S(1)}, u32[]{:S(2)}, u32[]{:S(2)}) collective-permute-start(bf16[64,768]{1,0:T(8,128)(2,1)S(1)} %norm_one.1.refs_0_.hidden_ref), channel_id=1, source_target_pairs={{0,3},{1,2},{2,1},{3,0},{4,7},{5,6},{6,5},{7,4},{8,11},{9,10},{10,... | collective-permute-start | bytes 294920 | tf_op jit(solution)/shard_map/ppermute | solution.py:244
  20.7 1.3 %copy-start.3 = (bf16[768,768]{1,0:T(8,128)(2,1)S(1)}, bf16[768,768]{1,0:T(8,128)(2,1)}, u32[]{:S(2)}) copy-start(bf16[768,768]{1,0:T(8,128)(2,1)} %w_out_ref.3) | copy-start | bytes 3538948
  22.0 2.8 %copy-start.23 = (s32[1,8,256]{2,1,0:T(8,128)S(1)}, s32[1,8,256]{2,1,0:T(8,128)}, u32[]{:S(2)}) copy-start(s32[1,8,256]{2,1,0:T(8,128)} %param.21) | copy-start | bytes 24580
  22.9 12.4 %collective-permute-start.6 = (bf16[64,768]{1,0:T(8,128)(2,1)S(1)}, bf16[64,768]{1,0:T(8,128)(2,1)S(1)}, u32[]{:S(2)}, u32[]{:S(2)}) collective-permute-start(bf16[64,768]{1,0:T(8,128)(2,1)S(1)} %get-tuple-element.20), channel_id=1, source_target_pairs={{0,1},{1,0},{2,3},{3,2},{4,5},{5,4},{6,7},{7,6},{8,9},{9,8},{10,11... | collective-permute-start | bytes 294920 | tf_op jit(solution)/shard_map/ppermute | solution.py:244
  23.2 12.2 %collective-permute-start.7 = (bf16[64,768]{1,0:T(8,128)(2,1)S(1)}, bf16[64,768]{1,0:T(8,128)(2,1)S(1)}, u32[]{:S(2)}, u32[]{:S(2)}) collective-permute-start(bf16[64,768]{1,0:T(8,128)(2,1)S(1)} %get-tuple-element.21), channel_id=1, source_target_pairs={{0,2},{1,3},{2,0},{3,1},{4,6},{5,7},{6,4},{7,5},{8,10},{9,11},{10,... | collective-permute-start | bytes 294920 | tf_op jit(solution)/shard_map/ppermute | solution.py:244
  24.7 10.6 %collective-permute-start.8 = (bf16[64,768]{1,0:T(8,128)(2,1)S(1)}, bf16[64,768]{1,0:T(8,128)(2,1)S(1)}, u32[]{:S(2)}, u32[]{:S(2)}) collective-permute-start(bf16[64,768]{1,0:T(8,128)(2,1)S(1)} %get-tuple-element.22), channel_id=1, source_target_pairs={{0,3},{1,2},{2,1},{3,0},{4,7},{5,6},{6,5},{7,4},{8,11},{9,10},{10,... | collective-permute-start | bytes 294920 | tf_op jit(solution)/shard_map/ppermute | solution.py:244
  27.9 12.3 %all-to-all-start.1 = ((s32[8,1,256]{2,1,0:T(1,128)}), s32[8,1,256]{2,1,0:T(1,128)S(1)}, u32[]{:S(2)}, u32[]{:S(2)}) async-start(s32[8,1,256]{2,1,0:T(1,128)} %fusion), calls=%async_computation.1 | async-start | bytes 16384 | tf_op jit(solution)/shard_map/all_to_all | solution.py:262
  33.7 9.9 %copy-start.19 = (bf16[512,768]{1,0:T(8,128)(2,1)S(1)}, bf16[512,768]{1,0:T(8,128)(2,1)}, u32[]{:S(2)}) copy-start(bf16[512,768]{1,0:T(8,128)(2,1)} %table_ref.1) | copy-start | bytes 2359300
  40.2 6.1 %copy-start.9 = (s32[8,1,256]{2,1,0:T(1,128)}, s32[8,1,256]{2,1,0:T(1,128)S(1)}, u32[]{:S(2)}) copy-start(s32[8,1,256]{2,1,0:T(1,128)S(1)} %all-to-all-done.1) | copy-start | bytes 24580
  40.2 10.7 %all-to-all-start.2 = ((bf16[32,2,384]{2,1,0:T(2,128)(2,1)}), bf16[32,2,384]{2,1,0:T(2,128)(2,1)S(1)}, u32[]{:S(2)}, u32[]{:S(2)}) async-start(bf16[32,2,384]{2,1,0:T(2,128)(2,1)} %reshape.64), calls=%async_computation.2 | async-start | bytes 98304 | tf_op jit(solution)/shard_map/all_to_all | solution.py:296
  46.3 1.2 %copy-start = (bf16[2048,384]{1,0:T(8,128)(2,1)}, bf16[2048,384]{1,0:T(8,128)(2,1)S(1)}, u32[]{:S(2)}) copy-start(bf16[2048,384]{1,0:T(8,128)(2,1)S(1)} %get-tuple-element.26) | copy-start | bytes 4718596
  47.4 0.7 copy-start.7
  50.9 0.6 copy-start.20
  50.9 6.6 %copy-start.22 = (s32[512,16]{0,1:T(8,128)S(1)}, s32[512,16]{0,1:T(8,128)}, u32[]{:S(2)}) copy-start(s32[512,16]{0,1:T(8,128)} %param.23) | copy-start | bytes 98308
  51.6 41.1 %all-to-all-start = ((bf16[8,256,384]{2,1,0:T(8,128)(2,1)}), bf16[8,256,384]{2,1,0:T(8,128)(2,1)S(1)}, u32[]{:S(2)}, u32[]{:S(2)}) async-start(bf16[8,256,384]{2,1,0:T(8,128)(2,1)} %bitcast.13), calls=%async_computation | async-start | bytes 3145728 | tf_op jit(solution)/shard_map/all_to_all | solution.py:254
  55.3 7.5 %collective-permute-start.10 = (bf16[64,768]{1,0:T(8,128)(2,1)S(1)}, bf16[64,768]{1,0:T(8,128)(2,1)}, u32[]{:S(2)}, u32[]{:S(2)}) collective-permute-start(bf16[64,768]{1,0:T(8,128)(2,1)S(1)} %get-tuple-element.23.refs_0_), channel_id=1, source_target_pairs={{0,2},{1,3},{2,0},{3,1},{4,6},{5,7},{6,4},{7,5},{8,10},{9,11},{10,... | collective-permute-start | bytes 294920 | tf_op jit(solution)/shard_map/ppermute | solution.py:244
  56.1 6.7 %collective-permute-start.11 = (bf16[64,768]{1,0:T(8,128)(2,1)S(1)}, bf16[64,768]{1,0:T(8,128)(2,1)}, u32[]{:S(2)}, u32[]{:S(2)}) collective-permute-start(bf16[64,768]{1,0:T(8,128)(2,1)S(1)} %get-tuple-element.23.refs_0_), channel_id=1, source_target_pairs={{0,3},{1,2},{2,1},{3,0},{4,7},{5,6},{6,5},{7,4},{8,11},{9,10},{10,... | collective-permute-start | bytes 294920 | tf_op jit(solution)/shard_map/ppermute | solution.py:244
  56.9 5.9 %collective-permute-start.9 = (bf16[64,768]{1,0:T(8,128)(2,1)S(1)}, bf16[64,768]{1,0:T(8,128)(2,1)}, u32[]{:S(2)}, u32[]{:S(2)}) collective-permute-start(bf16[64,768]{1,0:T(8,128)(2,1)S(1)} %get-tuple-element.23.refs_0_), channel_id=1, source_target_pairs={{0,1},{1,0},{2,3},{3,2},{4,5},{5,4},{6,7},{7,6},{8,9},{9,8},{10,11... | collective-permute-start | bytes 294920 | tf_op jit(solution)/shard_map/ppermute | solution.py:244
  57.7 5.1 %copy-start.21 = (bf16[32,2,384]{2,1,0:T(2,128)(2,1)S(1)}, bf16[32,2,384]{2,1,0:T(2,128)(2,1)}, u32[]{:S(2)}) copy-start(bf16[32,2,384]{2,1,0:T(2,128)(2,1)} %copy-done.20) | copy-start | bytes 147460
  61.8 0.9 copy-start.4
  62.8 0.7 copy-start.17
  92.6 1.1 %copy-start.5 = (bf16[512,768]{1,0:T(8,128)(2,1)S(1)}, bf16[512,768]{1,0:T(8,128)(2,1)}, u32[]{:S(2)}) copy-start(bf16[512,768]{1,0:T(8,128)(2,1)} %copy-done.4) | copy-start | bytes 2359300
  93.8 0.9 copy-start.8
  94.7 0.7 copy-start.10
  95.4 0.7 copy-start.13
  96.1 0.6 copy-start.15
  96.7 0.7 copy-start.18

commit v2 on v1

v2 whole, which is shorter than its diff:
```python
import jax
import jax.numpy as jnp
from jax import lax
from jax.experimental import pallas as pl
from jax.experimental.pallas import tpu as pltpu
from jax.sharding import PartitionSpec as P

SEQ = 128
TILE = 128
DEG = 16
TPR = 6
HD = 64
GHD = 96

eps_norm = 1e-06
bf = jnp.bfloat16
f32 = jnp.float32

VMEM = pl.BlockSpec(memory_space=pltpu.VMEM)
SMEM = pl.BlockSpec(memory_space=pltpu.SMEM)
HBM = pl.BlockSpec(memory_space=pl.ANY)
AUTO = pl.BlockSpec()
NT = (((1,), (1,)), ((), ()))
TN = (((0,), (0,)), ((), ()))


def call(kernel, outs, args, smem=(), hbm=(), auto=(), scratch=(), out_specs=None, flops=0, name=None):
    def spec(i):
        return SMEM if i in smem else HBM if i in hbm else AUTO if i in auto else VMEM

    specs = [spec(i) for i in range(len(args))]
    nbytes = sum(a.size * a.dtype.itemsize for a in args)
    return pl.pallas_call(
        kernel,
        out_shape=outs,
        in_specs=specs,
        out_specs=jax.tree.map(lambda _: VMEM, outs) if out_specs is None else out_specs,
        scratch_shapes=list(scratch),
        compiler_params=pltpu.CompilerParams(vmem_limit_bytes=40 * 1024 * 1024),
        cost_estimate=pl.CostEstimate(flops=flops, bytes_accessed=nbytes, transcendentals=0),
        name=name,
    )(*args)


def shape(dims, dtype):
    return jax.ShapeDtypeStruct(dims, dtype)


def dot(a, b):
    return jnp.dot(a, b, preferred_element_type=f32)


def dot_nt(a, b):
    return lax.dot_general(a, b, NT, preferred_element_type=f32)


def dot_tn(a, b):
    return lax.dot_general(a, b, TN, preferred_element_type=f32)


def layer_norm(values, gain):
    mean = jnp.mean(values, axis=-1, keepdims=True)
    centred = values - mean
    var = jnp.mean(centred * centred, axis=-1, keepdims=True)
    return centred * lax.rsqrt(var + eps_norm) * gain


def send_kernel(me_ref, at_ref, ids_ref, table_ref, w_ref, sent_ref, kv_ref, q_ref):
    table = table_ref[...]
    cols = w_ref.shape[1]
    kv = jnp.concatenate([dot_nt(table, w_ref[1]), dot_nt(table, w_ref[2])], axis=1).astype(bf)
    kv_ref[...] = kv
    nodes = table.shape[0]
    per_part = at_ref.shape[0]
    parts, fetch = ids_ref.shape
    ids = ids_ref[...].astype(f32).T.astype(jnp.int32)
    lanes = lax.broadcasted_iota(jnp.int32, (fetch, nodes), 1)
    lead = lax.broadcasted_iota(jnp.int32, (fetch, 2 * cols), 1) == 0
    for part in range(parts):
        picked = ids[:, part : part + 1]
        hot = jnp.where(lanes == picked, 1.0, 0.0).astype(bf)
        rows = dot(hot, kv)
        code = jnp.full((fetch, 1), -1, jnp.int32)
        for title in range(per_part):
            code = jnp.where(picked == at_ref[title], me_ref[0] * per_part + title, code)
        mark = jnp.where(lead, jnp.nan, code.astype(f32))
        sent_ref[part * fetch : (part + 1) * fetch, :] = jnp.where(code >= 0, mark, rows).astype(bf)
    q_ref[...] = dot_nt(w_ref[0], table).astype(bf)


def mask_kernel(slots_ref, mask_ref):
    nodes = slots_ref.shape[1]
    for tile in range(nodes // TILE):
        slots = slots_ref[:, tile * TILE : (tile + 1) * TILE]
        keys = lax.broadcasted_iota(jnp.int32, (TPR * TILE, TILE), 0)
        edges = keys == lax.broadcasted_iota(jnp.int32, (TPR * TILE, TILE), 1)
        for edge in range(DEG):
            edges = edges | (keys == slots[edge : edge + 1, :])
        mask_ref[:, tile * TILE : (tile + 1) * TILE] = jnp.where(edges, 1.0, 0.0).astype(bf)


def attn_kernel(who_ref, titles_ref, w_in_ref, w_out_ref, *refs):
    outs, total = refs[:-1], refs[-1]
    titles = titles_ref[...]
    q = dot_nt(titles, w_in_ref[0]).astype(bf)
    k = dot_nt(titles, w_in_ref[1]).astype(bf)
    v = dot_nt(titles, w_in_ref[2]).astype(bf)
    cols = q.shape[1]
    heads = cols // HD
    lanes = lax.broadcasted_iota(jnp.int32, (SEQ, cols), 1) // HD
    for title in range(titles.shape[0] // SEQ):
        rows = slice(title * SEQ, (title + 1) * SEQ)
        qt, kt, vt = q[rows], k[rows], v[rows]
        stacked = jnp.concatenate(
            [jnp.where(lanes == h, qt, jnp.zeros_like(qt)) for h in range(heads)], axis=0
        )
        scores = dot_nt(stacked, kt) * (1.0 / HD**0.5)
        expo = jnp.exp(scores - jnp.max(scores, axis=-1, keepdims=True))
        probs = (expo / jnp.sum(expo, axis=-1, keepdims=True)).astype(bf)
        mixed = dot(probs, vt)
        context = mixed[:SEQ]
        for h in range(1, heads):
            context = jnp.where(lanes == h, mixed[h * SEQ : (h + 1) * SEQ], context)
        total[rows, :] = dot(context.astype(bf), w_out_ref[...])
    chunk = outs[0].shape[0]
    for step, out in enumerate(outs):
        out[...] = total[pl.ds(pl.multiple_of(who_ref[step] * chunk, chunk), chunk), :].astype(out.dtype)


def norm_one_kernel(who_ref, titles_ref, gains_ref, own_ref, *refs):
    parts, out = refs[:-1], refs[-1]
    chunk = own_ref.shape[0]
    total = own_ref[...]
    for part in parts:
        total = total + part[...].astype(f32)
    base = titles_ref[pl.ds(pl.multiple_of(who_ref[0] * chunk, chunk), chunk), :].astype(f32)
    out[...] = layer_norm(base + total, gains_ref[0:1, :]).astype(bf)


def gelu(x):
    return 0.5 * x * (1.0 + lax.erf(x * (0.5**0.5)))


def ffn_kernel(w_in_ref, w_out_ref, *refs):
    count = len(refs) // 2
    ins, outs = refs[:count], refs[count:]
    chunk = ins[0].shape[0]
    hidden = jnp.concatenate([ref[...] for ref in ins], axis=0)
    inner = gelu(dot(hidden, w_in_ref[...])).astype(bf)
    total = dot(inner, w_out_ref[...])
    for step, out in enumerate(outs):
        out[...] = total[step * chunk : (step + 1) * chunk].astype(out.dtype)


def norm_two_kernel(hidden_ref, gains_ref, own_ref, *refs):
    parts, out = refs[:-1], refs[-1]
    total = own_ref[...]
    for part in parts:
        total = total + part[...].astype(f32)
    out[...] = layer_norm(hidden_ref[...].astype(f32) + total, gains_ref[1:2, :]).astype(bf)


def place_kernel(who_ref, *refs):
    chunks, out, first = refs[:-2], refs[-2], refs[-1]
    chunk = chunks[0].shape[0]
    for step, ref in enumerate(chunks):
        out[pl.ds(pl.multiple_of(who_ref[step] * chunk, chunk), chunk), :] = ref[...]
    for title in range(first.shape[0]):
        first[title : title + 1, :] = out[title * SEQ : title * SEQ + 1, :]


def graph_kernel(
    cols_ref, at_ref, me_ref, firsts_ref, q_hbm, kv_hbm, far_hbm, w_hbm, mask_hbm,
    out_ref, k_all, v_all, q_ref, kv_ref, far_ref, w_ref, mask_ref, sems,
):
    moves = [
        pltpu.make_async_copy(source, target, sems.at[i])
        for i, (source, target) in enumerate(
            ((w_hbm, w_ref), (kv_hbm, kv_ref), (far_hbm, far_ref), (q_hbm, q_ref), (mask_hbm, mask_ref))
        )
    ]
    for move in moves:
        move.start()
    cols, nodes = q_ref.shape
    row_tiles = nodes // TILE
    per_part = at_ref.shape[0]
    firsts = firsts_ref[...]
    count = firsts.shape[0]
    moves[0].wait()
    first_kv = jnp.concatenate([dot_nt(firsts, w_ref[1]), dot_nt(firsts, w_ref[2])], axis=1).astype(bf)
    first_q = dot_nt(w_ref[0], firsts)
    lanes = lax.broadcasted_iota(jnp.int32, (TILE, count), 1).astype(f32)
    sub = lax.broadcasted_iota(jnp.int32, (TILE, 1), 0)
    slots = lax.broadcasted_iota(jnp.int32, (1, count), 1)

    moves[1].wait()
    for tile in range(row_tiles + far_ref.shape[0] // TILE):
        if tile < row_tiles:
            rows = kv_ref[tile * TILE : (tile + 1) * TILE, :].astype(f32)
            code = jnp.full((TILE, 1), -1, jnp.int32)
            for title in range(per_part):
                mine = me_ref[0] * per_part + title
                code = jnp.where(sub + tile * TILE == at_ref[title], mine, code)
            code = code.astype(f32)
        else:
            if tile == row_tiles:
                moves[2].wait()
            far = tile - row_tiles
            rows = far_ref[far * TILE : (far + 1) * TILE, :].astype(f32)
            code = jnp.where(rows[:, 0:1] != rows[:, 0:1], rows[:, 1:2], -1.0)
        hot = jnp.where(lanes == code, 1.0, 0.0).astype(bf)
        fixed = jnp.where(code >= 0.0, dot(hot, first_kv), rows).astype(bf)
        k_all[tile * TILE : (tile + 1) * TILE, :] = fixed[:, :cols]
        v_all[tile * TILE : (tile + 1) * TILE, :] = fixed[:, cols:]

    moves[3].wait()
    moves[4].wait()
    heads = cols // GHD
    head_of = lax.broadcasted_iota(jnp.int32, (cols, TILE), 0) // GHD
    node_lane = lax.broadcasted_iota(jnp.int32, (cols, TILE), 1)
    own_q = [
        jnp.sum(jnp.where(slots == me_ref[0] * per_part + title, first_q, 0.0), axis=1, keepdims=True)
        for title in range(per_part)
    ]
    for tile in range(row_tiles):
        q = q_ref[:, tile * TILE : (tile + 1) * TILE].astype(f32)
        for title in range(per_part):
            q = jnp.where(node_lane + tile * TILE == at_ref[title], own_q[title], q)
        stacked = jnp.concatenate(
            [jnp.where(head_of == h, q, 0.0) for h in range(heads)], axis=1
        ).astype(bf)
        starts = [pl.multiple_of(cols_ref[tile, c] * TILE, TILE) for c in range(TPR)]
        scores = jnp.concatenate(
            [dot(k_all[pl.ds(start, TILE), :], stacked) for start in starts], axis=0
        ) * (1.0 / GHD**0.5)
        mask = mask_ref[:, tile * TILE : (tile + 1) * TILE].astype(f32)
        mask = jnp.concatenate([mask] * heads, axis=1) > 0.5
        masked = jnp.where(mask, scores, -jnp.inf)
        expo = jnp.exp(masked - jnp.max(masked, axis=0, keepdims=True))
        weights = (expo * (1.0 / jnp.sum(expo, axis=0, keepdims=True))).astype(bf)
        mixed = jnp.zeros((cols, heads * TILE), f32)
        for c, start in enumerate(starts):
            mixed = mixed + dot_tn(v_all[pl.ds(start, TILE), :], weights[c * TILE : (c + 1) * TILE])
        out = mixed[:, :TILE]
        for h in range(1, heads):
            out = jnp.where(head_of == h, mixed[:, h * TILE : (h + 1) * TILE], out)
        out_ref[:, tile * TILE : (tile + 1) * TILE] = out.astype(bf)


def local(

    titles,
    w_attn_in,
    w_attn_out,
    w_ffn_in,
    w_ffn_out,
    gains,
    node_table,
    w_graph,
    title_nodes,
    send_ids,
    tile_cols,
    nbr_slots,
):
    tok_rows, width = titles.shape
    nodes = node_table.shape[0]
    cols = w_graph.shape[2]
    mp = lax.axis_size("mp")
    dp = lax.axis_size("dp")
    me_mp = lax.axis_index("mp").astype(jnp.int32)
    me_dp = lax.axis_index("dp").astype(jnp.int32).reshape(1)
    who = me_mp ^ jnp.arange(mp, dtype=jnp.int32)
    chunk = tok_rows // mp
    per_part = title_nodes.shape[0]
    fetch = send_ids.shape[2]

    def swap(value, step):
        return lax.ppermute(value, "mp", [(i, i ^ step) for i in range(mp)])

    w_attn_in = jnp.swapaxes(w_attn_in, 1, 2)
    w_graph = jnp.swapaxes(w_graph, 1, 2)
    sent, kv, q = call(
        send_kernel,
        (shape((dp * fetch, 2 * cols), bf), shape((nodes, 2 * cols), bf), shape((cols, nodes), bf)),
        (me_dp, title_nodes, send_ids[0], node_table, w_graph),
        smem=(0, 1),
        auto=(2, 3, 4),

        flops=2 * nodes * width * 3 * cols + 2 * dp * fetch * nodes * 2 * cols,
        name="send",
    )
    far = lax.all_to_all(
        sent.reshape(dp, fetch, 2 * cols), "dp", split_axis=0, concat_axis=0, tiled=True
    ).reshape(dp * fetch, 2 * cols)
    titles, _ = lax.optimization_barrier((titles, sent))

    terms = call(
        attn_kernel,
        tuple(shape((chunk, width), bf if step else f32) for step in range(mp)),
        (who, titles, w_attn_in, w_attn_out),
        smem=(0,),
        auto=(1, 2, 3),
        scratch=[pltpu.VMEM((tok_rows, width), f32)],
        flops=2 * tok_rows * width * 4 * w_attn_in.shape[1],
        name="attn",
    )
    parts = [swap(terms[step], step) for step in range(1, mp)]
    hidden = call(
        norm_one_kernel,
        shape((chunk, width), bf),
        (who, titles, gains, terms[0], *parts),
        smem=(0,),
        name="norm_one",
    )
    hiddens = [hidden] + [swap(hidden, step) for step in range(1, mp)]
    terms = call(
        ffn_kernel,
        tuple(shape((chunk, width), bf if step else f32) for step in range(mp)),
        (w_ffn_in, w_ffn_out, *hiddens),
        flops=4 * tok_rows * width * w_ffn_in.shape[1],
        name="ffn",
    )
    parts = [swap(terms[step], step) for step in range(1, mp)]
    done = call(
        norm_two_kernel,
        shape((chunk, width), bf),
        (hidden, gains, terms[0], *parts),
        name="norm_two",
    )
    dones = [done] + [swap(done, step) for step in range(1, mp)]
    encoded, first = call(
        place_kernel,
        (shape((tok_rows, width), bf), shape((per_part, width), bf)),
        (who, *dones),
        smem=(0,),
        name="place",
    )
    firsts = lax.all_gather(first, "dp", axis=0, tiled=True)

    mask = call(
        mask_kernel, shape((TPR * TILE, nodes), bf), (nbr_slots.T,), flops=10**9, name="mask"
    )
    graph_out = call(
        graph_kernel,
        shape((cols, nodes), bf),
        (tile_cols, title_nodes, me_dp, firsts, q, kv, far, w_graph, mask),
        smem=(0, 1, 2),
        hbm=(4, 5, 6, 7, 8),
        scratch=[
            pltpu.VMEM((nodes + dp * fetch, cols), bf),
            pltpu.VMEM((nodes + dp * fetch, cols), bf),
            pltpu.VMEM(q.shape, bf),
            pltpu.VMEM(kv.shape, bf),
            pltpu.VMEM(far.shape, bf),
            pltpu.VMEM(w_graph.shape, bf),
            pltpu.VMEM(mask.shape, bf),
            pltpu.SemaphoreType.DMA((5,)),
        ],
        flops=10**9,
        name="graph",
    )
    return (encoded, graph_out.T)


def solution(mesh):
    in_specs = (
        P("dp", None),
        P(None, None, "mp"),
        P("mp", None),
        P(None, "mp"),
        P("mp", None),
        P(),
        P("dp", None),
        P(None, None, "mp"),
        P("dp"),
        P("dp", None, None),
        P("dp", None),
        P("dp", None),
    )
    out_specs = (P("dp", None), P("dp", "mp"))
    return jax.shard_map(
        local, mesh=mesh, in_specs=in_specs, out_specs=out_specs, check_vma=False
    )
```

time: 104 us -> 92.1 us (0.89)
  blocking collectives: 0 us -> 30.8 us
  waiting for transfers between devices: 41.6 us -> 17.1 us
  local copies, waits for them, and re-layouts: 16.6 us -> 7.43 us
  starting transfers between devices: 22.2 us -> 15.5 us
  other arithmetic: 4.02 us -> 0.01 us
  Pallas kernels: 17.8 us -> 20 us
    all_gather x0 -> x1, blocking collectives: none -> 30.8 us  [local(): firsts = lax.all_gather(first, 'dp', axis=0, tiled=True)]
    all_to_all x1, waiting for transfers between devices: 27.4 us -> 0.01 us  [local(): lax.all_to_all(sent.reshape(dp, fetch, 2 * cols), 'dp', split_axis=0, con...]
    all_to_all x2 -> x0, starting transfers between devices: 9.16 us -> none  [the longest x1 5.78 us: local(): lax.all_to_all(code, 'dp', split_axis=0, concat_axis=0, tiled=True)]
    ppermute x12, waiting for transfers between devices: 9.02 us -> 17.1 us  [swap(): return lax.ppermute(value, 'mp', [(i, i ^ step) for i in range(mp)])]
    unnamed x55 -> x37, local copies, waits for them, and re-layouts: 14.9 us -> 7.43 us
    all_to_all x2 -> x0, waiting for transfers between devices: 5.25 us -> none  [the longest x1 2.78 us: local(): lax.all_to_all(jnp.broadcast_to(first, (dp * mp, width)), ('dp', 'mp'), s...]
    all_to_all x1, starting transfers between devices: 3.76 us -> 7.39 us  [local(): lax.all_to_all(sent.reshape(dp, fetch, 2 * cols), 'dp', split_axis=0, con...]
    select_n x1 -> x0, other arithmetic: 3.08 us -> none  [local(): code = jnp.where(send_ids[0] == title_nodes[title], place[title], code)]
  transfers between devices with their start and end apart: 15 -> 13, of which waited for: 7 -> 8; matrix products, arithmetic and copies ran while one was open for 8% -> 0% of each run, Pallas kernels for 6% -> 9%
where the time goes in v2:
time: 92.1 us; the launch traced here: 91.8 us
  blocking collectives  30.8 us (33%)
  Pallas kernels  20 us (22%)
  waiting for transfers between devices  17.1 us (19%)
  starting transfers between devices  15.5 us (17%)
  local copies, waits for them, and re-layouts  7.43 us (8%)
  between operations  1 us (1%)
    all_gather x1, blocking collectives, local(): firsts = lax.all_gather(first, 'dp', axis=0, tiled=True)  30.8 us
    pallas_call x8, Pallas kernels, call(): pl.pallas_call(kernel, out_shape=outs, in_specs=specs, out_specs=jax.tree...  20 us
    ppermute x12, waiting for transfers between devices, swap(): return lax.ppermute(value, 'mp', [(i, i ^ step) for i in range(mp)])  17.1 us
    ppermute x12, starting transfers between devices, swap(): return lax.ppermute(value, 'mp', [(i, i ^ step) for i in range(mp)])  8.07 us
    unnamed x37, local copies, waits for them, and re-layouts  7.43 us
    all_to_all x1, starting transfers between devices, local(): lax.all_to_all(sent.reshape(dp, fetch, 2 * cols), 'dp', split_axis=0, con...  7.39 us
  transfers between devices with their start and end apart: 13, of which 8 were waited for; matrix products, arithmetic and copies ran while one was open for 0% of the time, Pallas kernels for 9%

profile of v2, /device:TPU:0, one launch (start us, length us, event | category | flops | bytes accessed | tf_op | source)
XLA Modules:
  0.0 91.8 jit_solution(7536522931403613710)
XLA Ops:
  0.6 0.0 copy-start.4
  0.6 1.2 %copy-done.4 = bf16[3,768,192]{1,2,0:T(8,128)(2,1)S(1)} copy-done((bf16[3,768,192]{1,2,0:T(8,128)(2,1)S(1)}, bf16[3,768,192]{1,2,0:T(8,128)(2,1)}, u32[]{:S(2)}) %copy-start.4) | copy-done | bytes 884760
  1.8 0.0 copy-start.13
  1.8 0.7 copy-done.13
  2.5 0.0 copy-start.15
  2.5 1.1 %copy-done.15 = bf16[512,768]{1,0:T(8,128)(2,1)S(1)} copy-done((bf16[512,768]{1,0:T(8,128)(2,1)S(1)}, bf16[512,768]{1,0:T(8,128)(2,1)}, u32[]{:S(2)}) %copy-start.15) | copy-done | bytes 786456
  3.6 0.0 copy-start.17
  3.6 0.7 copy-done.17
  4.3 3.7 %send.1 = (bf16[2048,384]{1,0:T(8,128)(2,1)}, bf16[512,384]{1,0:T(8,128)(2,1)S(1)}, bf16[192,512]{1,0:T(8,128)(2,1)S(1)}) custom-call(s32[1]{0:T(128)} %bitcast.me_ref, s32[2]{0:T(128)S(1)} %copy-done.13, s32[8,256]{1,0:T(8,128)S(1)} %bitcast.15, bf16[512,768]{1,0:T(8,128)(2,1)S(1)} %copy-done.15, bf16[3,192,768]{2,1,0:T(8,128)(2,1)S(1)} %bitcast.11), custom_call_target="tpu_custom_call" | custom-call | flops 1258291200 | bytes 1679372 | tf_op jit(solution)/shard_map/send/pallas_call | solution.py:33
  7.9 0.0 copy-start.6
  8.0 0.7 copy-done.6
  8.7 0.7 copy-done.9
  9.4 7.4 %all-to-all-start = ((bf16[8,256,384]{2,1,0:T(8,128)(2,1)}), bf16[8,256,384]{2,1,0:T(8,128)(2,1)S(1)}, u32[]{:S(2)}, u32[]{:S(2)}) async-start(bf16[8,256,384]{2,1,0:T(8,128)(2,1)} %bitcast.5), calls=%async_computation | async-start | bytes 3145728 | tf_op jit(solution)/shard_map/all_to_all | solution.py:292
  16.8 0.0 copy-start.2
  16.8 0.0 copy-done
  16.8 0.0 copy-done.8
  16.8 0.0 copy-start.3
  16.8 1.3 %copy-done.3 = bf16[3,768,192]{1,2,0:T(8,128)(2,1)S(1)} copy-done((bf16[3,768,192]{1,2,0:T(8,128)(2,1)S(1)}, bf16[3,768,192]{1,2,0:T(8,128)(2,1)}, u32[]{:S(2)}) %copy-start.3) | copy-done | bytes 884760
  18.1 2.3 %attn.1 = (f32[64,768]{1,0:T(8,128)S(1)}, bf16[64,768]{1,0:T(8,128)(2,1)S(1)}, bf16[64,768]{1,0:T(8,128)(2,1)S(1)}, bf16[64,768]{1,0:T(8,128)(2,1)S(1)}) custom-call(s32[4]{0:T(128)S(1)} %iota_xor_fusion.who_ref, bf16[256,768]{1,0:T(8,128)(2,1)S(1)} %copy-done, bf16[3,192,768]{2,1,0:T(8,128)(2,1)S(1)} %bitcast.10, bf16[192,768]{1,0:T(8,128)(2,1)S(1)} %copy-done.8), custom_call_target="tpu_custom_call" | custom-call | flops 301989888 | bytes 1572880 | tf_op jit(solution)/shard_map/attn/pallas_call | solution.py:33
  20.4 0.1 collective-permute-start
  20.5 1.6 %collective-permute-start.1 = (bf16[64,768]{1,0:T(8,128)(2,1)S(1)}, bf16[64,768]{1,0:T(8,128)(2,1)S(1)}, u32[]{:S(2)}, u32[]{:S(2)}) collective-permute-start(bf16[64,768]{1,0:T(8,128)(2,1)S(1)} %get-tuple-element.20), channel_id=1, source_target_pairs={{0,2},{1,3},{2,0},{3,1},{4,6},{5,7},{6,4},{7,5},{8,10},{9,11},{10,... | collective-permute-start | bytes 294920 | tf_op jit(solution)/shard_map/ppermute | solution.py:278
  22.1 0.3 collective-permute-start.2
  22.3 0.0 collective-permute-done.refs_0_
  22.3 3.8 %collective-permute-done.1.refs_1_ = bf16[64,768]{1,0:T(8,128)(2,1)S(1)} collective-permute-done((bf16[64,768]{1,0:T(8,128)(2,1)S(1)}, bf16[64,768]{1,0:T(8,128)(2,1)S(1)}, u32[]{:S(2)}, u32[]{:S(2)}) %collective-permute-start.1) | collective-permute-done | bytes 98336 | tf_op jit(solution)/shard_map/ppermute | solution.py:278
  26.1 1.2 %collective-permute-done.2.refs_2_ = bf16[64,768]{1,0:T(8,128)(2,1)S(1)} collective-permute-done((bf16[64,768]{1,0:T(8,128)(2,1)S(1)}, bf16[64,768]{1,0:T(8,128)(2,1)S(1)}, u32[]{:S(2)}, u32[]{:S(2)}) %collective-permute-start.2) | collective-permute-done | bytes 98336 | tf_op jit(solution)/shard_map/ppermute | solution.py:278
  27.3 0.0 copy-done.11
  27.3 0.8 norm_one.1.refs_0_.hidden_ref
  28.1 0.0 copy-start.16
  28.1 0.6 collective-permute-start.3
  28.8 1.5 %collective-permute-start.4 = (bf16[64,768]{1,0:T(8,128)(2,1)S(1)}, bf16[64,768]{1,0:T(8,128)(2,1)S(1)}, u32[]{:S(2)}, u32[]{:S(2)}) collective-permute-start(bf16[64,768]{1,0:T(8,128)(2,1)S(1)} %norm_one.1.refs_0_.hidden_ref), channel_id=1, source_target_pairs={{0,2},{1,3},{2,0},{3,1},{4,6},{5,7},{6,4},{7,5},{8,10},{9,11},{10,... | collective-permute-start | bytes 294920 | tf_op jit(solution)/shard_map/ppermute | solution.py:278
  30.3 0.0 collective-permute-start.5
  30.3 0.0 collective-permute-done.3.refs_1_
  30.3 3.5 %collective-permute-done.4.refs_2_ = bf16[64,768]{1,0:T(8,128)(2,1)S(1)} collective-permute-done((bf16[64,768]{1,0:T(8,128)(2,1)S(1)}, bf16[64,768]{1,0:T(8,128)(2,1)S(1)}, u32[]{:S(2)}, u32[]{:S(2)}) %collective-permute-start.4) | collective-permute-done | bytes 98336 | tf_op jit(solution)/shard_map/ppermute | solution.py:278
  33.8 1.5 %collective-permute-done.5.refs_3_ = bf16[64,768]{1,0:T(8,128)(2,1)S(1)} collective-permute-done((bf16[64,768]{1,0:T(8,128)(2,1)S(1)}, bf16[64,768]{1,0:T(8,128)(2,1)S(1)}, u32[]{:S(2)}, u32[]{:S(2)}) %collective-permute-start.5) | collective-permute-done | bytes 98336 | tf_op jit(solution)/shard_map/ppermute | solution.py:278
  35.4 0.0 copy-done.1
  35.4 0.0 copy-done.2
  35.4 0.9 ffn.1
  36.3 0.5 collective-permute-start.6
  36.8 1.5 %collective-permute-start.7 = (bf16[64,768]{1,0:T(8,128)(2,1)S(1)}, bf16[64,768]{1,0:T(8,128)(2,1)S(1)}, u32[]{:S(2)}, u32[]{:S(2)}) collective-permute-start(bf16[64,768]{1,0:T(8,128)(2,1)S(1)} %get-tuple-element.24), channel_id=1, source_target_pairs={{0,2},{1,3},{2,0},{3,1},{4,6},{5,7},{6,4},{7,5},{8,10},{9,11},{10,... | collective-permute-start | bytes 294920 | tf_op jit(solution)/shard_map/ppermute | solution.py:278
  38.3 0.0 collective-permute-start.8
  38.3 0.0 collective-permute-done.6.refs_0_
  38.3 3.6 %collective-permute-done.7.refs_1_ = bf16[64,768]{1,0:T(8,128)(2,1)S(1)} collective-permute-done((bf16[64,768]{1,0:T(8,128)(2,1)S(1)}, bf16[64,768]{1,0:T(8,128)(2,1)S(1)}, u32[]{:S(2)}, u32[]{:S(2)}) %collective-permute-start.7) | collective-permute-done | bytes 98336 | tf_op jit(solution)/shard_map/ppermute | solution.py:278
  41.9 1.5 %collective-permute-done.8.refs_2_ = bf16[64,768]{1,0:T(8,128)(2,1)S(1)} collective-permute-done((bf16[64,768]{1,0:T(8,128)(2,1)S(1)}, bf16[64,768]{1,0:T(8,128)(2,1)S(1)}, u32[]{:S(2)}, u32[]{:S(2)}) %collective-permute-start.8) | collective-permute-done | bytes 98336 | tf_op jit(solution)/shard_map/ppermute | solution.py:278
  43.4 0.2 norm_two.1.refs_0_
  43.6 0.5 collective-permute-start.9
  44.1 1.5 %collective-permute-start.10 = (bf16[64,768]{1,0:T(8,128)(2,1)S(1)}, bf16[64,768]{1,0:T(8,128)(2,1)S(1)}, u32[]{:S(2)}, u32[]{:S(2)}) collective-permute-start(bf16[64,768]{1,0:T(8,128)(2,1)S(1)} %norm_two.1.refs_0_), channel_id=1, source_target_pairs={{0,2},{1,3},{2,0},{3,1},{4,6},{5,7},{6,4},{7,5},{8,10},{9,11},{10,... | collective-permute-start | bytes 294920 | tf_op jit(solution)/shard_map/ppermute | solution.py:278
  45.6 0.0 collective-permute-start.11
  45.6 0.0 copy-done.16
  45.6 0.0 copy-start.12
  45.6 0.0 copy-start.14
  45.6 3.1 %mask.1.mask_hbm = bf16[768,512]{1,0:T(8,128)(2,1)S(1)} custom-call(s32[16,512]{1,0:T(8,128)S(1)} %bitcast.14), custom_call_target="tpu_custom_call" | custom-call | flops 1000000000 | bytes 32768 | tf_op jit(solution)/shard_map/mask/pallas_call | solution.py:33
  48.7 0.0 collective-permute-done.9.refs_1_
  48.7 0.5 collective-permute-done.10.refs_2_
  49.2 1.5 %collective-permute-done.11.refs_3_ = bf16[64,768]{1,0:T(8,128)(2,1)S(1)} collective-permute-done((bf16[64,768]{1,0:T(8,128)(2,1)S(1)}, bf16[64,768]{1,0:T(8,128)(2,1)S(1)}, u32[]{:S(2)}, u32[]{:S(2)}) %collective-permute-start.11) | collective-permute-done | bytes 98336 | tf_op jit(solution)/shard_map/ppermute | solution.py:278
  50.7 1.3 %place.1 = (bf16[256,768]{1,0:T(8,128)(2,1)}, bf16[2,768]{1,0:T(2,128)(2,1)S(1)}) custom-call(s32[4]{0:T(128)S(1)} %iota_xor_fusion.who_ref, bf16[64,768]{1,0:T(8,128)(2,1)S(1)} %norm_two.1.refs_0_, bf16[64,768]{1,0:T(8,128)(2,1)S(1)} %collective-permute-done.9.refs_1_, bf16[64,768]{1,0:T(8,128)(2,1)S(1)} %collective-permute-done.10.refs_2_, ...), custom_call_target="tpu_custom_call" | custom-call | bytes 393232 | tf_op jit(solution)/shard_map/place/pallas_call | solution.py:33
  52.0 30.8 %all-gather = bf16[8,2,768]{2,1,0:T(2,128)(2,1)S(1)} all-gather(bf16[1,2,768]{2,1,0:T(2,128)(2,1)S(1)} %bitcast.13), channel_id=1, replica_groups=mesh['dp'=8,'mp'=4] {'dp'}, dimensions={0}, use_global_device_ids=true | all-gather | bytes 27648 | tf_op jit(solution)/shard_map/all_gather | solution.py:338
  82.8 0.0 all-to-all-done
  82.8 0.0 copy-done.5
  82.8 0.0 copy-done.10
  82.8 0.0 copy-done.12
  82.8 0.0 copy-done.14
  82.8 0.0 copy-start.7
  82.9 1.0 %copy-done.7 = bf16[512,384]{1,0:T(8,128)(2,1)S(1)} copy-done((bf16[512,384]{1,0:T(8,128)(2,1)S(1)}, bf16[512,384]{1,0:T(8,128)(2,1)}, u32[]{:S(2)}) %copy-start.7) | copy-done | bytes 393240
  83.8 7.8 %graph.1 = bf16[192,512]{1,0:T(8,128)(2,1)} custom-call(s32[4,6]{1,0:T(4,128)S(1)} %copy-done.12, s32[2]{0:T(128)S(1)} %copy-done.14, s32[1]{0:T(128)} %bitcast.me_ref, bf16[16,768]{1,0:T(8,128)(2,1)S(1)} %reshape.17.firsts_ref, bf16[192,512]{1,0:T(8,128)(2,1)S(1)} %copy-done.10, bf16[512,384]{1,0:T(8,128)(2,1)S(1)} %copy-done.7, ...), custom_call_target="tpu_custom_call" | custom-call | flops 1000000000 | bytes 3858540 | tf_op jit(solution)/shard_map/graph/pallas_call | solution.py:33
  (9 shorter events, 0.0 us)
Async XLA Ops:
  0.6 1.2 %copy-start.4 = (bf16[3,768,192]{1,2,0:T(8,128)(2,1)S(1)}, bf16[3,768,192]{1,2,0:T(8,128)(2,1)}, u32[]{:S(2)}) copy-start(bf16[3,768,192]{1,2,0:T(8,128)(2,1)} %param.19) | copy-start | bytes 2654212
  1.8 0.7 copy-start.13
  2.5 1.1 %copy-start.15 = (bf16[512,768]{1,0:T(8,128)(2,1)S(1)}, bf16[512,768]{1,0:T(8,128)(2,1)}, u32[]{:S(2)}) copy-start(bf16[512,768]{1,0:T(8,128)(2,1)} %table_ref.1) | copy-start | bytes 2359300
  3.6 0.7 copy-start.17
  7.9 0.7 copy-start.6
  8.7 0.7 copy-start.9
  9.4 7.4 %copy-start = (bf16[256,768]{1,0:T(8,128)(2,1)S(1)}, bf16[256,768]{1,0:T(8,128)(2,1)}, u32[]{:S(2)}) copy-start(bf16[256,768]{1,0:T(8,128)(2,1)} %titles_ref.1) | copy-start | bytes 1179652
  9.4 7.4 %copy-start.8 = (bf16[192,768]{1,0:T(8,128)(2,1)S(1)}, bf16[192,768]{1,0:T(8,128)(2,1)}, u32[]{:S(2)}) copy-start(bf16[192,768]{1,0:T(8,128)(2,1)} %w_out_ref.2) | copy-start | bytes 884740
  9.4 18.0 %copy-start.11 = (f32[2,768]{1,0:T(2,128)S(1)}, f32[2,768]{1,0:T(2,128)}, u32[]{:S(2)}) copy-start(f32[2,768]{1,0:T(2,128)} %gains_ref.3) | copy-start | bytes 18436
  9.4 73.4 %all-to-all-start = ((bf16[8,256,384]{2,1,0:T(8,128)(2,1)}), bf16[8,256,384]{2,1,0:T(8,128)(2,1)S(1)}, u32[]{:S(2)}, u32[]{:S(2)}) async-start(bf16[8,256,384]{2,1,0:T(8,128)(2,1)} %bitcast.5), calls=%async_computation | async-start | bytes 3145728 | tf_op jit(solution)/shard_map/all_to_all | solution.py:292
  16.8 18.6 %copy-start.1 = (bf16[768,768]{1,0:T(8,128)(2,1)S(1)}, bf16[768,768]{1,0:T(8,128)(2,1)}, u32[]{:S(2)}) copy-start(bf16[768,768]{1,0:T(8,128)(2,1)} %w_in_ref.1) | copy-start | bytes 3538948
  16.8 18.6 %copy-start.2 = (bf16[768,768]{1,0:T(8,128)(2,1)S(1)}, bf16[768,768]{1,0:T(8,128)(2,1)}, u32[]{:S(2)}) copy-start(bf16[768,768]{1,0:T(8,128)(2,1)} %w_out_ref.3) | copy-start | bytes 3538948
  16.8 1.3 %copy-start.3 = (bf16[3,768,192]{1,2,0:T(8,128)(2,1)S(1)}, bf16[3,768,192]{1,2,0:T(8,128)(2,1)}, u32[]{:S(2)}) copy-start(bf16[3,768,192]{1,2,0:T(8,128)(2,1)} %param.13) | copy-start | bytes 2654212
  20.4 1.9 %collective-permute-start = (bf16[64,768]{1,0:T(8,128)(2,1)S(1)}, bf16[64,768]{1,0:T(8,128)(2,1)S(1)}, u32[]{:S(2)}, u32[]{:S(2)}) collective-permute-start(bf16[64,768]{1,0:T(8,128)(2,1)S(1)} %get-tuple-element.19), channel_id=1, source_target_pairs={{0,1},{1,0},{2,3},{3,2},{4,5},{5,4},{6,7},{7,6},{8,9},{9,8},{10,11... | collective-permute-start | bytes 294920 | tf_op jit(solution)/shard_map/ppermute | solution.py:278
  20.5 5.7 %collective-permute-start.1 = (bf16[64,768]{1,0:T(8,128)(2,1)S(1)}, bf16[64,768]{1,0:T(8,128)(2,1)S(1)}, u32[]{:S(2)}, u32[]{:S(2)}) collective-permute-start(bf16[64,768]{1,0:T(8,128)(2,1)S(1)} %get-tuple-element.20), channel_id=1, source_target_pairs={{0,2},{1,3},{2,0},{3,1},{4,6},{5,7},{6,4},{7,5},{8,10},{9,11},{10,... | collective-permute-start | bytes 294920 | tf_op jit(solution)/shard_map/ppermute | solution.py:278
  22.1 5.3 %collective-permute-start.2 = (bf16[64,768]{1,0:T(8,128)(2,1)S(1)}, bf16[64,768]{1,0:T(8,128)(2,1)S(1)}, u32[]{:S(2)}, u32[]{:S(2)}) collective-permute-start(bf16[64,768]{1,0:T(8,128)(2,1)S(1)} %get-tuple-element.21), channel_id=1, source_target_pairs={{0,3},{1,2},{2,1},{3,0},{4,7},{5,6},{6,5},{7,4},{8,11},{9,10},{10,... | collective-permute-start | bytes 294920 | tf_op jit(solution)/shard_map/ppermute | solution.py:278
  28.1 17.5 %copy-start.16 = (s32[512,16]{0,1:T(8,128)S(1)}, s32[512,16]{0,1:T(8,128)}, u32[]{:S(2)}) copy-start(s32[512,16]{0,1:T(8,128)} %param.23) | copy-start | bytes 98308
  28.1 2.2 %collective-permute-start.3 = (bf16[64,768]{1,0:T(8,128)(2,1)S(1)}, bf16[64,768]{1,0:T(8,128)(2,1)S(1)}, u32[]{:S(2)}, u32[]{:S(2)}) collective-permute-start(bf16[64,768]{1,0:T(8,128)(2,1)S(1)} %norm_one.1.refs_0_.hidden_ref), channel_id=1, source_target_pairs={{0,1},{1,0},{2,3},{3,2},{4,5},{5,4},{6,7},{7,6},{8,9},{9,8},{10,11... | collective-permute-start | bytes 294920 | tf_op jit(solution)/shard_map/ppermute | solution.py:278
  28.8 5.1 %collective-permute-start.4 = (bf16[64,768]{1,0:T(8,128)(2,1)S(1)}, bf16[64,768]{1,0:T(8,128)(2,1)S(1)}, u32[]{:S(2)}, u32[]{:S(2)}) collective-permute-start(bf16[64,768]{1,0:T(8,128)(2,1)S(1)} %norm_one.1.refs_0_.hidden_ref), channel_id=1, source_target_pairs={{0,2},{1,3},{2,0},{3,1},{4,6},{5,7},{6,4},{7,5},{8,10},{9,11},{10,... | collective-permute-start | bytes 294920 | tf_op jit(solution)/shard_map/ppermute | solution.py:278
  30.3 5.1 %collective-permute-start.5 = (bf16[64,768]{1,0:T(8,128)(2,1)S(1)}, bf16[64,768]{1,0:T(8,128)(2,1)S(1)}, u32[]{:S(2)}, u32[]{:S(2)}) collective-permute-start(bf16[64,768]{1,0:T(8,128)(2,1)S(1)} %norm_one.1.refs_0_.hidden_ref), channel_id=1, source_target_pairs={{0,3},{1,2},{2,1},{3,0},{4,7},{5,6},{6,5},{7,4},{8,11},{9,10},{10,... | collective-permute-start | bytes 294920 | tf_op jit(solution)/shard_map/ppermute | solution.py:278
  36.3 2.0 %collective-permute-start.6 = (bf16[64,768]{1,0:T(8,128)(2,1)S(1)}, bf16[64,768]{1,0:T(8,128)(2,1)S(1)}, u32[]{:S(2)}, u32[]{:S(2)}) collective-permute-start(bf16[64,768]{1,0:T(8,128)(2,1)S(1)} %get-tuple-element.23), channel_id=1, source_target_pairs={{0,1},{1,0},{2,3},{3,2},{4,5},{5,4},{6,7},{7,6},{8,9},{9,8},{10,11... | collective-permute-start | bytes 294920 | tf_op jit(solution)/shard_map/ppermute | solution.py:278
  36.8 5.1 %collective-permute-start.7 = (bf16[64,768]{1,0:T(8,128)(2,1)S(1)}, bf16[64,768]{1,0:T(8,128)(2,1)S(1)}, u32[]{:S(2)}, u32[]{:S(2)}) collective-permute-start(bf16[64,768]{1,0:T(8,128)(2,1)S(1)} %get-tuple-element.24), channel_id=1, source_target_pairs={{0,2},{1,3},{2,0},{3,1},{4,6},{5,7},{6,4},{7,5},{8,10},{9,11},{10,... | collective-permute-start | bytes 294920 | tf_op jit(solution)/shard_map/ppermute | solution.py:278
  38.3 5.1 %collective-permute-start.8 = (bf16[64,768]{1,0:T(8,128)(2,1)S(1)}, bf16[64,768]{1,0:T(8,128)(2,1)S(1)}, u32[]{:S(2)}, u32[]{:S(2)}) collective-permute-start(bf16[64,768]{1,0:T(8,128)(2,1)S(1)} %get-tuple-element.25), channel_id=1, source_target_pairs={{0,3},{1,2},{2,1},{3,0},{4,7},{5,6},{6,5},{7,4},{8,11},{9,10},{10,... | collective-permute-start | bytes 294920 | tf_op jit(solution)/shard_map/ppermute | solution.py:278
  43.6 5.1 %collective-permute-start.9 = (bf16[64,768]{1,0:T(8,128)(2,1)S(1)}, bf16[64,768]{1,0:T(8,128)(2,1)S(1)}, u32[]{:S(2)}, u32[]{:S(2)}) collective-permute-start(bf16[64,768]{1,0:T(8,128)(2,1)S(1)} %norm_two.1.refs_0_), channel_id=1, source_target_pairs={{0,1},{1,0},{2,3},{3,2},{4,5},{5,4},{6,7},{7,6},{8,9},{9,8},{10,11... | collective-permute-start | bytes 294920 | tf_op jit(solution)/shard_map/ppermute | solution.py:278
  44.1 5.1 %collective-permute-start.10 = (bf16[64,768]{1,0:T(8,128)(2,1)S(1)}, bf16[64,768]{1,0:T(8,128)(2,1)S(1)}, u32[]{:S(2)}, u32[]{:S(2)}) collective-permute-start(bf16[64,768]{1,0:T(8,128)(2,1)S(1)} %norm_two.1.refs_0_), channel_id=1, source_target_pairs={{0,2},{1,3},{2,0},{3,1},{4,6},{5,7},{6,4},{7,5},{8,10},{9,11},{10,... | collective-permute-start | bytes 294920 | tf_op jit(solution)/shard_map/ppermute | solution.py:278
  45.6 5.1 %collective-permute-start.11 = (bf16[64,768]{1,0:T(8,128)(2,1)S(1)}, bf16[64,768]{1,0:T(8,128)(2,1)S(1)}, u32[]{:S(2)}, u32[]{:S(2)}) collective-permute-start(bf16[64,768]{1,0:T(8,128)(2,1)S(1)} %norm_two.1.refs_0_), channel_id=1, source_target_pairs={{0,3},{1,2},{2,1},{3,0},{4,7},{5,6},{6,5},{7,4},{8,11},{9,10},{10,... | collective-permute-start | bytes 294920 | tf_op jit(solution)/shard_map/ppermute | solution.py:278
  45.6 37.2 %copy-start.5 = (bf16[3,768,192]{1,2,0:T(8,128)(2,1)S(1)}, bf16[3,768,192]{1,2,0:T(8,128)(2,1)}, u32[]{:S(2)}) copy-start(bf16[3,768,192]{1,2,0:T(8,128)(2,1)} %param.19) | copy-start | bytes 2654212
  45.6 37.2 %copy-start.10 = (bf16[192,512]{1,0:T(8,128)(2,1)S(1)}, bf16[192,512]{1,0:T(8,128)(2,1)}, u32[]{:S(2)}) copy-start(bf16[192,512]{1,0:T(8,128)(2,1)} %copy-done.9) | copy-start | bytes 589828
  45.6 37.2 %copy-start.12 = (s32[4,6]{1,0:T(4,128)S(1)}, s32[4,6]{1,0:T(4,128)}, u32[]{:S(2)}) copy-start(s32[4,6]{1,0:T(4,128)} %cols_ref.1) | copy-start | bytes 292
  45.6 37.2 %copy-start.14 = (s32[2]{0:T(128)S(1)}, s32[2]{0:T(128)}, u32[]{:S(2)}) copy-start(s32[2]{0:T(128)} %at_ref.3) | copy-start | bytes 28
  82.8 1.0 %copy-start.7 = (bf16[512,384]{1,0:T(8,128)(2,1)S(1)}, bf16[512,384]{1,0:T(8,128)(2,1)}, u32[]{:S(2)}) copy-start(bf16[512,384]{1,0:T(8,128)(2,1)} %copy-done.6) | copy-start | bytes 1179652

commit v3 on v2

v3 whole, which is shorter than its diff:
```python
import jax
import jax.numpy as jnp
from jax import lax
from jax.experimental import pallas as pl
from jax.experimental.pallas import tpu as pltpu
from jax.sharding import PartitionSpec as P

SEQ = 128
TILE = 128
DEG = 16
TPR = 6
HD = 64
GHD = 96

eps_norm = 1e-06
bf = jnp.bfloat16
f32 = jnp.float32

VMEM = pl.BlockSpec(memory_space=pltpu.VMEM)
SMEM = pl.BlockSpec(memory_space=pltpu.SMEM)
ANY = pl.BlockSpec(memory_space=pl.ANY)
NT = (((1,), (1,)), ((), ()))
TN = (((0,), (0,)), ((), ()))


def call(kernel, outs, args, smem=(), hbm=(), scratch=(), flops=0, name=None):
    count, out_count, own = len(args), len(jax.tree.leaves(outs)), len(scratch)
    specs = [SMEM if i in smem else ANY if i in hbm else VMEM for i in range(count)]
    nbytes = sum(a.size * a.dtype.itemsize for a in args)
    buffers = [pltpu.VMEM(args[i].shape, args[i].dtype) for i in hbm]
    sems = [pltpu.SemaphoreType.DMA((len(hbm),))] if hbm else []

    def body(*refs):
        ins, rest = list(refs[:count]), refs[count:]
        kept, moved = rest[: out_count + own], rest[out_count + own :]
        moves = {}
        for j, i in enumerate(hbm):
            moves[i] = pltpu.make_async_copy(ins[i], moved[j], moved[-1].at[j])
            moves[i].start()
            ins[i] = moved[j]

        def ready(*wanted):
            for i in wanted:
                moves[i].wait()

        kernel(ready, *ins, *kept)

    return pl.pallas_call(
        body,
        out_shape=outs,
        in_specs=specs,
        out_specs=jax.tree.map(lambda _: VMEM, outs),
        scratch_shapes=list(scratch) + buffers + sems,
        compiler_params=pltpu.CompilerParams(vmem_limit_bytes=40 * 1024 * 1024),
        cost_estimate=pl.CostEstimate(flops=flops, bytes_accessed=nbytes, transcendentals=0),
        name=name,
    )(*args)


def shape(dims, dtype):
    return jax.ShapeDtypeStruct(dims, dtype)


def dot(a, b):
    return jnp.dot(a, b, preferred_element_type=f32)


def dot_nt(a, b):
    return lax.dot_general(a, b, NT, preferred_element_type=f32)


def dot_tn(a, b):
    return lax.dot_general(a, b, TN, preferred_element_type=f32)


def layer_norm(values, gain):
    mean = jnp.mean(values, axis=-1, keepdims=True)
    centred = values - mean
    var = jnp.mean(centred * centred, axis=-1, keepdims=True)
    return centred * lax.rsqrt(var + eps_norm) * gain


def send_kernel(ready, me_ref, at_ref, ids_ref, table_ref, w_ref, kv_ref, q_ref, sent_ref):
    cols = w_ref.shape[1]
    per_part = at_ref.shape[0]
    fetch, nodes = ids_ref.shape[1], table_ref.shape[0]
    ready(2, 3, 4)
    table = table_ref[...]
    kv = jnp.concatenate([dot_nt(table, w_ref[1]), dot_nt(table, w_ref[2])], axis=1).astype(bf)
    ids = ids_ref[...].astype(f32).T.astype(jnp.int32)
    lanes = lax.broadcasted_iota(jnp.int32, (fetch, nodes), 1)
    lead = lax.broadcasted_iota(jnp.int32, (fetch, 2 * cols), 1) == 0
    for part in range(ids.shape[1]):
        step = me_ref[0] ^ part
        picked = ids[:, part : part + 1]
        hot = jnp.where(lanes == picked, 1.0, 0.0).astype(bf)
        rows = dot(hot, kv)
        code = jnp.full((fetch, 1), -1, jnp.int32)
        for title in range(per_part):
            code = jnp.where(picked == at_ref[title], step * per_part + title, code)
        mark = jnp.where(lead, jnp.nan, code.astype(f32))
        sent_ref[part * fetch : (part + 1) * fetch, :] = jnp.where(code >= 0, mark, rows).astype(bf)
    kv_ref[...] = kv
    q_ref[...] = dot_nt(table, w_ref[0]).astype(bf)


def mask_kernel(ready, slots_ref, mask_ref):
    all_slots = slots_ref[...].astype(f32).T.astype(jnp.int32)
    for tile in range(all_slots.shape[0] // TILE):
        slots = all_slots[tile * TILE : (tile + 1) * TILE, :]
        lanes = lax.broadcasted_iota(jnp.int32, (TILE, TPR * TILE), 1)
        edges = lanes == lax.broadcasted_iota(jnp.int32, (TILE, TPR * TILE), 0)
        for edge in range(DEG):
            edges = edges | (lanes == slots[:, edge : edge + 1])
        mask_ref[tile * TILE : (tile + 1) * TILE, :] = jnp.where(edges, 1.0, 0.0).astype(bf)


def attn_kernel(ready, who_ref, titles_ref, w_in_ref, w_out_ref, *refs):
    outs, total = refs[:-1], refs[-1]
    titles = titles_ref[...]
    q = dot_nt(titles, w_in_ref[0]).astype(bf)
    k = dot_nt(titles, w_in_ref[1]).astype(bf)
    v = dot_nt(titles, w_in_ref[2]).astype(bf)
    cols = q.shape[1]
    heads = cols // HD
    lanes = lax.broadcasted_iota(jnp.int32, (SEQ, cols), 1) // HD
    for title in range(titles.shape[0] // SEQ):
        rows = slice(title * SEQ, (title + 1) * SEQ)
        qt, kt, vt = q[rows], k[rows], v[rows]
        stacked = jnp.concatenate(
            [jnp.where(lanes == h, qt, jnp.zeros_like(qt)) for h in range(heads)], axis=0
        )
        scores = dot_nt(stacked, kt) * (1.0 / HD**0.5)
        expo = jnp.exp(scores - jnp.max(scores, axis=-1, keepdims=True))
        probs = (expo / jnp.sum(expo, axis=-1, keepdims=True)).astype(bf)
        mixed = dot(probs, vt)
        context = mixed[:SEQ]
        for h in range(1, heads):
            context = jnp.where(lanes == h, mixed[h * SEQ : (h + 1) * SEQ], context)
        total[rows, :] = dot(context.astype(bf), w_out_ref[...])
    chunk = outs[0].shape[0]
    for step, out in enumerate(outs):
        out[...] = total[pl.ds(pl.multiple_of(who_ref[step] * chunk, chunk), chunk), :].astype(out.dtype)


def norm_one_kernel(ready, who_ref, titles_ref, gains_ref, own_ref, *refs):
    parts, out = refs[:-1], refs[-1]
    chunk = own_ref.shape[0]
    total = own_ref[...]
    for part in parts:
        total = total + part[...].astype(f32)
    base = titles_ref[pl.ds(pl.multiple_of(who_ref[0] * chunk, chunk), chunk), :].astype(f32)
    out[...] = layer_norm(base + total, gains_ref[0:1, :]).astype(bf)


def gelu(x):
    return 0.5 * x * (1.0 + lax.erf(x * (0.5**0.5)))


def ffn_kernel(ready, w_in_ref, w_out_ref, *refs):
    count = len(refs) // 2
    ins, outs = refs[:count], refs[count:]
    chunk = ins[0].shape[0]
    hidden = jnp.concatenate([ref[...] for ref in ins], axis=0)
    inner = gelu(dot(hidden, w_in_ref[...])).astype(bf)
    total = dot(inner, w_out_ref[...])
    for step, out in enumerate(outs):
        out[...] = total[step * chunk : (step + 1) * chunk].astype(out.dtype)


def norm_two_kernel(ready, hidden_ref, gains_ref, own_ref, *refs):
    parts, out = refs[:-1], refs[-1]
    total = own_ref[...]
    for part in parts:
        total = total + part[...].astype(f32)
    out[...] = layer_norm(hidden_ref[...].astype(f32) + total, gains_ref[1:2, :]).astype(bf)


def place_kernel(ready, who_ref, *refs):
    chunks, out, first = refs[:-2], refs[-2], refs[-1]
    chunk = chunks[0].shape[0]
    for step, ref in enumerate(chunks):
        out[pl.ds(pl.multiple_of(who_ref[step] * chunk, chunk), chunk), :] = ref[...]
    for title in range(first.shape[0]):
        first[title : title + 1, :] = out[title * SEQ : title * SEQ + 1, :]


def graph_kernel(
    ready, cols_ref, at_ref, q_ref, kv_ref, w_ref, mask_ref, far_ref, *refs
):
    *firsts, out_ref, k_all, v_all, firsts_ref = refs
    nodes, cols = q_ref.shape
    per_part = at_ref.shape[0]
    row_tiles = nodes // TILE
    for step, ref in enumerate(firsts):
        firsts_ref[step * per_part : (step + 1) * per_part, :] = ref[...].astype(f32)
    first = firsts_ref[...].astype(bf)
    count = first.shape[0]
    ready(4)
    first_kv = jnp.concatenate([dot_nt(first, w_ref[1]), dot_nt(first, w_ref[2])], axis=1).astype(bf)
    first_q = dot_nt(first, w_ref[0])
    lanes = lax.broadcasted_iota(jnp.int32, (TILE, count), 1).astype(f32)
    sub = lax.broadcasted_iota(jnp.int32, (TILE, 1), 0)

    ready(3)
    for tile in range(row_tiles + far_ref.shape[0] // TILE):
        if tile < row_tiles:
            rows = kv_ref[tile * TILE : (tile + 1) * TILE, :].astype(f32)
            code = jnp.full((TILE, 1), -1.0, f32)
            for title in range(per_part):
                code = jnp.where(sub + tile * TILE == at_ref[title], float(title), code)
        else:
            if tile == row_tiles:
                ready(6)
            start = (tile - row_tiles) * TILE
            rows = far_ref[start : start + TILE, :].astype(f32)
            code = jnp.where(rows[:, 0:1] != rows[:, 0:1], rows[:, 1:2], -1.0)
        hot = jnp.where(lanes == code, 1.0, 0.0).astype(bf)
        fixed = jnp.where(code >= 0.0, dot(hot, first_kv), rows).astype(bf)
        k_all[tile * TILE : (tile + 1) * TILE, :] = fixed[:, :cols]
        v_all[tile * TILE : (tile + 1) * TILE, :] = fixed[:, cols:]

    ready(2, 5)
    heads = cols // GHD
    head_of = lax.broadcasted_iota(jnp.int32, (TILE, cols), 1) // GHD
    for tile in range(row_tiles):
        q = q_ref[tile * TILE : (tile + 1) * TILE, :].astype(f32)
        for title in range(per_part):
            q = jnp.where(sub + tile * TILE == at_ref[title], first_q[title : title + 1], q)
        stacked = jnp.concatenate(
            [jnp.where(head_of == h, q, 0.0) for h in range(heads)], axis=0
        ).astype(bf)
        starts = [pl.multiple_of(cols_ref[tile, c] * TILE, TILE) for c in range(TPR)]
        keys = jnp.concatenate([k_all[pl.ds(start, TILE), :] for start in starts], axis=0)
        values = jnp.concatenate([v_all[pl.ds(start, TILE), :] for start in starts], axis=0)
        scores = dot_nt(stacked, keys) * (1.0 / GHD**0.5)
        mask = mask_ref[tile * TILE : (tile + 1) * TILE, :].astype(f32)
        mask = jnp.concatenate([mask] * heads, axis=0) > 0.5
        masked = jnp.where(mask, scores, -jnp.inf)
        expo = jnp.exp(masked - jnp.max(masked, axis=-1, keepdims=True))
        weights = (expo * (1.0 / jnp.sum(expo, axis=-1, keepdims=True))).astype(bf)
        mixed = dot(weights, values)
        out = mixed[:TILE]
        for h in range(1, heads):
            out = jnp.where(head_of == h, mixed[h * TILE : (h + 1) * TILE], out)
        out_ref[:, tile * TILE : (tile + 1) * TILE] = out.T.astype(bf)


def local(

    titles,
    w_attn_in,
    w_attn_out,
    w_ffn_in,
    w_ffn_out,
    gains,
    node_table,
    w_graph,
    title_nodes,
    send_ids,
    tile_cols,
    nbr_slots,
):
    tok_rows, width = titles.shape
    nodes = node_table.shape[0]
    cols = w_graph.shape[2]
    mp = lax.axis_size("mp")
    dp = lax.axis_size("dp")
    me_mp = lax.axis_index("mp").astype(jnp.int32)
    me_dp = lax.axis_index("dp").astype(jnp.int32).reshape(1)
    who = me_mp ^ jnp.arange(mp, dtype=jnp.int32)
    chunk = tok_rows // mp
    per_part = title_nodes.shape[0]
    fetch = send_ids.shape[2]

    def swap(value, step, axis="mp"):
        return lax.ppermute(value, axis, [(i, i ^ step) for i in range(lax.axis_size(axis))])

    w_attn_in = jnp.swapaxes(w_attn_in, 1, 2)
    w_graph = jnp.swapaxes(w_graph, 1, 2)
    kv, q, sent = call(
        send_kernel,
        (shape((nodes, 2 * cols), bf), shape((nodes, cols), bf), shape((dp * fetch, 2 * cols), bf)),
        (me_dp, title_nodes, send_ids[0], node_table, w_graph),
        smem=(0, 1),
        hbm=(2, 3, 4),
        flops=2 * nodes * width * 3 * cols + 2 * dp * fetch * nodes * 2 * cols,
        name="send",
    )
    far = lax.all_to_all(
        sent.reshape(dp, fetch, 2 * cols), "dp", split_axis=0, concat_axis=0, tiled=True
    ).reshape(dp * fetch, 2 * cols)
    titles, _ = lax.optimization_barrier((titles, kv))

    terms = call(
        attn_kernel,
        tuple(shape((chunk, width), bf if step else f32) for step in range(mp)),
        (who, titles, w_attn_in, w_attn_out),
        smem=(0,),
        scratch=[pltpu.VMEM((tok_rows, width), f32)],
        flops=2 * tok_rows * width * 4 * w_attn_in.shape[1],
        name="attn",
    )
    parts = [swap(terms[step], step) for step in range(1, mp)]
    hidden = call(
        norm_one_kernel,
        shape((chunk, width), bf),
        (who, titles, gains, terms[0], *parts),
        smem=(0,),
        name="norm_one",
    )
    hiddens = [hidden] + [swap(hidden, step) for step in range(1, mp)]
    terms = call(
        ffn_kernel,
        tuple(shape((chunk, width), bf if step else f32) for step in range(mp)),
        (w_ffn_in, w_ffn_out, *hiddens),
        flops=4 * tok_rows * width * w_ffn_in.shape[1],
        name="ffn",
    )
    parts = [swap(terms[step], step) for step in range(1, mp)]
    done = call(
        norm_two_kernel,
        shape((chunk, width), bf),
        (hidden, gains, terms[0], *parts),
        name="norm_two",
    )
    dones = [done] + [swap(done, step) for step in range(1, mp)]
    encoded, first = call(
        place_kernel,
        (shape((tok_rows, width), bf), shape((per_part, width), bf)),
        (who, *dones),
        smem=(0,),
        name="place",
    )
    firsts = [first] + [swap(first, step, "dp") for step in range(1, dp)]

    mask = call(
        mask_kernel, shape((nodes, TPR * TILE), bf), (nbr_slots.T,), flops=10**9, name="mask"
    )
    keys = nodes + dp * fetch
    graph_out = call(
        graph_kernel,
        shape((cols, nodes), bf),
        (tile_cols, title_nodes, q, kv, w_graph, mask, far, *firsts),
        smem=(0, 1),
        hbm=(2, 3, 4, 5, 6),
        scratch=[
            pltpu.VMEM((keys, cols), bf),
            pltpu.VMEM((keys, cols), bf),
            pltpu.VMEM((dp * per_part, width), f32),
        ],
        flops=10**9,
        name="graph",
    )
    return (encoded, graph_out.T)


def solution(mesh):
    in_specs = (
        P("dp", None),
        P(None, None, "mp"),
        P("mp", None),
        P(None, "mp"),
        P("mp", None),
        P(),
        P("dp", None),
        P(None, None, "mp"),
        P("dp"),
        P("dp", None, None),
        P("dp", None),
        P("dp", None),
    )
    out_specs = (P("dp", None), P("dp", "mp"))
    return jax.shard_map(
        local, mesh=mesh, in_specs=in_specs, out_specs=out_specs, check_vma=False
    )
```

time: 92.1 us -> 78.5 us (0.85)
  blocking collectives: 30.8 us -> 0 us
  starting transfers between devices: 15.5 us -> 26.8 us
  waiting for transfers between devices: 17.1 us -> 21.8 us
  Pallas kernels: 20 us -> 21 us
    all_gather x1 -> x0, blocking collectives: 30.8 us -> none  [local(): firsts = lax.all_gather(first, 'dp', axis=0, tiled=True)]
    ppermute x12 -> x19, starting transfers between devices: 8.07 us -> 19.4 us  [swap(): lax.ppermute(value, axis, [(i, i ^ step) for i in range(lax.axis_size(axi...]
    ppermute x12 -> x19, waiting for transfers between devices: 17.1 us -> 21.8 us  [swap(): lax.ppermute(value, axis, [(i, i ^ step) for i in range(lax.axis_size(axi...]
    pallas_call x8, Pallas kernels: 20 us -> 21 us  [call(): pl.pallas_call(body, out_shape=outs, in_specs=specs, out_specs=jax.tree.m...]
    unnamed x37 -> x36, local copies, waits for them, and re-layouts: 7.43 us -> 7.45 us
  transfers between devices with their start and end apart: 13 -> 20, of which waited for: 8 -> 9; matrix products, arithmetic and copies ran while one was open for 0% -> 0% of each run, Pallas kernels for 9% -> 12%
where the time goes in v3:
time: 78.5 us; the launch traced here: 78.1 us
  starting transfers between devices  26.8 us (34%)
  waiting for transfers between devices  21.8 us (28%)
  Pallas kernels  21 us (27%)
  local copies, waits for them, and re-layouts  7.45 us (9%)
  between operations  1.02 us (1%)
    ppermute x19, waiting for transfers between devices, swap(): lax.ppermute(value, axis, [(i, i ^ step) for i in range(lax.axis_size(axi...  21.8 us
    pallas_call x8, Pallas kernels, call(): pl.pallas_call(body, out_shape=outs, in_specs=specs, out_specs=jax.tree.m...  21 us
    ppermute x19, starting transfers between devices, swap(): lax.ppermute(value, axis, [(i, i ^ step) for i in range(lax.axis_size(axi...  19.4 us
    unnamed x36, local copies, waits for them, and re-layouts  7.45 us
    all_to_all x1, starting transfers between devices, local(): lax.all_to_all(sent.reshape(dp, fetch, 2 * cols), 'dp', split_axis=0, con...  7.38 us
  transfers between devices with their start and end apart: 20, of which 9 were waited for; matrix products, arithmetic and copies ran while one was open for 0% of the time, Pallas kernels for 12%

profile of v3, /device:TPU:0, one launch (start us, length us, event | category | flops | bytes accessed | tf_op | source)
XLA Modules:
  0.0 78.1 jit_solution(12545043726922151470)
XLA Ops:
  0.6 0.0 copy-start.4
  0.6 1.2 %copy-done.4 = bf16[3,768,192]{1,2,0:T(8,128)(2,1)S(1)} copy-done((bf16[3,768,192]{1,2,0:T(8,128)(2,1)S(1)}, bf16[3,768,192]{1,2,0:T(8,128)(2,1)}, u32[]{:S(2)}) %copy-start.4) | copy-done | bytes 884760
  1.8 0.7 copy-done.13
  2.5 1.1 %copy-done.15 = bf16[512,768]{1,0:T(8,128)(2,1)S(1)} copy-done((bf16[512,768]{1,0:T(8,128)(2,1)S(1)}, bf16[512,768]{1,0:T(8,128)(2,1)}, u32[]{:S(2)}) %copy-start.15) | copy-done | bytes 786456
  3.6 0.7 copy-done.17
  4.3 4.1 %send.1 = (bf16[512,384]{1,0:T(8,128)(2,1)S(1)}, bf16[512,192]{1,0:T(8,128)(2,1)S(1)}, bf16[2048,384]{1,0:T(8,128)(2,1)}) custom-call(s32[1]{0:T(128)} %bitcast.refs_0_, s32[2]{0:T(128)S(1)} %copy-done.13, s32[8,256]{1,0:T(8,128)S(1)} %bitcast.13, bf16[512,768]{1,0:T(8,128)(2,1)S(1)} %copy-done.15, bf16[3,192,768]{2,1,0:T(8,128)(2,1)S(1)} %bitcast.10), custom_call_target="tpu_custom_call" | custom-call | flops 1258291200 | bytes 1679372 | tf_op jit(solution)/shard_map/send/pallas_call | solution.py:48
  8.4 0.0 copy-start.6
  8.4 0.7 copy-done.6
  9.1 0.7 copy-done.9
  9.9 7.4 %all-to-all-start = ((bf16[8,256,384]{2,1,0:T(8,128)(2,1)}), bf16[8,256,384]{2,1,0:T(8,128)(2,1)S(1)}, u32[]{:S(2)}, u32[]{:S(2)}) async-start(bf16[8,256,384]{2,1,0:T(8,128)(2,1)} %bitcast.5), calls=%async_computation | async-start | bytes 3145728 | tf_op jit(solution)/shard_map/all_to_all | solution.py:290
  17.2 0.0 copy-start.2
  17.3 0.0 copy-start.3
  17.3 1.3 %copy-done.3 = bf16[3,768,192]{1,2,0:T(8,128)(2,1)S(1)} copy-done((bf16[3,768,192]{1,2,0:T(8,128)(2,1)S(1)}, bf16[3,768,192]{1,2,0:T(8,128)(2,1)}, u32[]{:S(2)}) %copy-start.3) | copy-done | bytes 884760
  18.6 2.3 %attn.1 = (f32[64,768]{1,0:T(8,128)S(1)}, bf16[64,768]{1,0:T(8,128)(2,1)S(1)}, bf16[64,768]{1,0:T(8,128)(2,1)S(1)}, bf16[64,768]{1,0:T(8,128)(2,1)S(1)}) custom-call(s32[4]{0:T(128)S(1)} %iota_xor_fusion.refs_0_, bf16[256,768]{1,0:T(8,128)(2,1)S(1)} %copy-done, bf16[3,192,768]{2,1,0:T(8,128)(2,1)S(1)} %bitcast.9, bf16[192,768]{1,0:T(8,128)(2,1)S(1)} %copy-done.8), custom_call_target="tpu_custom_call" | custom-call | flops 301989888 | bytes 1572880 | tf_op jit(solution)/shard_map/attn/pallas_call | solution.py:48
  20.9 0.1 collective-permute-start
  21.0 1.6 %collective-permute-start.1 = (bf16[64,768]{1,0:T(8,128)(2,1)S(1)}, bf16[64,768]{1,0:T(8,128)(2,1)S(1)}, u32[]{:S(2)}, u32[]{:S(2)}) collective-permute-start(bf16[64,768]{1,0:T(8,128)(2,1)S(1)} %get-tuple-element.20), channel_id=1, source_target_pairs={{0,2},{1,3},{2,0},{3,1},{4,6},{5,7},{6,4},{7,5},{8,10},{9,11},{10,... | collective-permute-start | bytes 294920 | tf_op jit(solution)/shard_map/ppermute | solution.py:277
  22.5 0.3 collective-permute-start.2
  22.8 0.0 collective-permute-done.refs_4_
  22.8 3.8 %collective-permute-done.1.refs_5_ = bf16[64,768]{1,0:T(8,128)(2,1)S(1)} collective-permute-done((bf16[64,768]{1,0:T(8,128)(2,1)S(1)}, bf16[64,768]{1,0:T(8,128)(2,1)S(1)}, u32[]{:S(2)}, u32[]{:S(2)}) %collective-permute-start.1) | collective-permute-done | bytes 98336 | tf_op jit(solution)/shard_map/ppermute | solution.py:277
  26.6 1.2 %collective-permute-done.2.refs_6_ = bf16[64,768]{1,0:T(8,128)(2,1)S(1)} collective-permute-done((bf16[64,768]{1,0:T(8,128)(2,1)S(1)}, bf16[64,768]{1,0:T(8,128)(2,1)S(1)}, u32[]{:S(2)}, u32[]{:S(2)}) %collective-permute-start.2) | collective-permute-done | bytes 98336 | tf_op jit(solution)/shard_map/ppermute | solution.py:277
  27.8 0.8 norm_one.1.refs_2_.refs_0_
  28.6 0.0 copy-start.16
  28.6 0.6 collective-permute-start.3
  29.2 1.5 %collective-permute-start.4 = (bf16[64,768]{1,0:T(8,128)(2,1)S(1)}, bf16[64,768]{1,0:T(8,128)(2,1)S(1)}, u32[]{:S(2)}, u32[]{:S(2)}) collective-permute-start(bf16[64,768]{1,0:T(8,128)(2,1)S(1)} %norm_one.1.refs_2_.refs_0_), channel_id=1, source_target_pairs={{0,2},{1,3},{2,0},{3,1},{4,6},{5,7},{6,4},{7,5},{8,10},{9,11},{10,... | collective-permute-start | bytes 294920 | tf_op jit(solution)/shard_map/ppermute | solution.py:277
  30.8 0.0 collective-permute-start.5
  30.8 0.0 collective-permute-done.3.refs_3_
  30.8 3.5 %collective-permute-done.4.refs_4_ = bf16[64,768]{1,0:T(8,128)(2,1)S(1)} collective-permute-done((bf16[64,768]{1,0:T(8,128)(2,1)S(1)}, bf16[64,768]{1,0:T(8,128)(2,1)S(1)}, u32[]{:S(2)}, u32[]{:S(2)}) %collective-permute-start.4) | collective-permute-done | bytes 98336 | tf_op jit(solution)/shard_map/ppermute | solution.py:277
  34.3 1.6 %collective-permute-done.5.refs_5_ = bf16[64,768]{1,0:T(8,128)(2,1)S(1)} collective-permute-done((bf16[64,768]{1,0:T(8,128)(2,1)S(1)}, bf16[64,768]{1,0:T(8,128)(2,1)S(1)}, u32[]{:S(2)}, u32[]{:S(2)}) %collective-permute-start.5) | collective-permute-done | bytes 98336 | tf_op jit(solution)/shard_map/ppermute | solution.py:277
  35.9 0.0 copy-done.1
  35.9 0.9 %ffn.1 = (f32[64,768]{1,0:T(8,128)S(1)}, bf16[64,768]{1,0:T(8,128)(2,1)S(1)}, bf16[64,768]{1,0:T(8,128)(2,1)S(1)}, bf16[64,768]{1,0:T(8,128)(2,1)S(1)}) custom-call(bf16[768,768]{1,0:T(8,128)(2,1)S(1)} %copy-done.1, bf16[768,768]{1,0:T(8,128)(2,1)S(1)} %copy-done.2, bf16[64,768]{1,0:T(8,128)(2,1)S(1)} %norm_one.1.refs_2_.refs_0_, ...), custom_call_target="tpu_custom_call" | custom-call | flops 603979776 | bytes 2752512 | tf_op jit(solution)/shard_map/ffn/pallas_call | solution.py:48
  36.8 0.5 collective-permute-start.6
  37.2 1.5 %collective-permute-start.7 = (bf16[64,768]{1,0:T(8,128)(2,1)S(1)}, bf16[64,768]{1,0:T(8,128)(2,1)S(1)}, u32[]{:S(2)}, u32[]{:S(2)}) collective-permute-start(bf16[64,768]{1,0:T(8,128)(2,1)S(1)} %get-tuple-element.24), channel_id=1, source_target_pairs={{0,2},{1,3},{2,0},{3,1},{4,6},{5,7},{6,4},{7,5},{8,10},{9,11},{10,... | collective-permute-start | bytes 294920 | tf_op jit(solution)/shard_map/ppermute | solution.py:277
  38.8 0.0 collective-permute-start.8
  38.8 0.0 collective-permute-done.6.refs_3_
  38.8 3.6 %collective-permute-done.7.refs_4_ = bf16[64,768]{1,0:T(8,128)(2,1)S(1)} collective-permute-done((bf16[64,768]{1,0:T(8,128)(2,1)S(1)}, bf16[64,768]{1,0:T(8,128)(2,1)S(1)}, u32[]{:S(2)}, u32[]{:S(2)}) %collective-permute-start.7) | collective-permute-done | bytes 98336 | tf_op jit(solution)/shard_map/ppermute | solution.py:277
  42.4 1.5 %collective-permute-done.8.refs_5_ = bf16[64,768]{1,0:T(8,128)(2,1)S(1)} collective-permute-done((bf16[64,768]{1,0:T(8,128)(2,1)S(1)}, bf16[64,768]{1,0:T(8,128)(2,1)S(1)}, u32[]{:S(2)}, u32[]{:S(2)}) %collective-permute-start.8) | collective-permute-done | bytes 98336 | tf_op jit(solution)/shard_map/ppermute | solution.py:277
  43.8 0.2 norm_two.1.refs_1_
  44.1 1.0 %collective-permute-start.10 = (bf16[64,768]{1,0:T(8,128)(2,1)S(1)}, bf16[64,768]{1,0:T(8,128)(2,1)S(1)}, u32[]{:S(2)}, u32[]{:S(2)}) collective-permute-start(bf16[64,768]{1,0:T(8,128)(2,1)S(1)} %norm_two.1.refs_1_), channel_id=1, source_target_pairs={{0,2},{1,3},{2,0},{3,1},{4,6},{5,7},{6,4},{7,5},{8,10},{9,11},{10,... | collective-permute-start | bytes 294920 | tf_op jit(solution)/shard_map/ppermute | solution.py:277
  45.1 0.9 %collective-permute-start.11 = (bf16[64,768]{1,0:T(8,128)(2,1)S(1)}, bf16[64,768]{1,0:T(8,128)(2,1)S(1)}, u32[]{:S(2)}, u32[]{:S(2)}) collective-permute-start(bf16[64,768]{1,0:T(8,128)(2,1)S(1)} %norm_two.1.refs_1_), channel_id=1, source_target_pairs={{0,3},{1,2},{2,1},{3,0},{4,7},{5,6},{6,5},{7,4},{8,11},{9,10},{10,... | collective-permute-start | bytes 294920 | tf_op jit(solution)/shard_map/ppermute | solution.py:277
  45.9 0.3 collective-permute-start.9
  46.3 3.5 %collective-permute-done.10.refs_3_ = bf16[64,768]{1,0:T(8,128)(2,1)S(1)} collective-permute-done((bf16[64,768]{1,0:T(8,128)(2,1)S(1)}, bf16[64,768]{1,0:T(8,128)(2,1)S(1)}, u32[]{:S(2)}, u32[]{:S(2)}) %collective-permute-start.10) | collective-permute-done | bytes 98336 | tf_op jit(solution)/shard_map/ppermute | solution.py:277
  49.7 1.2 %collective-permute-done.11.refs_4_ = bf16[64,768]{1,0:T(8,128)(2,1)S(1)} collective-permute-done((bf16[64,768]{1,0:T(8,128)(2,1)S(1)}, bf16[64,768]{1,0:T(8,128)(2,1)S(1)}, u32[]{:S(2)}, u32[]{:S(2)}) %collective-permute-start.11) | collective-permute-done | bytes 98336 | tf_op jit(solution)/shard_map/ppermute | solution.py:277
  50.9 0.0 collective-permute-done.9.refs_2_
  51.0 1.3 %place.1 = (bf16[256,768]{1,0:T(8,128)(2,1)}, bf16[2,768]{1,0:T(2,128)(2,1)S(1)}) custom-call(s32[4]{0:T(128)S(1)} %iota_xor_fusion.refs_0_, bf16[64,768]{1,0:T(8,128)(2,1)S(1)} %norm_two.1.refs_1_, bf16[64,768]{1,0:T(8,128)(2,1)S(1)} %collective-permute-done.9.refs_2_, bf16[64,768]{1,0:T(8,128)(2,1)S(1)} %collective-permute-done.10.refs_3_, ...), custom_call_target="tpu_custom_call" | custom-call | bytes 393232 | tf_op jit(solution)/shard_map/place/pallas_call | solution.py:48
  52.3 1.6 %collective-permute-start.12 = (bf16[2,768]{1,0:T(2,128)(2,1)S(1)}, bf16[2,768]{1,0:T(2,128)(2,1)S(1)}, u32[]{:S(2)}, u32[]{:S(2)}) collective-permute-start(bf16[2,768]{1,0:T(2,128)(2,1)S(1)} %get-tuple-element.29.refs_7_), channel_id=1, source_target_pairs={{0,4},{4,0},{8,12},{12,8},{16,20},{20,16},{24,28},{28,24},{1,5},{5... | collective-permute-start | bytes 9224 | tf_op jit(solution)/shard_map/ppermute | solution.py:277
  53.9 1.9 %collective-permute-start.13 = (bf16[2,768]{1,0:T(2,128)(2,1)S(1)}, bf16[2,768]{1,0:T(2,128)(2,1)S(1)}, u32[]{:S(2)}, u32[]{:S(2)}) collective-permute-start(bf16[2,768]{1,0:T(2,128)(2,1)S(1)} %get-tuple-element.29.refs_7_), channel_id=1, source_target_pairs={{0,8},{4,12},{8,0},{12,4},{16,24},{20,28},{24,16},{28,20},{1,9},{5... | collective-permute-start | bytes 9224 | tf_op jit(solution)/shard_map/ppermute | solution.py:277
  55.7 0.0 collective-permute-start.14
  55.8 2.7 %collective-permute-start.15 = (bf16[2,768]{1,0:T(2,128)(2,1)S(1)}, bf16[2,768]{1,0:T(2,128)(2,1)S(1)}, u32[]{:S(2)}, u32[]{:S(2)}) collective-permute-start(bf16[2,768]{1,0:T(2,128)(2,1)S(1)} %get-tuple-element.29.refs_7_), channel_id=1, source_target_pairs={{0,16},{4,20},{8,24},{12,28},{16,0},{20,4},{24,8},{28,12},{1,17},{... | collective-permute-start | bytes 9224 | tf_op jit(solution)/shard_map/ppermute | solution.py:277
  58.5 1.3 %collective-permute-start.16 = (bf16[2,768]{1,0:T(2,128)(2,1)S(1)}, bf16[2,768]{1,0:T(2,128)(2,1)S(1)}, u32[]{:S(2)}, u32[]{:S(2)}) collective-permute-start(bf16[2,768]{1,0:T(2,128)(2,1)S(1)} %get-tuple-element.29.refs_7_), channel_id=1, source_target_pairs={{0,20},{4,16},{8,28},{12,24},{16,4},{20,0},{24,12},{28,8},{1,21},{... | collective-permute-start | bytes 9224 | tf_op jit(solution)/shard_map/ppermute | solution.py:277
  59.7 0.0 collective-permute-done.12.refs_8_
  59.7 3.6 %collective-permute-start.17 = (bf16[2,768]{1,0:T(2,128)(2,1)S(1)}, bf16[2,768]{1,0:T(2,128)(2,1)S(1)}, u32[]{:S(2)}, u32[]{:S(2)}) collective-permute-start(bf16[2,768]{1,0:T(2,128)(2,1)S(1)} %get-tuple-element.29.refs_7_), channel_id=1, source_target_pairs={{0,24},{4,28},{8,16},{12,20},{16,8},{20,12},{24,0},{28,4},{1,25},{... | collective-permute-start | bytes 9224 | tf_op jit(solution)/shard_map/ppermute | solution.py:277
  63.4 0.0 collective-permute-done.13.refs_9_
  63.4 0.0 collective-permute-start.18
  63.4 0.0 copy-start.12
  63.4 0.0 copy-start.14
  63.4 4.2 %mask.1.refs_5_ = bf16[512,768]{1,0:T(8,128)(2,1)S(1)} custom-call(s32[16,512]{1,0:T(8,128)S(1)} %bitcast.12), custom_call_target="tpu_custom_call" | custom-call | flops 1000000000 | bytes 32768 | tf_op jit(solution)/shard_map/mask/pallas_call | solution.py:48
  67.7 0.0 collective-permute-done.14.refs_10_
  67.7 0.0 collective-permute-done.15.refs_11_
  67.7 0.0 collective-permute-done.16.refs_12_
  67.7 0.0 collective-permute-done.17.refs_13_
  67.7 1.9 %collective-permute-done.18.refs_14_ = bf16[2,768]{1,0:T(2,128)(2,1)S(1)} collective-permute-done((bf16[2,768]{1,0:T(2,128)(2,1)S(1)}, bf16[2,768]{1,0:T(2,128)(2,1)S(1)}, u32[]{:S(2)}, u32[]{:S(2)}) %collective-permute-start.18) | collective-permute-done | bytes 3104 | tf_op jit(solution)/shard_map/ppermute | solution.py:277
  69.7 0.0 all-to-all-done
  69.7 1.0 %copy-done.7 = bf16[512,384]{1,0:T(8,128)(2,1)S(1)} copy-done((bf16[512,384]{1,0:T(8,128)(2,1)S(1)}, bf16[512,384]{1,0:T(8,128)(2,1)}, u32[]{:S(2)}) %copy-start.7) | copy-done | bytes 393240
  70.7 7.2 %graph.1 = bf16[192,512]{1,0:T(8,128)(2,1)} custom-call(s32[4,6]{1,0:T(4,128)S(1)} %copy-done.12, s32[2]{0:T(128)S(1)} %copy-done.14, bf16[512,192]{1,0:T(8,128)(2,1)S(1)} %copy-done.10, bf16[512,384]{1,0:T(8,128)(2,1)S(1)} %copy-done.7, bf16[3,192,768]{2,1,0:T(8,128)(2,1)S(1)} %bitcast.11, bf16[512,768]{1,0:T(8,128)(2,1)S(1)} %mask.1.refs_5_, ...), custom_call_target="tpu_custom_call" | custom-call | flops 1000000000 | bytes 3858536 | tf_op jit(solution)/shard_map/graph/pallas_call | solution.py:48
  (21 shorter events, 0.0 us)
Async XLA Ops:
  0.6 1.2 %copy-start.4 = (bf16[3,768,192]{1,2,0:T(8,128)(2,1)S(1)}, bf16[3,768,192]{1,2,0:T(8,128)(2,1)}, u32[]{:S(2)}) copy-start(bf16[3,768,192]{1,2,0:T(8,128)(2,1)} %param.19) | copy-start | bytes 2654212
  1.8 0.7 copy-start.13
  2.5 1.1 %copy-start.15 = (bf16[512,768]{1,0:T(8,128)(2,1)S(1)}, bf16[512,768]{1,0:T(8,128)(2,1)}, u32[]{:S(2)}) copy-start(bf16[512,768]{1,0:T(8,128)(2,1)} %refs_3_.2) | copy-start | bytes 2359300
  3.6 0.7 copy-start.17
  8.4 0.8 copy-start.6
  9.1 0.7 copy-start.9
  9.8 7.4 %copy-start = (bf16[256,768]{1,0:T(8,128)(2,1)S(1)}, bf16[256,768]{1,0:T(8,128)(2,1)}, u32[]{:S(2)}) copy-start(bf16[256,768]{1,0:T(8,128)(2,1)} %refs_1_.6) | copy-start | bytes 1179652
  9.8 7.4 %copy-start.8 = (bf16[192,768]{1,0:T(8,128)(2,1)S(1)}, bf16[192,768]{1,0:T(8,128)(2,1)}, u32[]{:S(2)}) copy-start(bf16[192,768]{1,0:T(8,128)(2,1)} %refs_3_.3) | copy-start | bytes 884740
  9.8 18.0 %copy-start.11 = (f32[2,768]{1,0:T(2,128)S(1)}, f32[2,768]{1,0:T(2,128)}, u32[]{:S(2)}) copy-start(f32[2,768]{1,0:T(2,128)} %refs_1_.8) | copy-start | bytes 18436
  9.9 59.8 %all-to-all-start = ((bf16[8,256,384]{2,1,0:T(8,128)(2,1)}), bf16[8,256,384]{2,1,0:T(8,128)(2,1)S(1)}, u32[]{:S(2)}, u32[]{:S(2)}) async-start(bf16[8,256,384]{2,1,0:T(8,128)(2,1)} %bitcast.5), calls=%async_computation | async-start | bytes 3145728 | tf_op jit(solution)/shard_map/all_to_all | solution.py:290
  17.2 18.6 %copy-start.1 = (bf16[768,768]{1,0:T(8,128)(2,1)S(1)}, bf16[768,768]{1,0:T(8,128)(2,1)}, u32[]{:S(2)}) copy-start(bf16[768,768]{1,0:T(8,128)(2,1)} %refs_0_.2) | copy-start | bytes 3538948
  17.2 18.6 %copy-start.2 = (bf16[768,768]{1,0:T(8,128)(2,1)S(1)}, bf16[768,768]{1,0:T(8,128)(2,1)}, u32[]{:S(2)}) copy-start(bf16[768,768]{1,0:T(8,128)(2,1)} %refs_1_.7) | copy-start | bytes 3538948
  17.3 1.3 %copy-start.3 = (bf16[3,768,192]{1,2,0:T(8,128)(2,1)S(1)}, bf16[3,768,192]{1,2,0:T(8,128)(2,1)}, u32[]{:S(2)}) copy-start(bf16[3,768,192]{1,2,0:T(8,128)(2,1)} %param.13) | copy-start | bytes 2654212
  20.9 1.9 %collective-permute-start = (bf16[64,768]{1,0:T(8,128)(2,1)S(1)}, bf16[64,768]{1,0:T(8,128)(2,1)S(1)}, u32[]{:S(2)}, u32[]{:S(2)}) collective-permute-start(bf16[64,768]{1,0:T(8,128)(2,1)S(1)} %get-tuple-element.19), channel_id=1, source_target_pairs={{0,1},{1,0},{2,3},{3,2},{4,5},{5,4},{6,7},{7,6},{8,9},{9,8},{10,11... | collective-permute-start | bytes 294920 | tf_op jit(solution)/shard_map/ppermute | solution.py:277
  21.0 5.7 %collective-permute-start.1 = (bf16[64,768]{1,0:T(8,128)(2,1)S(1)}, bf16[64,768]{1,0:T(8,128)(2,1)S(1)}, u32[]{:S(2)}, u32[]{:S(2)}) collective-permute-start(bf16[64,768]{1,0:T(8,128)(2,1)S(1)} %get-tuple-element.20), channel_id=1, source_target_pairs={{0,2},{1,3},{2,0},{3,1},{4,6},{5,7},{6,4},{7,5},{8,10},{9,11},{10,... | collective-permute-start | bytes 294920 | tf_op jit(solution)/shard_map/ppermute | solution.py:277
  22.5 5.3 %collective-permute-start.2 = (bf16[64,768]{1,0:T(8,128)(2,1)S(1)}, bf16[64,768]{1,0:T(8,128)(2,1)S(1)}, u32[]{:S(2)}, u32[]{:S(2)}) collective-permute-start(bf16[64,768]{1,0:T(8,128)(2,1)S(1)} %get-tuple-element.21), channel_id=1, source_target_pairs={{0,3},{1,2},{2,1},{3,0},{4,7},{5,6},{6,5},{7,4},{8,11},{9,10},{10,... | collective-permute-start | bytes 294920 | tf_op jit(solution)/shard_map/ppermute | solution.py:277
  28.6 34.8 %copy-start.16 = (s32[512,16]{0,1:T(8,128)S(1)}, s32[512,16]{0,1:T(8,128)}, u32[]{:S(2)}) copy-start(s32[512,16]{0,1:T(8,128)} %param.23) | copy-start | bytes 98308
  28.6 2.2 %collective-permute-start.3 = (bf16[64,768]{1,0:T(8,128)(2,1)S(1)}, bf16[64,768]{1,0:T(8,128)(2,1)S(1)}, u32[]{:S(2)}, u32[]{:S(2)}) collective-permute-start(bf16[64,768]{1,0:T(8,128)(2,1)S(1)} %norm_one.1.refs_2_.refs_0_), channel_id=1, source_target_pairs={{0,1},{1,0},{2,3},{3,2},{4,5},{5,4},{6,7},{7,6},{8,9},{9,8},{10,11... | collective-permute-start | bytes 294920 | tf_op jit(solution)/shard_map/ppermute | solution.py:277
  29.2 5.1 %collective-permute-start.4 = (bf16[64,768]{1,0:T(8,128)(2,1)S(1)}, bf16[64,768]{1,0:T(8,128)(2,1)S(1)}, u32[]{:S(2)}, u32[]{:S(2)}) collective-permute-start(bf16[64,768]{1,0:T(8,128)(2,1)S(1)} %norm_one.1.refs_2_.refs_0_), channel_id=1, source_target_pairs={{0,2},{1,3},{2,0},{3,1},{4,6},{5,7},{6,4},{7,5},{8,10},{9,11},{10,... | collective-permute-start | bytes 294920 | tf_op jit(solution)/shard_map/ppermute | solution.py:277
  30.8 5.1 %collective-permute-start.5 = (bf16[64,768]{1,0:T(8,128)(2,1)S(1)}, bf16[64,768]{1,0:T(8,128)(2,1)S(1)}, u32[]{:S(2)}, u32[]{:S(2)}) collective-permute-start(bf16[64,768]{1,0:T(8,128)(2,1)S(1)} %norm_one.1.refs_2_.refs_0_), channel_id=1, source_target_pairs={{0,3},{1,2},{2,1},{3,0},{4,7},{5,6},{6,5},{7,4},{8,11},{9,10},{10,... | collective-permute-start | bytes 294920 | tf_op jit(solution)/shard_map/ppermute | solution.py:277
  36.8 2.0 %collective-permute-start.6 = (bf16[64,768]{1,0:T(8,128)(2,1)S(1)}, bf16[64,768]{1,0:T(8,128)(2,1)S(1)}, u32[]{:S(2)}, u32[]{:S(2)}) collective-permute-start(bf16[64,768]{1,0:T(8,128)(2,1)S(1)} %get-tuple-element.23), channel_id=1, source_target_pairs={{0,1},{1,0},{2,3},{3,2},{4,5},{5,4},{6,7},{7,6},{8,9},{9,8},{10,11... | collective-permute-start | bytes 294920 | tf_op jit(solution)/shard_map/ppermute | solution.py:277
  37.2 5.1 %collective-permute-start.7 = (bf16[64,768]{1,0:T(8,128)(2,1)S(1)}, bf16[64,768]{1,0:T(8,128)(2,1)S(1)}, u32[]{:S(2)}, u32[]{:S(2)}) collective-permute-start(bf16[64,768]{1,0:T(8,128)(2,1)S(1)} %get-tuple-element.24), channel_id=1, source_target_pairs={{0,2},{1,3},{2,0},{3,1},{4,6},{5,7},{6,4},{7,5},{8,10},{9,11},{10,... | collective-permute-start | bytes 294920 | tf_op jit(solution)/shard_map/ppermute | solution.py:277
  38.8 5.1 %collective-permute-start.8 = (bf16[64,768]{1,0:T(8,128)(2,1)S(1)}, bf16[64,768]{1,0:T(8,128)(2,1)S(1)}, u32[]{:S(2)}, u32[]{:S(2)}) collective-permute-start(bf16[64,768]{1,0:T(8,128)(2,1)S(1)} %get-tuple-element.25), channel_id=1, source_target_pairs={{0,3},{1,2},{2,1},{3,0},{4,7},{5,6},{6,5},{7,4},{8,11},{9,10},{10,... | collective-permute-start | bytes 294920 | tf_op jit(solution)/shard_map/ppermute | solution.py:277
  44.1 5.7 %collective-permute-start.10 = (bf16[64,768]{1,0:T(8,128)(2,1)S(1)}, bf16[64,768]{1,0:T(8,128)(2,1)S(1)}, u32[]{:S(2)}, u32[]{:S(2)}) collective-permute-start(bf16[64,768]{1,0:T(8,128)(2,1)S(1)} %norm_two.1.refs_1_), channel_id=1, source_target_pairs={{0,2},{1,3},{2,0},{3,1},{4,6},{5,7},{6,4},{7,5},{8,10},{9,11},{10,... | collective-permute-start | bytes 294920 | tf_op jit(solution)/shard_map/ppermute | solution.py:277
  45.1 5.9 %collective-permute-start.11 = (bf16[64,768]{1,0:T(8,128)(2,1)S(1)}, bf16[64,768]{1,0:T(8,128)(2,1)S(1)}, u32[]{:S(2)}, u32[]{:S(2)}) collective-permute-start(bf16[64,768]{1,0:T(8,128)(2,1)S(1)} %norm_two.1.refs_1_), channel_id=1, source_target_pairs={{0,3},{1,2},{2,1},{3,0},{4,7},{5,6},{6,5},{7,4},{8,11},{9,10},{10,... | collective-permute-start | bytes 294920 | tf_op jit(solution)/shard_map/ppermute | solution.py:277
  45.9 5.0 %collective-permute-start.9 = (bf16[64,768]{1,0:T(8,128)(2,1)S(1)}, bf16[64,768]{1,0:T(8,128)(2,1)S(1)}, u32[]{:S(2)}, u32[]{:S(2)}) collective-permute-start(bf16[64,768]{1,0:T(8,128)(2,1)S(1)} %norm_two.1.refs_1_), channel_id=1, source_target_pairs={{0,1},{1,0},{2,3},{3,2},{4,5},{5,4},{6,7},{7,6},{8,9},{9,8},{10,11... | collective-permute-start | bytes 294920 | tf_op jit(solution)/shard_map/ppermute | solution.py:277
  52.3 7.5 %collective-permute-start.12 = (bf16[2,768]{1,0:T(2,128)(2,1)S(1)}, bf16[2,768]{1,0:T(2,128)(2,1)S(1)}, u32[]{:S(2)}, u32[]{:S(2)}) collective-permute-start(bf16[2,768]{1,0:T(2,128)(2,1)S(1)} %get-tuple-element.29.refs_7_), channel_id=1, source_target_pairs={{0,4},{4,0},{8,12},{12,8},{16,20},{20,16},{24,28},{28,24},{1,5},{5... | collective-permute-start | bytes 9224 | tf_op jit(solution)/shard_map/ppermute | solution.py:277
  53.9 9.5 %collective-permute-start.13 = (bf16[2,768]{1,0:T(2,128)(2,1)S(1)}, bf16[2,768]{1,0:T(2,128)(2,1)S(1)}, u32[]{:S(2)}, u32[]{:S(2)}) collective-permute-start(bf16[2,768]{1,0:T(2,128)(2,1)S(1)} %get-tuple-element.29.refs_7_), channel_id=1, source_target_pairs={{0,8},{4,12},{8,0},{12,4},{16,24},{20,28},{24,16},{28,20},{1,9},{5... | collective-permute-start | bytes 9224 | tf_op jit(solution)/shard_map/ppermute | solution.py:277
  55.7 12.0 %collective-permute-start.14 = (bf16[2,768]{1,0:T(2,128)(2,1)S(1)}, bf16[2,768]{1,0:T(2,128)(2,1)S(1)}, u32[]{:S(2)}, u32[]{:S(2)}) collective-permute-start(bf16[2,768]{1,0:T(2,128)(2,1)S(1)} %get-tuple-element.29.refs_7_), channel_id=1, source_target_pairs={{0,12},{4,8},{8,4},{12,0},{16,28},{20,24},{24,20},{28,16},{1,13},{... | collective-permute-start | bytes 9224 | tf_op jit(solution)/shard_map/ppermute | solution.py:277
  55.8 12.0 %collective-permute-start.15 = (bf16[2,768]{1,0:T(2,128)(2,1)S(1)}, bf16[2,768]{1,0:T(2,128)(2,1)S(1)}, u32[]{:S(2)}, u32[]{:S(2)}) collective-permute-start(bf16[2,768]{1,0:T(2,128)(2,1)S(1)} %get-tuple-element.29.refs_7_), channel_id=1, source_target_pairs={{0,16},{4,20},{8,24},{12,28},{16,0},{20,4},{24,8},{28,12},{1,17},{... | collective-permute-start | bytes 9224 | tf_op jit(solution)/shard_map/ppermute | solution.py:277
  58.5 9.2 %collective-permute-start.16 = (bf16[2,768]{1,0:T(2,128)(2,1)S(1)}, bf16[2,768]{1,0:T(2,128)(2,1)S(1)}, u32[]{:S(2)}, u32[]{:S(2)}) collective-permute-start(bf16[2,768]{1,0:T(2,128)(2,1)S(1)} %get-tuple-element.29.refs_7_), channel_id=1, source_target_pairs={{0,20},{4,16},{8,28},{12,24},{16,4},{20,0},{24,12},{28,8},{1,21},{... | collective-permute-start | bytes 9224 | tf_op jit(solution)/shard_map/ppermute | solution.py:277
  59.7 8.0 %collective-permute-start.17 = (bf16[2,768]{1,0:T(2,128)(2,1)S(1)}, bf16[2,768]{1,0:T(2,128)(2,1)S(1)}, u32[]{:S(2)}, u32[]{:S(2)}) collective-permute-start(bf16[2,768]{1,0:T(2,128)(2,1)S(1)} %get-tuple-element.29.refs_7_), channel_id=1, source_target_pairs={{0,24},{4,28},{8,16},{12,20},{16,8},{20,12},{24,0},{28,4},{1,25},{... | collective-permute-start | bytes 9224 | tf_op jit(solution)/shard_map/ppermute | solution.py:277
  63.4 6.3 %collective-permute-start.18 = (bf16[2,768]{1,0:T(2,128)(2,1)S(1)}, bf16[2,768]{1,0:T(2,128)(2,1)S(1)}, u32[]{:S(2)}, u32[]{:S(2)}) collective-permute-start(bf16[2,768]{1,0:T(2,128)(2,1)S(1)} %get-tuple-element.29.refs_7_), channel_id=1, source_target_pairs={{0,28},{4,24},{8,20},{12,16},{16,12},{20,8},{24,4},{28,0},{1,29},{... | collective-permute-start | bytes 9224 | tf_op jit(solution)/shard_map/ppermute | solution.py:277
  63.4 6.3 %copy-start.5 = (bf16[3,768,192]{1,2,0:T(8,128)(2,1)S(1)}, bf16[3,768,192]{1,2,0:T(8,128)(2,1)}, u32[]{:S(2)}) copy-start(bf16[3,768,192]{1,2,0:T(8,128)(2,1)} %param.19) | copy-start | bytes 2654212
  63.4 6.3 %copy-start.10 = (bf16[512,192]{1,0:T(8,128)(2,1)S(1)}, bf16[512,192]{1,0:T(8,128)(2,1)}, u32[]{:S(2)}) copy-start(bf16[512,192]{1,0:T(8,128)(2,1)} %copy-done.9) | copy-start | bytes 589828
  63.4 6.3 %copy-start.12 = (s32[4,6]{1,0:T(4,128)S(1)}, s32[4,6]{1,0:T(4,128)}, u32[]{:S(2)}) copy-start(s32[4,6]{1,0:T(4,128)} %refs_0_.3) | copy-start | bytes 292
  63.4 6.3 %copy-start.14 = (s32[2]{0:T(128)S(1)}, s32[2]{0:T(128)}, u32[]{:S(2)}) copy-start(s32[2]{0:T(128)} %refs_1_.9) | copy-start | bytes 28
  69.7 1.0 %copy-start.7 = (bf16[512,384]{1,0:T(8,128)(2,1)S(1)}, bf16[512,384]{1,0:T(8,128)(2,1)}, u32[]{:S(2)}) copy-start(bf16[512,384]{1,0:T(8,128)(2,1)} %copy-done.6) | copy-start | bytes 1179652

commit v4 on v3

v4 whole, which is shorter than its diff:
```python
import jax
import jax.numpy as jnp
from jax import lax
from jax.experimental import pallas as pl
from jax.experimental.pallas import tpu as pltpu
from jax.sharding import PartitionSpec as P

SEQ = 128
TILE = 128
DEG = 16
TPR = 6
HD = 64
GHD = 96

eps_norm = 1e-06
bf = jnp.bfloat16
f32 = jnp.float32

VMEM = pl.BlockSpec(memory_space=pltpu.VMEM)
SMEM = pl.BlockSpec(memory_space=pltpu.SMEM)
HBM = pl.BlockSpec(memory_space=pltpu.HBM)
PAD = 16
NT = (((1,), (1,)), ((), ()))
TN = (((0,), (0,)), ((), ()))


def call(kernel, outs, args, smem=(), hbm=(), scratch=(), out_specs=None, flops=0, name=None):
    count, out_count, own = len(args), len(jax.tree.leaves(outs)), len(scratch)
    specs = [SMEM if i in smem else HBM if i in hbm else VMEM for i in range(count)]
    nbytes = sum(a.size * a.dtype.itemsize for a in args)
    buffers = [pltpu.VMEM(args[i].shape, args[i].dtype) for i in hbm]
    sems = [pltpu.SemaphoreType.DMA((len(hbm),))] if hbm else []

    def body(*refs):
        ins, rest = list(refs[:count]), refs[count:]
        kept, moved = rest[: out_count + own], rest[out_count + own :]
        moves = {}
        for j, i in enumerate(hbm):
            moves[i] = pltpu.make_async_copy(ins[i], moved[j], moved[-1].at[j])
            moves[i].start()
            ins[i] = moved[j]

        def ready(*wanted):
            for i in wanted:
                moves[i].wait()

        kernel(ready, *ins, *kept)

    return pl.pallas_call(
        body,
        out_shape=outs,
        in_specs=specs,
        out_specs=jax.tree.map(lambda _: VMEM, outs) if out_specs is None else out_specs,
        scratch_shapes=list(scratch) + buffers + sems,
        compiler_params=pltpu.CompilerParams(vmem_limit_bytes=40 * 1024 * 1024),
        cost_estimate=pl.CostEstimate(flops=flops, bytes_accessed=nbytes, transcendentals=0),
        name=name,
    )(*args)


def shape(dims, dtype):
    return jax.ShapeDtypeStruct(dims, dtype)


def dot(a, b):
    return jnp.dot(a, b, preferred_element_type=f32)


def dot_nt(a, b):
    return lax.dot_general(a, b, NT, preferred_element_type=f32)


def dot_tn(a, b):
    return lax.dot_general(a, b, TN, preferred_element_type=f32)


def layer_norm(values, gain):
    mean = jnp.mean(values, axis=-1, keepdims=True)
    centred = values - mean
    var = jnp.mean(centred * centred, axis=-1, keepdims=True)
    return centred * lax.rsqrt(var + eps_norm) * gain


def send_kernel(ready, me_ref, at_ref, ids_ref, table_ref, w_ref, sent_ref, rows_ref, sems):
    cols = w_ref.shape[1]
    per_part = at_ref.shape[0]
    fetch, nodes = ids_ref.shape[1], table_ref.shape[0]
    ready(2, 3, 4)
    table = table_ref[...]
    kv = jnp.concatenate([dot_nt(table, w_ref[1]), dot_nt(table, w_ref[2])], axis=1).astype(bf)
    ids = ids_ref[...].astype(f32).T.astype(jnp.int32)
    lanes = lax.broadcasted_iota(jnp.int32, (fetch, nodes), 1)
    lead = lax.broadcasted_iota(jnp.int32, (fetch, 2 * cols), 1) == 0
    moves = []
    for part in range(ids.shape[1]):
        step = me_ref[0] ^ part
        picked = ids[:, part : part + 1]
        hot = jnp.where(lanes == picked, 1.0, 0.0).astype(bf)
        rows = dot(hot, kv)
        code = jnp.full((fetch, 1), -1, jnp.int32)
        for title in range(per_part):
            code = jnp.where(picked == at_ref[title], step * per_part + title, code)
        mark = jnp.where(lead, jnp.nan, code.astype(f32))
        at = pl.ds(part * fetch, fetch)
        rows_ref[at, :] = jnp.where(code >= 0, mark, rows).astype(bf)
        moves.append(pltpu.make_async_copy(rows_ref.at[at, :], sent_ref.at[at, :], sems.at[part]))
        moves[-1].start()
    for move in moves:
        move.wait()


def mask_kernel(ready, slots_ref, mask_ref):
    all_slots = slots_ref[...].astype(f32).T.astype(jnp.int32)
    for tile in range(all_slots.shape[0] // TILE):
        slots = all_slots[tile * TILE : (tile + 1) * TILE, :]
        lanes = lax.broadcasted_iota(jnp.int32, (TILE, TPR * TILE), 1)
        edges = lanes == lax.broadcasted_iota(jnp.int32, (TILE, TPR * TILE), 0)
        for edge in range(DEG):
            edges = edges | (lanes == slots[:, edge : edge + 1])
        mask_ref[tile * TILE : (tile + 1) * TILE, :] = jnp.where(edges, 1.0, 0.0).astype(bf)


def attn_kernel(ready, who_ref, titles_ref, w_in_ref, w_out_ref, *refs):
    outs, total = refs[:-1], refs[-1]
    titles = titles_ref[...]
    q = dot_nt(titles, w_in_ref[0]).astype(bf)
    k = dot_nt(titles, w_in_ref[1]).astype(bf)
    v = dot_nt(titles, w_in_ref[2]).astype(bf)
    cols = q.shape[1]
    heads = cols // HD
    lanes = lax.broadcasted_iota(jnp.int32, (SEQ, cols), 1) // HD
    for title in range(titles.shape[0] // SEQ):
        rows = slice(title * SEQ, (title + 1) * SEQ)
        qt, kt, vt = q[rows], k[rows], v[rows]
        stacked = jnp.concatenate(
            [jnp.where(lanes == h, qt, jnp.zeros_like(qt)) for h in range(heads)], axis=0
        )
        scores = dot_nt(stacked, kt) * (1.0 / HD**0.5)
        expo = jnp.exp(scores - jnp.max(scores, axis=-1, keepdims=True))
        probs = (expo / jnp.sum(expo, axis=-1, keepdims=True)).astype(bf)
        mixed = dot(probs, vt)
        context = mixed[:SEQ]
        for h in range(1, heads):
            context = jnp.where(lanes == h, mixed[h * SEQ : (h + 1) * SEQ], context)
        total[rows, :] = dot(context.astype(bf), w_out_ref[...])
    chunk = outs[0].shape[0] - PAD
    firsts = first_rows(total)
    for step, out in enumerate(outs):
        at = pl.ds(pl.multiple_of(who_ref[step] * chunk, chunk), chunk)
        out[:chunk, :] = total[at, :].astype(out.dtype)
        out[chunk:, :] = firsts.astype(out.dtype)


def first_rows(ref):
    sub = lax.broadcasted_iota(jnp.int32, (PAD, ref.shape[1]), 0)
    rows = jnp.zeros((PAD, ref.shape[1]), f32)
    for title in range(ref.shape[0] // SEQ):
        row = ref[title * SEQ : title * SEQ + 1, :].astype(f32)
        rows = jnp.where(sub == title, row, rows)
    return rows


def norm_one_kernel(
    ready, who_ref, titles_ref, gains_ref, w_in_ref, w_out_ref, own_ref, *refs
):
    *parts, out, first_hidden, first_terms = refs
    chunk = own_ref.shape[0] - PAD
    total = own_ref[...]
    for part in parts:
        total = total + part[...].astype(f32)
    at = pl.ds(pl.multiple_of(who_ref[0] * chunk, chunk), chunk)
    base = jnp.concatenate([titles_ref[at, :].astype(f32), first_rows(titles_ref)], axis=0)
    hidden = layer_norm(base + total, gains_ref[0:1, :]).astype(bf)
    out[:chunk, :] = hidden[:chunk]
    firsts = hidden[chunk:]
    first_hidden[...] = firsts
    terms = dot(gelu(dot(firsts, w_in_ref[...])).astype(bf), w_out_ref[...])
    first_terms[...] = terms
    out[chunk:, :] = terms.astype(bf)


def gelu(x):
    return 0.5 * x * (1.0 + lax.erf(x * (0.5**0.5)))


def ffn_kernel(ready, w_in_ref, w_out_ref, gains_ref, first_hidden, first_terms, *refs):
    *refs, first = refs
    count = len(refs) // 2
    ins, outs = refs[:count], refs[count:]
    chunk = outs[0].shape[0]
    hidden = jnp.concatenate([ref[:chunk, :] for ref in ins], axis=0)
    inner = gelu(dot(hidden, w_in_ref[...])).astype(bf)
    total = dot(inner, w_out_ref[...])
    for step, out in enumerate(outs):
        out[...] = total[step * chunk : (step + 1) * chunk].astype(out.dtype)
    terms = first_terms[...]
    for ref in ins[1:]:
        terms = terms + ref[chunk:, :].astype(f32)
    done = layer_norm(first_hidden[...].astype(f32) + terms, gains_ref[1:2, :])
    first[...] = done[: first.shape[0]].astype(bf)


def norm_two_kernel(ready, hidden_ref, gains_ref, own_ref, *refs):
    *refs, out = refs
    parts = [ref for ref in refs if ref.shape == own_ref.shape]
    firsts = [ref for ref in refs if ref.shape != own_ref.shape]
    chunk = own_ref.shape[0]
    total = own_ref[...]
    for part in parts:
        total = total + part[...].astype(f32)
    hidden = hidden_ref[:chunk, :].astype(f32)
    out[:chunk, :] = layer_norm(hidden + total, gains_ref[1:2, :]).astype(bf)
    tail = out.shape[0] - chunk
    sub = lax.broadcasted_iota(jnp.int32, (tail, out.shape[1]), 0)
    rows = jnp.zeros((tail, out.shape[1]), f32)
    for turn, ref in enumerate(firsts):
        per_part = ref.shape[0]
        for title in range(per_part):
            row = ref[title : title + 1, :].astype(f32)
            rows = jnp.where(sub == turn * per_part + title, row, rows)
    out[chunk:, :] = rows.astype(bf)


def place_kernel(ready, who_ref, *refs):
    *chunks, out = refs
    chunk = out.shape[0] // len(chunks)
    for step, ref in enumerate(chunks):
        out[pl.ds(pl.multiple_of(who_ref[step] * chunk, chunk), chunk), :] = ref[:chunk, :]


def own_kernel(ready, who_ref, at_ref, table_ref, w_ref, first_ref, *refs):
    *chunks, kv_ref, q_ref, first_kv_ref, features, firsts = refs
    members = len(chunks)
    per_part, width = first_ref.shape
    cols = w_ref.shape[1]
    turns = firsts.shape[0] // per_part // members
    for step, ref in enumerate(chunks):
        base = ref.shape[0] - tail_rows(turns * per_part)
        rows = ref[base:, :].astype(f32)
        for turn in range(turns):
            for title in range(per_part):
                place = (turn * members + who_ref[step]) * per_part + title
                firsts[pl.ds(place, 1), :] = rows[turn * per_part + title][None]
    firsts[0:per_part, :] = first_ref[...].astype(f32)
    ready(2, 3)
    nodes = table_ref.shape[0]
    for tile in range(nodes // TILE):
        span = slice(tile * TILE, (tile + 1) * TILE)
        rows = table_ref[span, :].astype(f32)
        sub = lax.broadcasted_iota(jnp.int32, (TILE, width), 0) + tile * TILE
        for title in range(per_part):
            rows = jnp.where(sub == at_ref[title], firsts[title : title + 1, :], rows)
        features[span, :] = rows.astype(bf)
    first = firsts[...].astype(bf)
    table = features[...]
    for j in (1, 2):
        span = slice((j - 1) * cols, j * cols)
        first_kv_ref[:, span] = dot_nt(first, w_ref[j]).astype(bf)
        kv_ref[:, span] = dot_nt(table, w_ref[j]).astype(bf)
    q_ref[...] = dot_nt(table, w_ref[0]).astype(bf)


def tail_rows(count):
    return -(-count // PAD) * PAD


def graph_kernel(
    ready, cols_ref, q_ref, kv_ref, first_ref, mask_ref, far_ref, out_ref, k_all, v_all
):
    nodes, cols = q_ref.shape
    row_tiles = nodes // TILE
    first_kv = first_ref[...]
    k_all[:nodes, :] = kv_ref[:, :cols]
    v_all[:nodes, :] = kv_ref[:, cols:]
    lanes = lax.broadcasted_iota(jnp.int32, (TILE, first_kv.shape[0]), 1).astype(f32)
    for tile in range(far_ref.shape[0] // TILE):
        rows = far_ref[tile * TILE : (tile + 1) * TILE, :].astype(f32)
        code = jnp.where(rows[:, 0:1] != rows[:, 0:1], rows[:, 1:2], -1.0)
        hot = jnp.where(lanes == code, 1.0, 0.0).astype(bf)
        fixed = jnp.where(code >= 0.0, dot(hot, first_kv), rows).astype(bf)
        span = slice(nodes + tile * TILE, nodes + (tile + 1) * TILE)
        k_all[span, :] = fixed[:, :cols]
        v_all[span, :] = fixed[:, cols:]

    heads = cols // GHD
    head_of = lax.broadcasted_iota(jnp.int32, (TILE, cols), 1) // GHD
    for tile in range(row_tiles):
        q = q_ref[tile * TILE : (tile + 1) * TILE, :]
        stacked = jnp.concatenate(
            [jnp.where(head_of == h, q, jnp.zeros_like(q)) for h in range(heads)], axis=0
        )
        starts = [pl.multiple_of(cols_ref[tile, c] * TILE, TILE) for c in range(TPR)]
        keys = jnp.concatenate([k_all[pl.ds(start, TILE), :] for start in starts], axis=0)
        values = jnp.concatenate([v_all[pl.ds(start, TILE), :] for start in starts], axis=0)
        scores = dot_nt(stacked, keys) * (1.0 / GHD**0.5)
        mask = mask_ref[tile * TILE : (tile + 1) * TILE, :].astype(f32)
        mask = jnp.concatenate([mask] * heads, axis=0) > 0.5
        masked = jnp.where(mask, scores, -jnp.inf)
        expo = jnp.exp(masked - jnp.max(masked, axis=-1, keepdims=True))
        scale = 1.0 / jnp.sum(expo, axis=-1, keepdims=True)
        mixed = dot(expo.astype(bf), values) * scale
        out = mixed[:TILE]
        for h in range(1, heads):
            out = jnp.where(head_of == h, mixed[h * TILE : (h + 1) * TILE], out)
        out_ref[:, tile * TILE : (tile + 1) * TILE] = out.T.astype(bf)


def local(

    titles,
    w_attn_in,
    w_attn_out,
    w_ffn_in,
    w_ffn_out,
    gains,
    node_table,
    w_graph,
    title_nodes,
    send_ids,
    tile_cols,
    nbr_slots,
):
    tok_rows, width = titles.shape
    nodes = node_table.shape[0]
    cols = w_graph.shape[2]
    mp = lax.axis_size("mp")
    dp = lax.axis_size("dp")
    me_mp = lax.axis_index("mp").astype(jnp.int32)
    me_dp = lax.axis_index("dp").astype(jnp.int32).reshape(1)
    who = me_mp ^ jnp.arange(mp, dtype=jnp.int32)
    chunk = tok_rows // mp
    per_part = title_nodes.shape[0]
    fetch = send_ids.shape[2]

    def swap(value, step, axis="mp"):
        return lax.ppermute(value, axis, [(i, i ^ step) for i in range(lax.axis_size(axis))])

    w_attn_in = jnp.swapaxes(w_attn_in, 1, 2)
    w_graph = jnp.swapaxes(w_graph, 1, 2)
    sent = call(
        send_kernel,
        shape((dp * fetch, 2 * cols), bf),
        (me_dp, title_nodes, send_ids[0], node_table, w_graph),
        smem=(0, 1),
        hbm=(2, 3, 4),
        out_specs=HBM,
        scratch=[pltpu.VMEM((dp * fetch, 2 * cols), bf), pltpu.SemaphoreType.DMA((dp,))],
        flops=2 * nodes * width * 2 * cols + 2 * dp * fetch * nodes * 2 * cols,
        name="send",
    )
    far = lax.all_to_all(
        sent.reshape(dp, fetch, 2 * cols), "dp", split_axis=0, concat_axis=0, tiled=True
    ).reshape(dp * fetch, 2 * cols)
    titles, _ = lax.optimization_barrier((titles, sent))

    terms = call(
        attn_kernel,
        tuple(shape((chunk + PAD, width), bf if step else f32) for step in range(mp)),
        (who, titles, w_attn_in, w_attn_out),
        smem=(0,),
        scratch=[pltpu.VMEM((tok_rows, width), f32)],
        flops=2 * tok_rows * width * 4 * w_attn_in.shape[1],
        name="attn",
    )
    parts = [swap(terms[step], step) for step in range(1, mp)]
    hidden, first_hidden, first_terms = call(
        norm_one_kernel,
        (shape((chunk + PAD, width), bf), shape((PAD, width), bf), shape((PAD, width), f32)),
        (who, titles, gains, w_ffn_in, w_ffn_out, terms[0], *parts),
        smem=(0,),
        name="norm_one",
    )
    hiddens = [hidden] + [swap(hidden, step) for step in range(1, mp)]
    *terms, first = call(
        ffn_kernel,
        tuple(shape((chunk, width), bf if step else f32) for step in range(mp))
        + (shape((per_part, width), bf),),
        (w_ffn_in, w_ffn_out, gains, first_hidden, first_terms, *hiddens),
        flops=4 * tok_rows * width * w_ffn_in.shape[1],
        name="ffn",
    )
    parts = [swap(terms[step], step) for step in range(1, mp)]
    turns = dp // mp
    firsts = [
        lax.ppermute(
            first,
            ("dp", "mp"),
            [
                (p * mp + m, (p ^ (turn * mp + m)) * mp + m)
                for p in range(dp)
                for m in range(mp)
                if turn or m
            ],
        )
        for turn in range(turns)
    ]
    done = call(
        norm_two_kernel,
        shape((chunk + tail_rows(turns * per_part), width), bf),
        (hidden, gains, terms[0], *parts, *firsts),
        name="norm_two",
    )
    dones = [done] + [swap(done, step) for step in range(1, mp)]

    mask = call(
        mask_kernel, shape((nodes, TPR * TILE), bf), (nbr_slots.T,), flops=10**9, name="mask"
    )
    kv, q, first_kv = call(
        own_kernel,
        (shape((nodes, 2 * cols), bf), shape((nodes, cols), bf), shape((dp * per_part, 2 * cols), bf)),
        (who, title_nodes, node_table, w_graph, first, *dones),
        smem=(0, 1),
        hbm=(2, 3),
        scratch=[pltpu.VMEM((nodes, width), bf), pltpu.VMEM((dp * per_part, width), f32)],
        flops=2 * nodes * width * 3 * cols,
        name="own",
    )
    keys = nodes + dp * fetch
    graph_out = call(
        graph_kernel,
        shape((cols, nodes), bf),
        (tile_cols, q, kv, first_kv, mask, far),
        smem=(0,),
        scratch=[pltpu.VMEM((keys, cols), bf), pltpu.VMEM((keys, cols), bf)],
        flops=10**9,
        name="graph",
    )
    encoded = call(
        place_kernel, shape((tok_rows, width), bf), (who, *dones), smem=(0,), name="place"
    )
    return (encoded, graph_out.T)


def solution(mesh):
    in_specs = (
        P("dp", None),
        P(None, None, "mp"),
        P("mp", None),
        P(None, "mp"),
        P("mp", None),
        P(),
        P("dp", None),
        P(None, None, "mp"),
        P("dp"),
        P("dp", None, None),
        P("dp", None),
        P("dp", None),
    )
    out_specs = (P("dp", None), P("dp", "mp"))
    return jax.shard_map(
        local, mesh=mesh, in_specs=in_specs, out_specs=out_specs, check_vma=False
    )
```

time: 78.5 us -> 74.6 us (0.950)
  starting transfers between devices: 26.8 us -> 19.2 us
  Pallas kernels: 21 us -> 23.7 us
  waiting for transfers between devices: 21.8 us -> 23.1 us
    ppermute x19 -> x12, starting transfers between devices: 19.4 us -> 8.1 us  [swap(): lax.ppermute(value, axis, [(i, i ^ step) for i in range(lax.axis_size(axi...]
    ppermute x0 -> x2, waiting for transfers between devices: none -> 9.45 us  [local(): lax.ppermute(first, ('dp', 'mp'), [(p * mp + m, (p ^ turn * mp + m) * mp...]
    ppermute x19 -> x12, waiting for transfers between devices: 21.8 us -> 13.6 us  [swap(): lax.ppermute(value, axis, [(i, i ^ step) for i in range(lax.axis_size(axi...]
    ppermute x0 -> x2, starting transfers between devices: none -> 3.74 us  [local(): lax.ppermute(first, ('dp', 'mp'), [(p * mp + m, (p ^ turn * mp + m) * mp...]
    pallas_call x8 -> x9, Pallas kernels: 21 us -> 23.7 us  [call(): pl.pallas_call(body, out_shape=outs, in_specs=specs, out_specs=jax.tree.m...]
  transfers between devices with their start and end apart: 20 -> 15, of which waited for: 9 -> 6; matrix products, arithmetic and copies ran while one was open for 0% -> 0% of each run, Pallas kernels for 12% -> 16%
where the time goes in v4:
time: 74.6 us; the launch traced here: 74.1 us
  Pallas kernels  23.7 us (32%)
  waiting for transfers between devices  23.1 us (31%)
  starting transfers between devices  19.2 us (26%)
  local copies, waits for them, and re-layouts  7.22 us (10%)
  between operations  0.87 us (1%)
    pallas_call x9, Pallas kernels, call(): pl.pallas_call(body, out_shape=outs, in_specs=specs, out_specs=jax.tree.m...  23.7 us
    ppermute x12, waiting for transfers between devices, swap(): lax.ppermute(value, axis, [(i, i ^ step) for i in range(lax.axis_size(axi...  13.6 us
    ppermute x2, waiting for transfers between devices, local(): lax.ppermute(first, ('dp', 'mp'), [(p * mp + m, (p ^ turn * mp + m) * mp...  9.45 us
    ppermute x12, starting transfers between devices, swap(): lax.ppermute(value, axis, [(i, i ^ step) for i in range(lax.axis_size(axi...  8.1 us
    all_to_all x1, starting transfers between devices, local(): lax.all_to_all(sent.reshape(dp, fetch, 2 * cols), 'dp', split_axis=0, con...  7.4 us
    unnamed x36, local copies, waits for them, and re-layouts  7.22 us
    ppermute x2, starting transfers between devices, local(): lax.ppermute(first, ('dp', 'mp'), [(p * mp + m, (p ^ turn * mp + m) * mp...  3.74 us
  transfers between devices with their start and end apart: 15, of which 6 were waited for; matrix products, arithmetic and copies ran while one was open for 0% of the time, Pallas kernels for 16%

profile of v4, /device:TPU:0, one launch (start us, length us, event | category | flops | bytes accessed | tf_op | source)
XLA Modules:
  0.0 74.1 jit_solution(11911614779762047892)
XLA Ops:
  0.6 0.0 copy-start.5
  0.6 1.2 %copy-done.5 = bf16[3,768,192]{1,2,0:T(8,128)(2,1)S(1)} copy-done((bf16[3,768,192]{1,2,0:T(8,128)(2,1)S(1)}, bf16[3,768,192]{1,2,0:T(8,128)(2,1)}, u32[]{:S(2)}) %copy-start.5) | copy-done | bytes 884760
  1.8 0.0 copy-start.7
  1.8 1.1 %copy-done.7 = bf16[512,768]{1,0:T(8,128)(2,1)S(1)} copy-done((bf16[512,768]{1,0:T(8,128)(2,1)S(1)}, bf16[512,768]{1,0:T(8,128)(2,1)}, u32[]{:S(2)}) %copy-start.7) | copy-done | bytes 786456
  2.9 0.7 copy-done.11
  3.6 0.7 copy-done.14
  4.3 6.4 %send.1 = bf16[2048,384]{1,0:T(8,128)(2,1)S(1)} custom-call(s32[1]{0:T(128)} %bitcast.refs_0_, s32[2]{0:T(128)S(1)} %copy-done.11, s32[8,256]{1,0:T(8,128)S(1)} %bitcast.13, bf16[512,768]{1,0:T(8,128)(2,1)S(1)} %copy-done.7, bf16[3,192,768]{2,1,0:T(8,128)(2,1)S(1)} %bitcast.10), custom_call_target="tpu_custom_call" | custom-call | flops 1107296256 | bytes 1679372 | tf_op jit(solution)/shard_map/send/pallas_call | solution.py:49
  10.7 0.0 copy-start.2
  10.7 1.1 %copy-done.2 = bf16[2048,384]{1,0:T(8,128)(2,1)} copy-done((bf16[2048,384]{1,0:T(8,128)(2,1)}, bf16[2048,384]{1,0:T(8,128)(2,1)S(1)}, u32[]{:S(2)}) %copy-start.2) | copy-done | bytes 1572888
  11.8 7.4 %all-to-all-start = ((bf16[8,256,384]{2,1,0:T(8,128)(2,1)}), bf16[8,256,384]{2,1,0:T(8,128)(2,1)}, u32[]{:S(2)}, u32[]{:S(2)}) async-start(bf16[8,256,384]{2,1,0:T(8,128)(2,1)} %bitcast.8), calls=%async_computation | async-start | bytes 3145728 | tf_op jit(solution)/shard_map/all_to_all | solution.py:351
  19.3 0.0 copy-done.3
  19.3 0.0 copy-done.9
  19.3 0.0 copy-start.4
  19.3 1.2 %copy-done.4 = bf16[3,768,192]{1,2,0:T(8,128)(2,1)S(1)} copy-done((bf16[3,768,192]{1,2,0:T(8,128)(2,1)S(1)}, bf16[3,768,192]{1,2,0:T(8,128)(2,1)}, u32[]{:S(2)}) %copy-start.4) | copy-done | bytes 884760
  20.5 2.3 %attn.1 = (f32[80,768]{1,0:T(8,128)S(1)}, bf16[80,768]{1,0:T(8,128)(2,1)S(1)}, bf16[80,768]{1,0:T(8,128)(2,1)S(1)}, bf16[80,768]{1,0:T(8,128)(2,1)S(1)}) custom-call(s32[4]{0:T(128)S(1)} %iota_xor_fusion.refs_0_, bf16[256,768]{1,0:T(8,128)(2,1)S(1)} %copy-done.3, bf16[3,192,768]{2,1,0:T(8,128)(2,1)S(1)} %bitcast.9, bf16[192,768]{1,0:T(8,128)(2,1)S(1)} %copy-done.9), custom_call_target="tpu_custom_call" | custom-call | flops 301989888 | bytes 1572880 | tf_op jit(solution)/shard_map/attn/pallas_call | solution.py:49
  22.8 0.1 collective-permute-start
  22.9 1.6 %collective-permute-start.1 = (bf16[80,768]{1,0:T(8,128)(2,1)S(1)}, bf16[80,768]{1,0:T(8,128)(2,1)S(1)}, u32[]{:S(2)}, u32[]{:S(2)}) collective-permute-start(bf16[80,768]{1,0:T(8,128)(2,1)S(1)} %get-tuple-element.21), channel_id=1, source_target_pairs={{0,2},{1,3},{2,0},{3,1},{4,6},{5,7},{6,4},{7,5},{8,10},{9,11},{10,... | collective-permute-start | bytes 368648 | tf_op jit(solution)/shard_map/ppermute | solution.py:336
  24.5 0.3 collective-permute-start.2
  24.7 0.0 collective-permute-done.refs_6_
  24.7 4.3 %collective-permute-done.1.refs_7_ = bf16[80,768]{1,0:T(8,128)(2,1)S(1)} collective-permute-done((bf16[80,768]{1,0:T(8,128)(2,1)S(1)}, bf16[80,768]{1,0:T(8,128)(2,1)S(1)}, u32[]{:S(2)}, u32[]{:S(2)}) %collective-permute-start.1) | collective-permute-done | bytes 122912 | tf_op jit(solution)/shard_map/ppermute | solution.py:336
  29.1 1.7 %collective-permute-done.2.refs_8_ = bf16[80,768]{1,0:T(8,128)(2,1)S(1)} collective-permute-done((bf16[80,768]{1,0:T(8,128)(2,1)S(1)}, bf16[80,768]{1,0:T(8,128)(2,1)S(1)}, u32[]{:S(2)}, u32[]{:S(2)}) %collective-permute-start.2) | collective-permute-done | bytes 122912 | tf_op jit(solution)/shard_map/ppermute | solution.py:336
  30.8 0.0 copy-done.1
  30.8 0.0 copy-done.10
  30.8 0.0 copy-done
  30.8 1.3 %norm_one.1 = (bf16[80,768]{1,0:T(8,128)(2,1)S(1)}, bf16[16,768]{1,0:T(8,128)(2,1)S(1)}, f32[16,768]{1,0:T(8,128)S(1)}) custom-call(s32[4]{0:T(128)S(1)} %iota_xor_fusion.refs_0_, bf16[256,768]{1,0:T(8,128)(2,1)S(1)} %copy-done.3, f32[2,768]{1,0:T(2,128)S(1)} %copy-done.10, bf16[768,768]{1,0:T(8,128)(2,1)S(1)} %copy-done, bf16[768,768]{1,0:T(8,128)(2,1)S(1)} %copy-done.1, ...), custom_call_target="tpu_custom_call" | custom-call | bytes 3373072 | tf_op jit(solution)/shard_map/norm_one/pallas_call | solution.py:49
  32.1 1.8 %collective-permute-start.5 = (bf16[80,768]{1,0:T(8,128)(2,1)S(1)}, bf16[80,768]{1,0:T(8,128)(2,1)S(1)}, u32[]{:S(2)}, u32[]{:S(2)}) collective-permute-start(bf16[80,768]{1,0:T(8,128)(2,1)S(1)} %get-tuple-element.23.refs_5_.refs_0_), channel_id=1, source_target_pairs={{0,3},{1,2},{2,1},{3,0},{4,7},{5,6},{6,5},{7,4},{8,11},{9,10},{10,... | collective-permute-start | bytes 368648 | tf_op jit(solution)/shard_map/ppermute | solution.py:336
  33.9 0.5 collective-permute-start.4
  34.4 0.0 collective-permute-start.3
  34.4 3.2 %collective-permute-done.5.refs_8_ = bf16[80,768]{1,0:T(8,128)(2,1)S(1)} collective-permute-done((bf16[80,768]{1,0:T(8,128)(2,1)S(1)}, bf16[80,768]{1,0:T(8,128)(2,1)S(1)}, u32[]{:S(2)}, u32[]{:S(2)}) %collective-permute-start.5) | collective-permute-done | bytes 122912 | tf_op jit(solution)/shard_map/ppermute | solution.py:336
  37.6 2.8 %collective-permute-done.4.refs_7_ = bf16[80,768]{1,0:T(8,128)(2,1)S(1)} collective-permute-done((bf16[80,768]{1,0:T(8,128)(2,1)S(1)}, bf16[80,768]{1,0:T(8,128)(2,1)S(1)}, u32[]{:S(2)}, u32[]{:S(2)}) %collective-permute-start.4) | collective-permute-done | bytes 122912 | tf_op jit(solution)/shard_map/ppermute | solution.py:336
  40.4 0.0 collective-permute-done.3.refs_6_
  40.4 0.9 %ffn.1 = (f32[64,768]{1,0:T(8,128)S(1)}, bf16[64,768]{1,0:T(8,128)(2,1)S(1)}, bf16[64,768]{1,0:T(8,128)(2,1)S(1)}, bf16[64,768]{1,0:T(8,128)(2,1)S(1)}, bf16[2,768]{1,0:T(2,128)(2,1)S(1)}) custom-call(bf16[768,768]{1,0:T(8,128)(2,1)S(1)} %copy-done, bf16[768,768]{1,0:T(8,128)(2,1)S(1)} %copy-done.1, f32[2,768]{1,0:T(2,128)S(1)} %copy-done.10, ...), custom_call_target="tpu_custom_call" | custom-call | flops 603979776 | bytes 2930688 | tf_op jit(solution)/shard_map/ffn/pallas_call | solution.py:49
  41.3 0.1 collective-permute-start.6
  41.4 1.5 %collective-permute-start.7 = (bf16[64,768]{1,0:T(8,128)(2,1)S(1)}, bf16[64,768]{1,0:T(8,128)(2,1)S(1)}, u32[]{:S(2)}, u32[]{:S(2)}) collective-permute-start(bf16[64,768]{1,0:T(8,128)(2,1)S(1)} %get-tuple-element.28), channel_id=1, source_target_pairs={{0,2},{1,3},{2,0},{3,1},{4,6},{5,7},{6,4},{7,5},{8,10},{9,11},{10,... | collective-permute-start | bytes 294920 | tf_op jit(solution)/shard_map/ppermute | solution.py:336
  42.9 0.3 collective-permute-start.8
  43.3 2.9 %collective-permute-start.10 = (bf16[2,768]{1,0:T(2,128)(2,1)S(1)}, bf16[2,768]{1,0:T(2,128)(2,1)S(1)}, u32[]{:S(2)}, u32[]{:S(2)}) collective-permute-start(bf16[2,768]{1,0:T(2,128)(2,1)S(1)} %get-tuple-element.30.refs_4_), channel_id=1, source_target_pairs={{0,16},{1,21},{2,26},{3,31},{4,20},{5,17},{6,30},{7,27},{8,24},{9,... | collective-permute-start | bytes 9224 | tf_op jit(solution)/shard_map/ppermute | solution.py:385
  46.2 0.8 %collective-permute-start.9 = (bf16[2,768]{1,0:T(2,128)(2,1)S(1)}, bf16[2,768]{1,0:T(2,128)(2,1)S(1)}, u32[]{:S(2)}, u32[]{:S(2)}) collective-permute-start(bf16[2,768]{1,0:T(2,128)(2,1)S(1)} %get-tuple-element.30.refs_4_), channel_id=1, source_target_pairs={{1,5},{2,10},{3,15},{5,1},{6,14},{7,11},{9,13},{10,2},{11,7},{13,9... | collective-permute-start | bytes 9224 | tf_op jit(solution)/shard_map/ppermute | solution.py:385
  47.0 9.4 %collective-permute-done.10.refs_7_ = bf16[2,768]{1,0:T(2,128)(2,1)S(1)} collective-permute-done((bf16[2,768]{1,0:T(2,128)(2,1)S(1)}, bf16[2,768]{1,0:T(2,128)(2,1)S(1)}, u32[]{:S(2)}, u32[]{:S(2)}) %collective-permute-start.10) | collective-permute-done | bytes 3104 | tf_op jit(solution)/shard_map/ppermute | solution.py:385
  56.4 0.0 collective-permute-done.9.refs_6_
  56.4 0.0 collective-permute-done.6.refs_3_
  56.5 0.0 collective-permute-done.7.refs_4_
  56.5 0.0 collective-permute-done.8.refs_5_
  56.5 0.2 norm_two.1.refs_1_.refs_5_
  56.7 0.1 collective-permute-start.13
  56.8 1.2 %collective-permute-start.12 = (bf16[80,768]{1,0:T(8,128)(2,1)S(1)}, bf16[80,768]{1,0:T(8,128)(2,1)S(1)}, u32[]{:S(2)}, u32[]{:S(2)}) collective-permute-start(bf16[80,768]{1,0:T(8,128)(2,1)S(1)} %norm_two.1.refs_1_.refs_5_), channel_id=1, source_target_pairs={{0,2},{1,3},{2,0},{3,1},{4,6},{5,7},{6,4},{7,5},{8,10},{9,11},{10,... | collective-permute-start | bytes 368648 | tf_op jit(solution)/shard_map/ppermute | solution.py:336
  57.9 0.7 collective-permute-start.11
  58.6 0.0 copy-done.13
  58.6 4.2 %mask.1.refs_4_ = bf16[512,768]{1,0:T(8,128)(2,1)S(1)} custom-call(s32[16,512]{1,0:T(8,128)S(1)} %bitcast.12), custom_call_target="tpu_custom_call" | custom-call | flops 1000000000 | bytes 32768 | tf_op jit(solution)/shard_map/mask/pallas_call | solution.py:49
  62.9 0.0 copy-start.16
  62.9 0.0 copy-start.15
  62.9 0.0 collective-permute-done.13.refs_4_.refs_8_
  62.9 1.5 %collective-permute-done.12.refs_3_.refs_7_ = bf16[80,768]{1,0:T(8,128)(2,1)S(1)} collective-permute-done((bf16[80,768]{1,0:T(8,128)(2,1)S(1)}, bf16[80,768]{1,0:T(8,128)(2,1)S(1)}, u32[]{:S(2)}, u32[]{:S(2)}) %collective-permute-start.12) | collective-permute-done | bytes 122912 | tf_op jit(solution)/shard_map/ppermute | solution.py:336
  64.5 0.0 collective-permute-done.11.refs_2_.refs_6_
  64.5 1.3 %place.1 = bf16[256,768]{1,0:T(8,128)(2,1)} custom-call(s32[4]{0:T(128)S(1)} %iota_xor_fusion.refs_0_, bf16[80,768]{1,0:T(8,128)(2,1)S(1)} %norm_two.1.refs_1_.refs_5_, bf16[80,768]{1,0:T(8,128)(2,1)S(1)} %collective-permute-done.11.refs_2_.refs_6_, bf16[80,768]{1,0:T(8,128)(2,1)S(1)} %collective-permute-done.12.refs_3_.refs_7_, ...), custom_call_target="tpu_custom_call" | custom-call | bytes 491536 | tf_op jit(solution)/shard_map/place/pallas_call | solution.py:49
  65.8 0.0 copy-done.6
  65.8 0.0 copy-done.8
  65.8 0.0 copy-done.12
  65.8 1.9 %own.1 = (bf16[512,384]{1,0:T(8,128)(2,1)S(1)}, bf16[512,192]{1,0:T(8,128)(2,1)S(1)}, bf16[16,384]{1,0:T(8,128)(2,1)S(1)}) custom-call(s32[4]{0:T(128)S(1)} %iota_xor_fusion.refs_0_, s32[2]{0:T(128)S(1)} %copy-done.12, bf16[512,768]{1,0:T(8,128)(2,1)S(1)} %copy-done.8, bf16[3,192,768]{2,1,0:T(8,128)(2,1)S(1)} %bitcast.11, ...), custom_call_target="tpu_custom_call" | custom-call | flops 452984832 | bytes 2165784 | tf_op jit(solution)/shard_map/own/pallas_call | solution.py:49
  67.7 0.0 copy-done.16
  67.7 0.0 all-to-all-done
  67.7 0.0 copy-done.15
  67.7 0.0 copy-start.17
  67.7 1.1 %copy-done.17 = bf16[512,768]{1,0:T(8,128)(2,1)S(1)} copy-done((bf16[512,768]{1,0:T(8,128)(2,1)S(1)}, bf16[512,768]{1,0:T(8,128)(2,1)}, u32[]{:S(2)}) %copy-start.17) | copy-done | bytes 786456
  68.8 5.3 %graph.1 = bf16[192,512]{1,0:T(8,128)(2,1)} custom-call(s32[4,6]{1,0:T(4,128)S(1)} %copy-done.15, bf16[512,192]{1,0:T(8,128)(2,1)S(1)} %get-tuple-element.31.refs_1_, bf16[512,384]{1,0:T(8,128)(2,1)S(1)} %get-tuple-element.32.refs_2_, bf16[16,384]{1,0:T(8,128)(2,1)S(1)} %get-tuple-element.33.refs_3_, bf16[512,768]{1,0:T(8,128)(2,1)S(1)} %copy-done.17, ...), custom_call_target="tpu_custom_call" | custom-call | flops 1000000000 | bytes 2961504 | tf_op jit(solution)/shard_map/graph/pallas_call | solution.py:49
  (12 shorter events, 0.0 us)
Async XLA Ops:
  0.6 1.2 %copy-start.5 = (bf16[3,768,192]{1,2,0:T(8,128)(2,1)S(1)}, bf16[3,768,192]{1,2,0:T(8,128)(2,1)}, u32[]{:S(2)}) copy-start(bf16[3,768,192]{1,2,0:T(8,128)(2,1)} %param.19) | copy-start | bytes 2654212
  1.8 1.1 %copy-start.7 = (bf16[512,768]{1,0:T(8,128)(2,1)S(1)}, bf16[512,768]{1,0:T(8,128)(2,1)}, u32[]{:S(2)}) copy-start(bf16[512,768]{1,0:T(8,128)(2,1)} %refs_2_.5) | copy-start | bytes 2359300
  2.9 0.7 copy-start.11
  3.6 0.7 copy-start.14
  10.7 1.2 %copy-start.2 = (bf16[2048,384]{1,0:T(8,128)(2,1)}, bf16[2048,384]{1,0:T(8,128)(2,1)S(1)}, u32[]{:S(2)}) copy-start(bf16[2048,384]{1,0:T(8,128)(2,1)S(1)} %send.1) | copy-start | bytes 4718596
  11.8 7.4 %copy-start.3 = (bf16[256,768]{1,0:T(8,128)(2,1)S(1)}, bf16[256,768]{1,0:T(8,128)(2,1)}, u32[]{:S(2)}) copy-start(bf16[256,768]{1,0:T(8,128)(2,1)} %refs_1_.6) | copy-start | bytes 1179652
  11.8 7.4 %copy-start.9 = (bf16[192,768]{1,0:T(8,128)(2,1)S(1)}, bf16[192,768]{1,0:T(8,128)(2,1)}, u32[]{:S(2)}) copy-start(bf16[192,768]{1,0:T(8,128)(2,1)} %refs_3_.4) | copy-start | bytes 884740
  11.8 19.0 %copy-start.1 = (bf16[768,768]{1,0:T(8,128)(2,1)S(1)}, bf16[768,768]{1,0:T(8,128)(2,1)}, u32[]{:S(2)}) copy-start(bf16[768,768]{1,0:T(8,128)(2,1)} %refs_1_.7) | copy-start | bytes 3538948
  11.8 19.0 %copy-start.10 = (f32[2,768]{1,0:T(2,128)S(1)}, f32[2,768]{1,0:T(2,128)}, u32[]{:S(2)}) copy-start(f32[2,768]{1,0:T(2,128)} %refs_1_.8) | copy-start | bytes 18436
  11.8 55.8 %all-to-all-start = ((bf16[8,256,384]{2,1,0:T(8,128)(2,1)}), bf16[8,256,384]{2,1,0:T(8,128)(2,1)}, u32[]{:S(2)}, u32[]{:S(2)}) async-start(bf16[8,256,384]{2,1,0:T(8,128)(2,1)} %bitcast.8), calls=%async_computation | async-start | bytes 3145728 | tf_op jit(solution)/shard_map/all_to_all | solution.py:351
  19.2 11.6 %copy-start = (bf16[768,768]{1,0:T(8,128)(2,1)S(1)}, bf16[768,768]{1,0:T(8,128)(2,1)}, u32[]{:S(2)}) copy-start(bf16[768,768]{1,0:T(8,128)(2,1)} %refs_0_.2) | copy-start | bytes 3538948
  19.3 1.3 %copy-start.4 = (bf16[3,768,192]{1,2,0:T(8,128)(2,1)S(1)}, bf16[3,768,192]{1,2,0:T(8,128)(2,1)}, u32[]{:S(2)}) copy-start(bf16[3,768,192]{1,2,0:T(8,128)(2,1)} %param.13) | copy-start | bytes 2654212
  22.8 1.9 %collective-permute-start = (bf16[80,768]{1,0:T(8,128)(2,1)S(1)}, bf16[80,768]{1,0:T(8,128)(2,1)S(1)}, u32[]{:S(2)}, u32[]{:S(2)}) collective-permute-start(bf16[80,768]{1,0:T(8,128)(2,1)S(1)} %get-tuple-element.20), channel_id=1, source_target_pairs={{0,1},{1,0},{2,3},{3,2},{4,5},{5,4},{6,7},{7,6},{8,9},{9,8},{10,11... | collective-permute-start | bytes 368648 | tf_op jit(solution)/shard_map/ppermute | solution.py:336
  22.9 6.2 %collective-permute-start.1 = (bf16[80,768]{1,0:T(8,128)(2,1)S(1)}, bf16[80,768]{1,0:T(8,128)(2,1)S(1)}, u32[]{:S(2)}, u32[]{:S(2)}) collective-permute-start(bf16[80,768]{1,0:T(8,128)(2,1)S(1)} %get-tuple-element.21), channel_id=1, source_target_pairs={{0,2},{1,3},{2,0},{3,1},{4,6},{5,7},{6,4},{7,5},{8,10},{9,11},{10,... | collective-permute-start | bytes 368648 | tf_op jit(solution)/shard_map/ppermute | solution.py:336
  24.5 6.3 %collective-permute-start.2 = (bf16[80,768]{1,0:T(8,128)(2,1)S(1)}, bf16[80,768]{1,0:T(8,128)(2,1)S(1)}, u32[]{:S(2)}, u32[]{:S(2)}) collective-permute-start(bf16[80,768]{1,0:T(8,128)(2,1)S(1)} %get-tuple-element.22), channel_id=1, source_target_pairs={{0,3},{1,2},{2,1},{3,0},{4,7},{5,6},{6,5},{7,4},{8,11},{9,10},{10,... | collective-permute-start | bytes 368648 | tf_op jit(solution)/shard_map/ppermute | solution.py:336
  32.1 5.5 %collective-permute-start.5 = (bf16[80,768]{1,0:T(8,128)(2,1)S(1)}, bf16[80,768]{1,0:T(8,128)(2,1)S(1)}, u32[]{:S(2)}, u32[]{:S(2)}) collective-permute-start(bf16[80,768]{1,0:T(8,128)(2,1)S(1)} %get-tuple-element.23.refs_5_.refs_0_), channel_id=1, source_target_pairs={{0,3},{1,2},{2,1},{3,0},{4,7},{5,6},{6,5},{7,4},{8,11},{9,10},{10,... | collective-permute-start | bytes 368648 | tf_op jit(solution)/shard_map/ppermute | solution.py:336
  33.9 6.5 %collective-permute-start.4 = (bf16[80,768]{1,0:T(8,128)(2,1)S(1)}, bf16[80,768]{1,0:T(8,128)(2,1)S(1)}, u32[]{:S(2)}, u32[]{:S(2)}) collective-permute-start(bf16[80,768]{1,0:T(8,128)(2,1)S(1)} %get-tuple-element.23.refs_5_.refs_0_), channel_id=1, source_target_pairs={{0,2},{1,3},{2,0},{3,1},{4,6},{5,7},{6,4},{7,5},{8,10},{9,11},{10,... | collective-permute-start | bytes 368648 | tf_op jit(solution)/shard_map/ppermute | solution.py:336
  34.4 6.0 %collective-permute-start.3 = (bf16[80,768]{1,0:T(8,128)(2,1)S(1)}, bf16[80,768]{1,0:T(8,128)(2,1)S(1)}, u32[]{:S(2)}, u32[]{:S(2)}) collective-permute-start(bf16[80,768]{1,0:T(8,128)(2,1)S(1)} %get-tuple-element.23.refs_5_.refs_0_), channel_id=1, source_target_pairs={{0,1},{1,0},{2,3},{3,2},{4,5},{5,4},{6,7},{7,6},{8,9},{9,8},{10,11... | collective-permute-start | bytes 368648 | tf_op jit(solution)/shard_map/ppermute | solution.py:336
  40.4 18.3 %copy-start.13 = (s32[512,16]{0,1:T(8,128)S(1)}, s32[512,16]{0,1:T(8,128)}, u32[]{:S(2)}) copy-start(s32[512,16]{0,1:T(8,128)} %param.23) | copy-start | bytes 98308
  41.3 15.1 %collective-permute-start.6 = (bf16[64,768]{1,0:T(8,128)(2,1)S(1)}, bf16[64,768]{1,0:T(8,128)(2,1)S(1)}, u32[]{:S(2)}, u32[]{:S(2)}) collective-permute-start(bf16[64,768]{1,0:T(8,128)(2,1)S(1)} %get-tuple-element.27), channel_id=1, source_target_pairs={{0,1},{1,0},{2,3},{3,2},{4,5},{5,4},{6,7},{7,6},{8,9},{9,8},{10,11... | collective-permute-start | bytes 294920 | tf_op jit(solution)/shard_map/ppermute | solution.py:336
  41.4 15.1 %collective-permute-start.7 = (bf16[64,768]{1,0:T(8,128)(2,1)S(1)}, bf16[64,768]{1,0:T(8,128)(2,1)S(1)}, u32[]{:S(2)}, u32[]{:S(2)}) collective-permute-start(bf16[64,768]{1,0:T(8,128)(2,1)S(1)} %get-tuple-element.28), channel_id=1, source_target_pairs={{0,2},{1,3},{2,0},{3,1},{4,6},{5,7},{6,4},{7,5},{8,10},{9,11},{10,... | collective-permute-start | bytes 294920 | tf_op jit(solution)/shard_map/ppermute | solution.py:336
  42.9 13.5 %collective-permute-start.8 = (bf16[64,768]{1,0:T(8,128)(2,1)S(1)}, bf16[64,768]{1,0:T(8,128)(2,1)S(1)}, u32[]{:S(2)}, u32[]{:S(2)}) collective-permute-start(bf16[64,768]{1,0:T(8,128)(2,1)S(1)} %get-tuple-element.29), channel_id=1, source_target_pairs={{0,3},{1,2},{2,1},{3,0},{4,7},{5,6},{6,5},{7,4},{8,11},{9,10},{10,... | collective-permute-start | bytes 294920 | tf_op jit(solution)/shard_map/ppermute | solution.py:336
  43.3 13.2 %collective-permute-start.10 = (bf16[2,768]{1,0:T(2,128)(2,1)S(1)}, bf16[2,768]{1,0:T(2,128)(2,1)S(1)}, u32[]{:S(2)}, u32[]{:S(2)}) collective-permute-start(bf16[2,768]{1,0:T(2,128)(2,1)S(1)} %get-tuple-element.30.refs_4_), channel_id=1, source_target_pairs={{0,16},{1,21},{2,26},{3,31},{4,20},{5,17},{6,30},{7,27},{8,24},{9,... | collective-permute-start | bytes 9224 | tf_op jit(solution)/shard_map/ppermute | solution.py:385
  46.2 10.3 %collective-permute-start.9 = (bf16[2,768]{1,0:T(2,128)(2,1)S(1)}, bf16[2,768]{1,0:T(2,128)(2,1)S(1)}, u32[]{:S(2)}, u32[]{:S(2)}) collective-permute-start(bf16[2,768]{1,0:T(2,128)(2,1)S(1)} %get-tuple-element.30.refs_4_), channel_id=1, source_target_pairs={{1,5},{2,10},{3,15},{5,1},{6,14},{7,11},{9,13},{10,2},{11,7},{13,9... | collective-permute-start | bytes 9224 | tf_op jit(solution)/shard_map/ppermute | solution.py:385
  56.7 6.2 %collective-permute-start.13 = (bf16[80,768]{1,0:T(8,128)(2,1)S(1)}, bf16[80,768]{1,0:T(8,128)(2,1)S(1)}, u32[]{:S(2)}, u32[]{:S(2)}) collective-permute-start(bf16[80,768]{1,0:T(8,128)(2,1)S(1)} %norm_two.1.refs_1_.refs_5_), channel_id=1, source_target_pairs={{0,3},{1,2},{2,1},{3,0},{4,7},{5,6},{6,5},{7,4},{8,11},{9,10},{10,... | collective-permute-start | bytes 368648 | tf_op jit(solution)/shard_map/ppermute | solution.py:336
  56.8 7.7 %collective-permute-start.12 = (bf16[80,768]{1,0:T(8,128)(2,1)S(1)}, bf16[80,768]{1,0:T(8,128)(2,1)S(1)}, u32[]{:S(2)}, u32[]{:S(2)}) collective-permute-start(bf16[80,768]{1,0:T(8,128)(2,1)S(1)} %norm_two.1.refs_1_.refs_5_), channel_id=1, source_target_pairs={{0,2},{1,3},{2,0},{3,1},{4,6},{5,7},{6,4},{7,5},{8,10},{9,11},{10,... | collective-permute-start | bytes 368648 | tf_op jit(solution)/shard_map/ppermute | solution.py:336
  57.9 6.5 %collective-permute-start.11 = (bf16[80,768]{1,0:T(8,128)(2,1)S(1)}, bf16[80,768]{1,0:T(8,128)(2,1)S(1)}, u32[]{:S(2)}, u32[]{:S(2)}) collective-permute-start(bf16[80,768]{1,0:T(8,128)(2,1)S(1)} %norm_two.1.refs_1_.refs_5_), channel_id=1, source_target_pairs={{0,1},{1,0},{2,3},{3,2},{4,5},{5,4},{6,7},{7,6},{8,9},{9,8},{10,11... | collective-permute-start | bytes 368648 | tf_op jit(solution)/shard_map/ppermute | solution.py:336
  58.6 7.2 %copy-start.6 = (bf16[3,768,192]{1,2,0:T(8,128)(2,1)S(1)}, bf16[3,768,192]{1,2,0:T(8,128)(2,1)}, u32[]{:S(2)}) copy-start(bf16[3,768,192]{1,2,0:T(8,128)(2,1)} %param.19) | copy-start | bytes 2654212
  58.6 7.2 %copy-start.8 = (bf16[512,768]{1,0:T(8,128)(2,1)S(1)}, bf16[512,768]{1,0:T(8,128)(2,1)}, u32[]{:S(2)}) copy-start(bf16[512,768]{1,0:T(8,128)(2,1)} %refs_2_.5) | copy-start | bytes 2359300
  58.6 7.2 %copy-start.12 = (s32[2]{0:T(128)S(1)}, s32[2]{0:T(128)}, u32[]{:S(2)}) copy-start(s32[2]{0:T(128)} %refs_1_.9) | copy-start | bytes 28
  62.9 4.8 %copy-start.16 = (bf16[512,768]{1,0:T(8,128)(2,1)}, bf16[512,768]{1,0:T(8,128)(2,1)S(1)}, u32[]{:S(2)}) copy-start(bf16[512,768]{1,0:T(8,128)(2,1)S(1)} %mask.1.refs_4_) | copy-start | bytes 2359300
  62.9 4.8 %copy-start.15 = (s32[4,6]{1,0:T(4,128)S(1)}, s32[4,6]{1,0:T(4,128)}, u32[]{:S(2)}) copy-start(s32[4,6]{1,0:T(4,128)} %refs_0_.3) | copy-start | bytes 292
  67.7 1.1 %copy-start.17 = (bf16[512,768]{1,0:T(8,128)(2,1)S(1)}, bf16[512,768]{1,0:T(8,128)(2,1)}, u32[]{:S(2)}) copy-start(bf16[512,768]{1,0:T(8,128)(2,1)} %copy-done.16) | copy-start | bytes 2359300

commit v5 on v4

--- a/solution.py
+++ b/solution.py
@@ -24,11 +24,14 @@
 TN = (((0,), (0,)), ((), ()))
 
 
-def call(kernel, outs, args, smem=(), hbm=(), scratch=(), out_specs=None, flops=0, name=None):
+def call(
+    kernel, outs, args, smem=(), hbm=(), scalars=(), scratch=(), out_specs=None, flops=0, name=None
+):
     count, out_count, own = len(args), len(jax.tree.leaves(outs)), len(scratch)
     specs = [SMEM if i in smem else HBM if i in hbm else VMEM for i in range(count)]
     nbytes = sum(a.size * a.dtype.itemsize for a in args)
-    buffers = [pltpu.VMEM(args[i].shape, args[i].dtype) for i in hbm]
+    space = [pltpu.SMEM if i in scalars else pltpu.VMEM for i in hbm]
+    buffers = [kind(args[i].shape, args[i].dtype) for kind, i in zip(space, hbm)]
     sems = [pltpu.SemaphoreType.DMA((len(hbm),))] if hbm else []
 
     def body(*refs):
@@ -52,7 +55,7 @@
         in_specs=specs,
         out_specs=jax.tree.map(lambda _: VMEM, outs) if out_specs is None else out_specs,
         scratch_shapes=list(scratch) + buffers + sems,
-        compiler_params=pltpu.CompilerParams(vmem_limit_bytes=40 * 1024 * 1024),
+        compiler_params=pltpu.CompilerParams(vmem_limit_bytes=(60 if hbm else 40) * 1024 * 1024),
         cost_estimate=pl.CostEstimate(flops=flops, bytes_accessed=nbytes, transcendentals=0),
         name=name,
     )(*args)
@@ -85,7 +88,7 @@
     cols = w_ref.shape[1]
     per_part = at_ref.shape[0]
     fetch, nodes = ids_ref.shape[1], table_ref.shape[0]
-    ready(2, 3, 4)
+    ready(1, 2, 3, 4)
     table = table_ref[...]
     kv = jnp.concatenate([dot_nt(table, w_ref[1]), dot_nt(table, w_ref[2])], axis=1).astype(bf)
     ids = ids_ref[...].astype(f32).T.astype(jnp.int32)
@@ -201,77 +204,77 @@
 
 
 def norm_two_kernel(ready, hidden_ref, gains_ref, own_ref, *refs):
-    *refs, out = refs
-    parts = [ref for ref in refs if ref.shape == own_ref.shape]
-    firsts = [ref for ref in refs if ref.shape != own_ref.shape]
-    chunk = own_ref.shape[0]
+    *parts, out = refs
     total = own_ref[...]
     for part in parts:
         total = total + part[...].astype(f32)
-    hidden = hidden_ref[:chunk, :].astype(f32)
-    out[:chunk, :] = layer_norm(hidden + total, gains_ref[1:2, :]).astype(bf)
-    tail = out.shape[0] - chunk
-    sub = lax.broadcasted_iota(jnp.int32, (tail, out.shape[1]), 0)
-    rows = jnp.zeros((tail, out.shape[1]), f32)
-    for turn, ref in enumerate(firsts):
-        per_part = ref.shape[0]
+    hidden = hidden_ref[: out.shape[0], :].astype(f32)
+    out[...] = layer_norm(hidden + total, gains_ref[1:2, :]).astype(bf)
+
+
+def pack_kernel(ready, *refs):
+    *parts, out = refs
+    per_part = parts[0].shape[0]
+    sub = lax.broadcasted_iota(jnp.int32, out.shape, 0)
+    rows = jnp.zeros(out.shape, f32)
+    for turn, ref in enumerate(parts):
         for title in range(per_part):
             row = ref[title : title + 1, :].astype(f32)
             rows = jnp.where(sub == turn * per_part + title, row, rows)
-    out[chunk:, :] = rows.astype(bf)
+    out[...] = rows.astype(bf)
 
 
 def place_kernel(ready, who_ref, *refs):
     *chunks, out = refs
     chunk = out.shape[0] // len(chunks)
     for step, ref in enumerate(chunks):
-        out[pl.ds(pl.multiple_of(who_ref[step] * chunk, chunk), chunk), :] = ref[:chunk, :]
-
-
-def own_kernel(ready, who_ref, at_ref, table_ref, w_ref, first_ref, *refs):
-    *chunks, kv_ref, q_ref, first_kv_ref, features, firsts = refs
-    members = len(chunks)
-    per_part, width = first_ref.shape
+        out[pl.ds(pl.multiple_of(who_ref[step] * chunk, chunk), chunk), :] = ref[...]
+
+
+def own_kernel(ready, table_ref, w_ref, kv_ref, q_ref):
     cols = w_ref.shape[1]
-    turns = firsts.shape[0] // per_part // members
-    for step, ref in enumerate(chunks):
-        base = ref.shape[0] - tail_rows(turns * per_part)
-        rows = ref[base:, :].astype(f32)
-        for turn in range(turns):
+    table = table_ref[...]
+    kv_ref[:, :cols] = dot_nt(table, w_ref[1]).astype(bf)
+    kv_ref[:, cols:] = dot_nt(table, w_ref[2]).astype(bf)
+    q_ref[...] = dot_nt(table, w_ref[0]).astype(bf)
+
+
+def tail_rows(count):
+    return -(-count // PAD) * PAD
+
+
+def graph_kernel(
+    ready, who_ref, cols_ref, at_ref, q_ref, kv_ref, w_ref, mask_ref, far_ref, first_ref, *refs
+):
+    *packs, out_ref, k_all, v_all, firsts = refs
+    nodes, cols = q_ref.shape
+    row_tiles = nodes // TILE
+    per_part = first_ref.shape[0]
+    members = len(packs)
+    for step, ref in enumerate(packs):
+        rows = ref[...].astype(f32)
+        for turn in range(firsts.shape[0] // per_part // members):
             for title in range(per_part):
                 place = (turn * members + who_ref[step]) * per_part + title
-                firsts[pl.ds(place, 1), :] = rows[turn * per_part + title][None]
+                at = turn * per_part + title
+                firsts[pl.ds(place, 1), :] = rows[at : at + 1]
     firsts[0:per_part, :] = first_ref[...].astype(f32)
-    ready(2, 3)
-    nodes = table_ref.shape[0]
-    for tile in range(nodes // TILE):
+    first = firsts[...].astype(bf)
+    ready(5)
+    first_kv = jnp.concatenate([dot_nt(first, w_ref[1]), dot_nt(first, w_ref[2])], axis=1).astype(bf)
+    first_q = dot_nt(first, w_ref[0])
+    ready(2, 4)
+    for tile in range(row_tiles):
         span = slice(tile * TILE, (tile + 1) * TILE)
-        rows = table_ref[span, :].astype(f32)
-        sub = lax.broadcasted_iota(jnp.int32, (TILE, width), 0) + tile * TILE
+        rows = kv_ref[span, :].astype(f32)
+        sub = lax.broadcasted_iota(jnp.int32, (TILE, 2 * cols), 0) + tile * TILE
         for title in range(per_part):
-            rows = jnp.where(sub == at_ref[title], firsts[title : title + 1, :], rows)
-        features[span, :] = rows.astype(bf)
-    first = firsts[...].astype(bf)
-    table = features[...]
-    for j in (1, 2):
-        span = slice((j - 1) * cols, j * cols)
-        first_kv_ref[:, span] = dot_nt(first, w_ref[j]).astype(bf)
-        kv_ref[:, span] = dot_nt(table, w_ref[j]).astype(bf)
-    q_ref[...] = dot_nt(table, w_ref[0]).astype(bf)
-
-
-def tail_rows(count):
-    return -(-count // PAD) * PAD
-
-
-def graph_kernel(
-    ready, cols_ref, q_ref, kv_ref, first_ref, mask_ref, far_ref, out_ref, k_all, v_all
-):
-    nodes, cols = q_ref.shape
-    row_tiles = nodes // TILE
-    first_kv = first_ref[...]
-    k_all[:nodes, :] = kv_ref[:, :cols]
-    v_all[:nodes, :] = kv_ref[:, cols:]
+            row = first_kv[title : title + 1].astype(f32)
+            rows = jnp.where(sub == at_ref[title], row, rows)
+        rows = rows.astype(bf)
+        k_all[span, :] = rows[:, :cols]
+        v_all[span, :] = rows[:, cols:]
+    ready(7)
     lanes = lax.broadcasted_iota(jnp.int32, (TILE, first_kv.shape[0]), 1).astype(f32)
     for tile in range(far_ref.shape[0] // TILE):
         rows = far_ref[tile * TILE : (tile + 1) * TILE, :].astype(f32)
@@ -282,10 +285,15 @@
         k_all[span, :] = fixed[:, :cols]
         v_all[span, :] = fixed[:, cols:]
 
+    ready(1, 3, 6)
     heads = cols // GHD
     head_of = lax.broadcasted_iota(jnp.int32, (TILE, cols), 1) // GHD
     for tile in range(row_tiles):
-        q = q_ref[tile * TILE : (tile + 1) * TILE, :]
+        q = q_ref[tile * TILE : (tile + 1) * TILE, :].astype(f32)
+        sub = lax.broadcasted_iota(jnp.int32, (TILE, cols), 0) + tile * TILE
+        for title in range(per_part):
+            q = jnp.where(sub == at_ref[title], first_q[title : title + 1], q)
+        q = q.astype(bf)
         stacked = jnp.concatenate(
             [jnp.where(head_of == h, q, jnp.zeros_like(q)) for h in range(heads)], axis=0
         )
@@ -341,8 +349,9 @@
         send_kernel,
         shape((dp * fetch, 2 * cols), bf),
         (me_dp, title_nodes, send_ids[0], node_table, w_graph),
-        smem=(0, 1),
-        hbm=(2, 3, 4),
+        smem=(0,),
+        hbm=(4, 3, 2, 1),
+        scalars=(1,),
         out_specs=HBM,
         scratch=[pltpu.VMEM((dp * fetch, 2 * cols), bf), pltpu.SemaphoreType.DMA((dp,))],
         flops=2 * nodes * width * 2 * cols + 2 * dp * fetch * nodes * 2 * cols,
@@ -394,34 +403,41 @@
         )
         for turn in range(turns)
     ]
+    mask = call(
+        mask_kernel, shape((nodes, TPR * TILE), bf), (nbr_slots.T,), flops=4 * 10**9, name="mask"
+    )
+    kv, q = call(
+        own_kernel,
+        (shape((nodes, 2 * cols), bf), shape((nodes, cols), bf)),
+        (node_table, w_graph),
+        flops=2 * 10**9,
+        name="own",
+    )
+    hidden, kv, q = lax.optimization_barrier((hidden, kv, q))
     done = call(
         norm_two_kernel,
-        shape((chunk + tail_rows(turns * per_part), width), bf),
-        (hidden, gains, terms[0], *parts, *firsts),
+        shape((chunk, width), bf),
+        (hidden, gains, terms[0], *parts),
         name="norm_two",
     )
     dones = [done] + [swap(done, step) for step in range(1, mp)]
-
-    mask = call(
-        mask_kernel, shape((nodes, TPR * TILE), bf), (nbr_slots.T,), flops=10**9, name="mask"
-    )
-    kv, q, first_kv = call(
-        own_kernel,
-        (shape((nodes, 2 * cols), bf), shape((nodes, cols), bf), shape((dp * per_part, 2 * cols), bf)),
-        (who, title_nodes, node_table, w_graph, first, *dones),
-        smem=(0, 1),
-        hbm=(2, 3),
-        scratch=[pltpu.VMEM((nodes, width), bf), pltpu.VMEM((dp * per_part, width), f32)],
-        flops=2 * nodes * width * 3 * cols,
-        name="own",
-    )
+    dones, firsts, mask = lax.optimization_barrier((dones, firsts, mask))
+    pack = call(pack_kernel, shape((tail_rows(turns * per_part), width), bf), firsts, name="pack")
+    packs = [pack] + [swap(pack, step) for step in range(1, mp)]
+
     keys = nodes + dp * fetch
     graph_out = call(
         graph_kernel,
         shape((cols, nodes), bf),
-        (tile_cols, q, kv, first_kv, mask, far),
+        (who, tile_cols, title_nodes, q, kv, w_graph, mask, far, first, *packs),
         smem=(0,),
-        scratch=[pltpu.VMEM((keys, cols), bf), pltpu.VMEM((keys, cols), bf)],
+        hbm=(5, 2, 4, 7, 1, 3, 6),
+        scalars=(1, 2),
+        scratch=[
+            pltpu.VMEM((keys, cols), bf),
+            pltpu.VMEM((keys, cols), bf),
+            pltpu.VMEM((dp * per_part, width), f32),
+        ],
         flops=10**9,
         name="graph",
     )

time: 74.6 us -> 65.7 us (0.88)
  waiting for transfers between devices: 23.1 us -> 14.5 us
  starting transfers between devices: 19.2 us -> 23.9 us
  local copies, waits for them, and re-layouts: 7.22 us -> 3.48 us
  Pallas kernels: 23.7 us -> 22.4 us
    ppermute x2, waiting for transfers between devices: 9.45 us -> 0.01 us  [local(): lax.ppermute(first, ('dp', 'mp'), [(p * mp + m, (p ^ turn * mp + m) * mp...]
    ppermute x12 -> x15, starting transfers between devices: 8.1 us -> 12.8 us  [swap(): lax.ppermute(value, axis, [(i, i ^ step) for i in range(lax.axis_size(axi...]
    unnamed x36, local copies, waits for them, and re-layouts: 7.22 us -> 3.48 us
    pallas_call x9 -> x10, Pallas kernels: 23.7 us -> 22.4 us  [call(): pl.pallas_call(body, out_shape=outs, in_specs=specs, out_specs=jax.tree.m...]
    ppermute x12 -> x15, waiting for transfers between devices: 13.6 us -> 14.5 us  [swap(): lax.ppermute(value, axis, [(i, i ^ step) for i in range(lax.axis_size(axi...]
  transfers between devices with their start and end apart: 15 -> 18, of which waited for: 6 -> 6; matrix products, arithmetic and copies ran while one was open for 0% -> 0% of each run, Pallas kernels for 16% -> 17%
where the time goes in v5:
time: 65.7 us; the launch traced here: 65.3 us
  starting transfers between devices  23.9 us (36%)
  Pallas kernels  22.4 us (34%)
  waiting for transfers between devices  14.5 us (22%)
  local copies, waits for them, and re-layouts  3.48 us (5%)
  between operations  1.06 us (2%)
    pallas_call x10, Pallas kernels, call(): pl.pallas_call(body, out_shape=outs, in_specs=specs, out_specs=jax.tree.m...  22.4 us
    ppermute x15, waiting for transfers between devices, swap(): lax.ppermute(value, axis, [(i, i ^ step) for i in range(lax.axis_size(axi...  14.5 us
    ppermute x15, starting transfers between devices, swap(): lax.ppermute(value, axis, [(i, i ^ step) for i in range(lax.axis_size(axi...  12.8 us
    all_to_all x1, starting transfers between devices, local(): lax.all_to_all(sent.reshape(dp, fetch, 2 * cols), 'dp', split_axis=0, con...  7.4 us
    ppermute x2, starting transfers between devices, local(): lax.ppermute(first, ('dp', 'mp'), [(p * mp + m, (p ^ turn * mp + m) * mp...  3.74 us
    unnamed x36, local copies, waits for them, and re-layouts  3.48 us
  transfers between devices with their start and end apart: 18, of which 6 were waited for; matrix products, arithmetic and copies ran while one was open for 0% of the time, Pallas kernels for 17%

profile of v5, /device:TPU:0, one launch (start us, length us, event | category | flops | bytes accessed | tf_op | source)
XLA Modules:
  0.0 65.3 jit_solution(14353965265187950587)
XLA Ops:
  0.6 4.1 %send.1 = bf16[2048,384]{1,0:T(8,128)(2,1)} custom-call(s32[1]{0:T(128)} %bitcast.refs_0_, s32[2]{0:T(128)} %refs_2_.5, s32[8,256]{1,0:T(8,128)} %bitcast.15, bf16[512,768]{1,0:T(8,128)(2,1)} %refs_0_.2, bf16[3,192,768]{2,1,0:T(8,128)(2,1)} %bitcast.8), custom_call_target="tpu_custom_call" | custom-call | flops 1107296256 | bytes 1679372 | tf_op jit(solution)/shard_map/send/pallas_call | solution.py:52
  4.7 0.0 copy-start.2
  4.8 0.0 copy-start.7
  4.8 0.0 copy-start.1
  4.8 0.0 copy-start.10
  4.8 7.4 %all-to-all-start = ((bf16[8,256,384]{2,1,0:T(8,128)(2,1)}), bf16[8,256,384]{2,1,0:T(8,128)(2,1)}, u32[]{:S(2)}, u32[]{:S(2)}) async-start(bf16[8,256,384]{2,1,0:T(8,128)(2,1)} %bitcast.13), calls=%async_computation | async-start | bytes 3145728 | tf_op jit(solution)/shard_map/all_to_all | solution.py:360
  12.2 0.0 copy-start.11
  12.2 0.0 copy-done.2
  12.2 0.0 copy-done.7
  12.2 0.0 copy-start.4
  12.2 1.2 %copy-done.4 = bf16[3,768,192]{1,2,0:T(8,128)(2,1)S(1)} copy-done((bf16[3,768,192]{1,2,0:T(8,128)(2,1)S(1)}, bf16[3,768,192]{1,2,0:T(8,128)(2,1)}, u32[]{:S(2)}) %copy-start.4) | copy-done | bytes 884760
  13.5 2.3 %attn.1 = (f32[80,768]{1,0:T(8,128)S(1)}, bf16[80,768]{1,0:T(8,128)(2,1)S(1)}, bf16[80,768]{1,0:T(8,128)(2,1)S(1)}, bf16[80,768]{1,0:T(8,128)(2,1)S(1)}) custom-call(s32[4]{0:T(128)S(1)} %iota_xor_fusion.refs_0_, bf16[256,768]{1,0:T(8,128)(2,1)S(1)} %copy-done.2, bf16[3,192,768]{2,1,0:T(8,128)(2,1)S(1)} %bitcast.11, bf16[192,768]{1,0:T(8,128)(2,1)S(1)} %copy-done.7), custom_call_target="tpu_custom_call" | custom-call | flops 301989888 | bytes 1572880 | tf_op jit(solution)/shard_map/attn/pallas_call | solution.py:52
  15.8 0.1 collective-permute-start
  15.8 1.6 %collective-permute-start.1 = (bf16[80,768]{1,0:T(8,128)(2,1)S(1)}, bf16[80,768]{1,0:T(8,128)(2,1)S(1)}, u32[]{:S(2)}, u32[]{:S(2)}) collective-permute-start(bf16[80,768]{1,0:T(8,128)(2,1)S(1)} %get-tuple-element.30), channel_id=1, source_target_pairs={{0,2},{1,3},{2,0},{3,1},{4,6},{5,7},{6,4},{7,5},{8,10},{9,11},{10,... | collective-permute-start | bytes 368648 | tf_op jit(solution)/shard_map/ppermute | solution.py:344
  17.4 0.3 collective-permute-start.2
  17.7 0.0 collective-permute-done.refs_6_
  17.7 4.3 %collective-permute-done.1.refs_7_ = bf16[80,768]{1,0:T(8,128)(2,1)S(1)} collective-permute-done((bf16[80,768]{1,0:T(8,128)(2,1)S(1)}, bf16[80,768]{1,0:T(8,128)(2,1)S(1)}, u32[]{:S(2)}, u32[]{:S(2)}) %collective-permute-start.1) | collective-permute-done | bytes 122912 | tf_op jit(solution)/shard_map/ppermute | solution.py:344
  22.0 1.7 %collective-permute-done.2.refs_8_ = bf16[80,768]{1,0:T(8,128)(2,1)S(1)} collective-permute-done((bf16[80,768]{1,0:T(8,128)(2,1)S(1)}, bf16[80,768]{1,0:T(8,128)(2,1)S(1)}, u32[]{:S(2)}, u32[]{:S(2)}) %collective-permute-start.2) | collective-permute-done | bytes 122912 | tf_op jit(solution)/shard_map/ppermute | solution.py:344
  23.8 0.0 copy-done.1
  23.8 0.0 copy-done.10
  23.8 0.0 copy-done
  23.8 1.3 %norm_one.1 = (bf16[80,768]{1,0:T(8,128)(2,1)S(1)}, bf16[16,768]{1,0:T(8,128)(2,1)S(1)}, f32[16,768]{1,0:T(8,128)S(1)}) custom-call(s32[4]{0:T(128)S(1)} %iota_xor_fusion.refs_0_, bf16[256,768]{1,0:T(8,128)(2,1)S(1)} %copy-done.2, f32[2,768]{1,0:T(2,128)S(1)} %copy-done.10, bf16[768,768]{1,0:T(8,128)(2,1)S(1)} %copy-done, bf16[768,768]{1,0:T(8,128)(2,1)S(1)} %copy-done.1, ...), custom_call_target="tpu_custom_call" | custom-call | bytes 3373072 | tf_op jit(solution)/shard_map/norm_one/pallas_call | solution.py:52
  25.0 1.8 %collective-permute-start.5 = (bf16[80,768]{1,0:T(8,128)(2,1)S(1)}, bf16[80,768]{1,0:T(8,128)(2,1)S(1)}, u32[]{:S(2)}, u32[]{:S(2)}) collective-permute-start(bf16[80,768]{1,0:T(8,128)(2,1)S(1)} %get-tuple-element.35.refs_5_.refs_0_), channel_id=1, source_target_pairs={{0,3},{1,2},{2,1},{3,0},{4,7},{5,6},{6,5},{7,4},{8,11},{9,10},{10,... | collective-permute-start | bytes 368648 | tf_op jit(solution)/shard_map/ppermute | solution.py:344
  26.8 0.5 collective-permute-start.4
  27.3 0.0 collective-permute-start.3
  27.3 3.2 %collective-permute-done.5.refs_8_ = bf16[80,768]{1,0:T(8,128)(2,1)S(1)} collective-permute-done((bf16[80,768]{1,0:T(8,128)(2,1)S(1)}, bf16[80,768]{1,0:T(8,128)(2,1)S(1)}, u32[]{:S(2)}, u32[]{:S(2)}) %collective-permute-start.5) | collective-permute-done | bytes 122912 | tf_op jit(solution)/shard_map/ppermute | solution.py:344
  30.5 2.8 %collective-permute-done.4.refs_7_ = bf16[80,768]{1,0:T(8,128)(2,1)S(1)} collective-permute-done((bf16[80,768]{1,0:T(8,128)(2,1)S(1)}, bf16[80,768]{1,0:T(8,128)(2,1)S(1)}, u32[]{:S(2)}, u32[]{:S(2)}) %collective-permute-start.4) | collective-permute-done | bytes 122912 | tf_op jit(solution)/shard_map/ppermute | solution.py:344
  33.4 0.0 collective-permute-done.3.refs_6_
  33.4 0.9 %ffn.1 = (f32[64,768]{1,0:T(8,128)S(1)}, bf16[64,768]{1,0:T(8,128)(2,1)S(1)}, bf16[64,768]{1,0:T(8,128)(2,1)S(1)}, bf16[64,768]{1,0:T(8,128)(2,1)S(1)}, bf16[2,768]{1,0:T(2,128)(2,1)S(1)}) custom-call(bf16[768,768]{1,0:T(8,128)(2,1)S(1)} %copy-done, bf16[768,768]{1,0:T(8,128)(2,1)S(1)} %copy-done.1, f32[2,768]{1,0:T(2,128)S(1)} %copy-done.10, ...), custom_call_target="tpu_custom_call" | custom-call | flops 603979776 | bytes 2930688 | tf_op jit(solution)/shard_map/ffn/pallas_call | solution.py:52
  34.3 0.1 collective-permute-start.6
  34.4 1.5 %collective-permute-start.7 = (bf16[64,768]{1,0:T(8,128)(2,1)S(1)}, bf16[64,768]{1,0:T(8,128)(2,1)S(1)}, u32[]{:S(2)}, u32[]{:S(2)}) collective-permute-start(bf16[64,768]{1,0:T(8,128)(2,1)S(1)} %get-tuple-element.40), channel_id=1, source_target_pairs={{0,2},{1,3},{2,0},{3,1},{4,6},{5,7},{6,4},{7,5},{8,10},{9,11},{10,... | collective-permute-start | bytes 294920 | tf_op jit(solution)/shard_map/ppermute | solution.py:344
  35.9 0.3 collective-permute-start.8
  36.2 0.9 %own.1 = (bf16[512,384]{1,0:T(8,128)(2,1)S(1)}, bf16[512,192]{1,0:T(8,128)(2,1)S(1)}) custom-call(bf16[512,768]{1,0:T(8,128)(2,1)S(1)} %copy-done.13, bf16[3,192,768]{2,1,0:T(8,128)(2,1)S(1)} %bitcast.10), custom_call_target="tpu_custom_call" | custom-call | flops 2000000000 | bytes 1671168 | tf_op jit(solution)/shard_map/own/pallas_call | solution.py:52
  37.1 0.7 %copy-done.8 = bf16[512,192]{1,0:T(8,128)(2,1)} copy-done((bf16[512,192]{1,0:T(8,128)(2,1)}, bf16[512,192]{1,0:T(8,128)(2,1)S(1)}, u32[]{:S(2)}) %copy-start.8) | copy-done | bytes 196632
  37.8 2.9 %collective-permute-start.13 = (bf16[2,768]{1,0:T(2,128)(2,1)S(1)}, bf16[2,768]{1,0:T(2,128)(2,1)S(1)}, u32[]{:S(2)}, u32[]{:S(2)}) collective-permute-start(bf16[2,768]{1,0:T(2,128)(2,1)S(1)} %get-tuple-element.42.refs_8_), channel_id=1, source_target_pairs={{0,16},{1,21},{2,26},{3,31},{4,20},{5,17},{6,30},{7,27},{8,24},{9,... | collective-permute-start | bytes 9224 | tf_op jit(solution)/shard_map/ppermute | solution.py:394
  40.7 0.8 %collective-permute-start.12 = (bf16[2,768]{1,0:T(2,128)(2,1)S(1)}, bf16[2,768]{1,0:T(2,128)(2,1)S(1)}, u32[]{:S(2)}, u32[]{:S(2)}) collective-permute-start(bf16[2,768]{1,0:T(2,128)(2,1)S(1)} %get-tuple-element.42.refs_8_), channel_id=1, source_target_pairs={{1,5},{2,10},{3,15},{5,1},{6,14},{7,11},{9,13},{10,2},{11,7},{13,9... | collective-permute-start | bytes 9224 | tf_op jit(solution)/shard_map/ppermute | solution.py:394
  41.6 0.0 collective-permute-done.6.refs_3_
  41.6 0.0 collective-permute-done.7.refs_4_
  41.6 0.0 collective-permute-done.8.refs_5_
  41.6 0.2 norm_two.1.refs_1_
  41.8 4.3 %collective-permute-start.11 = (bf16[64,768]{1,0:T(8,128)(2,1)S(1)}, bf16[64,768]{1,0:T(8,128)(2,1)S(1)}, u32[]{:S(2)}, u32[]{:S(2)}) collective-permute-start(bf16[64,768]{1,0:T(8,128)(2,1)S(1)} %norm_two.1.refs_1_), channel_id=1, source_target_pairs={{0,3},{1,2},{2,1},{3,0},{4,7},{5,6},{6,5},{7,4},{8,11},{9,10},{10,... | collective-permute-start | bytes 294920 | tf_op jit(solution)/shard_map/ppermute | solution.py:344
  46.1 0.0 collective-permute-start.10
  46.1 0.2 collective-permute-start.9
  46.3 4.2 %mask.1.refs_6_ = bf16[512,768]{1,0:T(8,128)(2,1)S(1)} custom-call(s32[16,512]{1,0:T(8,128)S(1)} %bitcast.12), custom_call_target="tpu_custom_call" | custom-call | flops 4000000000 | bytes 32768 | tf_op jit(solution)/shard_map/mask/pallas_call | solution.py:52
  50.6 0.9 %copy-done.5 = bf16[512,768]{1,0:T(8,128)(2,1)} copy-done((bf16[512,768]{1,0:T(8,128)(2,1)}, bf16[512,768]{1,0:T(8,128)(2,1)S(1)}, u32[]{:S(2)}) %copy-start.5) | copy-done | bytes 786456
  51.4 0.0 collective-permute-done.13.refs_1_
  51.4 0.0 collective-permute-done.12.refs_0_
  51.4 0.0 collective-permute-done.11.refs_4_
  51.4 0.1 collective-permute-done.10.refs_3_
  51.6 0.0 collective-permute-done.9.refs_2_
  51.6 0.0 copy-start.9
  51.6 1.9 %collective-permute-start.16 = (bf16[16,768]{1,0:T(8,128)(2,1)S(1)}, bf16[16,768]{1,0:T(8,128)(2,1)S(1)}, u32[]{:S(2)}, u32[]{:S(2)}) collective-permute-start(bf16[16,768]{1,0:T(8,128)(2,1)S(1)} %pack.1.refs_9_), channel_id=1, source_target_pairs={{0,3},{1,2},{2,1},{3,0},{4,7},{5,6},{6,5},{7,4},{8,11},{9,10},{10,... | collective-permute-start | bytes 73736 | tf_op jit(solution)/shard_map/ppermute | solution.py:344
  53.5 0.0 collective-permute-start.15
  53.5 0.2 collective-permute-start.14
  53.7 1.3 %place.1 = bf16[256,768]{1,0:T(8,128)(2,1)} custom-call(s32[4]{0:T(128)S(1)} %iota_xor_fusion.refs_0_, bf16[64,768]{1,0:T(8,128)(2,1)S(1)} %norm_two.1.refs_1_, bf16[64,768]{1,0:T(8,128)(2,1)S(1)} %collective-permute-done.9.refs_2_, bf16[64,768]{1,0:T(8,128)(2,1)S(1)} %collective-permute-done.10.refs_3_, bf16[64,768]{1,0:T(8,128)(2,1)S(1)} %collective-permute-done.11.refs_4_), custom_call_target="tpu_custom_call" | custom-call | bytes 393232 | tf_op jit(solution)/shard_map/place/pallas_call | solution.py:52
  55.0 0.0 collective-permute-done.16.refs_12_
  55.0 2.3 %collective-permute-done.15.refs_11_ = bf16[16,768]{1,0:T(8,128)(2,1)S(1)} collective-permute-done((bf16[16,768]{1,0:T(8,128)(2,1)S(1)}, bf16[16,768]{1,0:T(8,128)(2,1)S(1)}, u32[]{:S(2)}, u32[]{:S(2)}) %collective-permute-start.15) | collective-permute-done | bytes 24608 | tf_op jit(solution)/shard_map/ppermute | solution.py:344
  57.3 0.0 collective-permute-done.14.refs_10_
  57.4 0.0 all-to-all-done
  57.4 0.0 copy-done.9
  57.4 0.0 copy-done.15
  57.4 0.6 copy-done.16
  57.9 0.0 copy-done.17
  58.0 7.2 %graph.1 = bf16[192,512]{1,0:T(8,128)(2,1)} custom-call(s32[4]{0:T(128)} %copy-done.11, s32[4,6]{1,0:T(4,128)} %refs_1_.9, s32[2]{0:T(128)} %refs_2_.5, bf16[512,192]{1,0:T(8,128)(2,1)} %copy-done.8, bf16[512,384]{1,0:T(8,128)(2,1)} %copy-done.6, bf16[3,192,768]{2,1,0:T(8,128)(2,1)} %bitcast.9, bf16[512,768]{1,0:T(8,128)(2,1)} %copy-done.5, ...), custom_call_target="tpu_custom_call" | custom-call | flops 1000000000 | bytes 3935352 | tf_op jit(solution)/shard_map/graph/pallas_call | solution.py:52
  (19 shorter events, 0.1 us)
Async XLA Ops:
  4.7 7.5 %copy-start.2 = (bf16[256,768]{1,0:T(8,128)(2,1)S(1)}, bf16[256,768]{1,0:T(8,128)(2,1)}, u32[]{:S(2)}) copy-start(bf16[256,768]{1,0:T(8,128)(2,1)} %refs_1_.6) | copy-start | bytes 1179652
  4.8 7.5 %copy-start.7 = (bf16[192,768]{1,0:T(8,128)(2,1)S(1)}, bf16[192,768]{1,0:T(8,128)(2,1)}, u32[]{:S(2)}) copy-start(bf16[192,768]{1,0:T(8,128)(2,1)} %refs_3_.4) | copy-start | bytes 884740
  4.8 19.0 %copy-start.1 = (bf16[768,768]{1,0:T(8,128)(2,1)S(1)}, bf16[768,768]{1,0:T(8,128)(2,1)}, u32[]{:S(2)}) copy-start(bf16[768,768]{1,0:T(8,128)(2,1)} %refs_1_.7) | copy-start | bytes 3538948
  4.8 19.0 %copy-start.10 = (f32[2,768]{1,0:T(2,128)S(1)}, f32[2,768]{1,0:T(2,128)}, u32[]{:S(2)}) copy-start(f32[2,768]{1,0:T(2,128)} %refs_1_.8) | copy-start | bytes 18436
  4.8 52.6 %all-to-all-start = ((bf16[8,256,384]{2,1,0:T(8,128)(2,1)}), bf16[8,256,384]{2,1,0:T(8,128)(2,1)}, u32[]{:S(2)}, u32[]{:S(2)}) async-start(bf16[8,256,384]{2,1,0:T(8,128)(2,1)} %bitcast.13), calls=%async_computation | async-start | bytes 3145728 | tf_op jit(solution)/shard_map/all_to_all | solution.py:360
  12.2 11.6 %copy-start = (bf16[768,768]{1,0:T(8,128)(2,1)S(1)}, bf16[768,768]{1,0:T(8,128)(2,1)}, u32[]{:S(2)}) copy-start(bf16[768,768]{1,0:T(8,128)(2,1)} %refs_0_.3) | copy-start | bytes 3538948
  12.2 41.5 %copy-start.11 = (s32[4]{0:T(128)}, s32[4]{0:T(128)S(1)}, u32[]{:S(2)}) copy-start(s32[4]{0:T(128)S(1)} %iota_xor_fusion.refs_0_) | copy-start | bytes 52
  12.2 1.3 %copy-start.4 = (bf16[3,768,192]{1,2,0:T(8,128)(2,1)S(1)}, bf16[3,768,192]{1,2,0:T(8,128)(2,1)}, u32[]{:S(2)}) copy-start(bf16[3,768,192]{1,2,0:T(8,128)(2,1)} %param.13) | copy-start | bytes 2654212
  15.8 1.9 %collective-permute-start = (bf16[80,768]{1,0:T(8,128)(2,1)S(1)}, bf16[80,768]{1,0:T(8,128)(2,1)S(1)}, u32[]{:S(2)}, u32[]{:S(2)}) collective-permute-start(bf16[80,768]{1,0:T(8,128)(2,1)S(1)} %get-tuple-element.29), channel_id=1, source_target_pairs={{0,1},{1,0},{2,3},{3,2},{4,5},{5,4},{6,7},{7,6},{8,9},{9,8},{10,11... | collective-permute-start | bytes 368648 | tf_op jit(solution)/shard_map/ppermute | solution.py:344
  15.8 6.2 %collective-permute-start.1 = (bf16[80,768]{1,0:T(8,128)(2,1)S(1)}, bf16[80,768]{1,0:T(8,128)(2,1)S(1)}, u32[]{:S(2)}, u32[]{:S(2)}) collective-permute-start(bf16[80,768]{1,0:T(8,128)(2,1)S(1)} %get-tuple-element.30), channel_id=1, source_target_pairs={{0,2},{1,3},{2,0},{3,1},{4,6},{5,7},{6,4},{7,5},{8,10},{9,11},{10,... | collective-permute-start | bytes 368648 | tf_op jit(solution)/shard_map/ppermute | solution.py:344
  17.4 6.3 %collective-permute-start.2 = (bf16[80,768]{1,0:T(8,128)(2,1)S(1)}, bf16[80,768]{1,0:T(8,128)(2,1)S(1)}, u32[]{:S(2)}, u32[]{:S(2)}) collective-permute-start(bf16[80,768]{1,0:T(8,128)(2,1)S(1)} %get-tuple-element.31), channel_id=1, source_target_pairs={{0,3},{1,2},{2,1},{3,0},{4,7},{5,6},{6,5},{7,4},{8,11},{9,10},{10,... | collective-permute-start | bytes 368648 | tf_op jit(solution)/shard_map/ppermute | solution.py:344
  25.0 11.2 %copy-start.3 = (bf16[3,768,192]{1,2,0:T(8,128)(2,1)S(1)}, bf16[3,768,192]{1,2,0:T(8,128)(2,1)}, u32[]{:S(2)}) copy-start(bf16[3,768,192]{1,2,0:T(8,128)(2,1)} %param.19) | copy-start | bytes 2654212
  25.0 11.2 %copy-start.13 = (bf16[512,768]{1,0:T(8,128)(2,1)S(1)}, bf16[512,768]{1,0:T(8,128)(2,1)}, u32[]{:S(2)}) copy-start(bf16[512,768]{1,0:T(8,128)(2,1)} %refs_0_.2) | copy-start | bytes 2359300
  25.0 5.5 %collective-permute-start.5 = (bf16[80,768]{1,0:T(8,128)(2,1)S(1)}, bf16[80,768]{1,0:T(8,128)(2,1)S(1)}, u32[]{:S(2)}, u32[]{:S(2)}) collective-permute-start(bf16[80,768]{1,0:T(8,128)(2,1)S(1)} %get-tuple-element.35.refs_5_.refs_0_), channel_id=1, source_target_pairs={{0,3},{1,2},{2,1},{3,0},{4,7},{5,6},{6,5},{7,4},{8,11},{9,10},{10,... | collective-permute-start | bytes 368648 | tf_op jit(solution)/shard_map/ppermute | solution.py:344
  26.8 6.5 %collective-permute-start.4 = (bf16[80,768]{1,0:T(8,128)(2,1)S(1)}, bf16[80,768]{1,0:T(8,128)(2,1)S(1)}, u32[]{:S(2)}, u32[]{:S(2)}) collective-permute-start(bf16[80,768]{1,0:T(8,128)(2,1)S(1)} %get-tuple-element.35.refs_5_.refs_0_), channel_id=1, source_target_pairs={{0,2},{1,3},{2,0},{3,1},{4,6},{5,7},{6,4},{7,5},{8,10},{9,11},{10,... | collective-permute-start | bytes 368648 | tf_op jit(solution)/shard_map/ppermute | solution.py:344
  27.3 6.0 %collective-permute-start.3 = (bf16[80,768]{1,0:T(8,128)(2,1)S(1)}, bf16[80,768]{1,0:T(8,128)(2,1)S(1)}, u32[]{:S(2)}, u32[]{:S(2)}) collective-permute-start(bf16[80,768]{1,0:T(8,128)(2,1)S(1)} %get-tuple-element.35.refs_5_.refs_0_), channel_id=1, source_target_pairs={{0,1},{1,0},{2,3},{3,2},{4,5},{5,4},{6,7},{7,6},{8,9},{9,8},{10,11... | collective-permute-start | bytes 368648 | tf_op jit(solution)/shard_map/ppermute | solution.py:344
  34.3 6.4 %copy-start.12 = (bf16[2,768]{1,0:T(2,128)(2,1)}, bf16[2,768]{1,0:T(2,128)(2,1)S(1)}, u32[]{:S(2)}) copy-start(bf16[2,768]{1,0:T(2,128)(2,1)S(1)} %get-tuple-element.42.refs_8_) | copy-start | bytes 9220
  34.3 7.3 %collective-permute-start.6 = (bf16[64,768]{1,0:T(8,128)(2,1)S(1)}, bf16[64,768]{1,0:T(8,128)(2,1)S(1)}, u32[]{:S(2)}, u32[]{:S(2)}) collective-permute-start(bf16[64,768]{1,0:T(8,128)(2,1)S(1)} %get-tuple-element.39), channel_id=1, source_target_pairs={{0,1},{1,0},{2,3},{3,2},{4,5},{5,4},{6,7},{7,6},{8,9},{9,8},{10,11... | collective-permute-start | bytes 294920 | tf_op jit(solution)/shard_map/ppermute | solution.py:344
  34.4 7.2 %collective-permute-start.7 = (bf16[64,768]{1,0:T(8,128)(2,1)S(1)}, bf16[64,768]{1,0:T(8,128)(2,1)S(1)}, u32[]{:S(2)}, u32[]{:S(2)}) collective-permute-start(bf16[64,768]{1,0:T(8,128)(2,1)S(1)} %get-tuple-element.40), channel_id=1, source_target_pairs={{0,2},{1,3},{2,0},{3,1},{4,6},{5,7},{6,4},{7,5},{8,10},{9,11},{10,... | collective-permute-start | bytes 294920 | tf_op jit(solution)/shard_map/ppermute | solution.py:344
  35.9 10.4 %copy-start.14 = (s32[512,16]{0,1:T(8,128)S(1)}, s32[512,16]{0,1:T(8,128)}, u32[]{:S(2)}) copy-start(s32[512,16]{0,1:T(8,128)} %param.23) | copy-start | bytes 98308
  35.9 5.7 %collective-permute-start.8 = (bf16[64,768]{1,0:T(8,128)(2,1)S(1)}, bf16[64,768]{1,0:T(8,128)(2,1)S(1)}, u32[]{:S(2)}, u32[]{:S(2)}) collective-permute-start(bf16[64,768]{1,0:T(8,128)(2,1)S(1)} %get-tuple-element.41), channel_id=1, source_target_pairs={{0,3},{1,2},{2,1},{3,0},{4,7},{5,6},{6,5},{7,4},{8,11},{9,10},{10,... | collective-permute-start | bytes 294920 | tf_op jit(solution)/shard_map/ppermute | solution.py:344
  37.1 0.7 %copy-start.8 = (bf16[512,192]{1,0:T(8,128)(2,1)}, bf16[512,192]{1,0:T(8,128)(2,1)S(1)}, u32[]{:S(2)}) copy-start(bf16[512,192]{1,0:T(8,128)(2,1)S(1)} %get-tuple-element.47.refs_3_) | copy-start | bytes 589828
  37.8 12.7 %copy-start.6 = (bf16[512,384]{1,0:T(8,128)(2,1)}, bf16[512,384]{1,0:T(8,128)(2,1)S(1)}, u32[]{:S(2)}) copy-start(bf16[512,384]{1,0:T(8,128)(2,1)S(1)} %get-tuple-element.48.refs_4_) | copy-start | bytes 1179652
  37.8 13.6 %collective-permute-start.13 = (bf16[2,768]{1,0:T(2,128)(2,1)S(1)}, bf16[2,768]{1,0:T(2,128)(2,1)S(1)}, u32[]{:S(2)}, u32[]{:S(2)}) collective-permute-start(bf16[2,768]{1,0:T(2,128)(2,1)S(1)} %get-tuple-element.42.refs_8_), channel_id=1, source_target_pairs={{0,16},{1,21},{2,26},{3,31},{4,20},{5,17},{6,30},{7,27},{8,24},{9,... | collective-permute-start | bytes 9224 | tf_op jit(solution)/shard_map/ppermute | solution.py:394
  40.7 10.7 %collective-permute-start.12 = (bf16[2,768]{1,0:T(2,128)(2,1)S(1)}, bf16[2,768]{1,0:T(2,128)(2,1)S(1)}, u32[]{:S(2)}, u32[]{:S(2)}) collective-permute-start(bf16[2,768]{1,0:T(2,128)(2,1)S(1)} %get-tuple-element.42.refs_8_), channel_id=1, source_target_pairs={{1,5},{2,10},{3,15},{5,1},{6,14},{7,11},{9,13},{10,2},{11,7},{13,9... | collective-permute-start | bytes 9224 | tf_op jit(solution)/shard_map/ppermute | solution.py:394
  41.8 9.6 %collective-permute-start.11 = (bf16[64,768]{1,0:T(8,128)(2,1)S(1)}, bf16[64,768]{1,0:T(8,128)(2,1)S(1)}, u32[]{:S(2)}, u32[]{:S(2)}) collective-permute-start(bf16[64,768]{1,0:T(8,128)(2,1)S(1)} %norm_two.1.refs_1_), channel_id=1, source_target_pairs={{0,3},{1,2},{2,1},{3,0},{4,7},{5,6},{6,5},{7,4},{8,11},{9,10},{10,... | collective-permute-start | bytes 294920 | tf_op jit(solution)/shard_map/ppermute | solution.py:344
  46.1 5.5 %collective-permute-start.10 = (bf16[64,768]{1,0:T(8,128)(2,1)S(1)}, bf16[64,768]{1,0:T(8,128)(2,1)S(1)}, u32[]{:S(2)}, u32[]{:S(2)}) collective-permute-start(bf16[64,768]{1,0:T(8,128)(2,1)S(1)} %norm_two.1.refs_1_), channel_id=1, source_target_pairs={{0,2},{1,3},{2,0},{3,1},{4,6},{5,7},{6,4},{7,5},{8,10},{9,11},{10,... | collective-permute-start | bytes 294920 | tf_op jit(solution)/shard_map/ppermute | solution.py:344
  46.1 5.5 %collective-permute-start.9 = (bf16[64,768]{1,0:T(8,128)(2,1)S(1)}, bf16[64,768]{1,0:T(8,128)(2,1)S(1)}, u32[]{:S(2)}, u32[]{:S(2)}) collective-permute-start(bf16[64,768]{1,0:T(8,128)(2,1)S(1)} %norm_two.1.refs_1_), channel_id=1, source_target_pairs={{0,1},{1,0},{2,3},{3,2},{4,5},{5,4},{6,7},{7,6},{8,9},{9,8},{10,11... | collective-permute-start | bytes 294920 | tf_op jit(solution)/shard_map/ppermute | solution.py:344
  50.6 0.9 %copy-start.5 = (bf16[512,768]{1,0:T(8,128)(2,1)}, bf16[512,768]{1,0:T(8,128)(2,1)S(1)}, u32[]{:S(2)}) copy-start(bf16[512,768]{1,0:T(8,128)(2,1)S(1)} %mask.1.refs_6_) | copy-start | bytes 2359300
  51.6 5.8 %copy-start.9 = (bf16[16,768]{1,0:T(8,128)(2,1)}, bf16[16,768]{1,0:T(8,128)(2,1)S(1)}, u32[]{:S(2)}) copy-start(bf16[16,768]{1,0:T(8,128)(2,1)S(1)} %pack.1.refs_9_) | copy-start | bytes 73732
  51.6 3.4 %collective-permute-start.16 = (bf16[16,768]{1,0:T(8,128)(2,1)S(1)}, bf16[16,768]{1,0:T(8,128)(2,1)S(1)}, u32[]{:S(2)}, u32[]{:S(2)}) collective-permute-start(bf16[16,768]{1,0:T(8,128)(2,1)S(1)} %pack.1.refs_9_), channel_id=1, source_target_pairs={{0,3},{1,2},{2,1},{3,0},{4,7},{5,6},{6,5},{7,4},{8,11},{9,10},{10,... | collective-permute-start | bytes 73736 | tf_op jit(solution)/shard_map/ppermute | solution.py:344
  53.5 3.8 %collective-permute-start.15 = (bf16[16,768]{1,0:T(8,128)(2,1)S(1)}, bf16[16,768]{1,0:T(8,128)(2,1)S(1)}, u32[]{:S(2)}, u32[]{:S(2)}) collective-permute-start(bf16[16,768]{1,0:T(8,128)(2,1)S(1)} %pack.1.refs_9_), channel_id=1, source_target_pairs={{0,2},{1,3},{2,0},{3,1},{4,6},{5,7},{6,4},{7,5},{8,10},{9,11},{10,... | collective-permute-start | bytes 73736 | tf_op jit(solution)/shard_map/ppermute | solution.py:344
  53.5 3.8 %collective-permute-start.14 = (bf16[16,768]{1,0:T(8,128)(2,1)S(1)}, bf16[16,768]{1,0:T(8,128)(2,1)S(1)}, u32[]{:S(2)}, u32[]{:S(2)}) collective-permute-start(bf16[16,768]{1,0:T(8,128)(2,1)S(1)} %pack.1.refs_9_), channel_id=1, source_target_pairs={{0,1},{1,0},{2,3},{3,2},{4,5},{5,4},{6,7},{7,6},{8,9},{9,8},{10,11... | collective-permute-start | bytes 73736 | tf_op jit(solution)/shard_map/ppermute | solution.py:344
  55.0 2.3 %copy-start.15 = (bf16[16,768]{1,0:T(8,128)(2,1)}, bf16[16,768]{1,0:T(8,128)(2,1)S(1)}, u32[]{:S(2)}) copy-start(bf16[16,768]{1,0:T(8,128)(2,1)S(1)} %collective-permute-done.16.refs_12_) | copy-start | bytes 73732
  57.3 0.6 copy-start.16
  57.3 0.6 copy-start.17

commit v6 on v5

--- a/solution.py
+++ b/solution.py
@@ -1,3 +1,4 @@
+import functools
 import jax
 import jax.numpy as jnp
 from jax import lax
@@ -125,6 +126,7 @@
 
 def attn_kernel(ready, who_ref, titles_ref, w_in_ref, w_out_ref, *refs):
     outs, total = refs[:-1], refs[-1]
+    ready(1, 2)
     titles = titles_ref[...]
     q = dot_nt(titles, w_in_ref[0]).astype(bf)
     k = dot_nt(titles, w_in_ref[1]).astype(bf)
@@ -132,6 +134,7 @@
     cols = q.shape[1]
     heads = cols // HD
     lanes = lax.broadcasted_iota(jnp.int32, (SEQ, cols), 1) // HD
+    ready(3)
     for title in range(titles.shape[0] // SEQ):
         rows = slice(title * SEQ, (title + 1) * SEQ)
         qt, kt, vt = q[rows], k[rows], v[rows]
@@ -224,11 +227,22 @@
     out[...] = rows.astype(bf)
 
 
-def place_kernel(ready, who_ref, *refs):
-    *chunks, out = refs
-    chunk = out.shape[0] // len(chunks)
-    for step, ref in enumerate(chunks):
-        out[pl.ds(pl.multiple_of(who_ref[step] * chunk, chunk), chunk), :] = ref[...]
+def join_kernel(ready, *refs):
+    *parts, out = refs
+    start = 0
+    for part in parts:
+        out[start : start + part.shape[0], :] = part[...]
+        start += part.shape[0]
+
+
+def place_kernel(whose, ready, who_ref, *refs):
+    *blocks, out = refs
+    chunk = out.shape[0] // len(whose)
+    pieces = [
+        block[start : start + chunk, :] for block in blocks for start in range(0, block.shape[0], chunk)
+    ]
+    for step, piece in zip(whose, pieces):
+        out[pl.ds(pl.multiple_of(who_ref[step] * chunk, chunk), chunk), :] = piece
 
 
 def own_kernel(ready, table_ref, w_ref, kv_ref, q_ref):
@@ -255,7 +269,7 @@
         rows = ref[...].astype(f32)
         for turn in range(firsts.shape[0] // per_part // members):
             for title in range(per_part):
-                place = (turn * members + who_ref[step]) * per_part + title
+                place = (turn * members + who_ref[step] % members) * per_part + title
                 at = turn * per_part + title
                 firsts[pl.ds(place, 1), :] = rows[at : at + 1]
     firsts[0:per_part, :] = first_ref[...].astype(f32)
@@ -367,11 +381,23 @@
         tuple(shape((chunk + PAD, width), bf if step else f32) for step in range(mp)),
         (who, titles, w_attn_in, w_attn_out),
         smem=(0,),
+        hbm=(1, 2, 3),
         scratch=[pltpu.VMEM((tok_rows, width), f32)],
         flops=2 * tok_rows * width * 4 * w_attn_in.shape[1],
         name="attn",
     )
     parts = [swap(terms[step], step) for step in range(1, mp)]
+    mask = call(
+        mask_kernel, shape((nodes, TPR * TILE), bf), (nbr_slots.T,), flops=4 * 10**9, name="mask"
+    )
+    kv, q = call(
+        own_kernel,
+        (shape((nodes, 2 * cols), bf), shape((nodes, cols), bf)),
+        (node_table, w_graph),
+        flops=2 * 10**9,
+        name="own",
+    )
+    parts, mask, kv, q = lax.optimization_barrier((parts, mask, kv, q))
     hidden, first_hidden, first_terms = call(
         norm_one_kernel,
         (shape((chunk + PAD, width), bf), shape((PAD, width), bf), shape((PAD, width), f32)),
@@ -389,41 +415,46 @@
         name="ffn",
     )
     parts = [swap(terms[step], step) for step in range(1, mp)]
-    turns = dp // mp
+    done = call(
+        norm_two_kernel,
+        shape((chunk, width), bf),
+        (hidden, gains, terms[0], *parts),
+        name="norm_two",
+    )
+    share = 2
+    turns = dp // share
     firsts = [
         lax.ppermute(
             first,
             ("dp", "mp"),
             [
-                (p * mp + m, (p ^ (turn * mp + m)) * mp + m)
+                (p * mp + m, (p ^ (turn * share + m % share)) * mp + m)
                 for p in range(dp)
                 for m in range(mp)
-                if turn or m
+                if turn or m % share
             ],
         )
         for turn in range(turns)
     ]
-    mask = call(
-        mask_kernel, shape((nodes, TPR * TILE), bf), (nbr_slots.T,), flops=4 * 10**9, name="mask"
-    )
-    kv, q = call(
-        own_kernel,
-        (shape((nodes, 2 * cols), bf), shape((nodes, cols), bf)),
-        (node_table, w_graph),
-        flops=2 * 10**9,
-        name="own",
-    )
-    hidden, kv, q = lax.optimization_barrier((hidden, kv, q))
-    done = call(
-        norm_two_kernel,
-        shape((chunk, width), bf),
-        (hidden, gains, terms[0], *parts),
-        name="norm_two",
-    )
-    dones = [done] + [swap(done, step) for step in range(1, mp)]
-    dones, firsts, mask = lax.optimization_barrier((dones, firsts, mask))
+    whose, blocks, step = [0], [done], mp // 2
+    while step:
+        rows = blocks[0]
+        if len(blocks) > 1:
+            dims = (sum(block.shape[0] for block in blocks), width)
+            rows = call(join_kernel, shape(dims, bf), blocks, name="join")
+        blocks = blocks + [swap(rows, step)]
+        whose = whose + [other ^ step for other in whose]
+        step //= 2
+    encoded = call(
+        functools.partial(place_kernel, whose),
+        shape((tok_rows, width), bf),
+        (who, *blocks),
+        smem=(0,),
+        name="place",
+    )
+    encoded, firsts = lax.optimization_barrier((encoded, firsts))
     pack = call(pack_kernel, shape((tail_rows(turns * per_part), width), bf), firsts, name="pack")
-    packs = [pack] + [swap(pack, step) for step in range(1, mp)]
+    packs = [pack, swap(pack, 1)]
 
     keys = nodes + dp * fetch
     graph_out = call(
@@ -441,9 +472,6 @@
         flops=10**9,
         name="graph",
     )
-    encoded = call(
-        place_kernel, shape((tok_rows, width), bf), (who, *dones), smem=(0,), name="place"
-    )
     return (encoded, graph_out.T)
 
 

time: 65.7 us -> 70.6 us (1.075)
  waiting for transfers between devices: 14.5 us -> 17.3 us
  Pallas kernels: 22.4 us -> 24.9 us
  starting transfers between devices: 23.9 us -> 22.8 us
    ppermute x15 -> x12, starting transfers between devices: 12.8 us -> 9.91 us  [swap(): lax.ppermute(value, axis, [(i, i ^ step) for i in range(lax.axis_size(axi...]
    pallas_call x10 -> x11, Pallas kernels: 22.4 us -> 24.9 us  [call(): pl.pallas_call(body, out_shape=outs, in_specs=specs, out_specs=jax.tree.m...]
    ppermute x2 -> x4, starting transfers between devices: 3.74 us -> 5.65 us  [local(): lax.ppermute(first, ('dp', 'mp'), [(p * mp + m, (p ^ turn * share + m % s...]
    ppermute x2 -> x4, waiting for transfers between devices: 0.01 us -> 1.69 us  [local(): lax.ppermute(first, ('dp', 'mp'), [(p * mp + m, (p ^ turn * share + m % s...]
    ppermute x15 -> x12, waiting for transfers between devices: 14.5 us -> 15.6 us  [swap(): lax.ppermute(value, axis, [(i, i ^ step) for i in range(lax.axis_size(axi...]
    unnamed x36 -> x32, local copies, waits for them, and re-layouts: 3.48 us -> 3.56 us
  transfers between devices with their start and end apart: 18 -> 17, of which waited for: 6 -> 7; matrix products, arithmetic and copies ran while one was open for 0% -> 1% of each run, Pallas kernels for 17% -> 19%
where the time goes in v6:
time: 70.6 us; the launch traced here: 70.2 us
  Pallas kernels  24.9 us (35%)
  starting transfers between devices  22.8 us (32%)
  waiting for transfers between devices  17.3 us (25%)
  local copies, waits for them, and re-layouts  3.56 us (5%)
  between operations  1.05 us (1%)
    pallas_call x11, Pallas kernels, call(): pl.pallas_call(body, out_shape=outs, in_specs=specs, out_specs=jax.tree.m...  24.9 us
    ppermute x12, waiting for transfers between devices, swap(): lax.ppermute(value, axis, [(i, i ^ step) for i in range(lax.axis_size(axi...  15.6 us
    ppermute x12, starting transfers between devices, swap(): lax.ppermute(value, axis, [(i, i ^ step) for i in range(lax.axis_size(axi...  9.91 us
    all_to_all x1, starting transfers between devices, local(): lax.all_to_all(sent.reshape(dp, fetch, 2 * cols), 'dp', split_axis=0, con...  7.27 us
    ppermute x4, starting transfers between devices, local(): lax.ppermute(first, ('dp', 'mp'), [(p * mp + m, (p ^ turn * share + m % s...  5.65 us
    unnamed x32, local copies, waits for them, and re-layouts  3.56 us
    ppermute x4, waiting for transfers between devices, local(): lax.ppermute(first, ('dp', 'mp'), [(p * mp + m, (p ^ turn * share + m % s...  1.69 us
  transfers between devices with their start and end apart: 17, of which 7 were waited for; matrix products, arithmetic and copies ran while one was open for 1% of the time, Pallas kernels for 19%

profile of v6, /device:TPU:0, one launch (start us, length us, event | category | flops | bytes accessed | tf_op | source)
XLA Modules:
  0.0 70.2 jit_solution(7092631699553351984)
XLA Ops:
  0.6 4.1 %send.1 = bf16[2048,384]{1,0:T(8,128)(2,1)} custom-call(s32[1]{0:T(128)} %bitcast.refs_0_, s32[2]{0:T(128)} %refs_2_.5, s32[8,256]{1,0:T(8,128)} %bitcast.16, bf16[512,768]{1,0:T(8,128)(2,1)} %refs_0_.2, bf16[3,192,768]{2,1,0:T(8,128)(2,1)} %bitcast.8), custom_call_target="tpu_custom_call" | custom-call | flops 1107296256 | bytes 1679372 | tf_op jit(solution)/shard_map/send/pallas_call | solution.py:53
  4.7 7.3 %all-to-all-start = ((bf16[8,256,384]{2,1,0:T(8,128)(2,1)}), bf16[8,256,384]{2,1,0:T(8,128)(2,1)S(1)}, u32[]{:S(2)}, u32[]{:S(2)}) async-start(bf16[8,256,384]{2,1,0:T(8,128)(2,1)} %bitcast.13), calls=%async_computation | async-start | bytes 3145728 | tf_op jit(solution)/shard_map/all_to_all | solution.py:374
  12.0 0.6 iota_xor_fusion.refs_0_
  12.6 4.7 %attn.1 = (f32[80,768]{1,0:T(8,128)}, bf16[80,768]{1,0:T(8,128)(2,1)}, bf16[80,768]{1,0:T(8,128)(2,1)}, bf16[80,768]{1,0:T(8,128)(2,1)}) custom-call(s32[4]{0:T(128)} %iota_xor_fusion.refs_0_, bf16[256,768]{1,0:T(8,128)(2,1)} %refs_1_.6, bf16[3,192,768]{2,1,0:T(8,128)(2,1)} %bitcast.14, bf16[192,768]{1,0:T(8,128)(2,1)} %refs_3_.4), custom_call_target="tpu_custom_call" | custom-call | flops 301989888 | bytes 1572880 | tf_op jit(solution)/shard_map/attn/pallas_call | solution.py:53
  17.3 0.1 collective-permute-start
  17.4 1.6 %collective-permute-start.1 = (bf16[80,768]{1,0:T(8,128)(2,1)}, bf16[80,768]{1,0:T(8,128)(2,1)S(1)}, u32[]{:S(2)}, u32[]{:S(2)}) collective-permute-start(bf16[80,768]{1,0:T(8,128)(2,1)} %get-tuple-element.31), channel_id=1, source_target_pairs={{0,2},{1,3},{2,0},{3,1},{4,6},{5,7},{6,4},{7,5},{8,10},{9,11},{10,... | collective-permute-start | bytes 368648 | tf_op jit(solution)/shard_map/ppermute | solution.py:358
  19.0 0.3 collective-permute-start.2
  19.3 0.0 copy-done.13
  19.3 4.2 %mask.1.refs_6_ = bf16[512,768]{1,0:T(8,128)(2,1)S(1)} custom-call(s32[16,512]{1,0:T(8,128)S(1)} %bitcast.11), custom_call_target="tpu_custom_call" | custom-call | flops 4000000000 | bytes 32768 | tf_op jit(solution)/shard_map/mask/pallas_call | solution.py:53
  23.5 0.0 copy-start.4
  23.6 0.9 %copy-done.4 = bf16[512,768]{1,0:T(8,128)(2,1)} copy-done((bf16[512,768]{1,0:T(8,128)(2,1)}, bf16[512,768]{1,0:T(8,128)(2,1)S(1)}, u32[]{:S(2)}) %copy-start.4) | copy-done | bytes 786456
  24.4 0.0 copy-done.3
  24.4 0.0 copy-done.12
  24.5 0.0 copy-start.2
  24.5 0.0 copy-start.7
  24.5 0.0 copy-start.9
  24.5 0.0 copy-start.10
  24.5 0.9 %own.1 = (bf16[512,384]{1,0:T(8,128)(2,1)S(1)}, bf16[512,192]{1,0:T(8,128)(2,1)S(1)}) custom-call(bf16[512,768]{1,0:T(8,128)(2,1)S(1)} %copy-done.12, bf16[3,192,768]{2,1,0:T(8,128)(2,1)S(1)} %bitcast.10), custom_call_target="tpu_custom_call" | custom-call | flops 2000000000 | bytes 1671168 | tf_op jit(solution)/shard_map/own/pallas_call | solution.py:53
  25.4 0.0 copy-start.5
  25.4 0.8 %copy-done.5 = bf16[512,384]{1,0:T(8,128)(2,1)} copy-done((bf16[512,384]{1,0:T(8,128)(2,1)}, bf16[512,384]{1,0:T(8,128)(2,1)S(1)}, u32[]{:S(2)}) %copy-start.5) | copy-done | bytes 393240
  26.1 0.7 copy-done.6
  26.8 0.0 collective-permute-done.refs_6_
  26.8 0.0 collective-permute-done.1.refs_7_
  26.8 0.0 collective-permute-done.2.refs_8_
  26.8 0.0 copy-done
  26.9 0.0 copy-done.1
  26.9 0.0 copy-done.2
  26.9 1.2 %norm_one.1 = (bf16[80,768]{1,0:T(8,128)(2,1)S(1)}, bf16[16,768]{1,0:T(8,128)(2,1)S(1)}, f32[16,768]{1,0:T(8,128)S(1)}) custom-call(s32[4]{0:T(128)S(1)} %copy-done.10, bf16[256,768]{1,0:T(8,128)(2,1)S(1)} %copy-done.2, f32[2,768]{1,0:T(2,128)S(1)} %copy-done.9, bf16[768,768]{1,0:T(8,128)(2,1)S(1)} %copy-done, bf16[768,768]{1,0:T(8,128)(2,1)S(1)} %copy-done.1, ...), custom_call_target="tpu_custom_call" | custom-call | bytes 3373072 | tf_op jit(solution)/shard_map/norm_one/pallas_call | solution.py:53
  28.2 1.5 %collective-permute-start.5 = (bf16[80,768]{1,0:T(8,128)(2,1)S(1)}, bf16[80,768]{1,0:T(8,128)(2,1)S(1)}, u32[]{:S(2)}, u32[]{:S(2)}) collective-permute-start(bf16[80,768]{1,0:T(8,128)(2,1)S(1)} %get-tuple-element.38.refs_5_.refs_0_), channel_id=1, source_target_pairs={{0,3},{1,2},{2,1},{3,0},{4,7},{5,6},{6,5},{7,4},{8,11},{9,10},{10,... | collective-permute-start | bytes 368648 | tf_op jit(solution)/shard_map/ppermute | solution.py:358
  29.6 0.5 collective-permute-start.4
  30.1 0.0 collective-permute-start.3
  30.1 3.2 %collective-permute-done.5.refs_8_ = bf16[80,768]{1,0:T(8,128)(2,1)S(1)} collective-permute-done((bf16[80,768]{1,0:T(8,128)(2,1)S(1)}, bf16[80,768]{1,0:T(8,128)(2,1)S(1)}, u32[]{:S(2)}, u32[]{:S(2)}) %collective-permute-start.5) | collective-permute-done | bytes 122912 | tf_op jit(solution)/shard_map/ppermute | solution.py:358
  33.3 3.1 %collective-permute-done.4.refs_7_ = bf16[80,768]{1,0:T(8,128)(2,1)S(1)} collective-permute-done((bf16[80,768]{1,0:T(8,128)(2,1)S(1)}, bf16[80,768]{1,0:T(8,128)(2,1)S(1)}, u32[]{:S(2)}, u32[]{:S(2)}) %collective-permute-start.4) | collective-permute-done | bytes 122912 | tf_op jit(solution)/shard_map/ppermute | solution.py:358
  36.4 0.0 collective-permute-done.3.refs_6_
  36.4 0.9 %ffn.1 = (f32[64,768]{1,0:T(8,128)S(1)}, bf16[64,768]{1,0:T(8,128)(2,1)S(1)}, bf16[64,768]{1,0:T(8,128)(2,1)S(1)}, bf16[64,768]{1,0:T(8,128)(2,1)S(1)}, bf16[2,768]{1,0:T(2,128)(2,1)S(1)}) custom-call(bf16[768,768]{1,0:T(8,128)(2,1)S(1)} %copy-done, bf16[768,768]{1,0:T(8,128)(2,1)S(1)} %copy-done.1, f32[2,768]{1,0:T(2,128)S(1)} %copy-done.9, ...), custom_call_target="tpu_custom_call" | custom-call | flops 603979776 | bytes 2930688 | tf_op jit(solution)/shard_map/ffn/pallas_call | solution.py:53
  37.3 0.0 copy-start.11
  37.4 0.1 collective-permute-start.6
  37.4 1.6 %collective-permute-start.7 = (bf16[64,768]{1,0:T(8,128)(2,1)S(1)}, bf16[64,768]{1,0:T(8,128)(2,1)S(1)}, u32[]{:S(2)}, u32[]{:S(2)}) collective-permute-start(bf16[64,768]{1,0:T(8,128)(2,1)S(1)} %get-tuple-element.43), channel_id=1, source_target_pairs={{0,2},{1,3},{2,0},{3,1},{4,6},{5,7},{6,4},{7,5},{8,10},{9,11},{10,... | collective-permute-start | bytes 294920 | tf_op jit(solution)/shard_map/ppermute | solution.py:358
  39.0 0.3 collective-permute-start.8
  39.3 0.0 collective-permute-done.6.refs_3_
  39.3 3.8 %collective-permute-done.7.refs_4_ = bf16[64,768]{1,0:T(8,128)(2,1)S(1)} collective-permute-done((bf16[64,768]{1,0:T(8,128)(2,1)S(1)}, bf16[64,768]{1,0:T(8,128)(2,1)S(1)}, u32[]{:S(2)}, u32[]{:S(2)}) %collective-permute-start.7) | collective-permute-done | bytes 98336 | tf_op jit(solution)/shard_map/ppermute | solution.py:358
  43.1 1.2 %collective-permute-done.8.refs_5_ = bf16[64,768]{1,0:T(8,128)(2,1)S(1)} collective-permute-done((bf16[64,768]{1,0:T(8,128)(2,1)S(1)}, bf16[64,768]{1,0:T(8,128)(2,1)S(1)}, u32[]{:S(2)}, u32[]{:S(2)}) %collective-permute-start.8) | collective-permute-done | bytes 98336 | tf_op jit(solution)/shard_map/ppermute | solution.py:358
  44.3 0.2 norm_two.1.refs_0_.refs_1_
  44.5 1.6 %collective-permute-start.9 = (bf16[64,768]{1,0:T(8,128)(2,1)S(1)}, bf16[64,768]{1,0:T(8,128)(2,1)S(1)}, u32[]{:S(2)}, u32[]{:S(2)}) collective-permute-start(bf16[64,768]{1,0:T(8,128)(2,1)S(1)} %norm_two.1.refs_0_.refs_1_), channel_id=1, source_target_pairs={{0,2},{1,3},{2,0},{3,1},{4,6},{5,7},{6,4},{7,5},{8,10},{9,11},{10,... | collective-permute-start | bytes 294920 | tf_op jit(solution)/shard_map/ppermute | solution.py:358
  46.1 3.5 %collective-permute-done.9.refs_1_.refs_2_ = bf16[64,768]{1,0:T(8,128)(2,1)S(1)} collective-permute-done((bf16[64,768]{1,0:T(8,128)(2,1)S(1)}, bf16[64,768]{1,0:T(8,128)(2,1)S(1)}, u32[]{:S(2)}, u32[]{:S(2)}) %collective-permute-start.9) | collective-permute-done | bytes 98336 | tf_op jit(solution)/shard_map/ppermute | solution.py:358
  49.6 0.1 collective-permute-start.10
  49.7 4.2 %collective-permute-start.14 = (bf16[2,768]{1,0:T(2,128)(2,1)S(1)}, bf16[2,768]{1,0:T(2,128)(2,1)S(1)}, u32[]{:S(2)}, u32[]{:S(2)}) collective-permute-start(bf16[2,768]{1,0:T(2,128)(2,1)S(1)} %get-tuple-element.45.refs_8_), channel_id=1, source_target_pairs={{0,24},{1,29},{2,26},{3,31},{4,28},{5,25},{6,30},{7,27},{8,16},{9,... | collective-permute-start | bytes 9224 | tf_op jit(solution)/shard_map/ppermute | solution.py:427
  53.8 0.0 collective-permute-start.13
  53.8 0.6 collective-permute-start.12
  54.5 0.8 %collective-permute-start.11 = (bf16[2,768]{1,0:T(2,128)(2,1)S(1)}, bf16[2,768]{1,0:T(2,128)(2,1)S(1)}, u32[]{:S(2)}, u32[]{:S(2)}) collective-permute-start(bf16[2,768]{1,0:T(2,128)(2,1)S(1)} %get-tuple-element.45.refs_8_), channel_id=1, source_target_pairs={{1,5},{3,7},{5,1},{7,3},{9,13},{11,15},{13,9},{15,11},{17,21},{19,... | collective-permute-start | bytes 9224 | tf_op jit(solution)/shard_map/ppermute | solution.py:427
  55.3 0.0 collective-permute-done.10.refs_3_
  55.3 1.3 %place.1 = bf16[256,768]{1,0:T(8,128)(2,1)} custom-call(s32[4]{0:T(128)S(1)} %copy-done.10, bf16[64,768]{1,0:T(8,128)(2,1)S(1)} %norm_two.1.refs_0_.refs_1_, bf16[64,768]{1,0:T(8,128)(2,1)S(1)} %collective-permute-done.9.refs_1_.refs_2_, bf16[128,768]{1,0:T(8,128)(2,1)S(1)} %collective-permute-done.10.refs_3_), custom_call_target="tpu_custom_call" | custom-call | bytes 393232 | tf_op jit(solution)/shard_map/place/pallas_call | solution.py:53
  56.6 0.0 collective-permute-done.14.refs_3_
  56.7 1.7 %collective-permute-done.13.refs_2_ = bf16[2,768]{1,0:T(2,128)(2,1)S(1)} collective-permute-done((bf16[2,768]{1,0:T(2,128)(2,1)S(1)}, bf16[2,768]{1,0:T(2,128)(2,1)S(1)}, u32[]{:S(2)}, u32[]{:S(2)}) %collective-permute-start.13) | collective-permute-done | bytes 3104 | tf_op jit(solution)/shard_map/ppermute | solution.py:427
  58.3 0.0 collective-permute-done.12.refs_1_
  58.3 0.0 collective-permute-done.11.refs_0_
  58.4 0.0 copy-start.8
  58.4 2.4 %collective-permute-start.15 = (bf16[16,768]{1,0:T(8,128)(2,1)S(1)}, bf16[16,768]{1,0:T(8,128)(2,1)S(1)}, u32[]{:S(2)}, u32[]{:S(2)}) collective-permute-start(bf16[16,768]{1,0:T(8,128)(2,1)S(1)} %pack.1.refs_9_), channel_id=1, source_target_pairs={{0,1},{1,0},{2,3},{3,2},{4,5},{5,4},{6,7},{7,6},{8,9},{9,8},{10,11... | collective-permute-start | bytes 73736 | tf_op jit(solution)/shard_map/ppermute | solution.py:358
  60.8 0.8 %collective-permute-done.15.refs_10_ = bf16[16,768]{1,0:T(8,128)(2,1)S(1)} collective-permute-done((bf16[16,768]{1,0:T(8,128)(2,1)S(1)}, bf16[16,768]{1,0:T(8,128)(2,1)S(1)}, u32[]{:S(2)}, u32[]{:S(2)}) %collective-permute-start.15) | collective-permute-done | bytes 24608 | tf_op jit(solution)/shard_map/ppermute | solution.py:358
  61.6 0.0 all-to-all-done
  61.7 0.0 copy-done.11
  61.7 0.6 copy-done.15
  62.2 0.6 copy-done.14
  62.8 7.2 %graph.1 = bf16[192,512]{1,0:T(8,128)(2,1)} custom-call(s32[4]{0:T(128)} %iota_xor_fusion.refs_0_, s32[4,6]{1,0:T(4,128)} %refs_1_.9, s32[2]{0:T(128)} %refs_2_.5, bf16[512,192]{1,0:T(8,128)(2,1)} %copy-done.6, bf16[512,384]{1,0:T(8,128)(2,1)} %copy-done.5, bf16[3,192,768]{2,1,0:T(8,128)(2,1)} %bitcast.9, bf16[512,768]{1,0:T(8,128)(2,1)} %copy-done.4, ...), custom_call_target="tpu_custom_call" | custom-call | flops 1000000000 | bytes 3886200 | tf_op jit(solution)/shard_map/graph/pallas_call | solution.py:53
  (14 shorter events, 0.1 us)
Async XLA Ops:
  4.7 56.9 %all-to-all-start = ((bf16[8,256,384]{2,1,0:T(8,128)(2,1)}), bf16[8,256,384]{2,1,0:T(8,128)(2,1)S(1)}, u32[]{:S(2)}, u32[]{:S(2)}) async-start(bf16[8,256,384]{2,1,0:T(8,128)(2,1)} %bitcast.13), calls=%async_computation | async-start | bytes 3145728 | tf_op jit(solution)/shard_map/all_to_all | solution.py:374
  12.0 7.3 %copy-start.13 = (s32[512,16]{0,1:T(8,128)S(1)}, s32[512,16]{0,1:T(8,128)}, u32[]{:S(2)}) copy-start(s32[512,16]{0,1:T(8,128)} %param.23) | copy-start | bytes 98308
  17.3 9.5 %collective-permute-start = (bf16[80,768]{1,0:T(8,128)(2,1)}, bf16[80,768]{1,0:T(8,128)(2,1)S(1)}, u32[]{:S(2)}, u32[]{:S(2)}) collective-permute-start(bf16[80,768]{1,0:T(8,128)(2,1)} %get-tuple-element.30), channel_id=1, source_target_pairs={{0,1},{1,0},{2,3},{3,2},{4,5},{5,4},{6,7},{7,6},{8,9},{9,8},{10,11... | collective-permute-start | bytes 368648 | tf_op jit(solution)/shard_map/ppermute | solution.py:358
  17.4 9.4 %collective-permute-start.1 = (bf16[80,768]{1,0:T(8,128)(2,1)}, bf16[80,768]{1,0:T(8,128)(2,1)S(1)}, u32[]{:S(2)}, u32[]{:S(2)}) collective-permute-start(bf16[80,768]{1,0:T(8,128)(2,1)} %get-tuple-element.31), channel_id=1, source_target_pairs={{0,2},{1,3},{2,0},{3,1},{4,6},{5,7},{6,4},{7,5},{8,10},{9,11},{10,... | collective-permute-start | bytes 368648 | tf_op jit(solution)/shard_map/ppermute | solution.py:358
  19.0 7.8 %collective-permute-start.2 = (bf16[80,768]{1,0:T(8,128)(2,1)}, bf16[80,768]{1,0:T(8,128)(2,1)S(1)}, u32[]{:S(2)}, u32[]{:S(2)}) collective-permute-start(bf16[80,768]{1,0:T(8,128)(2,1)} %get-tuple-element.32), channel_id=1, source_target_pairs={{0,3},{1,2},{2,1},{3,0},{4,7},{5,6},{6,5},{7,4},{8,11},{9,10},{10,... | collective-permute-start | bytes 368648 | tf_op jit(solution)/shard_map/ppermute | solution.py:358
  19.3 5.1 %copy-start.3 = (bf16[3,768,192]{1,2,0:T(8,128)(2,1)S(1)}, bf16[3,768,192]{1,2,0:T(8,128)(2,1)}, u32[]{:S(2)}) copy-start(bf16[3,768,192]{1,2,0:T(8,128)(2,1)} %param.19) | copy-start | bytes 2654212
  19.3 5.1 %copy-start.12 = (bf16[512,768]{1,0:T(8,128)(2,1)S(1)}, bf16[512,768]{1,0:T(8,128)(2,1)}, u32[]{:S(2)}) copy-start(bf16[512,768]{1,0:T(8,128)(2,1)} %refs_0_.2) | copy-start | bytes 2359300
  23.5 0.9 %copy-start.4 = (bf16[512,768]{1,0:T(8,128)(2,1)}, bf16[512,768]{1,0:T(8,128)(2,1)S(1)}, u32[]{:S(2)}) copy-start(bf16[512,768]{1,0:T(8,128)(2,1)S(1)} %mask.1.refs_6_) | copy-start | bytes 2359300
  24.4 2.4 %copy-start = (bf16[768,768]{1,0:T(8,128)(2,1)S(1)}, bf16[768,768]{1,0:T(8,128)(2,1)}, u32[]{:S(2)}) copy-start(bf16[768,768]{1,0:T(8,128)(2,1)} %refs_0_.3) | copy-start | bytes 3538948
  24.4 2.4 %copy-start.1 = (bf16[768,768]{1,0:T(8,128)(2,1)S(1)}, bf16[768,768]{1,0:T(8,128)(2,1)}, u32[]{:S(2)}) copy-start(bf16[768,768]{1,0:T(8,128)(2,1)} %refs_1_.7) | copy-start | bytes 3538948
  24.5 2.4 %copy-start.2 = (bf16[256,768]{1,0:T(8,128)(2,1)S(1)}, bf16[256,768]{1,0:T(8,128)(2,1)}, u32[]{:S(2)}) copy-start(bf16[256,768]{1,0:T(8,128)(2,1)} %refs_1_.6) | copy-start | bytes 1179652
  24.5 2.4 %copy-start.7 = (f32[80,768]{1,0:T(8,128)S(1)}, f32[80,768]{1,0:T(8,128)}, u32[]{:S(2)}) copy-start(f32[80,768]{1,0:T(8,128)} %get-tuple-element.29.refs_5_) | copy-start | bytes 737284
  24.5 2.4 %copy-start.9 = (f32[2,768]{1,0:T(2,128)S(1)}, f32[2,768]{1,0:T(2,128)}, u32[]{:S(2)}) copy-start(f32[2,768]{1,0:T(2,128)} %refs_1_.8) | copy-start | bytes 18436
  24.5 2.4 %copy-start.10 = (s32[4]{0:T(128)S(1)}, s32[4]{0:T(128)}, u32[]{:S(2)}) copy-start(s32[4]{0:T(128)} %iota_xor_fusion.refs_0_) | copy-start | bytes 52
  25.4 0.8 %copy-start.5 = (bf16[512,384]{1,0:T(8,128)(2,1)}, bf16[512,384]{1,0:T(8,128)(2,1)S(1)}, u32[]{:S(2)}) copy-start(bf16[512,384]{1,0:T(8,128)(2,1)S(1)} %get-tuple-element.48.refs_4_) | copy-start | bytes 1179652
  26.1 0.7 copy-start.6
  28.2 5.2 %collective-permute-start.5 = (bf16[80,768]{1,0:T(8,128)(2,1)S(1)}, bf16[80,768]{1,0:T(8,128)(2,1)S(1)}, u32[]{:S(2)}, u32[]{:S(2)}) collective-permute-start(bf16[80,768]{1,0:T(8,128)(2,1)S(1)} %get-tuple-element.38.refs_5_.refs_0_), channel_id=1, source_target_pairs={{0,3},{1,2},{2,1},{3,0},{4,7},{5,6},{6,5},{7,4},{8,11},{9,10},{10,... | collective-permute-start | bytes 368648 | tf_op jit(solution)/shard_map/ppermute | solution.py:358
  29.6 6.8 %collective-permute-start.4 = (bf16[80,768]{1,0:T(8,128)(2,1)S(1)}, bf16[80,768]{1,0:T(8,128)(2,1)S(1)}, u32[]{:S(2)}, u32[]{:S(2)}) collective-permute-start(bf16[80,768]{1,0:T(8,128)(2,1)S(1)} %get-tuple-element.38.refs_5_.refs_0_), channel_id=1, source_target_pairs={{0,2},{1,3},{2,0},{3,1},{4,6},{5,7},{6,4},{7,5},{8,10},{9,11},{10,... | collective-permute-start | bytes 368648 | tf_op jit(solution)/shard_map/ppermute | solution.py:358
  30.1 6.3 %collective-permute-start.3 = (bf16[80,768]{1,0:T(8,128)(2,1)S(1)}, bf16[80,768]{1,0:T(8,128)(2,1)S(1)}, u32[]{:S(2)}, u32[]{:S(2)}) collective-permute-start(bf16[80,768]{1,0:T(8,128)(2,1)S(1)} %get-tuple-element.38.refs_5_.refs_0_), channel_id=1, source_target_pairs={{0,1},{1,0},{2,3},{3,2},{4,5},{5,4},{6,7},{7,6},{8,9},{9,8},{10,11... | collective-permute-start | bytes 368648 | tf_op jit(solution)/shard_map/ppermute | solution.py:358
  37.3 24.3 %copy-start.11 = (bf16[2,768]{1,0:T(2,128)(2,1)}, bf16[2,768]{1,0:T(2,128)(2,1)S(1)}, u32[]{:S(2)}) copy-start(bf16[2,768]{1,0:T(2,128)(2,1)S(1)} %get-tuple-element.45.refs_8_) | copy-start | bytes 9220
  37.4 1.9 %collective-permute-start.6 = (bf16[64,768]{1,0:T(8,128)(2,1)S(1)}, bf16[64,768]{1,0:T(8,128)(2,1)S(1)}, u32[]{:S(2)}, u32[]{:S(2)}) collective-permute-start(bf16[64,768]{1,0:T(8,128)(2,1)S(1)} %get-tuple-element.42), channel_id=1, source_target_pairs={{0,1},{1,0},{2,3},{3,2},{4,5},{5,4},{6,7},{7,6},{8,9},{9,8},{10,11... | collective-permute-start | bytes 294920 | tf_op jit(solution)/shard_map/ppermute | solution.py:358
  37.4 5.7 %collective-permute-start.7 = (bf16[64,768]{1,0:T(8,128)(2,1)S(1)}, bf16[64,768]{1,0:T(8,128)(2,1)S(1)}, u32[]{:S(2)}, u32[]{:S(2)}) collective-permute-start(bf16[64,768]{1,0:T(8,128)(2,1)S(1)} %get-tuple-element.43), channel_id=1, source_target_pairs={{0,2},{1,3},{2,0},{3,1},{4,6},{5,7},{6,4},{7,5},{8,10},{9,11},{10,... | collective-permute-start | bytes 294920 | tf_op jit(solution)/shard_map/ppermute | solution.py:358
  39.0 5.3 %collective-permute-start.8 = (bf16[64,768]{1,0:T(8,128)(2,1)S(1)}, bf16[64,768]{1,0:T(8,128)(2,1)S(1)}, u32[]{:S(2)}, u32[]{:S(2)}) collective-permute-start(bf16[64,768]{1,0:T(8,128)(2,1)S(1)} %get-tuple-element.44), channel_id=1, source_target_pairs={{0,3},{1,2},{2,1},{3,0},{4,7},{5,6},{6,5},{7,4},{8,11},{9,10},{10,... | collective-permute-start | bytes 294920 | tf_op jit(solution)/shard_map/ppermute | solution.py:358
  44.5 5.0 %collective-permute-start.9 = (bf16[64,768]{1,0:T(8,128)(2,1)S(1)}, bf16[64,768]{1,0:T(8,128)(2,1)S(1)}, u32[]{:S(2)}, u32[]{:S(2)}) collective-permute-start(bf16[64,768]{1,0:T(8,128)(2,1)S(1)} %norm_two.1.refs_0_.refs_1_), channel_id=1, source_target_pairs={{0,2},{1,3},{2,0},{3,1},{4,6},{5,7},{6,4},{7,5},{8,10},{9,11},{10,... | collective-permute-start | bytes 294920 | tf_op jit(solution)/shard_map/ppermute | solution.py:358
  49.6 5.7 %collective-permute-start.10 = (bf16[128,768]{1,0:T(8,128)(2,1)S(1)}, bf16[128,768]{1,0:T(8,128)(2,1)S(1)}, u32[]{:S(2)}, u32[]{:S(2)}) collective-permute-start(bf16[128,768]{1,0:T(8,128)(2,1)S(1)} %join.1), channel_id=1, source_target_pairs={{0,1},{1,0},{2,3},{3,2},{4,5},{5,4},{6,7},{7,6},{8,9},{9,8},{10,11... | collective-permute-start | bytes 589832 | tf_op jit(solution)/shard_map/ppermute | solution.py:358
  49.7 7.0 %collective-permute-start.14 = (bf16[2,768]{1,0:T(2,128)(2,1)S(1)}, bf16[2,768]{1,0:T(2,128)(2,1)S(1)}, u32[]{:S(2)}, u32[]{:S(2)}) collective-permute-start(bf16[2,768]{1,0:T(2,128)(2,1)S(1)} %get-tuple-element.45.refs_8_), channel_id=1, source_target_pairs={{0,24},{1,29},{2,26},{3,31},{4,28},{5,25},{6,30},{7,27},{8,16},{9,... | collective-permute-start | bytes 9224 | tf_op jit(solution)/shard_map/ppermute | solution.py:427
  53.8 4.5 %collective-permute-start.13 = (bf16[2,768]{1,0:T(2,128)(2,1)S(1)}, bf16[2,768]{1,0:T(2,128)(2,1)S(1)}, u32[]{:S(2)}, u32[]{:S(2)}) collective-permute-start(bf16[2,768]{1,0:T(2,128)(2,1)S(1)} %get-tuple-element.45.refs_8_), channel_id=1, source_target_pairs={{0,16},{1,21},{2,18},{3,23},{4,20},{5,17},{6,22},{7,19},{8,24},{9,... | collective-permute-start | bytes 9224 | tf_op jit(solution)/shard_map/ppermute | solution.py:427
  53.8 4.5 %collective-permute-start.12 = (bf16[2,768]{1,0:T(2,128)(2,1)S(1)}, bf16[2,768]{1,0:T(2,128)(2,1)S(1)}, u32[]{:S(2)}, u32[]{:S(2)}) collective-permute-start(bf16[2,768]{1,0:T(2,128)(2,1)S(1)} %get-tuple-element.45.refs_8_), channel_id=1, source_target_pairs={{0,8},{1,13},{2,10},{3,15},{4,12},{5,9},{6,14},{7,11},{8,0},{9,5},... | collective-permute-start | bytes 9224 | tf_op jit(solution)/shard_map/ppermute | solution.py:427
  54.5 3.9 %collective-permute-start.11 = (bf16[2,768]{1,0:T(2,128)(2,1)S(1)}, bf16[2,768]{1,0:T(2,128)(2,1)S(1)}, u32[]{:S(2)}, u32[]{:S(2)}) collective-permute-start(bf16[2,768]{1,0:T(2,128)(2,1)S(1)} %get-tuple-element.45.refs_8_), channel_id=1, source_target_pairs={{1,5},{3,7},{5,1},{7,3},{9,13},{11,15},{13,9},{15,11},{17,21},{19,... | collective-permute-start | bytes 9224 | tf_op jit(solution)/shard_map/ppermute | solution.py:427
  58.4 3.3 %copy-start.8 = (bf16[16,768]{1,0:T(8,128)(2,1)}, bf16[16,768]{1,0:T(8,128)(2,1)S(1)}, u32[]{:S(2)}) copy-start(bf16[16,768]{1,0:T(8,128)(2,1)S(1)} %pack.1.refs_9_) | copy-start | bytes 73732
  58.4 3.3 %collective-permute-start.15 = (bf16[16,768]{1,0:T(8,128)(2,1)S(1)}, bf16[16,768]{1,0:T(8,128)(2,1)S(1)}, u32[]{:S(2)}, u32[]{:S(2)}) collective-permute-start(bf16[16,768]{1,0:T(8,128)(2,1)S(1)} %pack.1.refs_9_), channel_id=1, source_target_pairs={{0,1},{1,0},{2,3},{3,2},{4,5},{5,4},{6,7},{7,6},{8,9},{9,8},{10,11... | collective-permute-start | bytes 73736 | tf_op jit(solution)/shard_map/ppermute | solution.py:358
  61.6 0.6 copy-start.15
  61.6 1.2 %copy-start.14 = (bf16[8,256,384]{2,1,0:T(8,128)(2,1)}, bf16[8,256,384]{2,1,0:T(8,128)(2,1)S(1)}, u32[]{:S(2)}) copy-start(bf16[8,256,384]{2,1,0:T(8,128)(2,1)S(1)} %all-to-all-done) | copy-start | bytes 4718596

commit v7 on v5

--- a/solution.py
+++ b/solution.py
@@ -1,3 +1,4 @@
+import functools
 import jax
 import jax.numpy as jnp
 from jax import lax
@@ -224,11 +225,22 @@
     out[...] = rows.astype(bf)
 
 
-def place_kernel(ready, who_ref, *refs):
-    *chunks, out = refs
-    chunk = out.shape[0] // len(chunks)
-    for step, ref in enumerate(chunks):
-        out[pl.ds(pl.multiple_of(who_ref[step] * chunk, chunk), chunk), :] = ref[...]
+def join_kernel(ready, *refs):
+    *parts, out = refs
+    start = 0
+    for part in parts:
+        out[start : start + part.shape[0], :] = part[...]
+        start += part.shape[0]
+
+
+def place_kernel(whose, ready, who_ref, *refs):
+    *blocks, out = refs
+    chunk = out.shape[0] // len(whose)
+    pieces = [
+        block[start : start + chunk, :] for block in blocks for start in range(0, block.shape[0], chunk)
+    ]
+    for step, piece in zip(whose, pieces):
+        out[pl.ds(pl.multiple_of(who_ref[step] * chunk, chunk), chunk), :] = piece
 
 
 def own_kernel(ready, table_ref, w_ref, kv_ref, q_ref):
@@ -260,10 +272,8 @@
                 firsts[pl.ds(place, 1), :] = rows[at : at + 1]
     firsts[0:per_part, :] = first_ref[...].astype(f32)
     first = firsts[...].astype(bf)
-    ready(5)
     first_kv = jnp.concatenate([dot_nt(first, w_ref[1]), dot_nt(first, w_ref[2])], axis=1).astype(bf)
     first_q = dot_nt(first, w_ref[0])
-    ready(2, 4)
     for tile in range(row_tiles):
         span = slice(tile * TILE, (tile + 1) * TILE)
         rows = kv_ref[span, :].astype(f32)
@@ -274,7 +284,6 @@
         rows = rows.astype(bf)
         k_all[span, :] = rows[:, :cols]
         v_all[span, :] = rows[:, cols:]
-    ready(7)
     lanes = lax.broadcasted_iota(jnp.int32, (TILE, first_kv.shape[0]), 1).astype(f32)
     for tile in range(far_ref.shape[0] // TILE):
         rows = far_ref[tile * TILE : (tile + 1) * TILE, :].astype(f32)
@@ -285,7 +294,6 @@
         k_all[span, :] = fixed[:, :cols]
         v_all[span, :] = fixed[:, cols:]
 
-    ready(1, 3, 6)
     heads = cols // GHD
     head_of = lax.broadcasted_iota(jnp.int32, (TILE, cols), 1) // GHD
     for tile in range(row_tiles):
@@ -372,6 +380,10 @@
         name="attn",
     )
     parts = [swap(terms[step], step) for step in range(1, mp)]
+    mask = call(
+        mask_kernel, shape((nodes, TPR * TILE), bf), (nbr_slots.T,), flops=4 * 10**9, name="mask"
+    )
+    parts, mask = lax.optimization_barrier((parts, mask))
     hidden, first_hidden, first_terms = call(
         norm_one_kernel,
         (shape((chunk + PAD, width), bf), shape((PAD, width), bf), shape((PAD, width), f32)),
@@ -403,9 +415,6 @@
         )
         for turn in range(turns)
     ]
-    mask = call(
-        mask_kernel, shape((nodes, TPR * TILE), bf), (nbr_slots.T,), flops=4 * 10**9, name="mask"
-    )
     kv, q = call(
         own_kernel,
         (shape((nodes, 2 * cols), bf), shape((nodes, cols), bf)),
@@ -420,8 +429,23 @@
         (hidden, gains, terms[0], *parts),
         name="norm_two",
     )
-    dones = [done] + [swap(done, step) for step in range(1, mp)]
-    dones, firsts, mask = lax.optimization_barrier((dones, firsts, mask))
+    whose, blocks, step = [0], [done], mp // 2
+    while step:
+        rows = blocks[0]
+        if len(blocks) > 1:
+            dims = (sum(block.shape[0] for block in blocks), width)
+            rows = call(join_kernel, shape(dims, bf), blocks, name="join")
+        blocks = blocks + [swap(rows, step)]
+        whose = whose + [other ^ step for other in whose]
+        step //= 2
+    encoded = call(
+        functools.partial(place_kernel, whose),
+        shape((tok_rows, width), bf),
+        (who, *blocks),
+        smem=(0,),
+        name="place",
+    )
+    encoded, firsts, far = lax.optimization_barrier((encoded, firsts, far))
     pack = call(pack_kernel, shape((tail_rows(turns * per_part), width), bf), firsts, name="pack")
     packs = [pack] + [swap(pack, step) for step in range(1, mp)]
 
@@ -430,9 +454,7 @@
         graph_kernel,
         shape((cols, nodes), bf),
         (who, tile_cols, title_nodes, q, kv, w_graph, mask, far, first, *packs),
-        smem=(0,),
-        hbm=(5, 2, 4, 7, 1, 3, 6),
-        scalars=(1, 2),
+        smem=(0, 1, 2),
         scratch=[
             pltpu.VMEM((keys, cols), bf),
             pltpu.VMEM((keys, cols), bf),
@@ -440,9 +462,6 @@
         ],
         flops=10**9,
         name="graph",
-    )
-    encoded = call(
-        place_kernel, shape((tok_rows, width), bf), (who, *dones), smem=(0,), name="place"
     )
     return (encoded, graph_out.T)
 

time: 65.7 us -> 66.6 us (1.014)
  waiting for transfers between devices: 14.5 us -> 19 us
  Pallas kernels: 22.4 us -> 19.7 us
  local copies, waits for them, and re-layouts: 3.48 us -> 1.05 us
  starting transfers between devices: 23.9 us -> 25.6 us
    ppermute x15 -> x14, waiting for transfers between devices: 14.5 us -> 19 us  [swap(): lax.ppermute(value, axis, [(i, i ^ step) for i in range(lax.axis_size(axi...]
    pallas_call x10 -> x11, Pallas kernels: 22.4 us -> 19.7 us  [call(): pl.pallas_call(body, out_shape=outs, in_specs=specs, out_specs=jax.tree.m...]
    unnamed x36 -> x26, local copies, waits for them, and re-layouts: 3.48 us -> 1.05 us
    ppermute x15 -> x14, starting transfers between devices: 12.8 us -> 14.1 us  [swap(): lax.ppermute(value, axis, [(i, i ^ step) for i in range(lax.axis_size(axi...]
  transfers between devices with their start and end apart: 18 -> 17, of which waited for: 6 -> 9; matrix products, arithmetic and copies ran while one was open for 0% -> 0% of each run, Pallas kernels for 17% -> 17%
where the time goes in v7:
time: 66.6 us; the launch traced here: 66.3 us
  starting transfers between devices  25.6 us (38%)
  Pallas kernels  19.7 us (30%)
  waiting for transfers between devices  19 us (29%)
  local copies, waits for them, and re-layouts  1.05 us (2%)
  between operations  0.88 us (1%)
    pallas_call x11, Pallas kernels, call(): pl.pallas_call(body, out_shape=outs, in_specs=specs, out_specs=jax.tree.m...  19.7 us
    ppermute x14, waiting for transfers between devices, swap(): lax.ppermute(value, axis, [(i, i ^ step) for i in range(lax.axis_size(axi...  19 us
    ppermute x14, starting transfers between devices, swap(): lax.ppermute(value, axis, [(i, i ^ step) for i in range(lax.axis_size(axi...  14.1 us
    all_to_all x1, starting transfers between devices, local(): lax.all_to_all(sent.reshape(dp, fetch, 2 * cols), 'dp', split_axis=0, con...  7.4 us
    ppermute x2, starting transfers between devices, local(): lax.ppermute(first, ('dp', 'mp'), [(p * mp + m, (p ^ turn * mp + m) * mp...  4.1 us
  transfers between devices with their start and end apart: 17, of which 9 were waited for; matrix products, arithmetic and copies ran while one was open for 0% of the time, Pallas kernels for 17%

profile of v7, /device:TPU:0, one launch (start us, length us, event | category | flops | bytes accessed | tf_op | source)
XLA Modules:
  0.0 66.3 jit_solution(5571370484817766862)
XLA Ops:
  0.6 4.1 %send.1 = bf16[2048,384]{1,0:T(8,128)(2,1)} custom-call(s32[1]{0:T(128)} %bitcast.refs_0_, s32[2]{0:T(128)} %refs_2_.5, s32[8,256]{1,0:T(8,128)} %bitcast.16, bf16[512,768]{1,0:T(8,128)(2,1)} %refs_0_.2, bf16[3,192,768]{2,1,0:T(8,128)(2,1)} %bitcast.9), custom_call_target="tpu_custom_call" | custom-call | flops 1107296256 | bytes 1679372 | tf_op jit(solution)/shard_map/send/pallas_call | solution.py:53
  4.7 0.0 copy-start.2
  4.8 0.0 copy-start.4
  4.8 0.0 copy-start.7
  4.8 7.4 %all-to-all-start = ((bf16[8,256,384]{2,1,0:T(8,128)(2,1)}), bf16[8,256,384]{2,1,0:T(8,128)(2,1)S(1)}, u32[]{:S(2)}, u32[]{:S(2)}) async-start(bf16[8,256,384]{2,1,0:T(8,128)(2,1)} %bitcast.14), calls=%async_computation | async-start | bytes 3145728 | tf_op jit(solution)/shard_map/all_to_all | solution.py:368
  12.2 0.0 copy-start.12
  12.2 0.0 copy-done.2
  12.2 0.0 copy-done.4
  12.2 0.0 copy-done.7
  12.2 2.3 %attn.1 = (f32[80,768]{1,0:T(8,128)S(1)}, bf16[80,768]{1,0:T(8,128)(2,1)S(1)}, bf16[80,768]{1,0:T(8,128)(2,1)S(1)}, bf16[80,768]{1,0:T(8,128)(2,1)S(1)}) custom-call(s32[4]{0:T(128)S(1)} %iota_xor_fusion.refs_0_, bf16[256,768]{1,0:T(8,128)(2,1)S(1)} %copy-done.2, bf16[3,192,768]{2,1,0:T(8,128)(2,1)S(1)} %bitcast.12, bf16[192,768]{1,0:T(8,128)(2,1)S(1)} %copy-done.7), custom_call_target="tpu_custom_call" | custom-call | flops 301989888 | bytes 1572880 | tf_op jit(solution)/shard_map/attn/pallas_call | solution.py:53
  14.5 0.1 collective-permute-start
  14.6 1.6 %collective-permute-start.1 = (bf16[80,768]{1,0:T(8,128)(2,1)S(1)}, bf16[80,768]{1,0:T(8,128)(2,1)S(1)}, u32[]{:S(2)}, u32[]{:S(2)}) collective-permute-start(bf16[80,768]{1,0:T(8,128)(2,1)S(1)} %get-tuple-element.31), channel_id=1, source_target_pairs={{0,2},{1,3},{2,0},{3,1},{4,6},{5,7},{6,4},{7,5},{8,10},{9,11},{10,... | collective-permute-start | bytes 368648 | tf_op jit(solution)/shard_map/ppermute | solution.py:352
  16.2 0.3 collective-permute-start.2
  16.4 0.0 copy-done.12
  16.4 4.2 %mask.1.refs_6_ = bf16[512,768]{1,0:T(8,128)(2,1)S(1)} custom-call(s32[16,512]{1,0:T(8,128)S(1)} %bitcast.13), custom_call_target="tpu_custom_call" | custom-call | flops 4000000000 | bytes 32768 | tf_op jit(solution)/shard_map/mask/pallas_call | solution.py:53
  20.7 0.0 collective-permute-done.refs_6_
  20.7 0.1 collective-permute-done.1.refs_7_
  20.8 1.7 %collective-permute-done.2.refs_8_ = bf16[80,768]{1,0:T(8,128)(2,1)S(1)} collective-permute-done((bf16[80,768]{1,0:T(8,128)(2,1)S(1)}, bf16[80,768]{1,0:T(8,128)(2,1)S(1)}, u32[]{:S(2)}, u32[]{:S(2)}) %collective-permute-start.2) | collective-permute-done | bytes 122912 | tf_op jit(solution)/shard_map/ppermute | solution.py:352
  22.5 0.0 copy-done
  22.5 0.0 copy-done.1
  22.5 0.0 copy-done.8
  22.5 1.3 %norm_one.1 = (bf16[80,768]{1,0:T(8,128)(2,1)S(1)}, bf16[16,768]{1,0:T(8,128)(2,1)S(1)}, f32[16,768]{1,0:T(8,128)S(1)}) custom-call(s32[4]{0:T(128)S(1)} %iota_xor_fusion.refs_0_, bf16[256,768]{1,0:T(8,128)(2,1)S(1)} %copy-done.2, f32[2,768]{1,0:T(2,128)S(1)} %copy-done.8, bf16[768,768]{1,0:T(8,128)(2,1)S(1)} %copy-done, bf16[768,768]{1,0:T(8,128)(2,1)S(1)} %copy-done.1, ...), custom_call_target="tpu_custom_call" | custom-call | bytes 3373072 | tf_op jit(solution)/shard_map/norm_one/pallas_call | solution.py:53
  23.8 1.7 %collective-permute-start.5 = (bf16[80,768]{1,0:T(8,128)(2,1)S(1)}, bf16[80,768]{1,0:T(8,128)(2,1)S(1)}, u32[]{:S(2)}, u32[]{:S(2)}) collective-permute-start(bf16[80,768]{1,0:T(8,128)(2,1)S(1)} %get-tuple-element.39.refs_5_.refs_0_), channel_id=1, source_target_pairs={{0,3},{1,2},{2,1},{3,0},{4,7},{5,6},{6,5},{7,4},{8,11},{9,10},{10,... | collective-permute-start | bytes 368648 | tf_op jit(solution)/shard_map/ppermute | solution.py:352
  25.5 0.5 collective-permute-start.4
  26.0 0.0 collective-permute-start.3
  26.0 3.2 %collective-permute-done.5.refs_8_ = bf16[80,768]{1,0:T(8,128)(2,1)S(1)} collective-permute-done((bf16[80,768]{1,0:T(8,128)(2,1)S(1)}, bf16[80,768]{1,0:T(8,128)(2,1)S(1)}, u32[]{:S(2)}, u32[]{:S(2)}) %collective-permute-start.5) | collective-permute-done | bytes 122912 | tf_op jit(solution)/shard_map/ppermute | solution.py:352
  29.1 2.9 %collective-permute-done.4.refs_7_ = bf16[80,768]{1,0:T(8,128)(2,1)S(1)} collective-permute-done((bf16[80,768]{1,0:T(8,128)(2,1)S(1)}, bf16[80,768]{1,0:T(8,128)(2,1)S(1)}, u32[]{:S(2)}, u32[]{:S(2)}) %collective-permute-start.4) | collective-permute-done | bytes 122912 | tf_op jit(solution)/shard_map/ppermute | solution.py:352
  32.0 0.0 collective-permute-done.3.refs_6_
  32.0 0.9 %ffn.1 = (f32[64,768]{1,0:T(8,128)S(1)}, bf16[64,768]{1,0:T(8,128)(2,1)S(1)}, bf16[64,768]{1,0:T(8,128)(2,1)S(1)}, bf16[64,768]{1,0:T(8,128)(2,1)S(1)}, bf16[2,768]{1,0:T(2,128)(2,1)S(1)}) custom-call(bf16[768,768]{1,0:T(8,128)(2,1)S(1)} %copy-done, bf16[768,768]{1,0:T(8,128)(2,1)S(1)} %copy-done.1, f32[2,768]{1,0:T(2,128)S(1)} %copy-done.8, ...), custom_call_target="tpu_custom_call" | custom-call | flops 603979776 | bytes 2930688 | tf_op jit(solution)/shard_map/ffn/pallas_call | solution.py:53
  32.9 0.1 collective-permute-start.6
  33.0 1.6 %collective-permute-start.7 = (bf16[64,768]{1,0:T(8,128)(2,1)S(1)}, bf16[64,768]{1,0:T(8,128)(2,1)S(1)}, u32[]{:S(2)}, u32[]{:S(2)}) collective-permute-start(bf16[64,768]{1,0:T(8,128)(2,1)S(1)} %get-tuple-element.44), channel_id=1, source_target_pairs={{0,2},{1,3},{2,0},{3,1},{4,6},{5,7},{6,4},{7,5},{8,10},{9,11},{10,... | collective-permute-start | bytes 294920 | tf_op jit(solution)/shard_map/ppermute | solution.py:352
  34.6 0.3 collective-permute-start.8
  34.9 0.0 copy-done.3
  34.9 0.0 copy-done.11
  34.9 0.9 %own.1 = (bf16[512,384]{1,0:T(8,128)(2,1)S(1)}, bf16[512,192]{1,0:T(8,128)(2,1)S(1)}) custom-call(bf16[512,768]{1,0:T(8,128)(2,1)S(1)} %copy-done.11, bf16[3,192,768]{2,1,0:T(8,128)(2,1)S(1)} %bitcast.10), custom_call_target="tpu_custom_call" | custom-call | flops 2000000000 | bytes 1671168 | tf_op jit(solution)/shard_map/own/pallas_call | solution.py:53
  35.8 0.0 copy-start.5
  35.8 0.0 copy-start.9
  35.8 0.0 copy-start.10
  35.8 0.0 collective-permute-done.6.refs_3_
  35.8 2.9 %collective-permute-done.7.refs_4_ = bf16[64,768]{1,0:T(8,128)(2,1)S(1)} collective-permute-done((bf16[64,768]{1,0:T(8,128)(2,1)S(1)}, bf16[64,768]{1,0:T(8,128)(2,1)S(1)}, u32[]{:S(2)}, u32[]{:S(2)}) %collective-permute-start.7) | collective-permute-done | bytes 98336 | tf_op jit(solution)/shard_map/ppermute | solution.py:352
  38.7 1.2 %collective-permute-done.8.refs_5_ = bf16[64,768]{1,0:T(8,128)(2,1)S(1)} collective-permute-done((bf16[64,768]{1,0:T(8,128)(2,1)S(1)}, bf16[64,768]{1,0:T(8,128)(2,1)S(1)}, u32[]{:S(2)}, u32[]{:S(2)}) %collective-permute-start.8) | collective-permute-done | bytes 98336 | tf_op jit(solution)/shard_map/ppermute | solution.py:352
  39.9 0.2 norm_two.1.refs_0_.refs_1_
  40.1 1.6 %collective-permute-start.9 = (bf16[64,768]{1,0:T(8,128)(2,1)S(1)}, bf16[64,768]{1,0:T(8,128)(2,1)S(1)}, u32[]{:S(2)}, u32[]{:S(2)}) collective-permute-start(bf16[64,768]{1,0:T(8,128)(2,1)S(1)} %norm_two.1.refs_0_.refs_1_), channel_id=1, source_target_pairs={{0,2},{1,3},{2,0},{3,1},{4,6},{5,7},{6,4},{7,5},{8,10},{9,11},{10,... | collective-permute-start | bytes 294920 | tf_op jit(solution)/shard_map/ppermute | solution.py:352
  41.7 3.5 %collective-permute-done.9.refs_1_.refs_2_ = bf16[64,768]{1,0:T(8,128)(2,1)S(1)} collective-permute-done((bf16[64,768]{1,0:T(8,128)(2,1)S(1)}, bf16[64,768]{1,0:T(8,128)(2,1)S(1)}, u32[]{:S(2)}, u32[]{:S(2)}) %collective-permute-start.9) | collective-permute-done | bytes 98336 | tf_op jit(solution)/shard_map/ppermute | solution.py:352
  45.2 0.1 collective-permute-start.10
  45.3 3.3 %collective-permute-start.12 = (bf16[2,768]{1,0:T(2,128)(2,1)S(1)}, bf16[2,768]{1,0:T(2,128)(2,1)S(1)}, u32[]{:S(2)}, u32[]{:S(2)}) collective-permute-start(bf16[2,768]{1,0:T(2,128)(2,1)S(1)} %get-tuple-element.46.refs_8_), channel_id=1, source_target_pairs={{0,16},{1,21},{2,26},{3,31},{4,20},{5,17},{6,30},{7,27},{8,24},{9,... | collective-permute-start | bytes 9224 | tf_op jit(solution)/shard_map/ppermute | solution.py:406
  48.5 0.8 %collective-permute-start.11 = (bf16[2,768]{1,0:T(2,128)(2,1)S(1)}, bf16[2,768]{1,0:T(2,128)(2,1)S(1)}, u32[]{:S(2)}, u32[]{:S(2)}) collective-permute-start(bf16[2,768]{1,0:T(2,128)(2,1)S(1)} %get-tuple-element.46.refs_8_), channel_id=1, source_target_pairs={{1,5},{2,10},{3,15},{5,1},{6,14},{7,11},{9,13},{10,2},{11,7},{13,9... | collective-permute-start | bytes 9224 | tf_op jit(solution)/shard_map/ppermute | solution.py:406
  49.4 0.0 collective-permute-done.10.refs_3_
  49.4 1.3 %place.1 = bf16[256,768]{1,0:T(8,128)(2,1)} custom-call(s32[4]{0:T(128)S(1)} %iota_xor_fusion.refs_0_, bf16[64,768]{1,0:T(8,128)(2,1)S(1)} %norm_two.1.refs_0_.refs_1_, bf16[64,768]{1,0:T(8,128)(2,1)S(1)} %collective-permute-done.9.refs_1_.refs_2_, bf16[128,768]{1,0:T(8,128)(2,1)S(1)} %collective-permute-done.10.refs_3_), custom_call_target="tpu_custom_call" | custom-call | bytes 393232 | tf_op jit(solution)/shard_map/place/pallas_call | solution.py:53
  50.7 0.0 collective-permute-done.12.refs_1_
  50.7 0.0 copy-done.5
  50.7 0.0 collective-permute-done.11.refs_0_
  50.7 0.0 all-to-all-done
  50.8 6.2 %collective-permute-start.15 = (bf16[16,768]{1,0:T(8,128)(2,1)S(1)}, bf16[16,768]{1,0:T(8,128)(2,1)S(1)}, u32[]{:S(2)}, u32[]{:S(2)}) collective-permute-start(bf16[16,768]{1,0:T(8,128)(2,1)S(1)} %pack.1.refs_9_), channel_id=1, source_target_pairs={{0,3},{1,2},{2,1},{3,0},{4,7},{5,6},{6,5},{7,4},{8,11},{9,10},{10,... | collective-permute-start | bytes 73736 | tf_op jit(solution)/shard_map/ppermute | solution.py:352
  56.9 0.0 collective-permute-start.14
  56.9 0.2 collective-permute-start.13
  57.1 1.3 %collective-permute-done.15.refs_12_ = bf16[16,768]{1,0:T(8,128)(2,1)S(1)} collective-permute-done((bf16[16,768]{1,0:T(8,128)(2,1)S(1)}, bf16[16,768]{1,0:T(8,128)(2,1)S(1)}, u32[]{:S(2)}, u32[]{:S(2)}) %collective-permute-start.15) | collective-permute-done | bytes 24608 | tf_op jit(solution)/shard_map/ppermute | solution.py:352
  58.5 2.3 %collective-permute-done.14.refs_11_ = bf16[16,768]{1,0:T(8,128)(2,1)S(1)} collective-permute-done((bf16[16,768]{1,0:T(8,128)(2,1)S(1)}, bf16[16,768]{1,0:T(8,128)(2,1)S(1)}, u32[]{:S(2)}, u32[]{:S(2)}) %collective-permute-start.14) | collective-permute-done | bytes 24608 | tf_op jit(solution)/shard_map/ppermute | solution.py:352
  60.8 0.0 collective-permute-done.13.refs_10_
  60.8 0.0 copy-done.9
  60.8 0.0 copy-done.10
  60.8 0.0 copy-start.6
  60.8 1.0 %copy-done.6 = bf16[512,384]{1,0:T(8,128)(2,1)S(1)} copy-done((bf16[512,384]{1,0:T(8,128)(2,1)S(1)}, bf16[512,384]{1,0:T(8,128)(2,1)}, u32[]{:S(2)}) %copy-start.6) | copy-done | bytes 393240
  61.8 4.5 %graph.1 = bf16[192,512]{1,0:T(8,128)(2,1)} custom-call(s32[4]{0:T(128)S(1)} %iota_xor_fusion.refs_0_, s32[4,6]{1,0:T(4,128)S(1)} %copy-done.9, s32[2]{0:T(128)S(1)} %copy-done.10, bf16[512,192]{1,0:T(8,128)(2,1)S(1)} %get-tuple-element.48.refs_3_, bf16[512,384]{1,0:T(8,128)(2,1)S(1)} %copy-done.6, bf16[3,192,768]{2,1,0:T(8,128)(2,1)S(1)} %bitcast.11, ...), custom_call_target="tpu_custom_call" | custom-call | flops 1000000000 | bytes 3935352 | tf_op jit(solution)/shard_map/graph/pallas_call | solution.py:53
  (8 shorter events, 0.0 us)
Async XLA Ops:
  4.7 7.5 %copy-start.2 = (bf16[256,768]{1,0:T(8,128)(2,1)S(1)}, bf16[256,768]{1,0:T(8,128)(2,1)}, u32[]{:S(2)}) copy-start(bf16[256,768]{1,0:T(8,128)(2,1)} %refs_1_.6) | copy-start | bytes 1179652
  4.8 7.5 %copy-start.4 = (bf16[3,768,192]{1,2,0:T(8,128)(2,1)S(1)}, bf16[3,768,192]{1,2,0:T(8,128)(2,1)}, u32[]{:S(2)}) copy-start(bf16[3,768,192]{1,2,0:T(8,128)(2,1)} %param.13) | copy-start | bytes 2654212
  4.8 7.5 %copy-start.7 = (bf16[192,768]{1,0:T(8,128)(2,1)S(1)}, bf16[192,768]{1,0:T(8,128)(2,1)}, u32[]{:S(2)}) copy-start(bf16[192,768]{1,0:T(8,128)(2,1)} %refs_3_.4) | copy-start | bytes 884740
  4.8 45.9 %all-to-all-start = ((bf16[8,256,384]{2,1,0:T(8,128)(2,1)}), bf16[8,256,384]{2,1,0:T(8,128)(2,1)S(1)}, u32[]{:S(2)}, u32[]{:S(2)}) async-start(bf16[8,256,384]{2,1,0:T(8,128)(2,1)} %bitcast.14), calls=%async_computation | async-start | bytes 3145728 | tf_op jit(solution)/shard_map/all_to_all | solution.py:368
  12.2 4.3 %copy-start.12 = (s32[512,16]{0,1:T(8,128)S(1)}, s32[512,16]{0,1:T(8,128)}, u32[]{:S(2)}) copy-start(s32[512,16]{0,1:T(8,128)} %param.23) | copy-start | bytes 98308
  14.5 6.2 %collective-permute-start = (bf16[80,768]{1,0:T(8,128)(2,1)S(1)}, bf16[80,768]{1,0:T(8,128)(2,1)S(1)}, u32[]{:S(2)}, u32[]{:S(2)}) collective-permute-start(bf16[80,768]{1,0:T(8,128)(2,1)S(1)} %get-tuple-element.30), channel_id=1, source_target_pairs={{0,1},{1,0},{2,3},{3,2},{4,5},{5,4},{6,7},{7,6},{8,9},{9,8},{10,11... | collective-permute-start | bytes 368648 | tf_op jit(solution)/shard_map/ppermute | solution.py:352
  14.6 6.2 %collective-permute-start.1 = (bf16[80,768]{1,0:T(8,128)(2,1)S(1)}, bf16[80,768]{1,0:T(8,128)(2,1)S(1)}, u32[]{:S(2)}, u32[]{:S(2)}) collective-permute-start(bf16[80,768]{1,0:T(8,128)(2,1)S(1)} %get-tuple-element.31), channel_id=1, source_target_pairs={{0,2},{1,3},{2,0},{3,1},{4,6},{5,7},{6,4},{7,5},{8,10},{9,11},{10,... | collective-permute-start | bytes 368648 | tf_op jit(solution)/shard_map/ppermute | solution.py:352
  16.2 6.3 %collective-permute-start.2 = (bf16[80,768]{1,0:T(8,128)(2,1)S(1)}, bf16[80,768]{1,0:T(8,128)(2,1)S(1)}, u32[]{:S(2)}, u32[]{:S(2)}) collective-permute-start(bf16[80,768]{1,0:T(8,128)(2,1)S(1)} %get-tuple-element.32), channel_id=1, source_target_pairs={{0,3},{1,2},{2,1},{3,0},{4,7},{5,6},{6,5},{7,4},{8,11},{9,10},{10,... | collective-permute-start | bytes 368648 | tf_op jit(solution)/shard_map/ppermute | solution.py:352
  16.4 6.1 %copy-start = (bf16[768,768]{1,0:T(8,128)(2,1)S(1)}, bf16[768,768]{1,0:T(8,128)(2,1)}, u32[]{:S(2)}) copy-start(bf16[768,768]{1,0:T(8,128)(2,1)} %refs_0_.3) | copy-start | bytes 3538948
  16.4 6.1 %copy-start.1 = (bf16[768,768]{1,0:T(8,128)(2,1)S(1)}, bf16[768,768]{1,0:T(8,128)(2,1)}, u32[]{:S(2)}) copy-start(bf16[768,768]{1,0:T(8,128)(2,1)} %refs_1_.7) | copy-start | bytes 3538948
  16.4 6.1 %copy-start.8 = (f32[2,768]{1,0:T(2,128)S(1)}, f32[2,768]{1,0:T(2,128)}, u32[]{:S(2)}) copy-start(f32[2,768]{1,0:T(2,128)} %refs_1_.8) | copy-start | bytes 18436
  23.8 11.1 %copy-start.3 = (bf16[3,768,192]{1,2,0:T(8,128)(2,1)S(1)}, bf16[3,768,192]{1,2,0:T(8,128)(2,1)}, u32[]{:S(2)}) copy-start(bf16[3,768,192]{1,2,0:T(8,128)(2,1)} %param.19) | copy-start | bytes 2654212
  23.8 11.1 %copy-start.11 = (bf16[512,768]{1,0:T(8,128)(2,1)S(1)}, bf16[512,768]{1,0:T(8,128)(2,1)}, u32[]{:S(2)}) copy-start(bf16[512,768]{1,0:T(8,128)(2,1)} %refs_0_.2) | copy-start | bytes 2359300
  23.8 5.4 %collective-permute-start.5 = (bf16[80,768]{1,0:T(8,128)(2,1)S(1)}, bf16[80,768]{1,0:T(8,128)(2,1)S(1)}, u32[]{:S(2)}, u32[]{:S(2)}) collective-permute-start(bf16[80,768]{1,0:T(8,128)(2,1)S(1)} %get-tuple-element.39.refs_5_.refs_0_), channel_id=1, source_target_pairs={{0,3},{1,2},{2,1},{3,0},{4,7},{5,6},{6,5},{7,4},{8,11},{9,10},{10,... | collective-permute-start | bytes 368648 | tf_op jit(solution)/shard_map/ppermute | solution.py:352
  25.5 6.6 %collective-permute-start.4 = (bf16[80,768]{1,0:T(8,128)(2,1)S(1)}, bf16[80,768]{1,0:T(8,128)(2,1)S(1)}, u32[]{:S(2)}, u32[]{:S(2)}) collective-permute-start(bf16[80,768]{1,0:T(8,128)(2,1)S(1)} %get-tuple-element.39.refs_5_.refs_0_), channel_id=1, source_target_pairs={{0,2},{1,3},{2,0},{3,1},{4,6},{5,7},{6,4},{7,5},{8,10},{9,11},{10,... | collective-permute-start | bytes 368648 | tf_op jit(solution)/shard_map/ppermute | solution.py:352
  26.0 6.1 %collective-permute-start.3 = (bf16[80,768]{1,0:T(8,128)(2,1)S(1)}, bf16[80,768]{1,0:T(8,128)(2,1)S(1)}, u32[]{:S(2)}, u32[]{:S(2)}) collective-permute-start(bf16[80,768]{1,0:T(8,128)(2,1)S(1)} %get-tuple-element.39.refs_5_.refs_0_), channel_id=1, source_target_pairs={{0,1},{1,0},{2,3},{3,2},{4,5},{5,4},{6,7},{7,6},{8,9},{9,8},{10,11... | collective-permute-start | bytes 368648 | tf_op jit(solution)/shard_map/ppermute | solution.py:352
  32.9 2.8 %collective-permute-start.6 = (bf16[64,768]{1,0:T(8,128)(2,1)S(1)}, bf16[64,768]{1,0:T(8,128)(2,1)S(1)}, u32[]{:S(2)}, u32[]{:S(2)}) collective-permute-start(bf16[64,768]{1,0:T(8,128)(2,1)S(1)} %get-tuple-element.43), channel_id=1, source_target_pairs={{0,1},{1,0},{2,3},{3,2},{4,5},{5,4},{6,7},{7,6},{8,9},{9,8},{10,11... | collective-permute-start | bytes 294920 | tf_op jit(solution)/shard_map/ppermute | solution.py:352
  33.0 5.7 %collective-permute-start.7 = (bf16[64,768]{1,0:T(8,128)(2,1)S(1)}, bf16[64,768]{1,0:T(8,128)(2,1)S(1)}, u32[]{:S(2)}, u32[]{:S(2)}) collective-permute-start(bf16[64,768]{1,0:T(8,128)(2,1)S(1)} %get-tuple-element.44), channel_id=1, source_target_pairs={{0,2},{1,3},{2,0},{3,1},{4,6},{5,7},{6,4},{7,5},{8,10},{9,11},{10,... | collective-permute-start | bytes 294920 | tf_op jit(solution)/shard_map/ppermute | solution.py:352
  34.6 5.3 %collective-permute-start.8 = (bf16[64,768]{1,0:T(8,128)(2,1)S(1)}, bf16[64,768]{1,0:T(8,128)(2,1)S(1)}, u32[]{:S(2)}, u32[]{:S(2)}) collective-permute-start(bf16[64,768]{1,0:T(8,128)(2,1)S(1)} %get-tuple-element.45), channel_id=1, source_target_pairs={{0,3},{1,2},{2,1},{3,0},{4,7},{5,6},{6,5},{7,4},{8,11},{9,10},{10,... | collective-permute-start | bytes 294920 | tf_op jit(solution)/shard_map/ppermute | solution.py:352
  35.8 15.0 %copy-start.5 = (bf16[512,384]{1,0:T(8,128)(2,1)}, bf16[512,384]{1,0:T(8,128)(2,1)S(1)}, u32[]{:S(2)}) copy-start(bf16[512,384]{1,0:T(8,128)(2,1)S(1)} %get-tuple-element.49.refs_4_) | copy-start | bytes 1179652
  35.8 25.0 %copy-start.9 = (s32[4,6]{1,0:T(4,128)S(1)}, s32[4,6]{1,0:T(4,128)}, u32[]{:S(2)}) copy-start(s32[4,6]{1,0:T(4,128)} %refs_1_.9) | copy-start | bytes 292
  35.8 25.0 %copy-start.10 = (s32[2]{0:T(128)S(1)}, s32[2]{0:T(128)}, u32[]{:S(2)}) copy-start(s32[2]{0:T(128)} %refs_2_.5) | copy-start | bytes 28
  40.1 5.0 %collective-permute-start.9 = (bf16[64,768]{1,0:T(8,128)(2,1)S(1)}, bf16[64,768]{1,0:T(8,128)(2,1)S(1)}, u32[]{:S(2)}, u32[]{:S(2)}) collective-permute-start(bf16[64,768]{1,0:T(8,128)(2,1)S(1)} %norm_two.1.refs_0_.refs_1_), channel_id=1, source_target_pairs={{0,2},{1,3},{2,0},{3,1},{4,6},{5,7},{6,4},{7,5},{8,10},{9,11},{10,... | collective-permute-start | bytes 294920 | tf_op jit(solution)/shard_map/ppermute | solution.py:352
  45.2 4.2 %collective-permute-start.10 = (bf16[128,768]{1,0:T(8,128)(2,1)S(1)}, bf16[128,768]{1,0:T(8,128)(2,1)S(1)}, u32[]{:S(2)}, u32[]{:S(2)}) collective-permute-start(bf16[128,768]{1,0:T(8,128)(2,1)S(1)} %join.1), channel_id=1, source_target_pairs={{0,1},{1,0},{2,3},{3,2},{4,5},{5,4},{6,7},{7,6},{8,9},{9,8},{10,11... | collective-permute-start | bytes 589832 | tf_op jit(solution)/shard_map/ppermute | solution.py:352
  45.3 5.4 %collective-permute-start.12 = (bf16[2,768]{1,0:T(2,128)(2,1)S(1)}, bf16[2,768]{1,0:T(2,128)(2,1)S(1)}, u32[]{:S(2)}, u32[]{:S(2)}) collective-permute-start(bf16[2,768]{1,0:T(2,128)(2,1)S(1)} %get-tuple-element.46.refs_8_), channel_id=1, source_target_pairs={{0,16},{1,21},{2,26},{3,31},{4,20},{5,17},{6,30},{7,27},{8,24},{9,... | collective-permute-start | bytes 9224 | tf_op jit(solution)/shard_map/ppermute | solution.py:406
  48.5 2.2 %collective-permute-start.11 = (bf16[2,768]{1,0:T(2,128)(2,1)S(1)}, bf16[2,768]{1,0:T(2,128)(2,1)S(1)}, u32[]{:S(2)}, u32[]{:S(2)}) collective-permute-start(bf16[2,768]{1,0:T(2,128)(2,1)S(1)} %get-tuple-element.46.refs_8_), channel_id=1, source_target_pairs={{1,5},{2,10},{3,15},{5,1},{6,14},{7,11},{9,13},{10,2},{11,7},{13,9... | collective-permute-start | bytes 9224 | tf_op jit(solution)/shard_map/ppermute | solution.py:406
  50.8 7.7 %collective-permute-start.15 = (bf16[16,768]{1,0:T(8,128)(2,1)S(1)}, bf16[16,768]{1,0:T(8,128)(2,1)S(1)}, u32[]{:S(2)}, u32[]{:S(2)}) collective-permute-start(bf16[16,768]{1,0:T(8,128)(2,1)S(1)} %pack.1.refs_9_), channel_id=1, source_target_pairs={{0,3},{1,2},{2,1},{3,0},{4,7},{5,6},{6,5},{7,4},{8,11},{9,10},{10,... | collective-permute-start | bytes 73736 | tf_op jit(solution)/shard_map/ppermute | solution.py:352
  56.9 3.8 %collective-permute-start.14 = (bf16[16,768]{1,0:T(8,128)(2,1)S(1)}, bf16[16,768]{1,0:T(8,128)(2,1)S(1)}, u32[]{:S(2)}, u32[]{:S(2)}) collective-permute-start(bf16[16,768]{1,0:T(8,128)(2,1)S(1)} %pack.1.refs_9_), channel_id=1, source_target_pairs={{0,2},{1,3},{2,0},{3,1},{4,6},{5,7},{6,4},{7,5},{8,10},{9,11},{10,... | collective-permute-start | bytes 73736 | tf_op jit(solution)/shard_map/ppermute | solution.py:352
  56.9 3.8 %collective-permute-start.13 = (bf16[16,768]{1,0:T(8,128)(2,1)S(1)}, bf16[16,768]{1,0:T(8,128)(2,1)S(1)}, u32[]{:S(2)}, u32[]{:S(2)}) collective-permute-start(bf16[16,768]{1,0:T(8,128)(2,1)S(1)} %pack.1.refs_9_), channel_id=1, source_target_pairs={{0,1},{1,0},{2,3},{3,2},{4,5},{5,4},{6,7},{7,6},{8,9},{9,8},{10,11... | collective-permute-start | bytes 73736 | tf_op jit(solution)/shard_map/ppermute | solution.py:352
  60.8 1.0 %copy-start.6 = (bf16[512,384]{1,0:T(8,128)(2,1)S(1)}, bf16[512,384]{1,0:T(8,128)(2,1)}, u32[]{:S(2)}) copy-start(bf16[512,384]{1,0:T(8,128)(2,1)} %copy-done.5) | copy-start | bytes 1179652

commit v8 on v7

--- a/solution.py
+++ b/solution.py
@@ -26,10 +26,21 @@
 
 
 def call(
-    kernel, outs, args, smem=(), hbm=(), scalars=(), scratch=(), out_specs=None, flops=0, name=None
+    kernel,
+    outs,
+    args,
+    smem=(),
+    hbm=(),
+    held=(),
+    scalars=(),
+    scratch=(),
+    out_specs=None,
+    late=False,
+    flops=0,
+    name=None,
 ):
     count, out_count, own = len(args), len(jax.tree.leaves(outs)), len(scratch)
-    specs = [SMEM if i in smem else HBM if i in hbm else VMEM for i in range(count)]
+    specs = [SMEM if i in smem else HBM if i in hbm or i in held else VMEM for i in range(count)]
     nbytes = sum(a.size * a.dtype.itemsize for a in args)
     space = [pltpu.SMEM if i in scalars else pltpu.VMEM for i in hbm]
     buffers = [kind(args[i].shape, args[i].dtype) for kind, i in zip(space, hbm)]
@@ -41,13 +52,19 @@
         moves = {}
         for j, i in enumerate(hbm):
             moves[i] = pltpu.make_async_copy(ins[i], moved[j], moved[-1].at[j])
-            moves[i].start()
             ins[i] = moved[j]
+
+        def start():
+            for move in moves.values():
+                move.start()
 
         def ready(*wanted):
             for i in wanted:
                 moves[i].wait()
 
+        ready.start = start
+        if not late:
+            start()
         kernel(ready, *ins, *kept)
 
     return pl.pallas_call(
@@ -243,26 +260,13 @@
         out[pl.ds(pl.multiple_of(who_ref[step] * chunk, chunk), chunk), :] = piece
 
 
-def own_kernel(ready, table_ref, w_ref, kv_ref, q_ref):
+def own_kernel(
+    ready, who_ref, at_ref, table_ref, w_ref, first_ref, *refs
+):
+    *packs, kv_ref, q_ref, first_kv_ref, features, firsts = refs
+    members = len(packs)
+    per_part, width = first_ref.shape
     cols = w_ref.shape[1]
-    table = table_ref[...]
-    kv_ref[:, :cols] = dot_nt(table, w_ref[1]).astype(bf)
-    kv_ref[:, cols:] = dot_nt(table, w_ref[2]).astype(bf)
-    q_ref[...] = dot_nt(table, w_ref[0]).astype(bf)
-
-
-def tail_rows(count):
-    return -(-count // PAD) * PAD
-
-
-def graph_kernel(
-    ready, who_ref, cols_ref, at_ref, q_ref, kv_ref, w_ref, mask_ref, far_ref, first_ref, *refs
-):
-    *packs, out_ref, k_all, v_all, firsts = refs
-    nodes, cols = q_ref.shape
-    row_tiles = nodes // TILE
-    per_part = first_ref.shape[0]
-    members = len(packs)
     for step, ref in enumerate(packs):
         rows = ref[...].astype(f32)
         for turn in range(firsts.shape[0] // per_part // members):
@@ -271,21 +275,46 @@
                 at = turn * per_part + title
                 firsts[pl.ds(place, 1), :] = rows[at : at + 1]
     firsts[0:per_part, :] = first_ref[...].astype(f32)
+    ready(1, 2)
+    for tile in range(features.shape[0] // TILE):
+        span = slice(tile * TILE, (tile + 1) * TILE)
+        rows = table_ref[span, :].astype(f32)
+        sub = lax.broadcasted_iota(jnp.int32, (TILE, width), 0) + tile * TILE
+        for title in range(per_part):
+            rows = jnp.where(sub == at_ref[title], firsts[title : title + 1, :], rows)
+        features[span, :] = rows.astype(bf)
     first = firsts[...].astype(bf)
-    first_kv = jnp.concatenate([dot_nt(first, w_ref[1]), dot_nt(first, w_ref[2])], axis=1).astype(bf)
-    first_q = dot_nt(first, w_ref[0])
-    for tile in range(row_tiles):
-        span = slice(tile * TILE, (tile + 1) * TILE)
-        rows = kv_ref[span, :].astype(f32)
-        sub = lax.broadcasted_iota(jnp.int32, (TILE, 2 * cols), 0) + tile * TILE
-        for title in range(per_part):
-            row = first_kv[title : title + 1].astype(f32)
-            rows = jnp.where(sub == at_ref[title], row, rows)
-        rows = rows.astype(bf)
-        k_all[span, :] = rows[:, :cols]
-        v_all[span, :] = rows[:, cols:]
+    table = features[...]
+    ready(3)
+    for j in (1, 2):
+        span = slice((j - 1) * cols, j * cols)
+        first_kv_ref[:, span] = dot_nt(first, w_ref[j]).astype(bf)
+        kv_ref[:, span] = dot_nt(table, w_ref[j]).astype(bf)
+    q_ref[...] = dot_nt(table, w_ref[0]).astype(bf)
+
+
+def tail_rows(count):
+    return -(-count // PAD) * PAD
+
+
+def graph_kernel(
+    ready, cols_ref, q_ref, kv_ref, first_ref, mask_ref, far_hbm, out_ref, k_all, v_all, far_ref, sems
+):
+    pieces = sems.shape[0]
+    size = far_ref.shape[0] // pieces
+    moves = []
+    for piece in range(pieces):
+        at = pl.ds(piece * size, size)
+        moves.append(pltpu.make_async_copy(far_hbm.at[at, :], far_ref.at[at, :], sems.at[piece]))
+        moves[-1].start()
+    ready.start()
+    nodes, cols = q_ref.shape
+    row_tiles = nodes // TILE
+    first_kv = first_ref[...]
     lanes = lax.broadcasted_iota(jnp.int32, (TILE, first_kv.shape[0]), 1).astype(f32)
     for tile in range(far_ref.shape[0] // TILE):
+        if tile * TILE % size == 0:
+            moves[tile * TILE // size].wait()
         rows = far_ref[tile * TILE : (tile + 1) * TILE, :].astype(f32)
         code = jnp.where(rows[:, 0:1] != rows[:, 0:1], rows[:, 1:2], -1.0)
         hot = jnp.where(lanes == code, 1.0, 0.0).astype(bf)
@@ -294,14 +323,14 @@
         k_all[span, :] = fixed[:, :cols]
         v_all[span, :] = fixed[:, cols:]
 
+    ready(2)
+    k_all[:nodes, :] = kv_ref[:, :cols]
+    v_all[:nodes, :] = kv_ref[:, cols:]
+    ready(0, 1, 4)
     heads = cols // GHD
     head_of = lax.broadcasted_iota(jnp.int32, (TILE, cols), 1) // GHD
     for tile in range(row_tiles):
-        q = q_ref[tile * TILE : (tile + 1) * TILE, :].astype(f32)
-        sub = lax.broadcasted_iota(jnp.int32, (TILE, cols), 0) + tile * TILE
-        for title in range(per_part):
-            q = jnp.where(sub == at_ref[title], first_q[title : title + 1], q)
-        q = q.astype(bf)
+        q = q_ref[tile * TILE : (tile + 1) * TILE, :]
         stacked = jnp.concatenate(
             [jnp.where(head_of == h, q, jnp.zeros_like(q)) for h in range(heads)], axis=0
         )
@@ -415,20 +444,15 @@
         )
         for turn in range(turns)
     ]
-    kv, q = call(
-        own_kernel,
-        (shape((nodes, 2 * cols), bf), shape((nodes, cols), bf)),
-        (node_table, w_graph),
-        flops=2 * 10**9,
-        name="own",
-    )
-    hidden, kv, q = lax.optimization_barrier((hidden, kv, q))
+    parts, firsts = lax.optimization_barrier((parts, firsts))
     done = call(
         norm_two_kernel,
         shape((chunk, width), bf),
         (hidden, gains, terms[0], *parts),
         name="norm_two",
     )
+    pack = call(pack_kernel, shape((tail_rows(turns * per_part), width), bf), firsts, name="pack")
+    packs = [pack] + [swap(pack, step) for step in range(1, mp)]
     whose, blocks, step = [0], [done], mp // 2
     while step:
         rows = blocks[0]
@@ -445,20 +469,33 @@
         smem=(0,),
         name="place",
     )
-    encoded, firsts, far = lax.optimization_barrier((encoded, firsts, far))
-    pack = call(pack_kernel, shape((tail_rows(turns * per_part), width), bf), firsts, name="pack")
-    packs = [pack] + [swap(pack, step) for step in range(1, mp)]
-
+    encoded, far = lax.optimization_barrier((encoded, far))
+
+    kv, q, first_kv = call(
+        own_kernel,
+        (shape((nodes, 2 * cols), bf), shape((nodes, cols), bf), shape((dp * per_part, 2 * cols), bf)),
+        (who, title_nodes, node_table, w_graph, first, *packs),
+        smem=(0,),
+        hbm=(1, 2, 3),
+        scalars=(1,),
+        scratch=[pltpu.VMEM((nodes, width), bf), pltpu.VMEM((dp * per_part, width), f32)],
+        flops=2 * 10**9,
+        name="own",
+    )
     keys = nodes + dp * fetch
     graph_out = call(
         graph_kernel,
         shape((cols, nodes), bf),
-        (who, tile_cols, title_nodes, q, kv, w_graph, mask, far, first, *packs),
-        smem=(0, 1, 2),
+        (tile_cols, q, kv, first_kv, mask, far),
+        hbm=(2, 1, 4, 0),
+        held=(5,),
+        scalars=(0,),
+        late=True,
         scratch=[
             pltpu.VMEM((keys, cols), bf),
             pltpu.VMEM((keys, cols), bf),
-            pltpu.VMEM((dp * per_part, width), f32),
+            pltpu.VMEM(far.shape, bf),
+            pltpu.SemaphoreType.DMA((4,)),
         ],
         flops=10**9,
         name="graph",

time: 66.6 us -> 69.9 us (1.050)
  starting transfers between devices: 25.6 us -> 19.5 us
  Pallas kernels: 19.7 us -> 24.9 us
  waiting for transfers between devices: 19 us -> 21.5 us
  local copies, waits for them, and re-layouts: 1.05 us -> 2.43 us
    ppermute x2, waiting for transfers between devices: 0.01 us -> 10.7 us  [local(): lax.ppermute(first, ('dp', 'mp'), [(p * mp + m, (p ^ turn * mp + m) * mp...]
    ppermute x14, waiting for transfers between devices: 19 us -> 10.9 us  [swap(): lax.ppermute(value, axis, [(i, i ^ step) for i in range(lax.axis_size(axi...]
    ppermute x14, starting transfers between devices: 14.1 us -> 8.41 us  [swap(): lax.ppermute(value, axis, [(i, i ^ step) for i in range(lax.axis_size(axi...]
    pallas_call x11, Pallas kernels: 19.7 us -> 24.9 us  [call(): pl.pallas_call(body, out_shape=outs, in_specs=specs, out_specs=jax.tree.m...]
    unnamed x26 -> x32, local copies, waits for them, and re-layouts: 1.05 us -> 2.43 us
  transfers between devices with their start and end apart: 17 -> 17, of which waited for: 9 -> 6; matrix products, arithmetic and copies ran while one was open for 0% -> 0% of each run, Pallas kernels for 17% -> 21%
where the time goes in v8:
time: 69.9 us; the launch traced here: 69.5 us
  Pallas kernels  24.9 us (36%)
  waiting for transfers between devices  21.5 us (31%)
  starting transfers between devices  19.5 us (28%)
  local copies, waits for them, and re-layouts  2.43 us (3%)
  between operations  1.1 us (2%)
    pallas_call x11, Pallas kernels, call(): pl.pallas_call(body, out_shape=outs, in_specs=specs, out_specs=jax.tree.m...  24.9 us
    ppermute x14, waiting for transfers between devices, swap(): lax.ppermute(value, axis, [(i, i ^ step) for i in range(lax.axis_size(axi...  10.9 us
    ppermute x2, waiting for transfers between devices, local(): lax.ppermute(first, ('dp', 'mp'), [(p * mp + m, (p ^ turn * mp + m) * mp...  10.7 us
    ppermute x14, starting transfers between devices, swap(): lax.ppermute(value, axis, [(i, i ^ step) for i in range(lax.axis_size(axi...  8.41 us
    all_to_all x1, starting transfers between devices, local(): lax.all_to_all(sent.reshape(dp, fetch, 2 * cols), 'dp', split_axis=0, con...  7.4 us
    ppermute x2, starting transfers between devices, local(): lax.ppermute(first, ('dp', 'mp'), [(p * mp + m, (p ^ turn * mp + m) * mp...  3.74 us
    unnamed x32, local copies, waits for them, and re-layouts  2.43 us
  transfers between devices with their start and end apart: 17, of which 6 were waited for; matrix products, arithmetic and copies ran while one was open for 0% of the time, Pallas kernels for 21%

profile of v8, /device:TPU:0, one launch (start us, length us, event | category | flops | bytes accessed | tf_op | source)
XLA Modules:
  0.0 69.5 jit_solution(15410858459320575983)
XLA Ops:
  0.6 4.1 %send.1 = bf16[2048,384]{1,0:T(8,128)(2,1)} custom-call(s32[1]{0:T(128)} %bitcast.refs_0_, s32[2]{0:T(128)} %refs_1_.9, s32[8,256]{1,0:T(8,128)} %bitcast.14, bf16[512,768]{1,0:T(8,128)(2,1)} %refs_2_.5, bf16[3,192,768]{2,1,0:T(8,128)(2,1)} %bitcast.12), custom_call_target="tpu_custom_call" | custom-call | flops 1107296256 | bytes 1679372 | tf_op jit(solution)/shard_map/send/pallas_call | solution.py:70
  4.7 0.0 copy-start.2
  4.8 0.0 copy-start.3
  4.8 0.0 copy-start.4
  4.8 7.4 %all-to-all-start = ((bf16[8,256,384]{2,1,0:T(8,128)(2,1)}), bf16[8,256,384]{2,1,0:T(8,128)(2,1)S(1)}, u32[]{:S(2)}, u32[]{:S(2)}) async-start(bf16[8,256,384]{2,1,0:T(8,128)(2,1)} %bitcast.11), calls=%async_computation | async-start | bytes 3145728 | tf_op jit(solution)/shard_map/all_to_all | solution.py:397
  12.2 0.0 copy-start.7
  12.2 0.0 copy-done.2
  12.2 0.0 copy-done.3
  12.2 0.0 copy-done.4
  12.2 2.3 %attn.1 = (f32[80,768]{1,0:T(8,128)S(1)}, bf16[80,768]{1,0:T(8,128)(2,1)S(1)}, bf16[80,768]{1,0:T(8,128)(2,1)S(1)}, bf16[80,768]{1,0:T(8,128)(2,1)S(1)}) custom-call(s32[4]{0:T(128)S(1)} %iota_xor_fusion.refs_0_, bf16[256,768]{1,0:T(8,128)(2,1)S(1)} %copy-done.2, bf16[3,192,768]{2,1,0:T(8,128)(2,1)S(1)} %bitcast.8, bf16[192,768]{1,0:T(8,128)(2,1)S(1)} %copy-done.4), custom_call_target="tpu_custom_call" | custom-call | flops 301989888 | bytes 1572880 | tf_op jit(solution)/shard_map/attn/pallas_call | solution.py:70
  14.5 0.1 collective-permute-start
  14.6 1.6 %collective-permute-start.1 = (bf16[80,768]{1,0:T(8,128)(2,1)S(1)}, bf16[80,768]{1,0:T(8,128)(2,1)S(1)}, u32[]{:S(2)}, u32[]{:S(2)}) collective-permute-start(bf16[80,768]{1,0:T(8,128)(2,1)S(1)} %get-tuple-element.32), channel_id=1, source_target_pairs={{0,2},{1,3},{2,0},{3,1},{4,6},{5,7},{6,4},{7,5},{8,10},{9,11},{10,... | collective-permute-start | bytes 368648 | tf_op jit(solution)/shard_map/ppermute | solution.py:381
  16.2 0.3 collective-permute-start.2
  16.4 0.0 copy-done.9
  16.5 4.2 %mask.1.refs_4_ = bf16[512,768]{1,0:T(8,128)(2,1)S(1)} custom-call(s32[16,512]{1,0:T(8,128)S(1)} %bitcast.9), custom_call_target="tpu_custom_call" | custom-call | flops 4000000000 | bytes 32768 | tf_op jit(solution)/shard_map/mask/pallas_call | solution.py:70
  20.7 0.0 copy-start.11
  20.7 0.0 collective-permute-done.refs_6_
  20.7 0.0 collective-permute-done.1.refs_7_
  20.8 1.7 %collective-permute-done.2.refs_8_ = bf16[80,768]{1,0:T(8,128)(2,1)S(1)} collective-permute-done((bf16[80,768]{1,0:T(8,128)(2,1)S(1)}, bf16[80,768]{1,0:T(8,128)(2,1)S(1)}, u32[]{:S(2)}, u32[]{:S(2)}) %collective-permute-start.2) | collective-permute-done | bytes 122912 | tf_op jit(solution)/shard_map/ppermute | solution.py:381
  22.5 0.0 copy-done.7
  22.5 0.0 copy-done
  22.5 0.0 copy-done.1
  22.5 0.0 copy-done.5
  22.5 1.3 %norm_one.1 = (bf16[80,768]{1,0:T(8,128)(2,1)S(1)}, bf16[16,768]{1,0:T(8,128)(2,1)S(1)}, f32[16,768]{1,0:T(8,128)S(1)}) custom-call(s32[4]{0:T(128)S(1)} %iota_xor_fusion.refs_0_, bf16[256,768]{1,0:T(8,128)(2,1)S(1)} %copy-done.2, f32[2,768]{1,0:T(2,128)S(1)} %copy-done.5, bf16[768,768]{1,0:T(8,128)(2,1)S(1)} %copy-done, bf16[768,768]{1,0:T(8,128)(2,1)S(1)} %copy-done.1, ...), custom_call_target="tpu_custom_call" | custom-call | bytes 3373072 | tf_op jit(solution)/shard_map/norm_one/pallas_call | solution.py:70
  23.8 0.0 copy-done.11
  23.8 1.7 %collective-permute-start.5 = (bf16[80,768]{1,0:T(8,128)(2,1)S(1)}, bf16[80,768]{1,0:T(8,128)(2,1)S(1)}, u32[]{:S(2)}, u32[]{:S(2)}) collective-permute-start(bf16[80,768]{1,0:T(8,128)(2,1)S(1)} %get-tuple-element.37.refs_5_.refs_0_), channel_id=1, source_target_pairs={{0,3},{1,2},{2,1},{3,0},{4,7},{5,6},{6,5},{7,4},{8,11},{9,10},{10,... | collective-permute-start | bytes 368648 | tf_op jit(solution)/shard_map/ppermute | solution.py:381
  25.5 0.5 collective-permute-start.4
  26.0 0.0 collective-permute-start.3
  26.0 3.2 %collective-permute-done.5.refs_8_ = bf16[80,768]{1,0:T(8,128)(2,1)S(1)} collective-permute-done((bf16[80,768]{1,0:T(8,128)(2,1)S(1)}, bf16[80,768]{1,0:T(8,128)(2,1)S(1)}, u32[]{:S(2)}, u32[]{:S(2)}) %collective-permute-start.5) | collective-permute-done | bytes 122912 | tf_op jit(solution)/shard_map/ppermute | solution.py:381
  29.1 2.9 %collective-permute-done.4.refs_7_ = bf16[80,768]{1,0:T(8,128)(2,1)S(1)} collective-permute-done((bf16[80,768]{1,0:T(8,128)(2,1)S(1)}, bf16[80,768]{1,0:T(8,128)(2,1)S(1)}, u32[]{:S(2)}, u32[]{:S(2)}) %collective-permute-start.4) | collective-permute-done | bytes 122912 | tf_op jit(solution)/shard_map/ppermute | solution.py:381
  32.0 0.0 collective-permute-done.3.refs_6_
  32.0 0.9 %ffn.1 = (f32[64,768]{1,0:T(8,128)S(1)}, bf16[64,768]{1,0:T(8,128)(2,1)S(1)}, bf16[64,768]{1,0:T(8,128)(2,1)S(1)}, bf16[64,768]{1,0:T(8,128)(2,1)S(1)}, bf16[2,768]{1,0:T(2,128)(2,1)S(1)}) custom-call(bf16[768,768]{1,0:T(8,128)(2,1)S(1)} %copy-done, bf16[768,768]{1,0:T(8,128)(2,1)S(1)} %copy-done.1, f32[2,768]{1,0:T(2,128)S(1)} %copy-done.5, ...), custom_call_target="tpu_custom_call" | custom-call | flops 603979776 | bytes 2930688 | tf_op jit(solution)/shard_map/ffn/pallas_call | solution.py:70
  33.0 0.0 copy-start.10
  33.0 0.1 collective-permute-start.6
  33.0 1.6 %collective-permute-start.7 = (bf16[64,768]{1,0:T(8,128)(2,1)S(1)}, bf16[64,768]{1,0:T(8,128)(2,1)S(1)}, u32[]{:S(2)}, u32[]{:S(2)}) collective-permute-start(bf16[64,768]{1,0:T(8,128)(2,1)S(1)} %get-tuple-element.42), channel_id=1, source_target_pairs={{0,2},{1,3},{2,0},{3,1},{4,6},{5,7},{6,4},{7,5},{8,10},{9,11},{10,... | collective-permute-start | bytes 294920 | tf_op jit(solution)/shard_map/ppermute | solution.py:381
  34.6 0.3 collective-permute-start.8
  34.9 2.9 %collective-permute-start.10 = (bf16[2,768]{1,0:T(2,128)(2,1)S(1)}, bf16[2,768]{1,0:T(2,128)(2,1)S(1)}, u32[]{:S(2)}, u32[]{:S(2)}) collective-permute-start(bf16[2,768]{1,0:T(2,128)(2,1)S(1)} %get-tuple-element.44.refs_4_), channel_id=1, source_target_pairs={{0,16},{1,21},{2,26},{3,31},{4,20},{5,17},{6,30},{7,27},{8,24},{9,... | collective-permute-start | bytes 9224 | tf_op jit(solution)/shard_map/ppermute | solution.py:435
  37.8 0.8 %collective-permute-start.9 = (bf16[2,768]{1,0:T(2,128)(2,1)S(1)}, bf16[2,768]{1,0:T(2,128)(2,1)S(1)}, u32[]{:S(2)}, u32[]{:S(2)}) collective-permute-start(bf16[2,768]{1,0:T(2,128)(2,1)S(1)} %get-tuple-element.44.refs_4_), channel_id=1, source_target_pairs={{1,5},{2,10},{3,15},{5,1},{6,14},{7,11},{9,13},{10,2},{11,7},{13,9... | collective-permute-start | bytes 9224 | tf_op jit(solution)/shard_map/ppermute | solution.py:435
  38.7 10.7 %collective-permute-done.10.refs_1_ = bf16[2,768]{1,0:T(2,128)(2,1)S(1)} collective-permute-done((bf16[2,768]{1,0:T(2,128)(2,1)S(1)}, bf16[2,768]{1,0:T(2,128)(2,1)S(1)}, u32[]{:S(2)}, u32[]{:S(2)}) %collective-permute-start.10) | collective-permute-done | bytes 3104 | tf_op jit(solution)/shard_map/ppermute | solution.py:435
  49.3 0.0 collective-permute-done.9.refs_0_
  49.3 0.0 collective-permute-done.6.refs_3_
  49.3 0.0 collective-permute-done.7.refs_4_
  49.3 0.0 collective-permute-done.8.refs_5_
  49.3 0.2 norm_two.1.refs_0_.refs_1_
  49.6 0.1 collective-permute-start.11
  49.7 0.0 copy-start.6
  49.7 1.0 %collective-permute-start.15 = (bf16[16,768]{1,0:T(8,128)(2,1)S(1)}, bf16[16,768]{1,0:T(8,128)(2,1)S(1)}, u32[]{:S(2)}, u32[]{:S(2)}) collective-permute-start(bf16[16,768]{1,0:T(8,128)(2,1)S(1)} %pack.1.refs_5_), channel_id=1, source_target_pairs={{0,3},{1,2},{2,1},{3,0},{4,7},{5,6},{6,5},{7,4},{8,11},{9,10},{10,... | collective-permute-start | bytes 73736 | tf_op jit(solution)/shard_map/ppermute | solution.py:381
  50.7 1.1 %collective-permute-start.14 = (bf16[16,768]{1,0:T(8,128)(2,1)S(1)}, bf16[16,768]{1,0:T(8,128)(2,1)S(1)}, u32[]{:S(2)}, u32[]{:S(2)}) collective-permute-start(bf16[16,768]{1,0:T(8,128)(2,1)S(1)} %pack.1.refs_5_), channel_id=1, source_target_pairs={{0,2},{1,3},{2,0},{3,1},{4,6},{5,7},{6,4},{7,5},{8,10},{9,11},{10,... | collective-permute-start | bytes 73736 | tf_op jit(solution)/shard_map/ppermute | solution.py:381
  51.8 0.0 collective-permute-start.13
  51.9 2.4 %collective-permute-done.11.refs_1_.refs_2_ = bf16[64,768]{1,0:T(8,128)(2,1)S(1)} collective-permute-done((bf16[64,768]{1,0:T(8,128)(2,1)S(1)}, bf16[64,768]{1,0:T(8,128)(2,1)S(1)}, u32[]{:S(2)}, u32[]{:S(2)}) %collective-permute-start.11) | collective-permute-done | bytes 98336 | tf_op jit(solution)/shard_map/ppermute | solution.py:381
  54.3 0.1 collective-permute-start.12
  54.4 0.0 collective-permute-done.15.refs_8_
  54.4 0.0 copy-start.13
  54.4 0.7 collective-permute-done.14.refs_7_
  55.0 0.0 collective-permute-done.13.refs_6_
  55.1 0.0 copy-done.10
  55.1 0.6 copy-done.14
  55.7 0.6 copy-done.15
  56.3 4.1 %own.1 = (bf16[512,384]{1,0:T(8,128)(2,1)}, bf16[512,192]{1,0:T(8,128)(2,1)}, bf16[16,384]{1,0:T(8,128)(2,1)}) custom-call(s32[4]{0:T(128)} %copy-done.7, s32[2]{0:T(128)} %refs_1_.9, bf16[512,768]{1,0:T(8,128)(2,1)} %refs_2_.5, bf16[3,192,768]{2,1,0:T(8,128)(2,1)} %bitcast.13, bf16[2,768]{1,0:T(2,128)(2,1)} %copy-done.10, bf16[16,768]{1,0:T(8,128)(2,1)} %copy-done.6, ...), custom_call_target="tpu_custom_call" | custom-call | flops 2000000000 | bytes 1772568 | tf_op jit(solution)/shard_map/own/pallas_call | solution.py:70
  60.3 0.0 collective-permute-done.12.refs_3_
  60.4 1.3 %place.1 = bf16[256,768]{1,0:T(8,128)(2,1)} custom-call(s32[4]{0:T(128)S(1)} %copy-done.8, bf16[64,768]{1,0:T(8,128)(2,1)S(1)} %norm_two.1.refs_0_.refs_1_, bf16[64,768]{1,0:T(8,128)(2,1)S(1)} %collective-permute-done.11.refs_1_.refs_2_, bf16[128,768]{1,0:T(8,128)(2,1)S(1)} %collective-permute-done.12.refs_3_), custom_call_target="tpu_custom_call" | custom-call | bytes 393232 | tf_op jit(solution)/shard_map/place/pallas_call | solution.py:70
  61.7 0.0 all-to-all-done
  61.7 1.2 %copy-done.12 = bf16[8,256,384]{2,1,0:T(8,128)(2,1)} copy-done((bf16[8,256,384]{2,1,0:T(8,128)(2,1)}, bf16[8,256,384]{2,1,0:T(8,128)(2,1)S(1)}, u32[]{:S(2)}) %copy-start.12) | copy-done | bytes 1572888
  62.9 6.4 %graph.1 = bf16[192,512]{1,0:T(8,128)(2,1)} custom-call(s32[4,6]{1,0:T(4,128)} %refs_0_.3, bf16[512,192]{1,0:T(8,128)(2,1)} %get-tuple-element.51.refs_1_, bf16[512,384]{1,0:T(8,128)(2,1)} %get-tuple-element.52.refs_2_, bf16[16,384]{1,0:T(8,128)(2,1)} %get-tuple-element.53.refs_3_, bf16[512,768]{1,0:T(8,128)(2,1)} %copy-done.11, bf16[2048,384]{1,0:T(8,128)(2,1)} %bitcast.10), custom_call_target="tpu_custom_call" | custom-call | flops 1000000000 | bytes 2961504 | tf_op jit(solution)/shard_map/graph/pallas_call | solution.py:70
  (14 shorter events, 0.1 us)
Async XLA Ops:
  4.7 7.5 %copy-start.2 = (bf16[256,768]{1,0:T(8,128)(2,1)S(1)}, bf16[256,768]{1,0:T(8,128)(2,1)}, u32[]{:S(2)}) copy-start(bf16[256,768]{1,0:T(8,128)(2,1)} %refs_1_.6) | copy-start | bytes 1179652
  4.8 7.5 %copy-start.3 = (bf16[3,768,192]{1,2,0:T(8,128)(2,1)S(1)}, bf16[3,768,192]{1,2,0:T(8,128)(2,1)}, u32[]{:S(2)}) copy-start(bf16[3,768,192]{1,2,0:T(8,128)(2,1)} %param.13) | copy-start | bytes 2654212
  4.8 7.5 %copy-start.4 = (bf16[192,768]{1,0:T(8,128)(2,1)S(1)}, bf16[192,768]{1,0:T(8,128)(2,1)}, u32[]{:S(2)}) copy-start(bf16[192,768]{1,0:T(8,128)(2,1)} %refs_3_.4) | copy-start | bytes 884740
  4.8 56.9 %all-to-all-start = ((bf16[8,256,384]{2,1,0:T(8,128)(2,1)}), bf16[8,256,384]{2,1,0:T(8,128)(2,1)S(1)}, u32[]{:S(2)}, u32[]{:S(2)}) async-start(bf16[8,256,384]{2,1,0:T(8,128)(2,1)} %bitcast.11), calls=%async_computation | async-start | bytes 3145728 | tf_op jit(solution)/shard_map/all_to_all | solution.py:397
  12.2 4.3 %copy-start.9 = (s32[512,16]{0,1:T(8,128)S(1)}, s32[512,16]{0,1:T(8,128)}, u32[]{:S(2)}) copy-start(s32[512,16]{0,1:T(8,128)} %param.23) | copy-start | bytes 98308
  12.2 10.3 %copy-start.7 = (s32[4]{0:T(128)}, s32[4]{0:T(128)S(1)}, u32[]{:S(2)}) copy-start(s32[4]{0:T(128)S(1)} %iota_xor_fusion.refs_0_) | copy-start | bytes 52
  14.5 6.2 %collective-permute-start = (bf16[80,768]{1,0:T(8,128)(2,1)S(1)}, bf16[80,768]{1,0:T(8,128)(2,1)S(1)}, u32[]{:S(2)}, u32[]{:S(2)}) collective-permute-start(bf16[80,768]{1,0:T(8,128)(2,1)S(1)} %get-tuple-element.31), channel_id=1, source_target_pairs={{0,1},{1,0},{2,3},{3,2},{4,5},{5,4},{6,7},{7,6},{8,9},{9,8},{10,11... | collective-permute-start | bytes 368648 | tf_op jit(solution)/shard_map/ppermute | solution.py:381
  14.6 6.2 %collective-permute-start.1 = (bf16[80,768]{1,0:T(8,128)(2,1)S(1)}, bf16[80,768]{1,0:T(8,128)(2,1)S(1)}, u32[]{:S(2)}, u32[]{:S(2)}) collective-permute-start(bf16[80,768]{1,0:T(8,128)(2,1)S(1)} %get-tuple-element.32), channel_id=1, source_target_pairs={{0,2},{1,3},{2,0},{3,1},{4,6},{5,7},{6,4},{7,5},{8,10},{9,11},{10,... | collective-permute-start | bytes 368648 | tf_op jit(solution)/shard_map/ppermute | solution.py:381
  16.2 6.3 %collective-permute-start.2 = (bf16[80,768]{1,0:T(8,128)(2,1)S(1)}, bf16[80,768]{1,0:T(8,128)(2,1)S(1)}, u32[]{:S(2)}, u32[]{:S(2)}) collective-permute-start(bf16[80,768]{1,0:T(8,128)(2,1)S(1)} %get-tuple-element.33), channel_id=1, source_target_pairs={{0,3},{1,2},{2,1},{3,0},{4,7},{5,6},{6,5},{7,4},{8,11},{9,10},{10,... | collective-permute-start | bytes 368648 | tf_op jit(solution)/shard_map/ppermute | solution.py:381
  16.4 6.1 %copy-start = (bf16[768,768]{1,0:T(8,128)(2,1)S(1)}, bf16[768,768]{1,0:T(8,128)(2,1)}, u32[]{:S(2)}) copy-start(bf16[768,768]{1,0:T(8,128)(2,1)} %refs_0_.2) | copy-start | bytes 3538948
  16.5 6.1 %copy-start.1 = (bf16[768,768]{1,0:T(8,128)(2,1)S(1)}, bf16[768,768]{1,0:T(8,128)(2,1)}, u32[]{:S(2)}) copy-start(bf16[768,768]{1,0:T(8,128)(2,1)} %refs_1_.7) | copy-start | bytes 3538948
  16.5 6.1 %copy-start.5 = (f32[2,768]{1,0:T(2,128)S(1)}, f32[2,768]{1,0:T(2,128)}, u32[]{:S(2)}) copy-start(f32[2,768]{1,0:T(2,128)} %refs_1_.8) | copy-start | bytes 18436
  20.7 3.1 %copy-start.11 = (bf16[512,768]{1,0:T(8,128)(2,1)}, bf16[512,768]{1,0:T(8,128)(2,1)S(1)}, u32[]{:S(2)}) copy-start(bf16[512,768]{1,0:T(8,128)(2,1)S(1)} %mask.1.refs_4_) | copy-start | bytes 2359300
  23.8 5.4 %collective-permute-start.5 = (bf16[80,768]{1,0:T(8,128)(2,1)S(1)}, bf16[80,768]{1,0:T(8,128)(2,1)S(1)}, u32[]{:S(2)}, u32[]{:S(2)}) collective-permute-start(bf16[80,768]{1,0:T(8,128)(2,1)S(1)} %get-tuple-element.37.refs_5_.refs_0_), channel_id=1, source_target_pairs={{0,3},{1,2},{2,1},{3,0},{4,7},{5,6},{6,5},{7,4},{8,11},{9,10},{10,... | collective-permute-start | bytes 368648 | tf_op jit(solution)/shard_map/ppermute | solution.py:381
  25.5 6.6 %collective-permute-start.4 = (bf16[80,768]{1,0:T(8,128)(2,1)S(1)}, bf16[80,768]{1,0:T(8,128)(2,1)S(1)}, u32[]{:S(2)}, u32[]{:S(2)}) collective-permute-start(bf16[80,768]{1,0:T(8,128)(2,1)S(1)} %get-tuple-element.37.refs_5_.refs_0_), channel_id=1, source_target_pairs={{0,2},{1,3},{2,0},{3,1},{4,6},{5,7},{6,4},{7,5},{8,10},{9,11},{10,... | collective-permute-start | bytes 368648 | tf_op jit(solution)/shard_map/ppermute | solution.py:381
  26.0 6.1 %collective-permute-start.3 = (bf16[80,768]{1,0:T(8,128)(2,1)S(1)}, bf16[80,768]{1,0:T(8,128)(2,1)S(1)}, u32[]{:S(2)}, u32[]{:S(2)}) collective-permute-start(bf16[80,768]{1,0:T(8,128)(2,1)S(1)} %get-tuple-element.37.refs_5_.refs_0_), channel_id=1, source_target_pairs={{0,1},{1,0},{2,3},{3,2},{4,5},{5,4},{6,7},{7,6},{8,9},{9,8},{10,11... | collective-permute-start | bytes 368648 | tf_op jit(solution)/shard_map/ppermute | solution.py:381
  33.0 22.1 %copy-start.10 = (bf16[2,768]{1,0:T(2,128)(2,1)}, bf16[2,768]{1,0:T(2,128)(2,1)S(1)}, u32[]{:S(2)}) copy-start(bf16[2,768]{1,0:T(2,128)(2,1)S(1)} %get-tuple-element.44.refs_4_) | copy-start | bytes 9220
  33.0 16.3 %collective-permute-start.6 = (bf16[64,768]{1,0:T(8,128)(2,1)S(1)}, bf16[64,768]{1,0:T(8,128)(2,1)S(1)}, u32[]{:S(2)}, u32[]{:S(2)}) collective-permute-start(bf16[64,768]{1,0:T(8,128)(2,1)S(1)} %get-tuple-element.41), channel_id=1, source_target_pairs={{0,1},{1,0},{2,3},{3,2},{4,5},{5,4},{6,7},{7,6},{8,9},{9,8},{10,11... | collective-permute-start | bytes 294920 | tf_op jit(solution)/shard_map/ppermute | solution.py:381
  33.0 16.3 %collective-permute-start.7 = (bf16[64,768]{1,0:T(8,128)(2,1)S(1)}, bf16[64,768]{1,0:T(8,128)(2,1)S(1)}, u32[]{:S(2)}, u32[]{:S(2)}) collective-permute-start(bf16[64,768]{1,0:T(8,128)(2,1)S(1)} %get-tuple-element.42), channel_id=1, source_target_pairs={{0,2},{1,3},{2,0},{3,1},{4,6},{5,7},{6,4},{7,5},{8,10},{9,11},{10,... | collective-permute-start | bytes 294920 | tf_op jit(solution)/shard_map/ppermute | solution.py:381
  34.6 14.7 %collective-permute-start.8 = (bf16[64,768]{1,0:T(8,128)(2,1)S(1)}, bf16[64,768]{1,0:T(8,128)(2,1)S(1)}, u32[]{:S(2)}, u32[]{:S(2)}) collective-permute-start(bf16[64,768]{1,0:T(8,128)(2,1)S(1)} %get-tuple-element.43), channel_id=1, source_target_pairs={{0,3},{1,2},{2,1},{3,0},{4,7},{5,6},{6,5},{7,4},{8,11},{9,10},{10,... | collective-permute-start | bytes 294920 | tf_op jit(solution)/shard_map/ppermute | solution.py:381
  34.9 14.4 %collective-permute-start.10 = (bf16[2,768]{1,0:T(2,128)(2,1)S(1)}, bf16[2,768]{1,0:T(2,128)(2,1)S(1)}, u32[]{:S(2)}, u32[]{:S(2)}) collective-permute-start(bf16[2,768]{1,0:T(2,128)(2,1)S(1)} %get-tuple-element.44.refs_4_), channel_id=1, source_target_pairs={{0,16},{1,21},{2,26},{3,31},{4,20},{5,17},{6,30},{7,27},{8,24},{9,... | collective-permute-start | bytes 9224 | tf_op jit(solution)/shard_map/ppermute | solution.py:435
  37.8 11.5 %collective-permute-start.9 = (bf16[2,768]{1,0:T(2,128)(2,1)S(1)}, bf16[2,768]{1,0:T(2,128)(2,1)S(1)}, u32[]{:S(2)}, u32[]{:S(2)}) collective-permute-start(bf16[2,768]{1,0:T(2,128)(2,1)S(1)} %get-tuple-element.44.refs_4_), channel_id=1, source_target_pairs={{1,5},{2,10},{3,15},{5,1},{6,14},{7,11},{9,13},{10,2},{11,7},{13,9... | collective-permute-start | bytes 9224 | tf_op jit(solution)/shard_map/ppermute | solution.py:435
  49.6 4.7 %collective-permute-start.11 = (bf16[64,768]{1,0:T(8,128)(2,1)S(1)}, bf16[64,768]{1,0:T(8,128)(2,1)S(1)}, u32[]{:S(2)}, u32[]{:S(2)}) collective-permute-start(bf16[64,768]{1,0:T(8,128)(2,1)S(1)} %norm_two.1.refs_0_.refs_1_), channel_id=1, source_target_pairs={{0,2},{1,3},{2,0},{3,1},{4,6},{5,7},{6,4},{7,5},{8,10},{9,11},{10,... | collective-permute-start | bytes 294920 | tf_op jit(solution)/shard_map/ppermute | solution.py:381
  49.7 5.4 %copy-start.6 = (bf16[16,768]{1,0:T(8,128)(2,1)}, bf16[16,768]{1,0:T(8,128)(2,1)S(1)}, u32[]{:S(2)}) copy-start(bf16[16,768]{1,0:T(8,128)(2,1)S(1)} %pack.1.refs_5_) | copy-start | bytes 73732
  49.7 4.7 %collective-permute-start.15 = (bf16[16,768]{1,0:T(8,128)(2,1)S(1)}, bf16[16,768]{1,0:T(8,128)(2,1)S(1)}, u32[]{:S(2)}, u32[]{:S(2)}) collective-permute-start(bf16[16,768]{1,0:T(8,128)(2,1)S(1)} %pack.1.refs_5_), channel_id=1, source_target_pairs={{0,3},{1,2},{2,1},{3,0},{4,7},{5,6},{6,5},{7,4},{8,11},{9,10},{10,... | collective-permute-start | bytes 73736 | tf_op jit(solution)/shard_map/ppermute | solution.py:381
  50.7 4.3 %collective-permute-start.14 = (bf16[16,768]{1,0:T(8,128)(2,1)S(1)}, bf16[16,768]{1,0:T(8,128)(2,1)S(1)}, u32[]{:S(2)}, u32[]{:S(2)}) collective-permute-start(bf16[16,768]{1,0:T(8,128)(2,1)S(1)} %pack.1.refs_5_), channel_id=1, source_target_pairs={{0,2},{1,3},{2,0},{3,1},{4,6},{5,7},{6,4},{7,5},{8,10},{9,11},{10,... | collective-permute-start | bytes 73736 | tf_op jit(solution)/shard_map/ppermute | solution.py:381
  51.8 3.2 %collective-permute-start.13 = (bf16[16,768]{1,0:T(8,128)(2,1)S(1)}, bf16[16,768]{1,0:T(8,128)(2,1)S(1)}, u32[]{:S(2)}, u32[]{:S(2)}) collective-permute-start(bf16[16,768]{1,0:T(8,128)(2,1)S(1)} %pack.1.refs_5_), channel_id=1, source_target_pairs={{0,1},{1,0},{2,3},{3,2},{4,5},{5,4},{6,7},{7,6},{8,9},{9,8},{10,11... | collective-permute-start | bytes 73736 | tf_op jit(solution)/shard_map/ppermute | solution.py:381
  54.3 6.1 %copy-start.8 = (s32[4]{0:T(128)S(1)}, s32[4]{0:T(128)}, u32[]{:S(2)}) copy-start(s32[4]{0:T(128)} %copy-done.7) | copy-start | bytes 52
  54.3 6.1 %collective-permute-start.12 = (bf16[128,768]{1,0:T(8,128)(2,1)S(1)}, bf16[128,768]{1,0:T(8,128)(2,1)S(1)}, u32[]{:S(2)}, u32[]{:S(2)}) collective-permute-start(bf16[128,768]{1,0:T(8,128)(2,1)S(1)} %join.1), channel_id=1, source_target_pairs={{0,1},{1,0},{2,3},{3,2},{4,5},{5,4},{6,7},{7,6},{8,9},{9,8},{10,11... | collective-permute-start | bytes 589832 | tf_op jit(solution)/shard_map/ppermute | solution.py:381
  54.4 0.7 %copy-start.13 = (bf16[16,768]{1,0:T(8,128)(2,1)}, bf16[16,768]{1,0:T(8,128)(2,1)S(1)}, u32[]{:S(2)}) copy-start(bf16[16,768]{1,0:T(8,128)(2,1)S(1)} %collective-permute-done.15.refs_8_) | copy-start | bytes 73732
  55.0 0.6 copy-start.14
  55.6 0.6 copy-start.15
  61.7 1.2 %copy-start.12 = (bf16[8,256,384]{2,1,0:T(8,128)(2,1)}, bf16[8,256,384]{2,1,0:T(8,128)(2,1)S(1)}, u32[]{:S(2)}) copy-start(bf16[8,256,384]{2,1,0:T(8,128)(2,1)S(1)} %all-to-all-done) | copy-start | bytes 4718596

commit v9 on v8

--- a/solution.py
+++ b/solution.py
@@ -31,16 +31,14 @@
     args,
     smem=(),
     hbm=(),
-    held=(),
     scalars=(),
     scratch=(),
     out_specs=None,
-    late=False,
     flops=0,
     name=None,
 ):
     count, out_count, own = len(args), len(jax.tree.leaves(outs)), len(scratch)
-    specs = [SMEM if i in smem else HBM if i in hbm or i in held else VMEM for i in range(count)]
+    specs = [SMEM if i in smem else HBM if i in hbm else VMEM for i in range(count)]
     nbytes = sum(a.size * a.dtype.itemsize for a in args)
     space = [pltpu.SMEM if i in scalars else pltpu.VMEM for i in hbm]
     buffers = [kind(args[i].shape, args[i].dtype) for kind, i in zip(space, hbm)]
@@ -52,19 +50,13 @@
         moves = {}
         for j, i in enumerate(hbm):
             moves[i] = pltpu.make_async_copy(ins[i], moved[j], moved[-1].at[j])
+            moves[i].start()
             ins[i] = moved[j]
-
-        def start():
-            for move in moves.values():
-                move.start()
 
         def ready(*wanted):
             for i in wanted:
                 moves[i].wait()
 
-        ready.start = start
-        if not late:
-            start()
         kernel(ready, *ins, *kept)
 
     return pl.pallas_call(
@@ -102,32 +94,97 @@
     return centred * lax.rsqrt(var + eps_norm) * gain
 
 
-def send_kernel(ready, me_ref, at_ref, ids_ref, table_ref, w_ref, sent_ref, rows_ref, sems):
+def one_hot(picked, nodes):
+    lanes = lax.broadcasted_iota(jnp.int32, (picked.shape[0], nodes), 1)
+    return jnp.where(lanes == picked, 1.0, 0.0).astype(bf)
+
+
+def mark(rows, picked, at_ref, step):
+    per_part = at_ref.shape[0]
+    code = jnp.full(picked.shape, -1, jnp.int32)
+    for title in range(per_part):
+        code = jnp.where(picked == at_ref[title], step * per_part + title, code)
+    lead = lax.broadcasted_iota(jnp.int32, rows.shape, 1) == 0
+    return jnp.where(code >= 0, jnp.where(lead, jnp.nan, code.astype(f32)), rows)
+
+
+def send_kernel(ready, me_ref, who_ref, at_ref, ids_ref, table_ref, w_ref, sent_ref, ids_t):
     cols = w_ref.shape[1]
-    per_part = at_ref.shape[0]
-    fetch, nodes = ids_ref.shape[1], table_ref.shape[0]
-    ready(1, 2, 3, 4)
+    nodes, width = table_ref.shape
+    parts, fetch = ids_ref.shape
+    half, share = parts // 2, fetch // who_ref.shape[0]
+    size = sent_ref.shape[0] // parts
+    side, low = me_ref[1], me_ref[0] % half
+    ready(2, 3)
+    ids_t[...] = ids_ref[...].astype(f32).T
+
+    def picks(ids, this, count):
+        first = [ids[:, part : part + 1] for part in range(half)]
+        second = [ids[:, half + part : half + part + 1] for part in range(half)]
+        both = [jnp.where(this == 0, x, y).astype(jnp.int32) for x, y in zip(first, second)]
+        return both, one_hot(jnp.concatenate(both, axis=0), nodes)
+
+    def target(this, part):
+        return pl.ds(pl.multiple_of((this * half + part) * size, size), size)
+
+    mine = ids_t[pl.ds(pl.multiple_of(who_ref[0] * share, share), share), :]
+    picked, hot = picks(mine, 1 - side, share)
+    ready(4)
+    rows = dot(hot, table_ref[...])
+    for part in range(half):
+        step = half + (low ^ part)
+        raw = mark(rows[part * share : (part + 1) * share], picked[part], at_ref, step)
+        raw = jnp.concatenate([raw[:, : width // 2], raw[:, width // 2 :]], axis=0)
+        sent_ref[target(1 - side, part), :] = raw.astype(bf)
+    picked, hot = picks(ids_t[:size, :], side, size)
+    ready(5)
     table = table_ref[...]
     kv = jnp.concatenate([dot_nt(table, w_ref[1]), dot_nt(table, w_ref[2])], axis=1).astype(bf)
-    ids = ids_ref[...].astype(f32).T.astype(jnp.int32)
-    lanes = lax.broadcasted_iota(jnp.int32, (fetch, nodes), 1)
-    lead = lax.broadcasted_iota(jnp.int32, (fetch, 2 * cols), 1) == 0
-    moves = []
-    for part in range(ids.shape[1]):
-        step = me_ref[0] ^ part
-        picked = ids[:, part : part + 1]
-        hot = jnp.where(lanes == picked, 1.0, 0.0).astype(bf)
-        rows = dot(hot, kv)
-        code = jnp.full((fetch, 1), -1, jnp.int32)
-        for title in range(per_part):
-            code = jnp.where(picked == at_ref[title], step * per_part + title, code)
-        mark = jnp.where(lead, jnp.nan, code.astype(f32))
-        at = pl.ds(part * fetch, fetch)
-        rows_ref[at, :] = jnp.where(code >= 0, mark, rows).astype(bf)
-        moves.append(pltpu.make_async_copy(rows_ref.at[at, :], sent_ref.at[at, :], sems.at[part]))
-        moves[-1].start()
-    for move in moves:
-        move.wait()
+    rows = dot(hot, kv)
+    for part in range(half):
+        near = mark(rows[part * size : (part + 1) * size], picked[part], at_ref, low ^ part)
+        sent_ref[target(side, part), :] = near.astype(bf)
+
+
+def rest_kernel(ready, me_ref, at_ref, ids_ref, table_ref, w_ref, *refs):
+    *outs, ids_t = refs
+    size = outs[0].shape[0]
+    table = table_ref[...]
+    kv = jnp.concatenate([dot_nt(table, w_ref[1]), dot_nt(table, w_ref[2])], axis=1).astype(bf)
+    ids_t[...] = ids_ref[...].astype(f32).T
+    ids = ids_t[ids_t.shape[0] - size :, :]
+    part = lax.broadcasted_iota(jnp.int32, ids.shape, 1)
+    for step, out in enumerate(outs):
+        picked = jnp.sum(jnp.where(part == me_ref[0] ^ step, ids, 0.0), axis=1, keepdims=True)
+        picked = picked.astype(jnp.int32)
+        rows = dot(one_hot(picked, table.shape[0]), kv)
+        out[...] = mark(rows, picked, at_ref, step).astype(bf)
+
+
+def pick_kernel(ready, me_ref, far_ref, out_ref):
+    size = out_ref.shape[0]
+    out_ref[...] = far_ref[pl.ds(pl.multiple_of((1 - me_ref[1]) * size, size), size), :]
+
+
+def raw_kernel(half, whose, ready, me_ref, who_ref, w_ref, *refs):
+    *blocks, out = refs
+    cols = w_ref.shape[1]
+    share = blocks[0].shape[0] // (2 * half)
+    fetch = share * len(blocks)
+    for step, block in zip(whose, blocks):
+        spans = [slice(i * share, (i + 1) * share) for i in range(2 * half)]
+        left = jnp.concatenate([block[span, :].astype(f32) for span in spans[::2]], axis=0)
+        right = jnp.concatenate([block[span, :].astype(f32) for span in spans[1::2]], axis=0)
+        marked = left[:, 0:1] != left[:, 0:1]
+        code = left[:, 1:2]
+        clean = jnp.concatenate([left, right], axis=1)
+        clean = jnp.where(marked, 0.0, clean).astype(bf)
+        kv = jnp.concatenate([dot_nt(clean, w_ref[1]), dot_nt(clean, w_ref[2])], axis=1)
+        lead = lax.broadcasted_iota(jnp.int32, kv.shape, 1) == 0
+        kv = jnp.where(marked, jnp.where(lead, jnp.nan, code), kv).astype(out.dtype)
+        for part in range(half):
+            at = pl.multiple_of(part * fetch + who_ref[step] * share, share)
+            out[pl.ds(at, share), :] = kv[part * share : (part + 1) * share]
 
 
 def mask_kernel(ready, slots_ref, mask_ref):
@@ -164,12 +221,22 @@
         for h in range(1, heads):
             context = jnp.where(lanes == h, mixed[h * SEQ : (h + 1) * SEQ], context)
         total[rows, :] = dot(context.astype(bf), w_out_ref[...])
-    chunk = outs[0].shape[0] - PAD
+    chunk = (outs[0].shape[0] - PAD) // 2
     firsts = first_rows(total)
-    for step, out in enumerate(outs):
-        at = pl.ds(pl.multiple_of(who_ref[step] * chunk, chunk), chunk)
-        out[:chunk, :] = total[at, :].astype(out.dtype)
-        out[chunk:, :] = firsts.astype(out.dtype)
+    for out, pair in zip(outs, ((0, 2), (1, 3))):
+        for j, step in enumerate(pair):
+            at = pl.ds(pl.multiple_of(who_ref[step] * chunk, chunk), chunk)
+            out[j * chunk : (j + 1) * chunk, :] = total[at, :].astype(out.dtype)
+        out[2 * chunk :, :] = firsts.astype(out.dtype)
+
+
+def half_kernel(chunk, ready, kept_ref, came_ref, keep_ref, give_ref):
+    total = kept_ref[...] + came_ref[...].astype(f32)
+    keep_ref[:chunk, :] = total[:chunk]
+    give_ref[:chunk, :] = total[chunk : 2 * chunk].astype(bf)
+    if keep_ref.shape[0] > chunk:
+        keep_ref[chunk:, :] = total[2 * chunk :]
+        give_ref[chunk:, :] = total[2 * chunk :].astype(bf)
 
 
 def first_rows(ref):
@@ -205,15 +272,13 @@
 
 
 def ffn_kernel(ready, w_in_ref, w_out_ref, gains_ref, first_hidden, first_terms, *refs):
-    *refs, first = refs
-    count = len(refs) // 2
-    ins, outs = refs[:count], refs[count:]
-    chunk = outs[0].shape[0]
+    *ins, kept, sent, first = refs
+    chunk = kept.shape[0] // 2
     hidden = jnp.concatenate([ref[:chunk, :] for ref in ins], axis=0)
     inner = gelu(dot(hidden, w_in_ref[...])).astype(bf)
     total = dot(inner, w_out_ref[...])
-    for step, out in enumerate(outs):
-        out[...] = total[step * chunk : (step + 1) * chunk].astype(out.dtype)
+    kept[...] = total[: 2 * chunk]
+    sent[...] = total[2 * chunk :].astype(bf)
     terms = first_terms[...]
     for ref in ins[1:]:
         terms = terms + ref[chunk:, :].astype(f32)
@@ -240,14 +305,6 @@
             row = ref[title : title + 1, :].astype(f32)
             rows = jnp.where(sub == turn * per_part + title, row, rows)
     out[...] = rows.astype(bf)
-
-
-def join_kernel(ready, *refs):
-    *parts, out = refs
-    start = 0
-    for part in parts:
-        out[start : start + part.shape[0], :] = part[...]
-        start += part.shape[0]
 
 
 def place_kernel(whose, ready, who_ref, *refs):
@@ -275,7 +332,6 @@
                 at = turn * per_part + title
                 firsts[pl.ds(place, 1), :] = rows[at : at + 1]
     firsts[0:per_part, :] = first_ref[...].astype(f32)
-    ready(1, 2)
     for tile in range(features.shape[0] // TILE):
         span = slice(tile * TILE, (tile + 1) * TILE)
         rows = table_ref[span, :].astype(f32)
@@ -285,7 +341,6 @@
         features[span, :] = rows.astype(bf)
     first = firsts[...].astype(bf)
     table = features[...]
-    ready(3)
     for j in (1, 2):
         span = slice((j - 1) * cols, j * cols)
         first_kv_ref[:, span] = dot_nt(first, w_ref[j]).astype(bf)
@@ -298,35 +353,37 @@
 
 
 def graph_kernel(
-    ready, cols_ref, q_ref, kv_ref, first_ref, mask_ref, far_hbm, out_ref, k_all, v_all, far_ref, sems
+    ready, me_ref, cols_ref, q_ref, kv_ref, first_ref, mask_ref, far_ref, cross_ref, *refs
 ):
-    pieces = sems.shape[0]
-    size = far_ref.shape[0] // pieces
-    moves = []
-    for piece in range(pieces):
-        at = pl.ds(piece * size, size)
-        moves.append(pltpu.make_async_copy(far_hbm.at[at, :], far_ref.at[at, :], sems.at[piece]))
-        moves[-1].start()
-    ready.start()
+    *rest, out_ref, k_all, v_all = refs
     nodes, cols = q_ref.shape
     row_tiles = nodes // TILE
     first_kv = first_ref[...]
-    lanes = lax.broadcasted_iota(jnp.int32, (TILE, first_kv.shape[0]), 1).astype(f32)
-    for tile in range(far_ref.shape[0] // TILE):
-        if tile * TILE % size == 0:
-            moves[tile * TILE // size].wait()
-        rows = far_ref[tile * TILE : (tile + 1) * TILE, :].astype(f32)
+    k_all[:nodes, :] = kv_ref[:, :cols]
+    v_all[:nodes, :] = kv_ref[:, cols:]
+
+    def fix(rows, start):
+        count = rows.shape[0]
+        rows = rows.astype(f32)
+        lanes = lax.broadcasted_iota(jnp.int32, (count, first_kv.shape[0]), 1).astype(f32)
         code = jnp.where(rows[:, 0:1] != rows[:, 0:1], rows[:, 1:2], -1.0)
         hot = jnp.where(lanes == code, 1.0, 0.0).astype(bf)
         fixed = jnp.where(code >= 0.0, dot(hot, first_kv), rows).astype(bf)
-        span = slice(nodes + tile * TILE, nodes + (tile + 1) * TILE)
-        k_all[span, :] = fixed[:, :cols]
-        v_all[span, :] = fixed[:, cols:]
-
-    ready(2)
-    k_all[:nodes, :] = kv_ref[:, :cols]
-    v_all[:nodes, :] = kv_ref[:, cols:]
-    ready(0, 1, 4)
+        at = pl.ds(pl.multiple_of(start, count), count)
+        k_all[at, :] = fixed[:, :cols]
+        v_all[at, :] = fixed[:, cols:]
+
+    half = len(rest)
+    size = rest[0].shape[0]
+    side, low = me_ref[1], me_ref[0] % half
+    for start in range(0, cross_ref.shape[0], TILE):
+        fix(cross_ref[start : start + TILE, :], nodes + (1 - side) * cross_ref.shape[0] + start)
+    for part in range(half):
+        at = pl.ds(pl.multiple_of((side * half + part) * size, size), size)
+        fix(far_ref[at, :], nodes + (side * half + part) * 2 * size)
+    for step, ref in enumerate(rest):
+        fix(ref[...], nodes + (side * half + (low ^ step)) * 2 * size + size)
+
     heads = cols // GHD
     head_of = lax.broadcasted_iota(jnp.int32, (TILE, cols), 1) // GHD
     for tile in range(row_tiles):
@@ -370,66 +427,99 @@
     cols = w_graph.shape[2]
     mp = lax.axis_size("mp")
     dp = lax.axis_size("dp")
+    half = dp // 2
     me_mp = lax.axis_index("mp").astype(jnp.int32)
-    me_dp = lax.axis_index("dp").astype(jnp.int32).reshape(1)
+    me_dp = lax.axis_index("dp").astype(jnp.int32)
+    me = jnp.stack([me_dp, me_dp // half])
     who = me_mp ^ jnp.arange(mp, dtype=jnp.int32)
     chunk = tok_rows // mp
     per_part = title_nodes.shape[0]
     fetch = send_ids.shape[2]
+    share = fetch // mp
 
     def swap(value, step, axis="mp"):
         return lax.ppermute(value, axis, [(i, i ^ step) for i in range(lax.axis_size(axis))])
 
+    def gather(value):
+        whose, blocks, step = [0], [value], mp // 2
+        while step:
+            blocks = blocks + [swap(block, step) for block in blocks]
+            whose = whose + [other ^ step for other in whose]
+            step //= 2
+        return whose, blocks
+
+    def halves(kept, came, pad):
+        dims = (chunk + pad, width)
+        return call(
+            functools.partial(half_kernel, chunk),
+            (shape(dims, f32), shape(dims, bf)),
+            (kept, came),
+            name="half",
+        )
+
     w_attn_in = jnp.swapaxes(w_attn_in, 1, 2)
     w_graph = jnp.swapaxes(w_graph, 1, 2)
+    size = 2 * share
     sent = call(
         send_kernel,
-        shape((dp * fetch, 2 * cols), bf),
-        (me_dp, title_nodes, send_ids[0], node_table, w_graph),
-        smem=(0,),
-        hbm=(4, 3, 2, 1),
-        scalars=(1,),
-        out_specs=HBM,
-        scratch=[pltpu.VMEM((dp * fetch, 2 * cols), bf), pltpu.SemaphoreType.DMA((dp,))],
-        flops=2 * nodes * width * 2 * cols + 2 * dp * fetch * nodes * 2 * cols,
+        shape((dp * size, 2 * cols), bf),
+        (me, who, title_nodes, send_ids[0], node_table, w_graph),
+        smem=(0, 1),
+        hbm=(4, 3, 5, 2),
+        scalars=(2,),
+        scratch=[pltpu.VMEM((fetch, dp), f32)],
+        flops=3 * 10**9,
         name="send",
     )
     far = lax.all_to_all(
-        sent.reshape(dp, fetch, 2 * cols), "dp", split_axis=0, concat_axis=0, tiled=True
-    ).reshape(dp * fetch, 2 * cols)
+        sent.reshape(dp, size, 2 * cols), "dp", split_axis=0, concat_axis=0, tiled=True
+    ).reshape(dp * size, 2 * cols)
     titles, _ = lax.optimization_barrier((titles, sent))
 
-    terms = call(
+    kept, given = call(
         attn_kernel,
-        tuple(shape((chunk + PAD, width), bf if step else f32) for step in range(mp)),
+        (shape((2 * chunk + PAD, width), f32), shape((2 * chunk + PAD, width), bf)),
         (who, titles, w_attn_in, w_attn_out),
         smem=(0,),
         scratch=[pltpu.VMEM((tok_rows, width), f32)],
         flops=2 * tok_rows * width * 4 * w_attn_in.shape[1],
         name="attn",
     )
-    parts = [swap(terms[step], step) for step in range(1, mp)]
+    keep, give = halves(kept, swap(given, 1), PAD)
+    part = swap(give, 2)
     mask = call(
         mask_kernel, shape((nodes, TPR * TILE), bf), (nbr_slots.T,), flops=4 * 10**9, name="mask"
     )
-    parts, mask = lax.optimization_barrier((parts, mask))
+    rest = call(
+        rest_kernel,
+        (shape((size, 2 * cols), bf),) * half,
+        (me, title_nodes, send_ids[0], node_table, w_graph),
+        smem=(0, 1),
+        scratch=[pltpu.VMEM((fetch, dp), f32)],
+        flops=2 * 10**9,
+        name="rest",
+    )
+    part, mask = lax.optimization_barrier((part, mask))
     hidden, first_hidden, first_terms = call(
         norm_one_kernel,
         (shape((chunk + PAD, width), bf), shape((PAD, width), bf), shape((PAD, width), f32)),
-        (who, titles, gains, w_ffn_in, w_ffn_out, terms[0], *parts),
+        (who, titles, gains, w_ffn_in, w_ffn_out, keep, part),
         smem=(0,),
         name="norm_one",
     )
-    hiddens = [hidden] + [swap(hidden, step) for step in range(1, mp)]
-    *terms, first = call(
+    whose, hiddens = gather(hidden)
+    hiddens, rest = lax.optimization_barrier((hiddens, rest))
+    kept, given, first = call(
         ffn_kernel,
-        tuple(shape((chunk, width), bf if step else f32) for step in range(mp))
-        + (shape((per_part, width), bf),),
+        (
+            shape((2 * chunk, width), f32),
+            shape((2 * chunk, width), bf),
+            shape((per_part, width), bf),
+        ),
         (w_ffn_in, w_ffn_out, gains, first_hidden, first_terms, *hiddens),
         flops=4 * tok_rows * width * w_ffn_in.shape[1],
         name="ffn",
     )
-    parts = [swap(terms[step], step) for step in range(1, mp)]
     turns = dp // mp
     firsts = [
         lax.ppermute(
@@ -444,40 +534,42 @@
         )
         for turn in range(turns)
     ]
-    parts, firsts = lax.optimization_barrier((parts, firsts))
+    recv, far = lax.optimization_barrier((swap(given, 1), far))
+    keep, give = halves(kept, recv, 0)
+    give, far = lax.optimization_barrier((give, far))
+    raw = call(pick_kernel, shape((half * size, 2 * cols), bf), (me, far), smem=(0,), name="pick")
+    part = swap(give, 2)
+    across = swap(raw, 2)
+    rest = [rest[0]] + [swap(rest[step], step, "dp") for step in range(1, half)]
+    part, firsts, across, rest = lax.optimization_barrier((part, firsts, across, rest))
+    blocks = [raw, across, swap(raw, 1), swap(across, 1)]
     done = call(
-        norm_two_kernel,
-        shape((chunk, width), bf),
-        (hidden, gains, terms[0], *parts),
-        name="norm_two",
+        norm_two_kernel, shape((chunk, width), bf), (hidden, gains, keep, part), name="norm_two"
     )
     pack = call(pack_kernel, shape((tail_rows(turns * per_part), width), bf), firsts, name="pack")
     packs = [pack] + [swap(pack, step) for step in range(1, mp)]
-    whose, blocks, step = [0], [done], mp // 2
-    while step:
-        rows = blocks[0]
-        if len(blocks) > 1:
-            dims = (sum(block.shape[0] for block in blocks), width)
-            rows = call(join_kernel, shape(dims, bf), blocks, name="join")
-        blocks = blocks + [swap(rows, step)]
-        whose = whose + [other ^ step for other in whose]
-        step //= 2
+    _, dones = gather(done)
     encoded = call(
         functools.partial(place_kernel, whose),
         shape((tok_rows, width), bf),
-        (who, *blocks),
+        (who, *dones),
         smem=(0,),
         name="place",
     )
-    encoded, far = lax.optimization_barrier((encoded, far))
-
+
+    cross = call(
+        functools.partial(raw_kernel, half, whose),
+        shape((half * fetch, 2 * cols), bf if share % 16 == 0 else f32),
+        (me, who, w_graph, *blocks),
+        smem=(0, 1),
+        flops=2 * 10**9,
+        name="raw",
+    )
     kv, q, first_kv = call(
         own_kernel,
         (shape((nodes, 2 * cols), bf), shape((nodes, cols), bf), shape((dp * per_part, 2 * cols), bf)),
         (who, title_nodes, node_table, w_graph, first, *packs),
-        smem=(0,),
-        hbm=(1, 2, 3),
-        scalars=(1,),
+        smem=(0, 1),
         scratch=[pltpu.VMEM((nodes, width), bf), pltpu.VMEM((dp * per_part, width), f32)],
         flops=2 * 10**9,
         name="own",
@@ -486,18 +578,10 @@
     graph_out = call(
         graph_kernel,
         shape((cols, nodes), bf),
-        (tile_cols, q, kv, first_kv, mask, far),
-        hbm=(2, 1, 4, 0),
-        held=(5,),
-        scalars=(0,),
-        late=True,
-        scratch=[
-            pltpu.VMEM((keys, cols), bf),
-            pltpu.VMEM((keys, cols), bf),
-            pltpu.VMEM(far.shape, bf),
-            pltpu.SemaphoreType.DMA((4,)),
-        ],
-        flops=10**9,
+        (me, tile_cols, q, kv, first_kv, mask, far, cross, *rest),
+        smem=(0, 1),
+        scratch=[pltpu.VMEM((keys, cols), bf), pltpu.VMEM((keys, cols), bf)],
+        flops=4 * 10**9,
         name="graph",
     )
     return (encoded, graph_out.T)

time: 69.9 us -> 67 us (0.959)
  waiting for transfers between devices: 21.5 us -> 13 us
  starting transfers between devices: 19.5 us -> 26 us
  local copies, waits for them, and re-layouts: 2.43 us -> 0.98 us
  other arithmetic: 0.01 us -> 1.09 us
    ppermute x2, waiting for transfers between devices: 10.7 us -> 0.01 us  [local(): lax.ppermute(first, ('dp', 'mp'), [(p * mp + m, (p ^ turn * mp + m) * mp...]
    ppermute x14 -> x19, starting transfers between devices: 8.41 us -> 14.8 us  [swap(): lax.ppermute(value, axis, [(i, i ^ step) for i in range(lax.axis_size(axi...]
    ppermute x14 -> x19, waiting for transfers between devices: 10.9 us -> 13 us  [swap(): lax.ppermute(value, axis, [(i, i ^ step) for i in range(lax.axis_size(axi...]
    unnamed x32 -> x36, local copies, waits for them, and re-layouts: 2.43 us -> 0.98 us
    pallas_call x11 -> x15, Pallas kernels: 24.9 us -> 24.7 us  [call(): pl.pallas_call(body, out_shape=outs, in_specs=specs, out_specs=jax.tree.m...]
  transfers between devices with their start and end apart: 17 -> 22, of which waited for: 6 -> 7; matrix products, arithmetic and copies ran while one was open for 0% -> 0% of each run, Pallas kernels for 21% -> 20%
where the time goes in v9:
time: 67 us; the launch traced here: 66.8 us
  starting transfers between devices  26 us (39%)
  Pallas kernels  24.7 us (37%)
  waiting for transfers between devices  13 us (19%)
  other arithmetic  1.09 us (2%)
  between operations  1 us (1%)
  local copies, waits for them, and re-layouts  0.98 us (1%)
    pallas_call x15, Pallas kernels, call(): pl.pallas_call(body, out_shape=outs, in_specs=specs, out_specs=jax.tree.m...  24.7 us
    ppermute x19, starting transfers between devices, swap(): lax.ppermute(value, axis, [(i, i ^ step) for i in range(lax.axis_size(axi...  14.8 us
    ppermute x19, waiting for transfers between devices, swap(): lax.ppermute(value, axis, [(i, i ^ step) for i in range(lax.axis_size(axi...  13 us
    all_to_all x1, starting transfers between devices, local(): lax.all_to_all(sent.reshape(dp, size, 2 * cols), 'dp', split_axis=0, conc...  7.4 us
    ppermute x2, starting transfers between devices, local(): lax.ppermute(first, ('dp', 'mp'), [(p * mp + m, (p ^ turn * mp + m) * mp...  3.8 us
  transfers between devices with their start and end apart: 22, of which 7 were waited for; matrix products, arithmetic and copies ran while one was open for 0% of the time, Pallas kernels for 20%

profile of v9, /device:TPU:0, one launch (start us, length us, event | category | flops | bytes accessed | tf_op | source)
XLA Modules:
  0.0 66.8 jit_solution(16402349621896335877)
XLA Ops:
  0.6 0.5 iota_xor_fusion.refs_1_.refs_0_
  1.2 0.6 pad_add_fusion.refs_0_
  1.7 4.4 %send.1 = bf16[1024,384]{1,0:T(8,128)(2,1)} custom-call(s32[2]{0:T(128)} %pad_add_fusion.refs_0_, s32[4]{0:T(128)} %iota_xor_fusion.refs_1_.refs_0_, s32[2]{0:T(128)} %refs_1_.10, s32[8,256]{1,0:T(8,128)} %bitcast.17, bf16[512,768]{1,0:T(8,128)(2,1)} %refs_2_.7, bf16[3,192,768]{2,1,0:T(8,128)(2,1)} %bitcast.12), custom_call_target="tpu_custom_call" | custom-call | flops 3000000000 | bytes 1679392 | tf_op jit(solution)/shard_map/send/pallas_call | solution.py:62
  6.1 0.0 copy-start.2
  6.1 0.0 copy-start.3
  6.2 0.0 copy-start.4
  6.2 0.0 copy-start.6
  6.2 7.4 %all-to-all-start = ((bf16[8,128,384]{2,1,0:T(8,128)(2,1)}), bf16[8,128,384]{2,1,0:T(8,128)(2,1)S(1)}, u32[]{:S(2)}, u32[]{:S(2)}) async-start(bf16[8,128,384]{2,1,0:T(8,128)(2,1)} %bitcast.19), calls=%async_computation | async-start | bytes 1572864 | tf_op jit(solution)/shard_map/all_to_all | solution.py:474
  13.6 2.3 %attn.1 = (f32[144,768]{1,0:T(8,128)S(1)}, bf16[144,768]{1,0:T(8,128)(2,1)S(1)}) custom-call(s32[4]{0:T(128)S(1)} %copy-done.6, bf16[256,768]{1,0:T(8,128)(2,1)S(1)} %copy-done.2, bf16[3,192,768]{2,1,0:T(8,128)(2,1)S(1)} %bitcast.11, bf16[192,768]{1,0:T(8,128)(2,1)S(1)} %copy-done.4), custom_call_target="tpu_custom_call" | custom-call | flops 301989888 | bytes 1572880 | tf_op jit(solution)/shard_map/attn/pallas_call | solution.py:62
  15.9 0.1 collective-permute-start
  16.0 1.5 %collective-permute-done.refs_1_ = bf16[144,768]{1,0:T(8,128)(2,1)S(1)} collective-permute-done((bf16[144,768]{1,0:T(8,128)(2,1)S(1)}, bf16[144,768]{1,0:T(8,128)(2,1)S(1)}, u32[]{:S(2)}, u32[]{:S(2)}) %collective-permute-start) | collective-permute-done | bytes 221216 | tf_op jit(solution)/shard_map/ppermute | solution.py:441
  17.4 0.1 half.2
  17.5 1.6 %collective-permute-start.1 = (bf16[80,768]{1,0:T(8,128)(2,1)S(1)}, bf16[80,768]{1,0:T(8,128)(2,1)S(1)}, u32[]{:S(2)}, u32[]{:S(2)}) collective-permute-start(bf16[80,768]{1,0:T(8,128)(2,1)S(1)} %get-tuple-element.48), channel_id=1, source_target_pairs={{0,2},{1,3},{2,0},{3,1},{4,6},{5,7},{6,4},{7,5},{8,10},{9,11},{10,... | collective-permute-start | bytes 368648 | tf_op jit(solution)/shard_map/ppermute | solution.py:441
  19.1 4.2 %mask.1.refs_5_ = bf16[512,768]{1,0:T(8,128)(2,1)S(1)} custom-call(s32[16,512]{1,0:T(8,128)S(1)} %bitcast.16), custom_call_target="tpu_custom_call" | custom-call | flops 4000000000 | bytes 32768 | tf_op jit(solution)/shard_map/mask/pallas_call | solution.py:62
  23.4 0.9 %copy-done.14 = bf16[512,768]{1,0:T(8,128)(2,1)} copy-done((bf16[512,768]{1,0:T(8,128)(2,1)}, bf16[512,768]{1,0:T(8,128)(2,1)S(1)}, u32[]{:S(2)}) %copy-start.14) | copy-done | bytes 786456
  24.2 0.0 collective-permute-done.1.refs_6_
  24.3 0.0 copy-start.8
  24.3 0.0 copy-start.9
  24.3 0.0 copy-start.11
  24.3 0.0 copy-start.13
  24.3 1.2 %norm_one.1 = (bf16[80,768]{1,0:T(8,128)(2,1)S(1)}, bf16[16,768]{1,0:T(8,128)(2,1)S(1)}, f32[16,768]{1,0:T(8,128)S(1)}) custom-call(s32[4]{0:T(128)S(1)} %copy-done.6, bf16[256,768]{1,0:T(8,128)(2,1)S(1)} %copy-done.2, f32[2,768]{1,0:T(2,128)S(1)} %copy-done.5, bf16[768,768]{1,0:T(8,128)(2,1)S(1)} %copy-done, bf16[768,768]{1,0:T(8,128)(2,1)S(1)} %copy-done.1, ...), custom_call_target="tpu_custom_call" | custom-call | bytes 3127312 | tf_op jit(solution)/shard_map/norm_one/pallas_call | solution.py:62
  25.6 0.5 collective-permute-start.2
  26.1 0.0 collective-permute-start.3
  26.1 4.6 %collective-permute-done.2.refs_6_ = bf16[80,768]{1,0:T(8,128)(2,1)S(1)} collective-permute-done((bf16[80,768]{1,0:T(8,128)(2,1)S(1)}, bf16[80,768]{1,0:T(8,128)(2,1)S(1)}, u32[]{:S(2)}, u32[]{:S(2)}) %collective-permute-start.2) | collective-permute-done | bytes 122912 | tf_op jit(solution)/shard_map/ppermute | solution.py:441
  30.7 0.0 collective-permute-start.4
  30.7 1.6 %rest.1 = (bf16[128,384]{1,0:T(8,128)(2,1)S(1)}, bf16[128,384]{1,0:T(8,128)(2,1)S(1)}, bf16[128,384]{1,0:T(8,128)(2,1)S(1)}, bf16[128,384]{1,0:T(8,128)(2,1)S(1)}) custom-call(s32[2]{0:T(128)S(1)} %copy-done.7, s32[2]{0:T(128)S(1)} %copy-done.13, s32[8,256]{1,0:T(8,128)S(1)} %bitcast.18, bf16[512,768]{1,0:T(8,128)(2,1)S(1)} %copy-done.9, ...), custom_call_target="tpu_custom_call" | custom-call | flops 2000000000 | bytes 1679376 | tf_op jit(solution)/shard_map/rest/pallas_call | solution.py:62
  32.3 0.0 copy-start.16
  32.3 0.0 collective-permute-done.3.refs_7_
  32.4 0.0 collective-permute-done.4.refs_8_
  32.4 0.9 %ffn.1 = (f32[128,768]{1,0:T(8,128)S(1)}, bf16[128,768]{1,0:T(8,128)(2,1)S(1)}, bf16[2,768]{1,0:T(2,128)(2,1)S(1)}) custom-call(bf16[768,768]{1,0:T(8,128)(2,1)S(1)} %copy-done, bf16[768,768]{1,0:T(8,128)(2,1)S(1)} %copy-done.1, f32[2,768]{1,0:T(2,128)S(1)} %copy-done.5, bf16[16,768]{1,0:T(8,128)(2,1)S(1)} %get-tuple-element.51.refs_3_, ...), custom_call_target="tpu_custom_call" | custom-call | flops 603979776 | bytes 2930688 | tf_op jit(solution)/shard_map/ffn/pallas_call | solution.py:62
  33.3 0.6 collective-permute-start.5
  33.9 1.1 %collective-permute-done.5.refs_1_ = bf16[128,768]{1,0:T(8,128)(2,1)S(1)} collective-permute-done((bf16[128,768]{1,0:T(8,128)(2,1)S(1)}, bf16[128,768]{1,0:T(8,128)(2,1)S(1)}, u32[]{:S(2)}, u32[]{:S(2)}) %collective-permute-start.5) | collective-permute-done | bytes 196640 | tf_op jit(solution)/shard_map/ppermute | solution.py:441
  34.9 0.0 all-to-all-done
  35.0 0.6 pick.1.refs_3_
  35.6 0.6 collective-permute-start.9
  36.2 0.8 %collective-permute-start.7 = (bf16[2,768]{1,0:T(2,128)(2,1)S(1)}, bf16[2,768]{1,0:T(2,128)(2,1)S(1)}, u32[]{:S(2)}, u32[]{:S(2)}) collective-permute-start(bf16[2,768]{1,0:T(2,128)(2,1)S(1)} %get-tuple-element.68.refs_4_), channel_id=1, source_target_pairs={{1,5},{2,10},{3,15},{5,1},{6,14},{7,11},{9,13},{10,2},{11,7},{13,9... | collective-permute-start | bytes 9224 | tf_op jit(solution)/shard_map/ppermute | solution.py:525
  37.0 3.0 %collective-permute-start.8 = (bf16[2,768]{1,0:T(2,128)(2,1)S(1)}, bf16[2,768]{1,0:T(2,128)(2,1)S(1)}, u32[]{:S(2)}, u32[]{:S(2)}) collective-permute-start(bf16[2,768]{1,0:T(2,128)(2,1)S(1)} %get-tuple-element.68.refs_4_), channel_id=1, source_target_pairs={{0,16},{1,21},{2,26},{3,31},{4,20},{5,17},{6,30},{7,27},{8,24},{9,... | collective-permute-start | bytes 9224 | tf_op jit(solution)/shard_map/ppermute | solution.py:525
  40.0 1.5 %collective-permute-start.10 = (bf16[128,384]{1,0:T(8,128)(2,1)S(1)}, bf16[128,384]{1,0:T(8,128)(2,1)S(1)}, u32[]{:S(2)}, u32[]{:S(2)}) collective-permute-start(bf16[128,384]{1,0:T(8,128)(2,1)S(1)} %get-tuple-element.71), channel_id=1, source_target_pairs={{0,4},{4,0},{8,12},{12,8},{16,20},{20,16},{24,28},{28,24},{1,5},{5... | collective-permute-start | bytes 294920 | tf_op jit(solution)/shard_map/ppermute | solution.py:441
  41.4 1.5 %collective-permute-start.11 = (bf16[128,384]{1,0:T(8,128)(2,1)S(1)}, bf16[128,384]{1,0:T(8,128)(2,1)S(1)}, u32[]{:S(2)}, u32[]{:S(2)}) collective-permute-start(bf16[128,384]{1,0:T(8,128)(2,1)S(1)} %get-tuple-element.72), channel_id=1, source_target_pairs={{0,8},{4,12},{8,0},{12,4},{16,24},{20,28},{24,16},{28,20},{1,9},{5... | collective-permute-start | bytes 294920 | tf_op jit(solution)/shard_map/ppermute | solution.py:441
  42.9 0.0 collective-permute-done.7.refs_0_
  42.9 0.6 collective-permute-start.12
  43.5 0.0 collective-permute-done.8.refs_1_
  43.5 4.2 %collective-permute-start.6 = (bf16[64,768]{1,0:T(8,128)(2,1)S(1)}, bf16[64,768]{1,0:T(8,128)(2,1)S(1)}, u32[]{:S(2)}, u32[]{:S(2)}) collective-permute-start(bf16[64,768]{1,0:T(8,128)(2,1)S(1)} %get-tuple-element.67), channel_id=1, source_target_pairs={{0,2},{1,3},{2,0},{3,1},{4,6},{5,7},{6,4},{7,5},{8,10},{9,11},{10,... | collective-permute-start | bytes 294920 | tf_op jit(solution)/shard_map/ppermute | solution.py:441
  47.7 0.0 collective-permute-done.10.refs_9_
  47.7 0.0 collective-permute-start.19
  47.7 0.0 collective-permute-done.11.refs_10_
  47.7 1.1 %collective-permute-done.12.refs_11_ = bf16[128,384]{1,0:T(8,128)(2,1)S(1)} collective-permute-done((bf16[128,384]{1,0:T(8,128)(2,1)S(1)}, bf16[128,384]{1,0:T(8,128)(2,1)S(1)}, u32[]{:S(2)}, u32[]{:S(2)}) %collective-permute-start.12) | collective-permute-done | bytes 98336 | tf_op jit(solution)/shard_map/ppermute | solution.py:441
  48.8 1.9 %collective-permute-done.6.refs_3_ = bf16[64,768]{1,0:T(8,128)(2,1)S(1)} collective-permute-done((bf16[64,768]{1,0:T(8,128)(2,1)S(1)}, bf16[64,768]{1,0:T(8,128)(2,1)S(1)}, u32[]{:S(2)}, u32[]{:S(2)}) %collective-permute-start.6) | collective-permute-done | bytes 98336 | tf_op jit(solution)/shard_map/ppermute | solution.py:441
  50.7 0.0 collective-permute-done.9.refs_4_
  50.7 0.2 norm_two.1.refs_1_
  50.9 2.0 %collective-permute-start.13 = (bf16[64,768]{1,0:T(8,128)(2,1)S(1)}, bf16[64,768]{1,0:T(8,128)(2,1)S(1)}, u32[]{:S(2)}, u32[]{:S(2)}) collective-permute-start(bf16[64,768]{1,0:T(8,128)(2,1)S(1)} %norm_two.1.refs_1_), channel_id=1, source_target_pairs={{0,2},{1,3},{2,0},{3,1},{4,6},{5,7},{6,4},{7,5},{8,10},{9,11},{10,... | collective-permute-start | bytes 294920 | tf_op jit(solution)/shard_map/ppermute | solution.py:441
  52.9 0.3 collective-permute-start.16
  53.2 0.3 collective-permute-start.17
  53.5 0.7 %collective-permute-done.16.refs_6_ = bf16[16,768]{1,0:T(8,128)(2,1)S(1)} collective-permute-done((bf16[16,768]{1,0:T(8,128)(2,1)S(1)}, bf16[16,768]{1,0:T(8,128)(2,1)S(1)}, u32[]{:S(2)}, u32[]{:S(2)}) %collective-permute-start.16) | collective-permute-done | bytes 24608 | tf_op jit(solution)/shard_map/ppermute | solution.py:441
  54.2 0.7 %collective-permute-start.18 = (bf16[16,768]{1,0:T(8,128)(2,1)S(1)}, bf16[16,768]{1,0:T(8,128)(2,1)S(1)}, u32[]{:S(2)}, u32[]{:S(2)}) collective-permute-start(bf16[16,768]{1,0:T(8,128)(2,1)S(1)} %pack.1.refs_5_), channel_id=1, source_target_pairs={{0,3},{1,2},{2,1},{3,0},{4,7},{5,6},{6,5},{7,4},{8,11},{9,10},{10,... | collective-permute-start | bytes 73736 | tf_op jit(solution)/shard_map/ppermute | solution.py:441
  54.9 2.2 %collective-permute-done.17.refs_7_ = bf16[16,768]{1,0:T(8,128)(2,1)S(1)} collective-permute-done((bf16[16,768]{1,0:T(8,128)(2,1)S(1)}, bf16[16,768]{1,0:T(8,128)(2,1)S(1)}, u32[]{:S(2)}, u32[]{:S(2)}) %collective-permute-start.17) | collective-permute-done | bytes 24608 | tf_op jit(solution)/shard_map/ppermute | solution.py:441
  57.0 0.0 collective-permute-start.14
  57.0 0.5 collective-permute-start.15
  57.6 1.6 %own.1 = (bf16[512,384]{1,0:T(8,128)(2,1)S(1)}, bf16[512,192]{1,0:T(8,128)(2,1)S(1)}, bf16[16,384]{1,0:T(8,128)(2,1)S(1)}) custom-call(s32[4]{0:T(128)S(1)} %copy-done.6, s32[2]{0:T(128)S(1)} %copy-done.13, bf16[512,768]{1,0:T(8,128)(2,1)S(1)} %copy-done.9, bf16[3,192,768]{2,1,0:T(8,128)(2,1)S(1)} %bitcast.14, bf16[2,768]{1,0:T(2,128)(2,1)S(1)} %get-tuple-element.68.refs_4_, ...), custom_call_target="tpu_custom_call" | custom-call | flops 2000000000 | bytes 1772568 | tf_op jit(solution)/shard_map/own/pallas_call | solution.py:62
  59.2 0.0 collective-permute-done.15.refs_4_
  59.2 1.3 %place.1 = bf16[256,768]{1,0:T(8,128)(2,1)} custom-call(s32[4]{0:T(128)S(1)} %copy-done.6, bf16[64,768]{1,0:T(8,128)(2,1)S(1)} %norm_two.1.refs_1_, bf16[64,768]{1,0:T(8,128)(2,1)S(1)} %collective-permute-done.13.refs_2_, bf16[64,768]{1,0:T(8,128)(2,1)S(1)} %collective-permute-done.14.refs_3_, bf16[64,768]{1,0:T(8,128)(2,1)S(1)} %collective-permute-done.15.refs_4_), custom_call_target="tpu_custom_call" | custom-call | bytes 393232 | tf_op jit(solution)/shard_map/place/pallas_call | solution.py:62
  60.5 0.0 collective-permute-done.19.refs_5_
  60.5 1.7 %raw.1.refs_7_ = bf16[1024,384]{1,0:T(8,128)(2,1)S(1)} custom-call(s32[2]{0:T(128)S(1)} %copy-done.7, s32[4]{0:T(128)S(1)} %copy-done.6, bf16[3,192,768]{2,1,0:T(8,128)(2,1)S(1)} %bitcast.15, bf16[512,384]{1,0:T(8,128)(2,1)S(1)} %pick.1.refs_3_, bf16[512,384]{1,0:T(8,128)(2,1)S(1)} %collective-permute-done.9.refs_4_, ...), custom_call_target="tpu_custom_call" | custom-call | flops 2000000000 | bytes 2457624 | tf_op jit(solution)/shard_map/raw/pallas_call | solution.py:62
  62.3 4.5 %graph.1 = bf16[192,512]{1,0:T(8,128)(2,1)} custom-call(s32[2]{0:T(128)S(1)} %copy-done.7, s32[4,6]{1,0:T(4,128)S(1)} %copy-done.12, bf16[512,192]{1,0:T(8,128)(2,1)S(1)} %get-tuple-element.77.refs_2_, bf16[512,384]{1,0:T(8,128)(2,1)S(1)} %get-tuple-element.78.refs_3_, bf16[16,384]{1,0:T(8,128)(2,1)S(1)} %get-tuple-element.79.refs_4_, ...), custom_call_target="tpu_custom_call" | custom-call | flops 4000000000 | bytes 3354728 | tf_op jit(solution)/shard_map/graph/pallas_call | solution.py:62
  (33 shorter events, 0.1 us)
Async XLA Ops:
  6.1 7.5 %copy-start.2 = (bf16[256,768]{1,0:T(8,128)(2,1)S(1)}, bf16[256,768]{1,0:T(8,128)(2,1)}, u32[]{:S(2)}) copy-start(bf16[256,768]{1,0:T(8,128)(2,1)} %refs_1_.6) | copy-start | bytes 1179652
  6.1 7.4 %copy-start.3 = (bf16[3,768,192]{1,2,0:T(8,128)(2,1)S(1)}, bf16[3,768,192]{1,2,0:T(8,128)(2,1)}, u32[]{:S(2)}) copy-start(bf16[3,768,192]{1,2,0:T(8,128)(2,1)} %param.13) | copy-start | bytes 2654212
  6.2 7.4 %copy-start.4 = (bf16[192,768]{1,0:T(8,128)(2,1)S(1)}, bf16[192,768]{1,0:T(8,128)(2,1)}, u32[]{:S(2)}) copy-start(bf16[192,768]{1,0:T(8,128)(2,1)} %refs_3_.3) | copy-start | bytes 884740
  6.2 7.4 %copy-start.6 = (s32[4]{0:T(128)S(1)}, s32[4]{0:T(128)}, u32[]{:S(2)}) copy-start(s32[4]{0:T(128)} %iota_xor_fusion.refs_1_.refs_0_) | copy-start | bytes 52
  6.2 28.8 %all-to-all-start = ((bf16[8,128,384]{2,1,0:T(8,128)(2,1)}), bf16[8,128,384]{2,1,0:T(8,128)(2,1)S(1)}, u32[]{:S(2)}, u32[]{:S(2)}) async-start(bf16[8,128,384]{2,1,0:T(8,128)(2,1)} %bitcast.19), calls=%async_computation | async-start | bytes 1572864 | tf_op jit(solution)/shard_map/all_to_all | solution.py:474
  13.6 5.5 %copy-start.10 = (s32[512,16]{0,1:T(8,128)S(1)}, s32[512,16]{0,1:T(8,128)}, u32[]{:S(2)}) copy-start(s32[512,16]{0,1:T(8,128)} %param.23) | copy-start | bytes 98308
  15.9 1.5 %collective-permute-start = (bf16[144,768]{1,0:T(8,128)(2,1)S(1)}, bf16[144,768]{1,0:T(8,128)(2,1)S(1)}, u32[]{:S(2)}, u32[]{:S(2)}) collective-permute-start(bf16[144,768]{1,0:T(8,128)(2,1)S(1)} %get-tuple-element.46), channel_id=1, source_target_pairs={{0,1},{1,0},{2,3},{3,2},{4,5},{5,4},{6,7},{7,6},{8,9},{9,8},{10,11... | collective-permute-start | bytes 663560 | tf_op jit(solution)/shard_map/ppermute | solution.py:441
  17.5 6.8 %collective-permute-start.1 = (bf16[80,768]{1,0:T(8,128)(2,1)S(1)}, bf16[80,768]{1,0:T(8,128)(2,1)S(1)}, u32[]{:S(2)}, u32[]{:S(2)}) collective-permute-start(bf16[80,768]{1,0:T(8,128)(2,1)S(1)} %get-tuple-element.48), channel_id=1, source_target_pairs={{0,2},{1,3},{2,0},{3,1},{4,6},{5,7},{6,4},{7,5},{8,10},{9,11},{10,... | collective-permute-start | bytes 368648 | tf_op jit(solution)/shard_map/ppermute | solution.py:441
  19.1 5.2 %copy-start = (bf16[768,768]{1,0:T(8,128)(2,1)S(1)}, bf16[768,768]{1,0:T(8,128)(2,1)}, u32[]{:S(2)}) copy-start(bf16[768,768]{1,0:T(8,128)(2,1)} %refs_0_.1) | copy-start | bytes 3538948
  19.1 5.2 %copy-start.1 = (bf16[768,768]{1,0:T(8,128)(2,1)S(1)}, bf16[768,768]{1,0:T(8,128)(2,1)}, u32[]{:S(2)}) copy-start(bf16[768,768]{1,0:T(8,128)(2,1)} %refs_1_.8) | copy-start | bytes 3538948
  19.1 5.2 %copy-start.5 = (f32[2,768]{1,0:T(2,128)S(1)}, f32[2,768]{1,0:T(2,128)}, u32[]{:S(2)}) copy-start(f32[2,768]{1,0:T(2,128)} %refs_1_.9) | copy-start | bytes 18436
  23.3 0.9 %copy-start.14 = (bf16[512,768]{1,0:T(8,128)(2,1)}, bf16[512,768]{1,0:T(8,128)(2,1)S(1)}, u32[]{:S(2)}) copy-start(bf16[512,768]{1,0:T(8,128)(2,1)S(1)} %mask.1.refs_5_) | copy-start | bytes 2359300
  24.3 6.4 %copy-start.7 = (s32[2]{0:T(128)S(1)}, s32[2]{0:T(128)}, u32[]{:S(2)}) copy-start(s32[2]{0:T(128)} %pad_add_fusion.refs_0_) | copy-start | bytes 28
  24.3 6.4 %copy-start.8 = (bf16[3,768,192]{1,2,0:T(8,128)(2,1)S(1)}, bf16[3,768,192]{1,2,0:T(8,128)(2,1)}, u32[]{:S(2)}) copy-start(bf16[3,768,192]{1,2,0:T(8,128)(2,1)} %param.19) | copy-start | bytes 2654212
  24.3 6.4 %copy-start.9 = (bf16[512,768]{1,0:T(8,128)(2,1)S(1)}, bf16[512,768]{1,0:T(8,128)(2,1)}, u32[]{:S(2)}) copy-start(bf16[512,768]{1,0:T(8,128)(2,1)} %refs_2_.7) | copy-start | bytes 2359300
  24.3 6.4 %copy-start.11 = (s32[1,8,256]{2,1,0:T(8,128)S(1)}, s32[1,8,256]{2,1,0:T(8,128)}, u32[]{:S(2)}) copy-start(s32[1,8,256]{2,1,0:T(8,128)} %param.21) | copy-start | bytes 24580
  24.3 6.4 %copy-start.13 = (s32[2]{0:T(128)S(1)}, s32[2]{0:T(128)}, u32[]{:S(2)}) copy-start(s32[2]{0:T(128)} %refs_1_.10) | copy-start | bytes 28
  25.6 5.1 %collective-permute-start.2 = (bf16[80,768]{1,0:T(8,128)(2,1)S(1)}, bf16[80,768]{1,0:T(8,128)(2,1)S(1)}, u32[]{:S(2)}, u32[]{:S(2)}) collective-permute-start(bf16[80,768]{1,0:T(8,128)(2,1)S(1)} %get-tuple-element.57.refs_5_.refs_0_), channel_id=1, source_target_pairs={{0,2},{1,3},{2,0},{3,1},{4,6},{5,7},{6,4},{7,5},{8,10},{9,11},{10,... | collective-permute-start | bytes 368648 | tf_op jit(solution)/shard_map/ppermute | solution.py:441
  26.1 6.3 %collective-permute-start.3 = (bf16[80,768]{1,0:T(8,128)(2,1)S(1)}, bf16[80,768]{1,0:T(8,128)(2,1)S(1)}, u32[]{:S(2)}, u32[]{:S(2)}) collective-permute-start(bf16[80,768]{1,0:T(8,128)(2,1)S(1)} %get-tuple-element.57.refs_5_.refs_0_), channel_id=1, source_target_pairs={{0,1},{1,0},{2,3},{3,2},{4,5},{5,4},{6,7},{7,6},{8,9},{9,8},{10,11... | collective-permute-start | bytes 368648 | tf_op jit(solution)/shard_map/ppermute | solution.py:441
  30.7 1.7 %collective-permute-start.4 = (bf16[80,768]{1,0:T(8,128)(2,1)S(1)}, bf16[80,768]{1,0:T(8,128)(2,1)S(1)}, u32[]{:S(2)}, u32[]{:S(2)}) collective-permute-start(bf16[80,768]{1,0:T(8,128)(2,1)S(1)} %collective-permute-done.2.refs_6_), channel_id=1, source_target_pairs={{0,1},{1,0},{2,3},{3,2},{4,5},{5,4},{6,7},{7,6},{8,9},{9,8},{10,11... | collective-permute-start | bytes 368648 | tf_op jit(solution)/shard_map/ppermute | solution.py:441
  32.3 1.0 %copy-start.16 = (bf16[128,384]{1,0:T(8,128)(2,1)}, bf16[128,384]{1,0:T(8,128)(2,1)S(1)}, u32[]{:S(2)}) copy-start(bf16[128,384]{1,0:T(8,128)(2,1)S(1)} %get-tuple-element.82.refs_8_) | copy-start | bytes 294916
  33.3 1.6 %collective-permute-start.5 = (bf16[128,768]{1,0:T(8,128)(2,1)S(1)}, bf16[128,768]{1,0:T(8,128)(2,1)S(1)}, u32[]{:S(2)}, u32[]{:S(2)}) collective-permute-start(bf16[128,768]{1,0:T(8,128)(2,1)S(1)} %get-tuple-element.62), channel_id=1, source_target_pairs={{0,1},{1,0},{2,3},{3,2},{4,5},{5,4},{6,7},{7,6},{8,9},{9,8},{10,11... | collective-permute-start | bytes 589832 | tf_op jit(solution)/shard_map/ppermute | solution.py:441
  35.6 15.2 %collective-permute-start.9 = (bf16[512,384]{1,0:T(8,128)(2,1)S(1)}, bf16[512,384]{1,0:T(8,128)(2,1)S(1)}, u32[]{:S(2)}, u32[]{:S(2)}) collective-permute-start(bf16[512,384]{1,0:T(8,128)(2,1)S(1)} %pick.1.refs_3_), channel_id=1, source_target_pairs={{0,2},{1,3},{2,0},{3,1},{4,6},{5,7},{6,4},{7,5},{8,10},{9,11},{10,... | collective-permute-start | bytes 1179656 | tf_op jit(solution)/shard_map/ppermute | solution.py:441
  36.2 6.7 %collective-permute-start.7 = (bf16[2,768]{1,0:T(2,128)(2,1)S(1)}, bf16[2,768]{1,0:T(2,128)(2,1)S(1)}, u32[]{:S(2)}, u32[]{:S(2)}) collective-permute-start(bf16[2,768]{1,0:T(2,128)(2,1)S(1)} %get-tuple-element.68.refs_4_), channel_id=1, source_target_pairs={{1,5},{2,10},{3,15},{5,1},{6,14},{7,11},{9,13},{10,2},{11,7},{13,9... | collective-permute-start | bytes 9224 | tf_op jit(solution)/shard_map/ppermute | solution.py:525
  37.0 6.5 %collective-permute-start.8 = (bf16[2,768]{1,0:T(2,128)(2,1)S(1)}, bf16[2,768]{1,0:T(2,128)(2,1)S(1)}, u32[]{:S(2)}, u32[]{:S(2)}) collective-permute-start(bf16[2,768]{1,0:T(2,128)(2,1)S(1)} %get-tuple-element.68.refs_4_), channel_id=1, source_target_pairs={{0,16},{1,21},{2,26},{3,31},{4,20},{5,17},{6,30},{7,27},{8,24},{9,... | collective-permute-start | bytes 9224 | tf_op jit(solution)/shard_map/ppermute | solution.py:525
  40.0 7.7 %collective-permute-start.10 = (bf16[128,384]{1,0:T(8,128)(2,1)S(1)}, bf16[128,384]{1,0:T(8,128)(2,1)S(1)}, u32[]{:S(2)}, u32[]{:S(2)}) collective-permute-start(bf16[128,384]{1,0:T(8,128)(2,1)S(1)} %get-tuple-element.71), channel_id=1, source_target_pairs={{0,4},{4,0},{8,12},{12,8},{16,20},{20,16},{24,28},{28,24},{1,5},{5... | collective-permute-start | bytes 294920 | tf_op jit(solution)/shard_map/ppermute | solution.py:441
  41.4 6.3 %collective-permute-start.11 = (bf16[128,384]{1,0:T(8,128)(2,1)S(1)}, bf16[128,384]{1,0:T(8,128)(2,1)S(1)}, u32[]{:S(2)}, u32[]{:S(2)}) collective-permute-start(bf16[128,384]{1,0:T(8,128)(2,1)S(1)} %get-tuple-element.72), channel_id=1, source_target_pairs={{0,8},{4,12},{8,0},{12,4},{16,24},{20,28},{24,16},{28,20},{1,9},{5... | collective-permute-start | bytes 294920 | tf_op jit(solution)/shard_map/ppermute | solution.py:441
  42.9 5.9 %collective-permute-start.12 = (bf16[128,384]{1,0:T(8,128)(2,1)S(1)}, bf16[128,384]{1,0:T(8,128)(2,1)S(1)}, u32[]{:S(2)}, u32[]{:S(2)}) collective-permute-start(bf16[128,384]{1,0:T(8,128)(2,1)S(1)} %get-tuple-element.73), channel_id=1, source_target_pairs={{0,12},{4,8},{8,4},{12,0},{16,28},{20,24},{24,20},{28,16},{1,13},{... | collective-permute-start | bytes 294920 | tf_op jit(solution)/shard_map/ppermute | solution.py:441
  43.5 7.3 %collective-permute-start.6 = (bf16[64,768]{1,0:T(8,128)(2,1)S(1)}, bf16[64,768]{1,0:T(8,128)(2,1)S(1)}, u32[]{:S(2)}, u32[]{:S(2)}) collective-permute-start(bf16[64,768]{1,0:T(8,128)(2,1)S(1)} %get-tuple-element.67), channel_id=1, source_target_pairs={{0,2},{1,3},{2,0},{3,1},{4,6},{5,7},{6,4},{7,5},{8,10},{9,11},{10,... | collective-permute-start | bytes 294920 | tf_op jit(solution)/shard_map/ppermute | solution.py:441
  47.7 12.8 %collective-permute-start.19 = (bf16[512,384]{1,0:T(8,128)(2,1)S(1)}, bf16[512,384]{1,0:T(8,128)(2,1)S(1)}, u32[]{:S(2)}, u32[]{:S(2)}) collective-permute-start(bf16[512,384]{1,0:T(8,128)(2,1)S(1)} %pick.1.refs_3_), channel_id=1, source_target_pairs={{0,1},{1,0},{2,3},{3,2},{4,5},{5,4},{6,7},{7,6},{8,9},{9,8},{10,11... | collective-permute-start | bytes 1179656 | tf_op jit(solution)/shard_map/ppermute | solution.py:441
  50.7 9.8 %collective-permute-start.20 = (bf16[512,384]{1,0:T(8,128)(2,1)S(1)}, bf16[512,384]{1,0:T(8,128)(2,1)S(1)}, u32[]{:S(2)}, u32[]{:S(2)}) collective-permute-start(bf16[512,384]{1,0:T(8,128)(2,1)S(1)} %collective-permute-done.9.refs_4_), channel_id=1, source_target_pairs={{0,1},{1,0},{2,3},{3,2},{4,5},{5,4},{6,7},{7,6},{8,9},{9,8},{10,11... | collective-permute-start | bytes 1179656 | tf_op jit(solution)/shard_map/ppermute | solution.py:441
  50.9 6.1 %collective-permute-start.13 = (bf16[64,768]{1,0:T(8,128)(2,1)S(1)}, bf16[64,768]{1,0:T(8,128)(2,1)S(1)}, u32[]{:S(2)}, u32[]{:S(2)}) collective-permute-start(bf16[64,768]{1,0:T(8,128)(2,1)S(1)} %norm_two.1.refs_1_), channel_id=1, source_target_pairs={{0,2},{1,3},{2,0},{3,1},{4,6},{5,7},{6,4},{7,5},{8,10},{9,11},{10,... | collective-permute-start | bytes 294920 | tf_op jit(solution)/shard_map/ppermute | solution.py:441
  52.9 1.3 %collective-permute-start.16 = (bf16[16,768]{1,0:T(8,128)(2,1)S(1)}, bf16[16,768]{1,0:T(8,128)(2,1)S(1)}, u32[]{:S(2)}, u32[]{:S(2)}) collective-permute-start(bf16[16,768]{1,0:T(8,128)(2,1)S(1)} %pack.1.refs_5_), channel_id=1, source_target_pairs={{0,1},{1,0},{2,3},{3,2},{4,5},{5,4},{6,7},{7,6},{8,9},{9,8},{10,11... | collective-permute-start | bytes 73736 | tf_op jit(solution)/shard_map/ppermute | solution.py:441
  53.2 3.8 %collective-permute-start.17 = (bf16[16,768]{1,0:T(8,128)(2,1)S(1)}, bf16[16,768]{1,0:T(8,128)(2,1)S(1)}, u32[]{:S(2)}, u32[]{:S(2)}) collective-permute-start(bf16[16,768]{1,0:T(8,128)(2,1)S(1)} %pack.1.refs_5_), channel_id=1, source_target_pairs={{0,2},{1,3},{2,0},{3,1},{4,6},{5,7},{6,4},{7,5},{8,10},{9,11},{10,... | collective-permute-start | bytes 73736 | tf_op jit(solution)/shard_map/ppermute | solution.py:441
  54.2 3.4 %collective-permute-start.18 = (bf16[16,768]{1,0:T(8,128)(2,1)S(1)}, bf16[16,768]{1,0:T(8,128)(2,1)S(1)}, u32[]{:S(2)}, u32[]{:S(2)}) collective-permute-start(bf16[16,768]{1,0:T(8,128)(2,1)S(1)} %pack.1.refs_5_), channel_id=1, source_target_pairs={{0,3},{1,2},{2,1},{3,0},{4,7},{5,6},{6,5},{7,4},{8,11},{9,10},{10,... | collective-permute-start | bytes 73736 | tf_op jit(solution)/shard_map/ppermute | solution.py:441
  57.0 2.1 %collective-permute-start.14 = (bf16[64,768]{1,0:T(8,128)(2,1)S(1)}, bf16[64,768]{1,0:T(8,128)(2,1)S(1)}, u32[]{:S(2)}, u32[]{:S(2)}) collective-permute-start(bf16[64,768]{1,0:T(8,128)(2,1)S(1)} %norm_two.1.refs_1_), channel_id=1, source_target_pairs={{0,1},{1,0},{2,3},{3,2},{4,5},{5,4},{6,7},{7,6},{8,9},{9,8},{10,11... | collective-permute-start | bytes 294920 | tf_op jit(solution)/shard_map/ppermute | solution.py:441
  57.0 2.1 %collective-permute-start.15 = (bf16[64,768]{1,0:T(8,128)(2,1)S(1)}, bf16[64,768]{1,0:T(8,128)(2,1)S(1)}, u32[]{:S(2)}, u32[]{:S(2)}) collective-permute-start(bf16[64,768]{1,0:T(8,128)(2,1)S(1)} %collective-permute-done.13.refs_2_), channel_id=1, source_target_pairs={{0,1},{1,0},{2,3},{3,2},{4,5},{5,4},{6,7},{7,6},{8,9},{9,8},{10,11... | collective-permute-start | bytes 294920 | tf_op jit(solution)/shard_map/ppermute | solution.py:441
  60.5 1.8 %copy-start.12 = (s32[4,6]{1,0:T(4,128)S(1)}, s32[4,6]{1,0:T(4,128)}, u32[]{:S(2)}) copy-start(s32[4,6]{1,0:T(4,128)} %refs_1_.11) | copy-start | bytes 292
  60.5 1.8 %copy-start.15 = (bf16[512,768]{1,0:T(8,128)(2,1)S(1)}, bf16[512,768]{1,0:T(8,128)(2,1)}, u32[]{:S(2)}) copy-start(bf16[512,768]{1,0:T(8,128)(2,1)} %copy-done.14) | copy-start | bytes 2359300
  60.5 1.8 %copy-start.17 = (bf16[128,384]{1,0:T(8,128)(2,1)S(1)}, bf16[128,384]{1,0:T(8,128)(2,1)}, u32[]{:S(2)}) copy-start(bf16[128,384]{1,0:T(8,128)(2,1)} %copy-done.16) | copy-start | bytes 294916

commit v10 on v9

--- a/solution.py
+++ b/solution.py
@@ -112,9 +112,10 @@
     cols = w_ref.shape[1]
     nodes, width = table_ref.shape
     parts, fetch = ids_ref.shape
-    half, share = parts // 2, fetch // who_ref.shape[0]
+    half = parts // 2
     size = sent_ref.shape[0] // parts
-    side, low = me_ref[1], me_ref[0] % half
+    share = size // 2
+    side, low = lax.div(me_ref[0], half), lax.rem(me_ref[0], half)
     ready(2, 3)
     ids_t[...] = ids_ref[...].astype(f32).T
 
@@ -161,9 +162,10 @@
         out[...] = mark(rows, picked, at_ref, step).astype(bf)
 
 
-def pick_kernel(ready, me_ref, far_ref, out_ref):
+def pick_kernel(half, ready, me_ref, far_ref, out_ref):
     size = out_ref.shape[0]
-    out_ref[...] = far_ref[pl.ds(pl.multiple_of((1 - me_ref[1]) * size, size), size), :]
+    start = (1 - lax.div(me_ref[0], half)) * size
+    out_ref[...] = far_ref[pl.ds(pl.multiple_of(start, size), size), :]
 
 
 def raw_kernel(half, whose, ready, me_ref, who_ref, w_ref, *refs):
@@ -183,7 +185,7 @@
         lead = lax.broadcasted_iota(jnp.int32, kv.shape, 1) == 0
         kv = jnp.where(marked, jnp.where(lead, jnp.nan, code), kv).astype(out.dtype)
         for part in range(half):
-            at = pl.multiple_of(part * fetch + who_ref[step] * share, share)
+            at = pl.multiple_of(part * fetch + (who_ref[0] ^ step) * share, share)
             out[pl.ds(at, share), :] = kv[part * share : (part + 1) * share]
 
 
@@ -225,7 +227,7 @@
     firsts = first_rows(total)
     for out, pair in zip(outs, ((0, 2), (1, 3))):
         for j, step in enumerate(pair):
-            at = pl.ds(pl.multiple_of(who_ref[step] * chunk, chunk), chunk)
+            at = pl.ds(pl.multiple_of((who_ref[0] ^ step) * chunk, chunk), chunk)
             out[j * chunk : (j + 1) * chunk, :] = total[at, :].astype(out.dtype)
         out[2 * chunk :, :] = firsts.astype(out.dtype)
 
@@ -307,16 +309,6 @@
     out[...] = rows.astype(bf)
 
 
-def place_kernel(whose, ready, who_ref, *refs):
-    *blocks, out = refs
-    chunk = out.shape[0] // len(whose)
-    pieces = [
-        block[start : start + chunk, :] for block in blocks for start in range(0, block.shape[0], chunk)
-    ]
-    for step, piece in zip(whose, pieces):
-        out[pl.ds(pl.multiple_of(who_ref[step] * chunk, chunk), chunk), :] = piece
-
-
 def own_kernel(
     ready, who_ref, at_ref, table_ref, w_ref, first_ref, *refs
 ):
@@ -328,7 +320,7 @@
         rows = ref[...].astype(f32)
         for turn in range(firsts.shape[0] // per_part // members):
             for title in range(per_part):
-                place = (turn * members + who_ref[step]) * per_part + title
+                place = (turn * members + (who_ref[0] ^ step)) * per_part + title
                 at = turn * per_part + title
                 firsts[pl.ds(place, 1), :] = rows[at : at + 1]
     firsts[0:per_part, :] = first_ref[...].astype(f32)
@@ -353,9 +345,14 @@
 
 
 def graph_kernel(
-    ready, me_ref, cols_ref, q_ref, kv_ref, first_ref, mask_ref, far_ref, cross_ref, *refs
+    whose, ready, me_ref, who_ref, cols_ref, q_ref, kv_ref, first_ref, mask_ref, far_ref, cross_ref, *refs
 ):
-    *rest, out_ref, k_all, v_all = refs
+    *rest, out_ref, encoded_ref, k_all, v_all = refs
+    dones, rest = rest[: len(whose)], rest[len(whose) :]
+    chunk = dones[0].shape[0]
+    for step, ref in zip(whose, dones):
+        at = pl.multiple_of((who_ref[0] ^ step) * chunk, chunk)
+        encoded_ref[pl.ds(at, chunk), :] = ref[...]
     nodes, cols = q_ref.shape
     row_tiles = nodes // TILE
     first_kv = first_ref[...]
@@ -375,7 +372,7 @@
 
     half = len(rest)
     size = rest[0].shape[0]
-    side, low = me_ref[1], me_ref[0] % half
+    side, low = lax.div(me_ref[0], half), lax.rem(me_ref[0], half)
     for start in range(0, cross_ref.shape[0], TILE):
         fix(cross_ref[start : start + TILE, :], nodes + (1 - side) * cross_ref.shape[0] + start)
     for part in range(half):
@@ -430,8 +427,7 @@
     half = dp // 2
     me_mp = lax.axis_index("mp").astype(jnp.int32)
     me_dp = lax.axis_index("dp").astype(jnp.int32)
-    me = jnp.stack([me_dp, me_dp // half])
-    who = me_mp ^ jnp.arange(mp, dtype=jnp.int32)
+    me, who = me_dp.reshape(1), me_mp.reshape(1)
     chunk = tok_rows // mp
     per_part = title_nodes.shape[0]
     fetch = send_ids.shape[2]
@@ -485,11 +481,6 @@
         flops=2 * tok_rows * width * 4 * w_attn_in.shape[1],
         name="attn",
     )
-    keep, give = halves(kept, swap(given, 1), PAD)
-    part = swap(give, 2)
-    mask = call(
-        mask_kernel, shape((nodes, TPR * TILE), bf), (nbr_slots.T,), flops=4 * 10**9, name="mask"
-    )
     rest = call(
         rest_kernel,
         (shape((size, 2 * cols), bf),) * half,
@@ -499,6 +490,12 @@
         flops=2 * 10**9,
         name="rest",
     )
+    recv, rest = lax.optimization_barrier((swap(given, 1), rest))
+    keep, give = halves(kept, recv, PAD)
+    part = swap(give, 2)
+    mask = call(
+        mask_kernel, shape((nodes, TPR * TILE), bf), (nbr_slots.T,), flops=4 * 10**9, name="mask"
+    )
     part, mask = lax.optimization_barrier((part, mask))
     hidden, first_hidden, first_terms = call(
         norm_one_kernel,
@@ -508,7 +505,16 @@
         name="norm_one",
     )
     whose, hiddens = gather(hidden)
-    hiddens, rest = lax.optimization_barrier((hiddens, rest))
+    raw = call(
+        functools.partial(pick_kernel, half),
+        shape((half * size, 2 * cols), bf),
+        (me, far),
+        smem=(0,),
+        name="pick",
+    )
+    rest = [rest[0]] + [swap(rest[step], step, "dp") for step in range(1, half)]
+    hiddens, raw, rest = lax.optimization_barrier((hiddens, raw, rest))
+    across = swap(raw, 2)
     kept, given, first = call(
         ffn_kernel,
         (
@@ -534,14 +540,9 @@
         )
         for turn in range(turns)
     ]
-    recv, far = lax.optimization_barrier((swap(given, 1), far))
-    keep, give = halves(kept, recv, 0)
-    give, far = lax.optimization_barrier((give, far))
-    raw = call(pick_kernel, shape((half * size, 2 * cols), bf), (me, far), smem=(0,), name="pick")
+    keep, give = halves(kept, swap(given, 1), 0)
     part = swap(give, 2)
-    across = swap(raw, 2)
-    rest = [rest[0]] + [swap(rest[step], step, "dp") for step in range(1, half)]
-    part, firsts, across, rest = lax.optimization_barrier((part, firsts, across, rest))
+    part, firsts, across = lax.optimization_barrier((part, firsts, across))
     blocks = [raw, across, swap(raw, 1), swap(across, 1)]
     done = call(
         norm_two_kernel, shape((chunk, width), bf), (hidden, gains, keep, part), name="norm_two"
@@ -549,14 +550,6 @@
     pack = call(pack_kernel, shape((tail_rows(turns * per_part), width), bf), firsts, name="pack")
     packs = [pack] + [swap(pack, step) for step in range(1, mp)]
     _, dones = gather(done)
-    encoded = call(
-        functools.partial(place_kernel, whose),
-        shape((tok_rows, width), bf),
-        (who, *dones),
-        smem=(0,),
-        name="place",
-    )
-
     cross = call(
         functools.partial(raw_kernel, half, whose),
         shape((half * fetch, 2 * cols), bf if share % 16 == 0 else f32),
@@ -575,11 +568,11 @@
         name="own",
     )
     keys = nodes + dp * fetch
-    graph_out = call(
-        graph_kernel,
-        shape((cols, nodes), bf),
-        (me, tile_cols, q, kv, first_kv, mask, far, cross, *rest),
-        smem=(0, 1),
+    graph_out, encoded = call(
+        functools.partial(graph_kernel, whose),
+        (shape((cols, nodes), bf), shape((tok_rows, width), bf)),
+        (me, who, tile_cols, q, kv, first_kv, mask, far, cross, *dones, *rest),
+        smem=(0, 1, 2),
         scratch=[pltpu.VMEM((keys, cols), bf), pltpu.VMEM((keys, cols), bf)],
         flops=4 * 10**9,
         name="graph",

time: 67 us -> 70.3 us (1.049)
  waiting for transfers between devices: 13 us -> 15.4 us
  local copies, waits for them, and re-layouts: 0.98 us -> 3.32 us
  other arithmetic: 1.09 us -> 0 us
    unnamed x36 -> x44, local copies, waits for them, and re-layouts: 0.98 us -> 3.32 us
    ppermute x19, waiting for transfers between devices: 13 us -> 15.3 us  [swap(): lax.ppermute(value, axis, [(i, i ^ step) for i in range(lax.axis_size(axi...]
    pallas_call x15 -> x14, Pallas kernels: 24.7 us -> 24.3 us  [call(): pl.pallas_call(body, out_shape=outs, in_specs=specs, out_specs=jax.tree.m...]
  transfers between devices with their start and end apart: 22 -> 22, of which waited for: 7 -> 10; matrix products, arithmetic and copies ran while one was open for 0% -> 0% of each run, Pallas kernels for 20% -> 22%
where the time goes in v10:
time: 70.3 us; the launch traced here: 70 us
  starting transfers between devices  26 us (37%)
  Pallas kernels  24.3 us (35%)
  waiting for transfers between devices  15.4 us (22%)
  local copies, waits for them, and re-layouts  3.32 us (5%)
  between operations  0.94 us (1%)
    pallas_call x14, Pallas kernels, call(): pl.pallas_call(body, out_shape=outs, in_specs=specs, out_specs=jax.tree.m...  24.3 us
    ppermute x19, waiting for transfers between devices, swap(): lax.ppermute(value, axis, [(i, i ^ step) for i in range(lax.axis_size(axi...  15.3 us
    ppermute x19, starting transfers between devices, swap(): lax.ppermute(value, axis, [(i, i ^ step) for i in range(lax.axis_size(axi...  15.3 us
    all_to_all x1, starting transfers between devices, local(): lax.all_to_all(sent.reshape(dp, size, 2 * cols), 'dp', split_axis=0, conc...  7.4 us
    unnamed x44, local copies, waits for them, and re-layouts  3.32 us
    ppermute x2, starting transfers between devices, local(): lax.ppermute(first, ('dp', 'mp'), [(p * mp + m, (p ^ turn * mp + m) * mp...  3.28 us
  transfers between devices with their start and end apart: 22, of which 10 were waited for; matrix products, arithmetic and copies ran while one was open for 0% of the time, Pallas kernels for 22%

profile of v10, /device:TPU:0, one launch (start us, length us, event | category | flops | bytes accessed | tf_op | source)
XLA Modules:
  0.0 70.0 jit_solution(2022088202258850716)
XLA Ops:
  0.6 3.7 %send.1 = bf16[1024,384]{1,0:T(8,128)(2,1)} custom-call(s32[1]{0:T(128)} %bitcast.refs_0_, s32[1]{0:T(128)} %bitcast.1.refs_1_.refs_0_, s32[2]{0:T(128)} %refs_1_.8, s32[8,256]{1,0:T(8,128)} %bitcast.17, bf16[512,768]{1,0:T(8,128)(2,1)} %refs_2_.8, bf16[3,192,768]{2,1,0:T(8,128)(2,1)} %bitcast.12), custom_call_target="tpu_custom_call" | custom-call | flops 3000000000 | bytes 1679376 | tf_op jit(solution)/shard_map/send/pallas_call | solution.py:62
  4.4 0.0 copy-start.2
  4.4 0.0 copy-start.3
  4.4 0.0 copy-start.4
  4.4 7.4 %all-to-all-start = ((bf16[8,128,384]{2,1,0:T(8,128)(2,1)}), bf16[8,128,384]{2,1,0:T(8,128)(2,1)S(1)}, u32[]{:S(2)}, u32[]{:S(2)}) async-start(bf16[8,128,384]{2,1,0:T(8,128)(2,1)} %bitcast.19), calls=%async_computation | async-start | bytes 1572864 | tf_op jit(solution)/shard_map/all_to_all | solution.py:470
  11.8 0.0 copy-start.15
  11.8 0.0 copy-start.17
  11.9 1.7 %attn.1 = (f32[144,768]{1,0:T(8,128)S(1)}, bf16[144,768]{1,0:T(8,128)(2,1)S(1)}) custom-call(s32[1]{0:T(128)} %bitcast.1.refs_1_.refs_0_, bf16[256,768]{1,0:T(8,128)(2,1)S(1)} %copy-done.2, bf16[3,192,768]{2,1,0:T(8,128)(2,1)S(1)} %bitcast.11, bf16[192,768]{1,0:T(8,128)(2,1)S(1)} %copy-done.4), custom_call_target="tpu_custom_call" | custom-call | flops 301989888 | bytes 1572868 | tf_op jit(solution)/shard_map/attn/pallas_call | solution.py:62
  13.6 0.1 collective-permute-start
  13.7 0.0 copy-start.12
  13.7 1.1 %copy-done.12 = bf16[512,768]{1,0:T(8,128)(2,1)S(1)} copy-done((bf16[512,768]{1,0:T(8,128)(2,1)S(1)}, bf16[512,768]{1,0:T(8,128)(2,1)}, u32[]{:S(2)}) %copy-start.12) | copy-done | bytes 786456
  14.8 2.3 %rest.1 = (bf16[128,384]{1,0:T(8,128)(2,1)S(1)}, bf16[128,384]{1,0:T(8,128)(2,1)}, bf16[128,384]{1,0:T(8,128)(2,1)}, bf16[128,384]{1,0:T(8,128)(2,1)}) custom-call(s32[1]{0:T(128)} %bitcast.refs_0_, s32[2]{0:T(128)S(1)} %copy-done.17, s32[8,256]{1,0:T(8,128)S(1)} %bitcast.18, bf16[512,768]{1,0:T(8,128)(2,1)S(1)} %copy-done.12, bf16[3,192,768]{2,1,0:T(8,128)(2,1)S(1)} %bitcast.13), custom_call_target="tpu_custom_call" | custom-call | flops 2000000000 | bytes 1679372 | tf_op jit(solution)/shard_map/rest/pallas_call | solution.py:62
  17.1 0.0 collective-permute-done.refs_1_
  17.1 1.6 %collective-permute-start.1 = (bf16[80,768]{1,0:T(8,128)(2,1)S(1)}, bf16[80,768]{1,0:T(8,128)(2,1)S(1)}, u32[]{:S(2)}, u32[]{:S(2)}) collective-permute-start(bf16[80,768]{1,0:T(8,128)(2,1)S(1)} %get-tuple-element.53), channel_id=1, source_target_pairs={{0,2},{1,3},{2,0},{3,1},{4,6},{5,7},{6,4},{7,5},{8,10},{9,11},{10,... | collective-permute-start | bytes 368648 | tf_op jit(solution)/shard_map/ppermute | solution.py:437
  18.7 4.2 %mask.1.refs_6_ = bf16[512,768]{1,0:T(8,128)(2,1)S(1)} custom-call(s32[16,512]{1,0:T(8,128)S(1)} %bitcast.16), custom_call_target="tpu_custom_call" | custom-call | flops 4000000000 | bytes 32768 | tf_op jit(solution)/shard_map/mask/pallas_call | solution.py:62
  23.0 0.9 %copy-done.18 = bf16[512,768]{1,0:T(8,128)(2,1)} copy-done((bf16[512,768]{1,0:T(8,128)(2,1)}, bf16[512,768]{1,0:T(8,128)(2,1)S(1)}, u32[]{:S(2)}) %copy-start.18) | copy-done | bytes 786456
  23.9 0.0 collective-permute-done.1.refs_6_
  23.9 1.4 %norm_one.1 = (bf16[80,768]{1,0:T(8,128)(2,1)}, bf16[16,768]{1,0:T(8,128)(2,1)S(1)}, f32[16,768]{1,0:T(8,128)S(1)}) custom-call(s32[1]{0:T(128)} %bitcast.1.refs_1_.refs_0_, bf16[256,768]{1,0:T(8,128)(2,1)S(1)} %copy-done.2, f32[2,768]{1,0:T(2,128)S(1)} %copy-done.5, bf16[768,768]{1,0:T(8,128)(2,1)S(1)} %copy-done, bf16[768,768]{1,0:T(8,128)(2,1)S(1)} %copy-done.1, ...), custom_call_target="tpu_custom_call" | custom-call | bytes 3127300 | tf_op jit(solution)/shard_map/norm_one/pallas_call | solution.py:62
  25.3 0.6 copy-done.6
  25.9 0.6 copy-done.8
  26.5 0.5 collective-permute-start.2
  27.0 0.0 collective-permute-start.3
  27.0 5.1 %collective-permute-done.2.refs_6_ = bf16[80,768]{1,0:T(8,128)(2,1)S(1)} collective-permute-done((bf16[80,768]{1,0:T(8,128)(2,1)}, bf16[80,768]{1,0:T(8,128)(2,1)S(1)}, u32[]{:S(2)}, u32[]{:S(2)}) %collective-permute-start.2) | collective-permute-done | bytes 122912 | tf_op jit(solution)/shard_map/ppermute | solution.py:437
  32.1 0.0 collective-permute-start.4
  32.1 2.0 %collective-permute-start.5 = (bf16[128,384]{1,0:T(8,128)(2,1)}, bf16[128,384]{1,0:T(8,128)(2,1)}, u32[]{:S(2)}, u32[]{:S(2)}) collective-permute-start(bf16[128,384]{1,0:T(8,128)(2,1)} %get-tuple-element.59), channel_id=1, source_target_pairs={{0,4},{4,0},{8,12},{12,8},{16,20},{20,16},{24,28},{28,24},{1,5},{5... | collective-permute-start | bytes 294920 | tf_op jit(solution)/shard_map/ppermute | solution.py:437
  34.1 1.5 %collective-permute-start.6 = (bf16[128,384]{1,0:T(8,128)(2,1)}, bf16[128,384]{1,0:T(8,128)(2,1)}, u32[]{:S(2)}, u32[]{:S(2)}) collective-permute-start(bf16[128,384]{1,0:T(8,128)(2,1)} %get-tuple-element.60), channel_id=1, source_target_pairs={{0,8},{4,12},{8,0},{12,4},{16,24},{20,28},{24,16},{28,20},{1,9},{5... | collective-permute-start | bytes 294920 | tf_op jit(solution)/shard_map/ppermute | solution.py:437
  35.6 0.0 collective-permute-start.7
  35.6 0.0 all-to-all-done
  35.7 2.2 %collective-permute-done.5.refs_14_ = bf16[128,384]{1,0:T(8,128)(2,1)} collective-permute-done((bf16[128,384]{1,0:T(8,128)(2,1)}, bf16[128,384]{1,0:T(8,128)(2,1)}, u32[]{:S(2)}, u32[]{:S(2)}) %collective-permute-start.5) | collective-permute-done | bytes 98336 | tf_op jit(solution)/shard_map/ppermute | solution.py:437
  37.9 2.2 %collective-permute-done.6.refs_15_ = bf16[128,384]{1,0:T(8,128)(2,1)} collective-permute-done((bf16[128,384]{1,0:T(8,128)(2,1)}, bf16[128,384]{1,0:T(8,128)(2,1)}, u32[]{:S(2)}, u32[]{:S(2)}) %collective-permute-start.6) | collective-permute-done | bytes 98336 | tf_op jit(solution)/shard_map/ppermute | solution.py:437
  40.1 1.4 %collective-permute-done.7.refs_16_ = bf16[128,384]{1,0:T(8,128)(2,1)} collective-permute-done((bf16[128,384]{1,0:T(8,128)(2,1)}, bf16[128,384]{1,0:T(8,128)(2,1)}, u32[]{:S(2)}, u32[]{:S(2)}) %collective-permute-start.7) | collective-permute-done | bytes 98336 | tf_op jit(solution)/shard_map/ppermute | solution.py:437
  41.5 0.0 collective-permute-done.3.refs_7_
  41.5 0.0 collective-permute-done.4.refs_8_
  41.5 0.5 collective-permute-start.12
  42.0 1.9 %ffn.1 = (f32[128,768]{1,0:T(8,128)S(1)}, bf16[128,768]{1,0:T(8,128)(2,1)S(1)}, bf16[2,768]{1,0:T(2,128)(2,1)S(1)}) custom-call(bf16[768,768]{1,0:T(8,128)(2,1)S(1)} %copy-done, bf16[768,768]{1,0:T(8,128)(2,1)S(1)} %copy-done.1, f32[2,768]{1,0:T(2,128)S(1)} %copy-done.5, bf16[16,768]{1,0:T(8,128)(2,1)S(1)} %copy-done.9, f32[16,768]{1,0:T(8,128)S(1)} %copy-done.7, ...), custom_call_target="tpu_custom_call" | custom-call | flops 603979776 | bytes 2930688 | tf_op jit(solution)/shard_map/ffn/pallas_call | solution.py:62
  43.9 0.1 collective-permute-start.8
  44.0 1.4 %collective-permute-done.8.refs_1_ = bf16[128,768]{1,0:T(8,128)(2,1)S(1)} collective-permute-done((bf16[128,768]{1,0:T(8,128)(2,1)S(1)}, bf16[128,768]{1,0:T(8,128)(2,1)S(1)}, u32[]{:S(2)}, u32[]{:S(2)}) %collective-permute-start.8) | collective-permute-done | bytes 196640 | tf_op jit(solution)/shard_map/ppermute | solution.py:437
  45.5 1.6 %collective-permute-start.9 = (bf16[64,768]{1,0:T(8,128)(2,1)S(1)}, bf16[64,768]{1,0:T(8,128)(2,1)S(1)}, u32[]{:S(2)}, u32[]{:S(2)}) collective-permute-start(bf16[64,768]{1,0:T(8,128)(2,1)S(1)} %get-tuple-element.69), channel_id=1, source_target_pairs={{0,2},{1,3},{2,0},{3,1},{4,6},{5,7},{6,4},{7,5},{8,10},{9,11},{10,... | collective-permute-start | bytes 294920 | tf_op jit(solution)/shard_map/ppermute | solution.py:437
  47.1 0.8 %collective-permute-start.10 = (bf16[2,768]{1,0:T(2,128)(2,1)S(1)}, bf16[2,768]{1,0:T(2,128)(2,1)S(1)}, u32[]{:S(2)}, u32[]{:S(2)}) collective-permute-start(bf16[2,768]{1,0:T(2,128)(2,1)S(1)} %get-tuple-element.66.refs_4_), channel_id=1, source_target_pairs={{1,5},{2,10},{3,15},{5,1},{6,14},{7,11},{9,13},{10,2},{11,7},{13,9... | collective-permute-start | bytes 9224 | tf_op jit(solution)/shard_map/ppermute | solution.py:531
  47.9 2.5 %collective-permute-start.11 = (bf16[2,768]{1,0:T(2,128)(2,1)S(1)}, bf16[2,768]{1,0:T(2,128)(2,1)S(1)}, u32[]{:S(2)}, u32[]{:S(2)}) collective-permute-start(bf16[2,768]{1,0:T(2,128)(2,1)S(1)} %get-tuple-element.66.refs_4_), channel_id=1, source_target_pairs={{0,16},{1,21},{2,26},{3,31},{4,20},{5,17},{6,30},{7,27},{8,24},{9,... | collective-permute-start | bytes 9224 | tf_op jit(solution)/shard_map/ppermute | solution.py:531
  50.4 2.0 %collective-permute-start.16 = (bf16[512,384]{1,0:T(8,128)(2,1)S(1)}, bf16[512,384]{1,0:T(8,128)(2,1)S(1)}, u32[]{:S(2)}, u32[]{:S(2)}) collective-permute-start(bf16[512,384]{1,0:T(8,128)(2,1)S(1)} %pick.1.refs_3_), channel_id=1, source_target_pairs={{0,1},{1,0},{2,3},{3,2},{4,5},{5,4},{6,7},{7,6},{8,9},{9,8},{10,11... | collective-permute-start | bytes 1179656 | tf_op jit(solution)/shard_map/ppermute | solution.py:437
  52.4 0.0 collective-permute-done.10.refs_0_
  52.4 0.1 collective-permute-done.11.refs_1_
  52.5 1.2 %collective-permute-done.9.refs_3_ = bf16[64,768]{1,0:T(8,128)(2,1)S(1)} collective-permute-done((bf16[64,768]{1,0:T(8,128)(2,1)S(1)}, bf16[64,768]{1,0:T(8,128)(2,1)S(1)}, u32[]{:S(2)}, u32[]{:S(2)}) %collective-permute-start.9) | collective-permute-done | bytes 98336 | tf_op jit(solution)/shard_map/ppermute | solution.py:437
  53.7 0.0 collective-permute-done.12.refs_4_
  53.7 0.8 %collective-permute-start.17 = (bf16[512,384]{1,0:T(8,128)(2,1)S(1)}, bf16[512,384]{1,0:T(8,128)(2,1)S(1)}, u32[]{:S(2)}, u32[]{:S(2)}) collective-permute-start(bf16[512,384]{1,0:T(8,128)(2,1)S(1)} %collective-permute-done.12.refs_4_), channel_id=1, source_target_pairs={{0,1},{1,0},{2,3},{3,2},{4,5},{5,4},{6,7},{7,6},{8,9},{9,8},{10,11... | collective-permute-start | bytes 1179656 | tf_op jit(solution)/shard_map/ppermute | solution.py:437
  54.6 0.1 collective-permute-start.13
  54.6 2.6 %collective-permute-start.14 = (bf16[16,768]{1,0:T(8,128)(2,1)S(1)}, bf16[16,768]{1,0:T(8,128)(2,1)S(1)}, u32[]{:S(2)}, u32[]{:S(2)}) collective-permute-start(bf16[16,768]{1,0:T(8,128)(2,1)S(1)} %pack.1.refs_5_), channel_id=1, source_target_pairs={{0,2},{1,3},{2,0},{3,1},{4,6},{5,7},{6,4},{7,5},{8,10},{9,11},{10,... | collective-permute-start | bytes 73736 | tf_op jit(solution)/shard_map/ppermute | solution.py:437
  57.2 0.0 collective-permute-start.15
  57.2 1.1 %norm_two.1.refs_9_ = bf16[64,768]{1,0:T(8,128)(2,1)S(1)} custom-call(bf16[80,768]{1,0:T(8,128)(2,1)} %get-tuple-element.62.refs_5_.refs_0_, f32[2,768]{1,0:T(2,128)S(1)} %copy-done.5, f32[64,768]{1,0:T(8,128)S(1)} %get-tuple-element.78.refs_2_, bf16[64,768]{1,0:T(8,128)(2,1)S(1)} %collective-permute-done.9.refs_3_), custom_call_target="tpu_custom_call" | custom-call | bytes 423936 | tf_op jit(solution)/shard_map/norm_two/pallas_call | solution.py:62
  58.3 1.6 %collective-permute-start.18 = (bf16[64,768]{1,0:T(8,128)(2,1)S(1)}, bf16[64,768]{1,0:T(8,128)(2,1)S(1)}, u32[]{:S(2)}, u32[]{:S(2)}) collective-permute-start(bf16[64,768]{1,0:T(8,128)(2,1)S(1)} %norm_two.1.refs_9_), channel_id=1, source_target_pairs={{0,2},{1,3},{2,0},{3,1},{4,6},{5,7},{6,4},{7,5},{8,10},{9,11},{10,... | collective-permute-start | bytes 294920 | tf_op jit(solution)/shard_map/ppermute | solution.py:437
  60.0 0.0 collective-permute-done.14.refs_7_
  60.0 0.3 collective-permute-start.19
  60.3 0.3 collective-permute-done.15.refs_8_
  60.6 1.6 %own.1 = (bf16[512,384]{1,0:T(8,128)(2,1)S(1)}, bf16[512,192]{1,0:T(8,128)(2,1)S(1)}, bf16[16,384]{1,0:T(8,128)(2,1)S(1)}) custom-call(s32[1]{0:T(128)} %bitcast.1.refs_1_.refs_0_, s32[2]{0:T(128)S(1)} %copy-done.17, bf16[512,768]{1,0:T(8,128)(2,1)S(1)} %copy-done.13, bf16[3,192,768]{2,1,0:T(8,128)(2,1)S(1)} %bitcast.14, ...), custom_call_target="tpu_custom_call" | custom-call | flops 2000000000 | bytes 1772556 | tf_op jit(solution)/shard_map/own/pallas_call | solution.py:62
  62.2 0.0 copy-start.16
  62.2 1.3 %collective-permute-done.18.refs_10_ = bf16[64,768]{1,0:T(8,128)(2,1)S(1)} collective-permute-done((bf16[64,768]{1,0:T(8,128)(2,1)S(1)}, bf16[64,768]{1,0:T(8,128)(2,1)S(1)}, u32[]{:S(2)}, u32[]{:S(2)}) %collective-permute-start.18) | collective-permute-done | bytes 98336 | tf_op jit(solution)/shard_map/ppermute | solution.py:437
  63.5 0.0 collective-permute-start.20
  63.5 0.0 collective-permute-done.16.refs_5_
  63.5 0.0 collective-permute-done.17.refs_6_
  63.5 1.2 %raw.1.refs_8_ = bf16[1024,384]{1,0:T(8,128)(2,1)S(1)} custom-call(s32[1]{0:T(128)} %bitcast.refs_0_, s32[1]{0:T(128)} %bitcast.1.refs_1_.refs_0_, bf16[3,192,768]{2,1,0:T(8,128)(2,1)S(1)} %bitcast.15, bf16[512,384]{1,0:T(8,128)(2,1)S(1)} %pick.1.refs_3_, bf16[512,384]{1,0:T(8,128)(2,1)S(1)} %collective-permute-done.12.refs_4_, ...), custom_call_target="tpu_custom_call" | custom-call | flops 2000000000 | bytes 2457608 | tf_op jit(solution)/shard_map/raw/pallas_call | solution.py:62
  64.7 0.0 collective-permute-done.19.refs_11_
  64.7 0.1 collective-permute-done.20.refs_12_
  64.8 5.1 %graph.1 = (bf16[192,512]{1,0:T(8,128)(2,1)}, bf16[256,768]{1,0:T(8,128)(2,1)}) custom-call(s32[1]{0:T(128)} %bitcast.refs_0_, s32[1]{0:T(128)} %bitcast.1.refs_1_.refs_0_, s32[4,6]{1,0:T(4,128)S(1)} %copy-done.16, bf16[512,192]{1,0:T(8,128)(2,1)S(1)} %get-tuple-element.73.refs_3_, bf16[512,384]{1,0:T(8,128)(2,1)S(1)} %get-tuple-element.74.refs_4_, ...), custom_call_target="tpu_custom_call" | custom-call | flops 4000000000 | bytes 3747944 | tf_op jit(solution)/shard_map/graph/pallas_call | solution.py:62
  (38 shorter events, 0.2 us)
Async XLA Ops:
  4.4 7.5 %copy-start.2 = (bf16[256,768]{1,0:T(8,128)(2,1)S(1)}, bf16[256,768]{1,0:T(8,128)(2,1)}, u32[]{:S(2)}) copy-start(bf16[256,768]{1,0:T(8,128)(2,1)} %refs_1_.6) | copy-start | bytes 1179652
  4.4 7.5 %copy-start.3 = (bf16[3,768,192]{1,2,0:T(8,128)(2,1)S(1)}, bf16[3,768,192]{1,2,0:T(8,128)(2,1)}, u32[]{:S(2)}) copy-start(bf16[3,768,192]{1,2,0:T(8,128)(2,1)} %param.13) | copy-start | bytes 2654212
  4.4 7.5 %copy-start.4 = (bf16[192,768]{1,0:T(8,128)(2,1)S(1)}, bf16[192,768]{1,0:T(8,128)(2,1)}, u32[]{:S(2)}) copy-start(bf16[192,768]{1,0:T(8,128)(2,1)} %refs_3_.3) | copy-start | bytes 884740
  4.4 31.2 %all-to-all-start = ((bf16[8,128,384]{2,1,0:T(8,128)(2,1)}), bf16[8,128,384]{2,1,0:T(8,128)(2,1)S(1)}, u32[]{:S(2)}, u32[]{:S(2)}) async-start(bf16[8,128,384]{2,1,0:T(8,128)(2,1)} %bitcast.19), calls=%async_computation | async-start | bytes 1572864 | tf_op jit(solution)/shard_map/all_to_all | solution.py:470
  11.8 1.9 %copy-start.10 = (bf16[3,768,192]{1,2,0:T(8,128)(2,1)S(1)}, bf16[3,768,192]{1,2,0:T(8,128)(2,1)}, u32[]{:S(2)}) copy-start(bf16[3,768,192]{1,2,0:T(8,128)(2,1)} %param.19) | copy-start | bytes 2654212
  11.8 1.9 %copy-start.15 = (s32[1,8,256]{2,1,0:T(8,128)S(1)}, s32[1,8,256]{2,1,0:T(8,128)}, u32[]{:S(2)}) copy-start(s32[1,8,256]{2,1,0:T(8,128)} %param.21) | copy-start | bytes 24580
  11.8 1.9 %copy-start.17 = (s32[2]{0:T(128)S(1)}, s32[2]{0:T(128)}, u32[]{:S(2)}) copy-start(s32[2]{0:T(128)} %refs_1_.8) | copy-start | bytes 28
  13.6 3.5 %collective-permute-start = (bf16[144,768]{1,0:T(8,128)(2,1)S(1)}, bf16[144,768]{1,0:T(8,128)(2,1)S(1)}, u32[]{:S(2)}, u32[]{:S(2)}) collective-permute-start(bf16[144,768]{1,0:T(8,128)(2,1)S(1)} %get-tuple-element.46), channel_id=1, source_target_pairs={{0,1},{1,0},{2,3},{3,2},{4,5},{5,4},{6,7},{7,6},{8,9},{9,8},{10,11... | collective-permute-start | bytes 663560 | tf_op jit(solution)/shard_map/ppermute | solution.py:437
  13.7 1.1 %copy-start.12 = (bf16[512,768]{1,0:T(8,128)(2,1)S(1)}, bf16[512,768]{1,0:T(8,128)(2,1)}, u32[]{:S(2)}) copy-start(bf16[512,768]{1,0:T(8,128)(2,1)} %refs_2_.8) | copy-start | bytes 2359300
  14.8 3.9 %copy-start.14 = (s32[512,16]{0,1:T(8,128)S(1)}, s32[512,16]{0,1:T(8,128)}, u32[]{:S(2)}) copy-start(s32[512,16]{0,1:T(8,128)} %param.23) | copy-start | bytes 98308
  17.1 5.9 %copy-start.20 = (bf16[128,384]{1,0:T(8,128)(2,1)}, bf16[128,384]{1,0:T(8,128)(2,1)S(1)}, u32[]{:S(2)}) copy-start(bf16[128,384]{1,0:T(8,128)(2,1)S(1)} %get-tuple-element.80.refs_13_) | copy-start | bytes 294916
  17.1 6.8 %collective-permute-start.1 = (bf16[80,768]{1,0:T(8,128)(2,1)S(1)}, bf16[80,768]{1,0:T(8,128)(2,1)S(1)}, u32[]{:S(2)}, u32[]{:S(2)}) collective-permute-start(bf16[80,768]{1,0:T(8,128)(2,1)S(1)} %get-tuple-element.53), channel_id=1, source_target_pairs={{0,2},{1,3},{2,0},{3,1},{4,6},{5,7},{6,4},{7,5},{8,10},{9,11},{10,... | collective-permute-start | bytes 368648 | tf_op jit(solution)/shard_map/ppermute | solution.py:437
  18.7 5.2 %copy-start = (bf16[768,768]{1,0:T(8,128)(2,1)S(1)}, bf16[768,768]{1,0:T(8,128)(2,1)}, u32[]{:S(2)}) copy-start(bf16[768,768]{1,0:T(8,128)(2,1)} %refs_0_.1) | copy-start | bytes 3538948
  18.7 5.2 %copy-start.1 = (bf16[768,768]{1,0:T(8,128)(2,1)S(1)}, bf16[768,768]{1,0:T(8,128)(2,1)}, u32[]{:S(2)}) copy-start(bf16[768,768]{1,0:T(8,128)(2,1)} %refs_1_.7) | copy-start | bytes 3538948
  18.7 5.2 %copy-start.5 = (f32[2,768]{1,0:T(2,128)S(1)}, f32[2,768]{1,0:T(2,128)}, u32[]{:S(2)}) copy-start(f32[2,768]{1,0:T(2,128)} %refs_1_.9) | copy-start | bytes 18436
  23.0 0.9 %copy-start.18 = (bf16[512,768]{1,0:T(8,128)(2,1)}, bf16[512,768]{1,0:T(8,128)(2,1)S(1)}, u32[]{:S(2)}) copy-start(bf16[512,768]{1,0:T(8,128)(2,1)S(1)} %mask.1.refs_6_) | copy-start | bytes 2359300
  25.3 0.6 copy-start.6
  25.9 0.6 copy-start.8
  26.5 15.5 %copy-start.9 = (bf16[16,768]{1,0:T(8,128)(2,1)S(1)}, bf16[16,768]{1,0:T(8,128)(2,1)}, u32[]{:S(2)}) copy-start(bf16[16,768]{1,0:T(8,128)(2,1)} %copy-done.8) | copy-start | bytes 73732
  26.5 5.6 %collective-permute-start.2 = (bf16[80,768]{1,0:T(8,128)(2,1)}, bf16[80,768]{1,0:T(8,128)(2,1)S(1)}, u32[]{:S(2)}, u32[]{:S(2)}) collective-permute-start(bf16[80,768]{1,0:T(8,128)(2,1)} %get-tuple-element.62.refs_5_.refs_0_), channel_id=1, source_target_pairs={{0,2},{1,3},{2,0},{3,1},{4,6},{5,7},{6,4},{7,5},{8,10},{9,11},{10,... | collective-permute-start | bytes 368648 | tf_op jit(solution)/shard_map/ppermute | solution.py:437
  27.0 14.5 %collective-permute-start.3 = (bf16[80,768]{1,0:T(8,128)(2,1)}, bf16[80,768]{1,0:T(8,128)(2,1)S(1)}, u32[]{:S(2)}, u32[]{:S(2)}) collective-permute-start(bf16[80,768]{1,0:T(8,128)(2,1)} %get-tuple-element.62.refs_5_.refs_0_), channel_id=1, source_target_pairs={{0,1},{1,0},{2,3},{3,2},{4,5},{5,4},{6,7},{7,6},{8,9},{9,8},{10,11... | collective-permute-start | bytes 368648 | tf_op jit(solution)/shard_map/ppermute | solution.py:437
  32.1 9.3 %collective-permute-start.4 = (bf16[80,768]{1,0:T(8,128)(2,1)S(1)}, bf16[80,768]{1,0:T(8,128)(2,1)S(1)}, u32[]{:S(2)}, u32[]{:S(2)}) collective-permute-start(bf16[80,768]{1,0:T(8,128)(2,1)S(1)} %collective-permute-done.2.refs_6_), channel_id=1, source_target_pairs={{0,1},{1,0},{2,3},{3,2},{4,5},{5,4},{6,7},{7,6},{8,9},{9,8},{10,11... | collective-permute-start | bytes 368648 | tf_op jit(solution)/shard_map/ppermute | solution.py:437
  32.1 5.8 %collective-permute-start.5 = (bf16[128,384]{1,0:T(8,128)(2,1)}, bf16[128,384]{1,0:T(8,128)(2,1)}, u32[]{:S(2)}, u32[]{:S(2)}) collective-permute-start(bf16[128,384]{1,0:T(8,128)(2,1)} %get-tuple-element.59), channel_id=1, source_target_pairs={{0,4},{4,0},{8,12},{12,8},{16,20},{20,16},{24,28},{28,24},{1,5},{5... | collective-permute-start | bytes 294920 | tf_op jit(solution)/shard_map/ppermute | solution.py:437
  34.1 5.9 %collective-permute-start.6 = (bf16[128,384]{1,0:T(8,128)(2,1)}, bf16[128,384]{1,0:T(8,128)(2,1)}, u32[]{:S(2)}, u32[]{:S(2)}) collective-permute-start(bf16[128,384]{1,0:T(8,128)(2,1)} %get-tuple-element.60), channel_id=1, source_target_pairs={{0,8},{4,12},{8,0},{12,4},{16,24},{20,28},{24,16},{28,20},{1,9},{5... | collective-permute-start | bytes 294920 | tf_op jit(solution)/shard_map/ppermute | solution.py:437
  35.6 5.9 %collective-permute-start.7 = (bf16[128,384]{1,0:T(8,128)(2,1)}, bf16[128,384]{1,0:T(8,128)(2,1)}, u32[]{:S(2)}, u32[]{:S(2)}) collective-permute-start(bf16[128,384]{1,0:T(8,128)(2,1)} %get-tuple-element.61), channel_id=1, source_target_pairs={{0,12},{4,8},{8,4},{12,0},{16,28},{20,24},{24,20},{28,16},{1,13},{... | collective-permute-start | bytes 294920 | tf_op jit(solution)/shard_map/ppermute | solution.py:437
  35.6 6.4 %copy-start.7 = (f32[16,768]{1,0:T(8,128)S(1)}, f32[16,768]{1,0:T(8,128)}, u32[]{:S(2)}) copy-start(f32[16,768]{1,0:T(8,128)} %copy-done.6) | copy-start | bytes 147460
  41.5 12.2 %collective-permute-start.12 = (bf16[512,384]{1,0:T(8,128)(2,1)S(1)}, bf16[512,384]{1,0:T(8,128)(2,1)S(1)}, u32[]{:S(2)}, u32[]{:S(2)}) collective-permute-start(bf16[512,384]{1,0:T(8,128)(2,1)S(1)} %pick.1.refs_3_), channel_id=1, source_target_pairs={{0,2},{1,3},{2,0},{3,1},{4,6},{5,7},{6,4},{7,5},{8,10},{9,11},{10,... | collective-permute-start | bytes 1179656 | tf_op jit(solution)/shard_map/ppermute | solution.py:437
  42.0 18.6 %copy-start.11 = (bf16[3,768,192]{1,2,0:T(8,128)(2,1)S(1)}, bf16[3,768,192]{1,2,0:T(8,128)(2,1)}, u32[]{:S(2)}) copy-start(bf16[3,768,192]{1,2,0:T(8,128)(2,1)} %param.19) | copy-start | bytes 2654212
  42.0 18.6 %copy-start.13 = (bf16[512,768]{1,0:T(8,128)(2,1)S(1)}, bf16[512,768]{1,0:T(8,128)(2,1)}, u32[]{:S(2)}) copy-start(bf16[512,768]{1,0:T(8,128)(2,1)} %refs_2_.8) | copy-start | bytes 2359300
  43.9 1.5 %collective-permute-start.8 = (bf16[128,768]{1,0:T(8,128)(2,1)S(1)}, bf16[128,768]{1,0:T(8,128)(2,1)S(1)}, u32[]{:S(2)}, u32[]{:S(2)}) collective-permute-start(bf16[128,768]{1,0:T(8,128)(2,1)S(1)} %get-tuple-element.68), channel_id=1, source_target_pairs={{0,1},{1,0},{2,3},{3,2},{4,5},{5,4},{6,7},{7,6},{8,9},{9,8},{10,11... | collective-permute-start | bytes 589832 | tf_op jit(solution)/shard_map/ppermute | solution.py:437
  45.5 8.2 %collective-permute-start.9 = (bf16[64,768]{1,0:T(8,128)(2,1)S(1)}, bf16[64,768]{1,0:T(8,128)(2,1)S(1)}, u32[]{:S(2)}, u32[]{:S(2)}) collective-permute-start(bf16[64,768]{1,0:T(8,128)(2,1)S(1)} %get-tuple-element.69), channel_id=1, source_target_pairs={{0,2},{1,3},{2,0},{3,1},{4,6},{5,7},{6,4},{7,5},{8,10},{9,11},{10,... | collective-permute-start | bytes 294920 | tf_op jit(solution)/shard_map/ppermute | solution.py:437
  47.1 5.3 %collective-permute-start.10 = (bf16[2,768]{1,0:T(2,128)(2,1)S(1)}, bf16[2,768]{1,0:T(2,128)(2,1)S(1)}, u32[]{:S(2)}, u32[]{:S(2)}) collective-permute-start(bf16[2,768]{1,0:T(2,128)(2,1)S(1)} %get-tuple-element.66.refs_4_), channel_id=1, source_target_pairs={{1,5},{2,10},{3,15},{5,1},{6,14},{7,11},{9,13},{10,2},{11,7},{13,9... | collective-permute-start | bytes 9224 | tf_op jit(solution)/shard_map/ppermute | solution.py:531
  47.9 4.6 %collective-permute-start.11 = (bf16[2,768]{1,0:T(2,128)(2,1)S(1)}, bf16[2,768]{1,0:T(2,128)(2,1)S(1)}, u32[]{:S(2)}, u32[]{:S(2)}) collective-permute-start(bf16[2,768]{1,0:T(2,128)(2,1)S(1)} %get-tuple-element.66.refs_4_), channel_id=1, source_target_pairs={{0,16},{1,21},{2,26},{3,31},{4,20},{5,17},{6,30},{7,27},{8,24},{9,... | collective-permute-start | bytes 9224 | tf_op jit(solution)/shard_map/ppermute | solution.py:531
  50.4 13.2 %collective-permute-start.16 = (bf16[512,384]{1,0:T(8,128)(2,1)S(1)}, bf16[512,384]{1,0:T(8,128)(2,1)S(1)}, u32[]{:S(2)}, u32[]{:S(2)}) collective-permute-start(bf16[512,384]{1,0:T(8,128)(2,1)S(1)} %pick.1.refs_3_), channel_id=1, source_target_pairs={{0,1},{1,0},{2,3},{3,2},{4,5},{5,4},{6,7},{7,6},{8,9},{9,8},{10,11... | collective-permute-start | bytes 1179656 | tf_op jit(solution)/shard_map/ppermute | solution.py:437
  53.7 9.8 %collective-permute-start.17 = (bf16[512,384]{1,0:T(8,128)(2,1)S(1)}, bf16[512,384]{1,0:T(8,128)(2,1)S(1)}, u32[]{:S(2)}, u32[]{:S(2)}) collective-permute-start(bf16[512,384]{1,0:T(8,128)(2,1)S(1)} %collective-permute-done.12.refs_4_), channel_id=1, source_target_pairs={{0,1},{1,0},{2,3},{3,2},{4,5},{5,4},{6,7},{7,6},{8,9},{9,8},{10,11... | collective-permute-start | bytes 1179656 | tf_op jit(solution)/shard_map/ppermute | solution.py:437
  54.6 3.8 %collective-permute-start.13 = (bf16[16,768]{1,0:T(8,128)(2,1)S(1)}, bf16[16,768]{1,0:T(8,128)(2,1)S(1)}, u32[]{:S(2)}, u32[]{:S(2)}) collective-permute-start(bf16[16,768]{1,0:T(8,128)(2,1)S(1)} %pack.1.refs_5_), channel_id=1, source_target_pairs={{0,1},{1,0},{2,3},{3,2},{4,5},{5,4},{6,7},{7,6},{8,9},{9,8},{10,11... | collective-permute-start | bytes 73736 | tf_op jit(solution)/shard_map/ppermute | solution.py:437
  54.6 5.4 %collective-permute-start.14 = (bf16[16,768]{1,0:T(8,128)(2,1)S(1)}, bf16[16,768]{1,0:T(8,128)(2,1)S(1)}, u32[]{:S(2)}, u32[]{:S(2)}) collective-permute-start(bf16[16,768]{1,0:T(8,128)(2,1)S(1)} %pack.1.refs_5_), channel_id=1, source_target_pairs={{0,2},{1,3},{2,0},{3,1},{4,6},{5,7},{6,4},{7,5},{8,10},{9,11},{10,... | collective-permute-start | bytes 73736 | tf_op jit(solution)/shard_map/ppermute | solution.py:437
  57.2 3.4 %collective-permute-start.15 = (bf16[16,768]{1,0:T(8,128)(2,1)S(1)}, bf16[16,768]{1,0:T(8,128)(2,1)S(1)}, u32[]{:S(2)}, u32[]{:S(2)}) collective-permute-start(bf16[16,768]{1,0:T(8,128)(2,1)S(1)} %pack.1.refs_5_), channel_id=1, source_target_pairs={{0,3},{1,2},{2,1},{3,0},{4,7},{5,6},{6,5},{7,4},{8,11},{9,10},{10,... | collective-permute-start | bytes 73736 | tf_op jit(solution)/shard_map/ppermute | solution.py:437
  58.3 5.2 %collective-permute-start.18 = (bf16[64,768]{1,0:T(8,128)(2,1)S(1)}, bf16[64,768]{1,0:T(8,128)(2,1)S(1)}, u32[]{:S(2)}, u32[]{:S(2)}) collective-permute-start(bf16[64,768]{1,0:T(8,128)(2,1)S(1)} %norm_two.1.refs_9_), channel_id=1, source_target_pairs={{0,2},{1,3},{2,0},{3,1},{4,6},{5,7},{6,4},{7,5},{8,10},{9,11},{10,... | collective-permute-start | bytes 294920 | tf_op jit(solution)/shard_map/ppermute | solution.py:437
  60.0 4.7 %collective-permute-start.19 = (bf16[64,768]{1,0:T(8,128)(2,1)S(1)}, bf16[64,768]{1,0:T(8,128)(2,1)S(1)}, u32[]{:S(2)}, u32[]{:S(2)}) collective-permute-start(bf16[64,768]{1,0:T(8,128)(2,1)S(1)} %norm_two.1.refs_9_), channel_id=1, source_target_pairs={{0,1},{1,0},{2,3},{3,2},{4,5},{5,4},{6,7},{7,6},{8,9},{9,8},{10,11... | collective-permute-start | bytes 294920 | tf_op jit(solution)/shard_map/ppermute | solution.py:437
  62.2 2.6 %copy-start.16 = (s32[4,6]{1,0:T(4,128)S(1)}, s32[4,6]{1,0:T(4,128)}, u32[]{:S(2)}) copy-start(s32[4,6]{1,0:T(4,128)} %refs_2_.9) | copy-start | bytes 292
  62.2 2.6 %copy-start.19 = (bf16[512,768]{1,0:T(8,128)(2,1)S(1)}, bf16[512,768]{1,0:T(8,128)(2,1)}, u32[]{:S(2)}) copy-start(bf16[512,768]{1,0:T(8,128)(2,1)} %copy-done.18) | copy-start | bytes 2359300
  62.2 2.6 %copy-start.21 = (bf16[128,384]{1,0:T(8,128)(2,1)S(1)}, bf16[128,384]{1,0:T(8,128)(2,1)}, u32[]{:S(2)}) copy-start(bf16[128,384]{1,0:T(8,128)(2,1)} %copy-done.20) | copy-start | bytes 294916
  63.5 1.3 %collective-permute-start.20 = (bf16[64,768]{1,0:T(8,128)(2,1)S(1)}, bf16[64,768]{1,0:T(8,128)(2,1)S(1)}, u32[]{:S(2)}, u32[]{:S(2)}) collective-permute-start(bf16[64,768]{1,0:T(8,128)(2,1)S(1)} %collective-permute-done.18.refs_10_), channel_id=1, source_target_pairs={{0,1},{1,0},{2,3},{3,2},{4,5},{5,4},{6,7},{7,6},{8,9},{9,8},{10,11... | collective-permute-start | bytes 294920 | tf_op jit(solution)/shard_map/ppermute | solution.py:437

commit v11 on v5

--- a/solution.py
+++ b/solution.py
@@ -1,3 +1,4 @@
+import functools
 import jax
 import jax.numpy as jnp
 from jax import lax
@@ -25,7 +26,16 @@
 
 
 def call(
-    kernel, outs, args, smem=(), hbm=(), scalars=(), scratch=(), out_specs=None, flops=0, name=None
+    kernel,
+    outs,
+    args,
+    smem=(),
+    hbm=(),
+    scalars=(),
+    scratch=(),
+    out_specs=None,
+    flops=0,
+    name=None,
 ):
     count, out_count, own = len(args), len(jax.tree.leaves(outs)), len(scratch)
     specs = [SMEM if i in smem else HBM if i in hbm else VMEM for i in range(count)]
@@ -84,28 +94,34 @@
     return centred * lax.rsqrt(var + eps_norm) * gain
 
 
+def one_hot(picked, nodes):
+    lanes = lax.broadcasted_iota(jnp.int32, (picked.shape[0], nodes), 1)
+    return jnp.where(lanes == picked, 1.0, 0.0).astype(bf)
+
+
+def mark(rows, picked, at_ref, step):
+    per_part = at_ref.shape[0]
+    code = jnp.full(picked.shape, -1, jnp.int32)
+    for title in range(per_part):
+        code = jnp.where(picked == at_ref[title], step * per_part + title, code)
+    lead = lax.broadcasted_iota(jnp.int32, rows.shape, 1) == 0
+    return jnp.where(code >= 0, jnp.where(lead, jnp.nan, code.astype(f32)), rows)
+
+
 def send_kernel(ready, me_ref, at_ref, ids_ref, table_ref, w_ref, sent_ref, rows_ref, sems):
     cols = w_ref.shape[1]
-    per_part = at_ref.shape[0]
     fetch, nodes = ids_ref.shape[1], table_ref.shape[0]
-    ready(1, 2, 3, 4)
+    ready(2)
+    ids = ids_ref[...].astype(f32).T.astype(jnp.int32)
+    ready(1, 3, 4)
     table = table_ref[...]
     kv = jnp.concatenate([dot_nt(table, w_ref[1]), dot_nt(table, w_ref[2])], axis=1).astype(bf)
-    ids = ids_ref[...].astype(f32).T.astype(jnp.int32)
-    lanes = lax.broadcasted_iota(jnp.int32, (fetch, nodes), 1)
-    lead = lax.broadcasted_iota(jnp.int32, (fetch, 2 * cols), 1) == 0
     moves = []
     for part in range(ids.shape[1]):
-        step = me_ref[0] ^ part
         picked = ids[:, part : part + 1]
-        hot = jnp.where(lanes == picked, 1.0, 0.0).astype(bf)
-        rows = dot(hot, kv)
-        code = jnp.full((fetch, 1), -1, jnp.int32)
-        for title in range(per_part):
-            code = jnp.where(picked == at_ref[title], step * per_part + title, code)
-        mark = jnp.where(lead, jnp.nan, code.astype(f32))
+        rows = mark(dot(one_hot(picked, nodes), kv), picked, at_ref, me_ref[0] ^ part)
         at = pl.ds(part * fetch, fetch)
-        rows_ref[at, :] = jnp.where(code >= 0, mark, rows).astype(bf)
+        rows_ref[at, :] = rows.astype(bf)
         moves.append(pltpu.make_async_copy(rows_ref.at[at, :], sent_ref.at[at, :], sems.at[part]))
         moves[-1].start()
     for move in moves:
@@ -146,12 +162,22 @@
         for h in range(1, heads):
             context = jnp.where(lanes == h, mixed[h * SEQ : (h + 1) * SEQ], context)
         total[rows, :] = dot(context.astype(bf), w_out_ref[...])
-    chunk = outs[0].shape[0] - PAD
+    chunk = (outs[0].shape[0] - PAD) // 2
     firsts = first_rows(total)
-    for step, out in enumerate(outs):
-        at = pl.ds(pl.multiple_of(who_ref[step] * chunk, chunk), chunk)
-        out[:chunk, :] = total[at, :].astype(out.dtype)
-        out[chunk:, :] = firsts.astype(out.dtype)
+    for out, pair in zip(outs, ((0, 2), (1, 3))):
+        for j, step in enumerate(pair):
+            at = pl.ds(pl.multiple_of((who_ref[0] ^ step) * chunk, chunk), chunk)
+            out[j * chunk : (j + 1) * chunk, :] = total[at, :].astype(out.dtype)
+        out[2 * chunk :, :] = firsts.astype(out.dtype)
+
+
+def half_kernel(chunk, ready, kept_ref, came_ref, keep_ref, give_ref):
+    total = kept_ref[...] + came_ref[...].astype(f32)
+    keep_ref[:chunk, :] = total[:chunk]
+    give_ref[:chunk, :] = total[chunk : 2 * chunk].astype(bf)
+    if keep_ref.shape[0] > chunk:
+        keep_ref[chunk:, :] = total[2 * chunk :]
+        give_ref[chunk:, :] = total[2 * chunk :].astype(bf)
 
 
 def first_rows(ref):
@@ -187,15 +213,13 @@
 
 
 def ffn_kernel(ready, w_in_ref, w_out_ref, gains_ref, first_hidden, first_terms, *refs):
-    *refs, first = refs
-    count = len(refs) // 2
-    ins, outs = refs[:count], refs[count:]
-    chunk = outs[0].shape[0]
+    *ins, kept, sent, first = refs
+    chunk = kept.shape[0] // 2
     hidden = jnp.concatenate([ref[:chunk, :] for ref in ins], axis=0)
     inner = gelu(dot(hidden, w_in_ref[...])).astype(bf)
     total = dot(inner, w_out_ref[...])
-    for step, out in enumerate(outs):
-        out[...] = total[step * chunk : (step + 1) * chunk].astype(out.dtype)
+    kept[...] = total[: 2 * chunk]
+    sent[...] = total[2 * chunk :].astype(bf)
     terms = first_terms[...]
     for ref in ins[1:]:
         terms = terms + ref[chunk:, :].astype(f32)
@@ -224,13 +248,6 @@
     out[...] = rows.astype(bf)
 
 
-def place_kernel(ready, who_ref, *refs):
-    *chunks, out = refs
-    chunk = out.shape[0] // len(chunks)
-    for step, ref in enumerate(chunks):
-        out[pl.ds(pl.multiple_of(who_ref[step] * chunk, chunk), chunk), :] = ref[...]
-
-
 def own_kernel(ready, table_ref, w_ref, kv_ref, q_ref):
     cols = w_ref.shape[1]
     table = table_ref[...]
@@ -244,9 +261,14 @@
 
 
 def graph_kernel(
-    ready, who_ref, cols_ref, at_ref, q_ref, kv_ref, w_ref, mask_ref, far_ref, first_ref, *refs
+    whose, ready, who_ref, cols_ref, at_ref, q_ref, kv_ref, w_ref, mask_ref, far_ref, first_ref, *refs
 ):
-    *packs, out_ref, k_all, v_all, firsts = refs
+    *packs, out_ref, encoded_ref, k_all, v_all, firsts = refs
+    dones, packs = packs[: len(whose)], packs[len(whose) :]
+    chunk = dones[0].shape[0]
+    for step, ref in zip(whose, dones):
+        at = pl.multiple_of((who_ref[0] ^ step) * chunk, chunk)
+        encoded_ref[pl.ds(at, chunk), :] = ref[...]
     nodes, cols = q_ref.shape
     row_tiles = nodes // TILE
     per_part = first_ref.shape[0]
@@ -255,15 +277,13 @@
         rows = ref[...].astype(f32)
         for turn in range(firsts.shape[0] // per_part // members):
             for title in range(per_part):
-                place = (turn * members + who_ref[step]) * per_part + title
+                place = (turn * members + (who_ref[0] ^ step)) * per_part + title
                 at = turn * per_part + title
                 firsts[pl.ds(place, 1), :] = rows[at : at + 1]
     firsts[0:per_part, :] = first_ref[...].astype(f32)
     first = firsts[...].astype(bf)
-    ready(5)
     first_kv = jnp.concatenate([dot_nt(first, w_ref[1]), dot_nt(first, w_ref[2])], axis=1).astype(bf)
     first_q = dot_nt(first, w_ref[0])
-    ready(2, 4)
     for tile in range(row_tiles):
         span = slice(tile * TILE, (tile + 1) * TILE)
         rows = kv_ref[span, :].astype(f32)
@@ -274,7 +294,6 @@
         rows = rows.astype(bf)
         k_all[span, :] = rows[:, :cols]
         v_all[span, :] = rows[:, cols:]
-    ready(7)
     lanes = lax.broadcasted_iota(jnp.int32, (TILE, first_kv.shape[0]), 1).astype(f32)
     for tile in range(far_ref.shape[0] // TILE):
         rows = far_ref[tile * TILE : (tile + 1) * TILE, :].astype(f32)
@@ -285,7 +304,6 @@
         k_all[span, :] = fixed[:, :cols]
         v_all[span, :] = fixed[:, cols:]
 
-    ready(1, 3, 6)
     heads = cols // GHD
     head_of = lax.broadcasted_iota(jnp.int32, (TILE, cols), 1) // GHD
     for tile in range(row_tiles):
@@ -334,21 +352,38 @@
     mp = lax.axis_size("mp")
     dp = lax.axis_size("dp")
     me_mp = lax.axis_index("mp").astype(jnp.int32)
-    me_dp = lax.axis_index("dp").astype(jnp.int32).reshape(1)
-    who = me_mp ^ jnp.arange(mp, dtype=jnp.int32)
+    me_dp = lax.axis_index("dp").astype(jnp.int32)
+    me, who = me_dp.reshape(1), me_mp.reshape(1)
     chunk = tok_rows // mp
     per_part = title_nodes.shape[0]
     fetch = send_ids.shape[2]
 
     def swap(value, step, axis="mp"):
         return lax.ppermute(value, axis, [(i, i ^ step) for i in range(lax.axis_size(axis))])
+
+    def gather(value):
+        whose, blocks, step = [0], [value], mp // 2
+        while step:
+            blocks = blocks + [swap(block, step) for block in blocks]
+            whose = whose + [other ^ step for other in whose]
+            step //= 2
+        return whose, blocks
+
+    def halves(kept, came, pad):
+        dims = (chunk + pad, width)
+        return call(
+            functools.partial(half_kernel, chunk),
+            (shape(dims, f32), shape(dims, bf)),
+            (kept, came),
+            name="half",
+        )
 
     w_attn_in = jnp.swapaxes(w_attn_in, 1, 2)
     w_graph = jnp.swapaxes(w_graph, 1, 2)
     sent = call(
         send_kernel,
         shape((dp * fetch, 2 * cols), bf),
-        (me_dp, title_nodes, send_ids[0], node_table, w_graph),
+        (me, title_nodes, send_ids[0], node_table, w_graph),
         smem=(0,),
         hbm=(4, 3, 2, 1),
         scalars=(1,),
@@ -362,33 +397,40 @@
     ).reshape(dp * fetch, 2 * cols)
     titles, _ = lax.optimization_barrier((titles, sent))
 
-    terms = call(
+    kept, given = call(
         attn_kernel,
-        tuple(shape((chunk + PAD, width), bf if step else f32) for step in range(mp)),
+        (shape((2 * chunk + PAD, width), f32), shape((2 * chunk + PAD, width), bf)),
         (who, titles, w_attn_in, w_attn_out),
         smem=(0,),
         scratch=[pltpu.VMEM((tok_rows, width), f32)],
         flops=2 * tok_rows * width * 4 * w_attn_in.shape[1],
         name="attn",
     )
-    parts = [swap(terms[step], step) for step in range(1, mp)]
+    keep, give = halves(kept, swap(given, 1), PAD)
+    part = swap(give, 2)
+    mask = call(
+        mask_kernel, shape((nodes, TPR * TILE), bf), (nbr_slots.T,), flops=4 * 10**9, name="mask"
+    )
+    part, mask = lax.optimization_barrier((part, mask))
     hidden, first_hidden, first_terms = call(
         norm_one_kernel,
         (shape((chunk + PAD, width), bf), shape((PAD, width), bf), shape((PAD, width), f32)),
-        (who, titles, gains, w_ffn_in, w_ffn_out, terms[0], *parts),
+        (who, titles, gains, w_ffn_in, w_ffn_out, keep, part),
         smem=(0,),
         name="norm_one",
     )
-    hiddens = [hidden] + [swap(hidden, step) for step in range(1, mp)]
-    *terms, first = call(
+    whose, hiddens = gather(hidden)
+    kept, given, first = call(
         ffn_kernel,
-        tuple(shape((chunk, width), bf if step else f32) for step in range(mp))
-        + (shape((per_part, width), bf),),
+        (
+            shape((2 * chunk, width), f32),
+            shape((2 * chunk, width), bf),
+            shape((per_part, width), bf),
+        ),
         (w_ffn_in, w_ffn_out, gains, first_hidden, first_terms, *hiddens),
         flops=4 * tok_rows * width * w_ffn_in.shape[1],
         name="ffn",
     )
-    parts = [swap(terms[step], step) for step in range(1, mp)]
     turns = dp // mp
     firsts = [
         lax.ppermute(
@@ -403,9 +445,8 @@
         )
         for turn in range(turns)
     ]
-    mask = call(
-        mask_kernel, shape((nodes, TPR * TILE), bf), (nbr_slots.T,), flops=4 * 10**9, name="mask"
-    )
+    keep, give = halves(kept, swap(given, 1), 0)
+    part = swap(give, 2)
     kv, q = call(
         own_kernel,
         (shape((nodes, 2 * cols), bf), shape((nodes, cols), bf)),
@@ -413,36 +454,26 @@
         flops=2 * 10**9,
         name="own",
     )
-    hidden, kv, q = lax.optimization_barrier((hidden, kv, q))
+    part, firsts, kv, q = lax.optimization_barrier((part, firsts, kv, q))
     done = call(
-        norm_two_kernel,
-        shape((chunk, width), bf),
-        (hidden, gains, terms[0], *parts),
-        name="norm_two",
-    )
-    dones = [done] + [swap(done, step) for step in range(1, mp)]
-    dones, firsts, mask = lax.optimization_barrier((dones, firsts, mask))
+        norm_two_kernel, shape((chunk, width), bf), (hidden, gains, keep, part), name="norm_two"
+    )
     pack = call(pack_kernel, shape((tail_rows(turns * per_part), width), bf), firsts, name="pack")
     packs = [pack] + [swap(pack, step) for step in range(1, mp)]
-
+    _, dones = gather(done)
     keys = nodes + dp * fetch
-    graph_out = call(
-        graph_kernel,
-        shape((cols, nodes), bf),
-        (who, tile_cols, title_nodes, q, kv, w_graph, mask, far, first, *packs),
-        smem=(0,),
-        hbm=(5, 2, 4, 7, 1, 3, 6),
-        scalars=(1, 2),
+    graph_out, encoded = call(
+        functools.partial(graph_kernel, whose),
+        (shape((cols, nodes), bf), shape((tok_rows, width), bf)),
+        (who, tile_cols, title_nodes, q, kv, w_graph, mask, far, first, *dones, *packs),
+        smem=(0, 1, 2),
         scratch=[
             pltpu.VMEM((keys, cols), bf),
             pltpu.VMEM((keys, cols), bf),
             pltpu.VMEM((dp * per_part, width), f32),
         ],
-        flops=10**9,
+        flops=4 * 10**9,
         name="graph",
-    )
-    encoded = call(
-        place_kernel, shape((tok_rows, width), bf), (who, *dones), smem=(0,), name="place"
     )
     return (encoded, graph_out.T)
 

time: 65.7 us -> 65.4 us (level)
  waiting for transfers between devices: 14.5 us -> 24.6 us
  starting transfers between devices: 23.9 us -> 18.6 us
  Pallas kernels: 22.4 us -> 17.3 us
    ppermute x2, waiting for transfers between devices: 0.01 us -> 10.6 us  [local(): lax.ppermute(first, ('dp', 'mp'), [(p * mp + m, (p ^ turn * mp + m) * mp...]
    ppermute x15 -> x13, starting transfers between devices: 12.8 us -> 7.48 us  [swap(): lax.ppermute(value, axis, [(i, i ^ step) for i in range(lax.axis_size(axi...]
    pallas_call x10 -> x11, Pallas kernels: 22.4 us -> 17.3 us  [call(): pl.pallas_call(body, out_shape=outs, in_specs=specs, out_specs=jax.tree.m...]
    ppermute x15 -> x13, waiting for transfers between devices: 14.5 us -> 14 us  [swap(): lax.ppermute(value, axis, [(i, i ^ step) for i in range(lax.axis_size(axi...]
    unnamed x36 -> x30, local copies, waits for them, and re-layouts: 3.48 us -> 3.71 us
  transfers between devices with their start and end apart: 18 -> 16, of which waited for: 6 -> 7; matrix products, arithmetic and copies ran while one was open for 0% -> 0% of each run, Pallas kernels for 17% -> 13%
where the time goes in v11:
time: 65.4 us; the launch traced here: 65.1 us
  waiting for transfers between devices  24.6 us (38%)
  starting transfers between devices  18.6 us (28%)
  Pallas kernels  17.3 us (26%)
  local copies, waits for them, and re-layouts  3.71 us (6%)
  between operations  0.89 us (1%)
    pallas_call x11, Pallas kernels, call(): pl.pallas_call(body, out_shape=outs, in_specs=specs, out_specs=jax.tree.m...  17.3 us
    ppermute x13, waiting for transfers between devices, swap(): lax.ppermute(value, axis, [(i, i ^ step) for i in range(lax.axis_size(axi...  14 us
    ppermute x2, waiting for transfers between devices, local(): lax.ppermute(first, ('dp', 'mp'), [(p * mp + m, (p ^ turn * mp + m) * mp...  10.6 us
    ppermute x13, starting transfers between devices, swap(): lax.ppermute(value, axis, [(i, i ^ step) for i in range(lax.axis_size(axi...  7.48 us
    all_to_all x1, starting transfers between devices, local(): lax.all_to_all(sent.reshape(dp, fetch, 2 * cols), 'dp', split_axis=0, con...  7.4 us
    ppermute x2, starting transfers between devices, local(): lax.ppermute(first, ('dp', 'mp'), [(p * mp + m, (p ^ turn * mp + m) * mp...  3.73 us
    unnamed x30, local copies, waits for them, and re-layouts  3.71 us
  transfers between devices with their start and end apart: 16, of which 7 were waited for; matrix products, arithmetic and copies ran while one was open for 0% of the time, Pallas kernels for 13%

profile of v11, /device:TPU:0, one launch (start us, length us, event | category | flops | bytes accessed | tf_op | source)
XLA Modules:
  0.0 65.1 jit_solution(8655335980563924120)
XLA Ops:
  0.6 4.1 %send.1 = bf16[2048,384]{1,0:T(8,128)(2,1)} custom-call(s32[1]{0:T(128)} %bitcast.1.refs_0_, s32[2]{0:T(128)} %refs_2_.5, s32[8,256]{1,0:T(8,128)} %bitcast.16, bf16[512,768]{1,0:T(8,128)(2,1)} %refs_0_.3, bf16[3,192,768]{2,1,0:T(8,128)(2,1)} %bitcast.11), custom_call_target="tpu_custom_call" | custom-call | flops 1107296256 | bytes 1679372 | tf_op jit(solution)/shard_map/send/pallas_call | solution.py:62
  4.7 0.0 copy-start.2
  4.7 0.0 copy-start.3
  4.7 0.0 copy-start.4
  4.7 7.4 %all-to-all-start = ((bf16[8,256,384]{2,1,0:T(8,128)(2,1)}), bf16[8,256,384]{2,1,0:T(8,128)(2,1)S(1)}, u32[]{:S(2)}, u32[]{:S(2)}) async-start(bf16[8,256,384]{2,1,0:T(8,128)(2,1)} %bitcast.15), calls=%async_computation | async-start | bytes 3145728 | tf_op jit(solution)/shard_map/all_to_all | solution.py:395
  12.1 0.0 copy-start.8
  12.2 0.0 copy-done.2
  12.2 0.0 copy-done.3
  12.2 0.0 copy-done.4
  12.2 1.7 %attn.1 = (f32[144,768]{1,0:T(8,128)S(1)}, bf16[144,768]{1,0:T(8,128)(2,1)S(1)}) custom-call(s32[1]{0:T(128)} %bitcast.refs_0_, bf16[256,768]{1,0:T(8,128)(2,1)S(1)} %copy-done.2, bf16[3,192,768]{2,1,0:T(8,128)(2,1)S(1)} %bitcast.10, bf16[192,768]{1,0:T(8,128)(2,1)S(1)} %copy-done.4), custom_call_target="tpu_custom_call" | custom-call | flops 301989888 | bytes 1572868 | tf_op jit(solution)/shard_map/attn/pallas_call | solution.py:62
  13.9 0.1 collective-permute-start
  14.0 1.5 %collective-permute-done.refs_1_ = bf16[144,768]{1,0:T(8,128)(2,1)S(1)} collective-permute-done((bf16[144,768]{1,0:T(8,128)(2,1)S(1)}, bf16[144,768]{1,0:T(8,128)(2,1)S(1)}, u32[]{:S(2)}, u32[]{:S(2)}) %collective-permute-start) | collective-permute-done | bytes 221216 | tf_op jit(solution)/shard_map/ppermute | solution.py:362
  15.5 1.6 %collective-permute-start.1 = (bf16[80,768]{1,0:T(8,128)(2,1)S(1)}, bf16[80,768]{1,0:T(8,128)(2,1)S(1)}, u32[]{:S(2)}, u32[]{:S(2)}) collective-permute-start(bf16[80,768]{1,0:T(8,128)(2,1)S(1)} %get-tuple-element.30), channel_id=1, source_target_pairs={{0,2},{1,3},{2,0},{3,1},{4,6},{5,7},{6,4},{7,5},{8,10},{9,11},{10,... | collective-permute-start | bytes 368648 | tf_op jit(solution)/shard_map/ppermute | solution.py:362
  17.1 0.0 copy-done.8
  17.1 4.2 %mask.1.refs_6_ = bf16[512,768]{1,0:T(8,128)(2,1)S(1)} custom-call(s32[16,512]{1,0:T(8,128)S(1)} %bitcast.14), custom_call_target="tpu_custom_call" | custom-call | flops 4000000000 | bytes 32768 | tf_op jit(solution)/shard_map/mask/pallas_call | solution.py:62
  21.3 0.0 copy-start.13
  21.4 0.9 %copy-done.13 = bf16[512,768]{1,0:T(8,128)(2,1)} copy-done((bf16[512,768]{1,0:T(8,128)(2,1)}, bf16[512,768]{1,0:T(8,128)(2,1)S(1)}, u32[]{:S(2)}) %copy-start.13) | copy-done | bytes 786456
  22.2 0.0 collective-permute-done.1.refs_6_
  22.2 0.0 copy-done
  22.2 0.0 copy-done.1
  22.2 0.0 copy-done.5
  22.3 0.7 %norm_one.1 = (bf16[80,768]{1,0:T(8,128)(2,1)S(1)}, bf16[16,768]{1,0:T(8,128)(2,1)S(1)}, f32[16,768]{1,0:T(8,128)S(1)}) custom-call(s32[1]{0:T(128)} %bitcast.refs_0_, bf16[256,768]{1,0:T(8,128)(2,1)S(1)} %copy-done.2, f32[2,768]{1,0:T(2,128)S(1)} %copy-done.5, bf16[768,768]{1,0:T(8,128)(2,1)S(1)} %copy-done, bf16[768,768]{1,0:T(8,128)(2,1)S(1)} %copy-done.1, ...), custom_call_target="tpu_custom_call" | custom-call | bytes 3127300 | tf_op jit(solution)/shard_map/norm_one/pallas_call | solution.py:62
  22.9 0.5 collective-permute-start.2
  23.5 0.0 collective-permute-start.3
  23.5 4.6 %collective-permute-done.2.refs_6_ = bf16[80,768]{1,0:T(8,128)(2,1)S(1)} collective-permute-done((bf16[80,768]{1,0:T(8,128)(2,1)S(1)}, bf16[80,768]{1,0:T(8,128)(2,1)S(1)}, u32[]{:S(2)}, u32[]{:S(2)}) %collective-permute-start.2) | collective-permute-done | bytes 122912 | tf_op jit(solution)/shard_map/ppermute | solution.py:362
  28.0 0.0 collective-permute-start.4
  28.0 0.0 collective-permute-done.3.refs_7_
  28.0 1.3 %collective-permute-done.4.refs_8_ = bf16[80,768]{1,0:T(8,128)(2,1)S(1)} collective-permute-done((bf16[80,768]{1,0:T(8,128)(2,1)S(1)}, bf16[80,768]{1,0:T(8,128)(2,1)S(1)}, u32[]{:S(2)}, u32[]{:S(2)}) %collective-permute-start.4) | collective-permute-done | bytes 122912 | tf_op jit(solution)/shard_map/ppermute | solution.py:362
  29.4 0.9 %ffn.1 = (f32[128,768]{1,0:T(8,128)S(1)}, bf16[128,768]{1,0:T(8,128)(2,1)S(1)}, bf16[2,768]{1,0:T(2,128)(2,1)S(1)}) custom-call(bf16[768,768]{1,0:T(8,128)(2,1)S(1)} %copy-done, bf16[768,768]{1,0:T(8,128)(2,1)S(1)} %copy-done.1, f32[2,768]{1,0:T(2,128)S(1)} %copy-done.5, bf16[16,768]{1,0:T(8,128)(2,1)S(1)} %get-tuple-element.32.refs_3_, ...), custom_call_target="tpu_custom_call" | custom-call | flops 603979776 | bytes 2930688 | tf_op jit(solution)/shard_map/ffn/pallas_call | solution.py:62
  30.3 0.2 collective-permute-start.5
  30.5 2.9 %collective-permute-start.8 = (bf16[2,768]{1,0:T(2,128)(2,1)S(1)}, bf16[2,768]{1,0:T(2,128)(2,1)S(1)}, u32[]{:S(2)}, u32[]{:S(2)}) collective-permute-start(bf16[2,768]{1,0:T(2,128)(2,1)S(1)} %get-tuple-element.38.refs_8_), channel_id=1, source_target_pairs={{0,16},{1,21},{2,26},{3,31},{4,20},{5,17},{6,30},{7,27},{8,24},{9,... | collective-permute-start | bytes 9224 | tf_op jit(solution)/shard_map/ppermute | solution.py:436
  33.4 0.8 %collective-permute-start.7 = (bf16[2,768]{1,0:T(2,128)(2,1)S(1)}, bf16[2,768]{1,0:T(2,128)(2,1)S(1)}, u32[]{:S(2)}, u32[]{:S(2)}) collective-permute-start(bf16[2,768]{1,0:T(2,128)(2,1)S(1)} %get-tuple-element.38.refs_8_), channel_id=1, source_target_pairs={{1,5},{2,10},{3,15},{5,1},{6,14},{7,11},{9,13},{10,2},{11,7},{13,9... | collective-permute-start | bytes 9224 | tf_op jit(solution)/shard_map/ppermute | solution.py:436
  34.3 0.0 collective-permute-done.5.refs_1_
  34.3 0.0 copy-start.9
  34.3 0.0 copy-start.10
  34.3 2.7 %collective-permute-start.6 = (bf16[64,768]{1,0:T(8,128)(2,1)S(1)}, bf16[64,768]{1,0:T(8,128)(2,1)S(1)}, u32[]{:S(2)}, u32[]{:S(2)}) collective-permute-start(bf16[64,768]{1,0:T(8,128)(2,1)S(1)} %get-tuple-element.37), channel_id=1, source_target_pairs={{0,2},{1,3},{2,0},{3,1},{4,6},{5,7},{6,4},{7,5},{8,10},{9,11},{10,... | collective-permute-start | bytes 294920 | tf_op jit(solution)/shard_map/ppermute | solution.py:362
  37.1 0.0 copy-done.6
  37.1 0.0 copy-done.7
  37.1 0.9 %own.1 = (bf16[512,384]{1,0:T(8,128)(2,1)S(1)}, bf16[512,192]{1,0:T(8,128)(2,1)S(1)}) custom-call(bf16[512,768]{1,0:T(8,128)(2,1)S(1)} %copy-done.7, bf16[3,192,768]{2,1,0:T(8,128)(2,1)S(1)} %bitcast.12), custom_call_target="tpu_custom_call" | custom-call | flops 2000000000 | bytes 1671168 | tf_op jit(solution)/shard_map/own/pallas_call | solution.py:62
  37.9 0.0 copy-start.11
  38.0 0.7 %copy-done.11 = bf16[512,192]{1,0:T(8,128)(2,1)} copy-done((bf16[512,192]{1,0:T(8,128)(2,1)}, bf16[512,192]{1,0:T(8,128)(2,1)S(1)}, u32[]{:S(2)}) %copy-start.11) | copy-done | bytes 196632
  38.6 10.6 %collective-permute-done.8.refs_1_ = bf16[2,768]{1,0:T(2,128)(2,1)S(1)} collective-permute-done((bf16[2,768]{1,0:T(2,128)(2,1)S(1)}, bf16[2,768]{1,0:T(2,128)(2,1)S(1)}, u32[]{:S(2)}, u32[]{:S(2)}) %collective-permute-start.8) | collective-permute-done | bytes 3104 | tf_op jit(solution)/shard_map/ppermute | solution.py:436
  49.3 0.0 collective-permute-done.7.refs_0_
  49.3 0.0 collective-permute-done.6.refs_3_
  49.3 0.2 norm_two.1.refs_9_
  49.5 0.1 collective-permute-start.9
  49.6 0.1 collective-permute-start.10
  49.7 4.5 %collective-permute-done.9.refs_10_ = bf16[64,768]{1,0:T(8,128)(2,1)S(1)} collective-permute-done((bf16[64,768]{1,0:T(8,128)(2,1)S(1)}, bf16[64,768]{1,0:T(8,128)(2,1)S(1)}, u32[]{:S(2)}, u32[]{:S(2)}) %collective-permute-start.9) | collective-permute-done | bytes 98336 | tf_op jit(solution)/shard_map/ppermute | solution.py:362
  54.2 0.0 collective-permute-start.11
  54.2 0.2 collective-permute-start.14
  54.4 2.0 %collective-permute-start.13 = (bf16[16,768]{1,0:T(8,128)(2,1)S(1)}, bf16[16,768]{1,0:T(8,128)(2,1)S(1)}, u32[]{:S(2)}, u32[]{:S(2)}) collective-permute-start(bf16[16,768]{1,0:T(8,128)(2,1)S(1)} %pack.1.refs_13_), channel_id=1, source_target_pairs={{0,2},{1,3},{2,0},{3,1},{4,6},{5,7},{6,4},{7,5},{8,10},{9,11},{10,... | collective-permute-start | bytes 73736 | tf_op jit(solution)/shard_map/ppermute | solution.py:362
  56.4 0.0 collective-permute-start.12
  56.4 1.1 %collective-permute-done.14.refs_16_ = bf16[16,768]{1,0:T(8,128)(2,1)S(1)} collective-permute-done((bf16[16,768]{1,0:T(8,128)(2,1)S(1)}, bf16[16,768]{1,0:T(8,128)(2,1)S(1)}, u32[]{:S(2)}, u32[]{:S(2)}) %collective-permute-start.14) | collective-permute-done | bytes 24608 | tf_op jit(solution)/shard_map/ppermute | solution.py:362
  57.5 0.9 %collective-permute-done.13.refs_15_ = bf16[16,768]{1,0:T(8,128)(2,1)S(1)} collective-permute-done((bf16[16,768]{1,0:T(8,128)(2,1)S(1)}, bf16[16,768]{1,0:T(8,128)(2,1)S(1)}, u32[]{:S(2)}, u32[]{:S(2)}) %collective-permute-start.13) | collective-permute-done | bytes 24608 | tf_op jit(solution)/shard_map/ppermute | solution.py:362
  58.5 0.0 collective-permute-done.12.refs_14_
  58.5 0.0 collective-permute-done.10.refs_11_
  58.5 0.0 collective-permute-done.11.refs_12_
  58.5 0.0 all-to-all-done
  58.5 0.0 copy-done.9
  58.5 0.0 copy-done.10
  58.5 0.0 copy-start.12
  58.5 0.9 %copy-done.12 = bf16[512,192]{1,0:T(8,128)(2,1)S(1)} copy-done((bf16[512,192]{1,0:T(8,128)(2,1)S(1)}, bf16[512,192]{1,0:T(8,128)(2,1)}, u32[]{:S(2)}) %copy-start.12) | copy-done | bytes 196632
  59.5 1.1 %copy-done.14 = bf16[512,768]{1,0:T(8,128)(2,1)S(1)} copy-done((bf16[512,768]{1,0:T(8,128)(2,1)S(1)}, bf16[512,768]{1,0:T(8,128)(2,1)}, u32[]{:S(2)}) %copy-start.14) | copy-done | bytes 786456
  60.6 4.5 %graph.1 = (bf16[192,512]{1,0:T(8,128)(2,1)}, bf16[256,768]{1,0:T(8,128)(2,1)}) custom-call(s32[1]{0:T(128)} %bitcast.refs_0_, s32[4,6]{1,0:T(4,128)S(1)} %copy-done.9, s32[2]{0:T(128)S(1)} %copy-done.10, bf16[512,192]{1,0:T(8,128)(2,1)S(1)} %copy-done.12, bf16[512,384]{1,0:T(8,128)(2,1)S(1)} %get-tuple-element.42.refs_4_, ...), custom_call_target="tpu_custom_call" | custom-call | flops 4000000000 | bytes 4328556 | tf_op jit(solution)/shard_map/graph/pallas_call | solution.py:62
  (9 shorter events, 0.1 us)
Async XLA Ops:
  4.7 7.4 %copy-start.2 = (bf16[256,768]{1,0:T(8,128)(2,1)S(1)}, bf16[256,768]{1,0:T(8,128)(2,1)}, u32[]{:S(2)}) copy-start(bf16[256,768]{1,0:T(8,128)(2,1)} %refs_1_.6) | copy-start | bytes 1179652
  4.7 7.4 %copy-start.3 = (bf16[3,768,192]{1,2,0:T(8,128)(2,1)S(1)}, bf16[3,768,192]{1,2,0:T(8,128)(2,1)}, u32[]{:S(2)}) copy-start(bf16[3,768,192]{1,2,0:T(8,128)(2,1)} %param.13) | copy-start | bytes 2654212
  4.7 7.4 %copy-start.4 = (bf16[192,768]{1,0:T(8,128)(2,1)S(1)}, bf16[192,768]{1,0:T(8,128)(2,1)}, u32[]{:S(2)}) copy-start(bf16[192,768]{1,0:T(8,128)(2,1)} %refs_3_.4) | copy-start | bytes 884740
  4.7 53.7 %all-to-all-start = ((bf16[8,256,384]{2,1,0:T(8,128)(2,1)}), bf16[8,256,384]{2,1,0:T(8,128)(2,1)S(1)}, u32[]{:S(2)}, u32[]{:S(2)}) async-start(bf16[8,256,384]{2,1,0:T(8,128)(2,1)} %bitcast.15), calls=%async_computation | async-start | bytes 3145728 | tf_op jit(solution)/shard_map/all_to_all | solution.py:395
  12.1 4.9 %copy-start.8 = (s32[512,16]{0,1:T(8,128)S(1)}, s32[512,16]{0,1:T(8,128)}, u32[]{:S(2)}) copy-start(s32[512,16]{0,1:T(8,128)} %param.23) | copy-start | bytes 98308
  13.9 1.5 %collective-permute-start = (bf16[144,768]{1,0:T(8,128)(2,1)S(1)}, bf16[144,768]{1,0:T(8,128)(2,1)S(1)}, u32[]{:S(2)}, u32[]{:S(2)}) collective-permute-start(bf16[144,768]{1,0:T(8,128)(2,1)S(1)} %get-tuple-element.28), channel_id=1, source_target_pairs={{0,1},{1,0},{2,3},{3,2},{4,5},{5,4},{6,7},{7,6},{8,9},{9,8},{10,11... | collective-permute-start | bytes 663560 | tf_op jit(solution)/shard_map/ppermute | solution.py:362
  15.5 6.7 %collective-permute-start.1 = (bf16[80,768]{1,0:T(8,128)(2,1)S(1)}, bf16[80,768]{1,0:T(8,128)(2,1)S(1)}, u32[]{:S(2)}, u32[]{:S(2)}) collective-permute-start(bf16[80,768]{1,0:T(8,128)(2,1)S(1)} %get-tuple-element.30), channel_id=1, source_target_pairs={{0,2},{1,3},{2,0},{3,1},{4,6},{5,7},{6,4},{7,5},{8,10},{9,11},{10,... | collective-permute-start | bytes 368648 | tf_op jit(solution)/shard_map/ppermute | solution.py:362
  17.1 5.2 %copy-start = (bf16[768,768]{1,0:T(8,128)(2,1)S(1)}, bf16[768,768]{1,0:T(8,128)(2,1)}, u32[]{:S(2)}) copy-start(bf16[768,768]{1,0:T(8,128)(2,1)} %refs_0_.2) | copy-start | bytes 3538948
  17.1 5.2 %copy-start.1 = (bf16[768,768]{1,0:T(8,128)(2,1)S(1)}, bf16[768,768]{1,0:T(8,128)(2,1)}, u32[]{:S(2)}) copy-start(bf16[768,768]{1,0:T(8,128)(2,1)} %refs_1_.7) | copy-start | bytes 3538948
  17.1 5.2 %copy-start.5 = (f32[2,768]{1,0:T(2,128)S(1)}, f32[2,768]{1,0:T(2,128)}, u32[]{:S(2)}) copy-start(f32[2,768]{1,0:T(2,128)} %refs_1_.8) | copy-start | bytes 18436
  21.3 0.9 %copy-start.13 = (bf16[512,768]{1,0:T(8,128)(2,1)}, bf16[512,768]{1,0:T(8,128)(2,1)S(1)}, u32[]{:S(2)}) copy-start(bf16[512,768]{1,0:T(8,128)(2,1)S(1)} %mask.1.refs_6_) | copy-start | bytes 2359300
  22.9 5.1 %collective-permute-start.2 = (bf16[80,768]{1,0:T(8,128)(2,1)S(1)}, bf16[80,768]{1,0:T(8,128)(2,1)S(1)}, u32[]{:S(2)}, u32[]{:S(2)}) collective-permute-start(bf16[80,768]{1,0:T(8,128)(2,1)S(1)} %get-tuple-element.34.refs_5_.refs_0_), channel_id=1, source_target_pairs={{0,2},{1,3},{2,0},{3,1},{4,6},{5,7},{6,4},{7,5},{8,10},{9,11},{10,... | collective-permute-start | bytes 368648 | tf_op jit(solution)/shard_map/ppermute | solution.py:362
  23.5 4.6 %collective-permute-start.3 = (bf16[80,768]{1,0:T(8,128)(2,1)S(1)}, bf16[80,768]{1,0:T(8,128)(2,1)S(1)}, u32[]{:S(2)}, u32[]{:S(2)}) collective-permute-start(bf16[80,768]{1,0:T(8,128)(2,1)S(1)} %get-tuple-element.34.refs_5_.refs_0_), channel_id=1, source_target_pairs={{0,1},{1,0},{2,3},{3,2},{4,5},{5,4},{6,7},{7,6},{8,9},{9,8},{10,11... | collective-permute-start | bytes 368648 | tf_op jit(solution)/shard_map/ppermute | solution.py:362
  28.0 1.3 %collective-permute-start.4 = (bf16[80,768]{1,0:T(8,128)(2,1)S(1)}, bf16[80,768]{1,0:T(8,128)(2,1)S(1)}, u32[]{:S(2)}, u32[]{:S(2)}) collective-permute-start(bf16[80,768]{1,0:T(8,128)(2,1)S(1)} %collective-permute-done.2.refs_6_), channel_id=1, source_target_pairs={{0,1},{1,0},{2,3},{3,2},{4,5},{5,4},{6,7},{7,6},{8,9},{9,8},{10,11... | collective-permute-start | bytes 368648 | tf_op jit(solution)/shard_map/ppermute | solution.py:362
  29.4 7.7 %copy-start.6 = (bf16[3,768,192]{1,2,0:T(8,128)(2,1)S(1)}, bf16[3,768,192]{1,2,0:T(8,128)(2,1)}, u32[]{:S(2)}) copy-start(bf16[3,768,192]{1,2,0:T(8,128)(2,1)} %param.19) | copy-start | bytes 2654212
  29.4 7.7 %copy-start.7 = (bf16[512,768]{1,0:T(8,128)(2,1)S(1)}, bf16[512,768]{1,0:T(8,128)(2,1)}, u32[]{:S(2)}) copy-start(bf16[512,768]{1,0:T(8,128)(2,1)} %refs_0_.3) | copy-start | bytes 2359300
  30.3 4.0 %collective-permute-start.5 = (bf16[128,768]{1,0:T(8,128)(2,1)S(1)}, bf16[128,768]{1,0:T(8,128)(2,1)S(1)}, u32[]{:S(2)}, u32[]{:S(2)}) collective-permute-start(bf16[128,768]{1,0:T(8,128)(2,1)S(1)} %get-tuple-element.36), channel_id=1, source_target_pairs={{0,1},{1,0},{2,3},{3,2},{4,5},{5,4},{6,7},{7,6},{8,9},{9,8},{10,11... | collective-permute-start | bytes 589832 | tf_op jit(solution)/shard_map/ppermute | solution.py:362
  30.5 18.8 %collective-permute-start.8 = (bf16[2,768]{1,0:T(2,128)(2,1)S(1)}, bf16[2,768]{1,0:T(2,128)(2,1)S(1)}, u32[]{:S(2)}, u32[]{:S(2)}) collective-permute-start(bf16[2,768]{1,0:T(2,128)(2,1)S(1)} %get-tuple-element.38.refs_8_), channel_id=1, source_target_pairs={{0,16},{1,21},{2,26},{3,31},{4,20},{5,17},{6,30},{7,27},{8,24},{9,... | collective-permute-start | bytes 9224 | tf_op jit(solution)/shard_map/ppermute | solution.py:436
  33.4 15.9 %collective-permute-start.7 = (bf16[2,768]{1,0:T(2,128)(2,1)S(1)}, bf16[2,768]{1,0:T(2,128)(2,1)S(1)}, u32[]{:S(2)}, u32[]{:S(2)}) collective-permute-start(bf16[2,768]{1,0:T(2,128)(2,1)S(1)} %get-tuple-element.38.refs_8_), channel_id=1, source_target_pairs={{1,5},{2,10},{3,15},{5,1},{6,14},{7,11},{9,13},{10,2},{11,7},{13,9... | collective-permute-start | bytes 9224 | tf_op jit(solution)/shard_map/ppermute | solution.py:436
  34.3 24.2 %copy-start.9 = (s32[4,6]{1,0:T(4,128)S(1)}, s32[4,6]{1,0:T(4,128)}, u32[]{:S(2)}) copy-start(s32[4,6]{1,0:T(4,128)} %refs_1_.9) | copy-start | bytes 292
  34.3 24.2 %copy-start.10 = (s32[2]{0:T(128)S(1)}, s32[2]{0:T(128)}, u32[]{:S(2)}) copy-start(s32[2]{0:T(128)} %refs_2_.5) | copy-start | bytes 28
  34.3 14.9 %collective-permute-start.6 = (bf16[64,768]{1,0:T(8,128)(2,1)S(1)}, bf16[64,768]{1,0:T(8,128)(2,1)S(1)}, u32[]{:S(2)}, u32[]{:S(2)}) collective-permute-start(bf16[64,768]{1,0:T(8,128)(2,1)S(1)} %get-tuple-element.37), channel_id=1, source_target_pairs={{0,2},{1,3},{2,0},{3,1},{4,6},{5,7},{6,4},{7,5},{8,10},{9,11},{10,... | collective-permute-start | bytes 294920 | tf_op jit(solution)/shard_map/ppermute | solution.py:362
  37.9 0.7 %copy-start.11 = (bf16[512,192]{1,0:T(8,128)(2,1)}, bf16[512,192]{1,0:T(8,128)(2,1)S(1)}, u32[]{:S(2)}) copy-start(bf16[512,192]{1,0:T(8,128)(2,1)S(1)} %get-tuple-element.41.refs_3_) | copy-start | bytes 589828
  49.5 4.7 %collective-permute-start.9 = (bf16[64,768]{1,0:T(8,128)(2,1)S(1)}, bf16[64,768]{1,0:T(8,128)(2,1)S(1)}, u32[]{:S(2)}, u32[]{:S(2)}) collective-permute-start(bf16[64,768]{1,0:T(8,128)(2,1)S(1)} %norm_two.1.refs_9_), channel_id=1, source_target_pairs={{0,2},{1,3},{2,0},{3,1},{4,6},{5,7},{6,4},{7,5},{8,10},{9,11},{10,... | collective-permute-start | bytes 294920 | tf_op jit(solution)/shard_map/ppermute | solution.py:362
  49.6 8.9 %collective-permute-start.10 = (bf16[64,768]{1,0:T(8,128)(2,1)S(1)}, bf16[64,768]{1,0:T(8,128)(2,1)S(1)}, u32[]{:S(2)}, u32[]{:S(2)}) collective-permute-start(bf16[64,768]{1,0:T(8,128)(2,1)S(1)} %norm_two.1.refs_9_), channel_id=1, source_target_pairs={{0,1},{1,0},{2,3},{3,2},{4,5},{5,4},{6,7},{7,6},{8,9},{9,8},{10,11... | collective-permute-start | bytes 294920 | tf_op jit(solution)/shard_map/ppermute | solution.py:362
  54.2 4.3 %collective-permute-start.11 = (bf16[64,768]{1,0:T(8,128)(2,1)S(1)}, bf16[64,768]{1,0:T(8,128)(2,1)S(1)}, u32[]{:S(2)}, u32[]{:S(2)}) collective-permute-start(bf16[64,768]{1,0:T(8,128)(2,1)S(1)} %collective-permute-done.9.refs_10_), channel_id=1, source_target_pairs={{0,1},{1,0},{2,3},{3,2},{4,5},{5,4},{6,7},{7,6},{8,9},{9,8},{10,11... | collective-permute-start | bytes 294920 | tf_op jit(solution)/shard_map/ppermute | solution.py:362
  54.2 3.3 %collective-permute-start.14 = (bf16[16,768]{1,0:T(8,128)(2,1)S(1)}, bf16[16,768]{1,0:T(8,128)(2,1)S(1)}, u32[]{:S(2)}, u32[]{:S(2)}) collective-permute-start(bf16[16,768]{1,0:T(8,128)(2,1)S(1)} %pack.1.refs_13_), channel_id=1, source_target_pairs={{0,3},{1,2},{2,1},{3,0},{4,7},{5,6},{6,5},{7,4},{8,11},{9,10},{10,... | collective-permute-start | bytes 73736 | tf_op jit(solution)/shard_map/ppermute | solution.py:362
  54.4 4.1 %collective-permute-start.13 = (bf16[16,768]{1,0:T(8,128)(2,1)S(1)}, bf16[16,768]{1,0:T(8,128)(2,1)S(1)}, u32[]{:S(2)}, u32[]{:S(2)}) collective-permute-start(bf16[16,768]{1,0:T(8,128)(2,1)S(1)} %pack.1.refs_13_), channel_id=1, source_target_pairs={{0,2},{1,3},{2,0},{3,1},{4,6},{5,7},{6,4},{7,5},{8,10},{9,11},{10,... | collective-permute-start | bytes 73736 | tf_op jit(solution)/shard_map/ppermute | solution.py:362
  56.4 2.1 %collective-permute-start.12 = (bf16[16,768]{1,0:T(8,128)(2,1)S(1)}, bf16[16,768]{1,0:T(8,128)(2,1)S(1)}, u32[]{:S(2)}, u32[]{:S(2)}) collective-permute-start(bf16[16,768]{1,0:T(8,128)(2,1)S(1)} %pack.1.refs_13_), channel_id=1, source_target_pairs={{0,1},{1,0},{2,3},{3,2},{4,5},{5,4},{6,7},{7,6},{8,9},{9,8},{10,11... | collective-permute-start | bytes 73736 | tf_op jit(solution)/shard_map/ppermute | solution.py:362
  58.5 1.0 %copy-start.12 = (bf16[512,192]{1,0:T(8,128)(2,1)S(1)}, bf16[512,192]{1,0:T(8,128)(2,1)}, u32[]{:S(2)}) copy-start(bf16[512,192]{1,0:T(8,128)(2,1)} %copy-done.11) | copy-start | bytes 589828
  59.5 1.1 %copy-start.14 = (bf16[512,768]{1,0:T(8,128)(2,1)S(1)}, bf16[512,768]{1,0:T(8,128)(2,1)}, u32[]{:S(2)}) copy-start(bf16[512,768]{1,0:T(8,128)(2,1)} %copy-done.13) | copy-start | bytes 2359300

commit v12 on v11

--- a/solution.py
+++ b/solution.py
@@ -408,10 +408,6 @@
     )
     keep, give = halves(kept, swap(given, 1), PAD)
     part = swap(give, 2)
-    mask = call(
-        mask_kernel, shape((nodes, TPR * TILE), bf), (nbr_slots.T,), flops=4 * 10**9, name="mask"
-    )
-    part, mask = lax.optimization_barrier((part, mask))
     hidden, first_hidden, first_terms = call(
         norm_one_kernel,
         (shape((chunk + PAD, width), bf), shape((PAD, width), bf), shape((PAD, width), f32)),
@@ -454,13 +450,18 @@
         flops=2 * 10**9,
         name="own",
     )
-    part, firsts, kv, q = lax.optimization_barrier((part, firsts, kv, q))
+    mask = call(
+        mask_kernel, shape((nodes, TPR * TILE), bf), (nbr_slots.T,), flops=4 * 10**9, name="mask"
+    )
+    part, firsts, kv, q, mask = lax.optimization_barrier((part, firsts, kv, q, mask))
     done = call(
         norm_two_kernel, shape((chunk, width), bf), (hidden, gains, keep, part), name="norm_two"
     )
     pack = call(pack_kernel, shape((tail_rows(turns * per_part), width), bf), firsts, name="pack")
     packs = [pack] + [swap(pack, step) for step in range(1, mp)]
-    _, dones = gather(done)
+    across = swap(done, 2)
+    across, packs, far = lax.optimization_barrier((across, packs, far))
+    dones = [done, across, swap(done, 1), swap(across, 1)]
     keys = nodes + dp * fetch
     graph_out, encoded = call(
         functools.partial(graph_kernel, whose),

time: 65.4 us -> 63.5 us (0.971)
  waiting for transfers between devices: 24.6 us -> 20.2 us
  starting transfers between devices: 18.6 us -> 21.2 us
  local copies, waits for them, and re-layouts: 3.71 us -> 2.44 us
  Pallas kernels: 17.3 us -> 18.4 us
    ppermute x2, waiting for transfers between devices: 10.6 us -> 6.31 us  [local(): lax.ppermute(first, ('dp', 'mp'), [(p * mp + m, (p ^ turn * mp + m) * mp...]
    ppermute x13, starting transfers between devices: 7.48 us -> 10 us  [swap(): lax.ppermute(value, axis, [(i, i ^ step) for i in range(lax.axis_size(axi...]
    unnamed x30 -> x26, local copies, waits for them, and re-layouts: 3.71 us -> 2.44 us
    pallas_call x11, Pallas kernels: 17.3 us -> 18.4 us  [call(): pl.pallas_call(body, out_shape=outs, in_specs=specs, out_specs=jax.tree.m...]
  transfers between devices with their start and end apart: 16 -> 16, of which waited for: 7 -> 8; matrix products, arithmetic and copies ran while one was open for 0% -> 0% of each run, Pallas kernels for 13% -> 14%
where the time goes in v12:
time: 63.5 us; the launch traced here: 63.1 us
  starting transfers between devices  21.2 us (33%)
  waiting for transfers between devices  20.2 us (32%)
  Pallas kernels  18.4 us (29%)
  local copies, waits for them, and re-layouts  2.44 us (4%)
  between operations  0.85 us (1%)
    pallas_call x11, Pallas kernels, call(): pl.pallas_call(body, out_shape=outs, in_specs=specs, out_specs=jax.tree.m...  18.4 us
    ppermute x13, waiting for transfers between devices, swap(): lax.ppermute(value, axis, [(i, i ^ step) for i in range(lax.axis_size(axi...  13.9 us
    ppermute x13, starting transfers between devices, swap(): lax.ppermute(value, axis, [(i, i ^ step) for i in range(lax.axis_size(axi...  10 us
    all_to_all x1, starting transfers between devices, local(): lax.all_to_all(sent.reshape(dp, fetch, 2 * cols), 'dp', split_axis=0, con...  7.4 us
    ppermute x2, waiting for transfers between devices, local(): lax.ppermute(first, ('dp', 'mp'), [(p * mp + m, (p ^ turn * mp + m) * mp...  6.31 us
    ppermute x2, starting transfers between devices, local(): lax.ppermute(first, ('dp', 'mp'), [(p * mp + m, (p ^ turn * mp + m) * mp...  3.8 us
    unnamed x26, local copies, waits for them, and re-layouts  2.44 us
  transfers between devices with their start and end apart: 16, of which 8 were waited for; matrix products, arithmetic and copies ran while one was open for 0% of the time, Pallas kernels for 14%

profile of v12, /device:TPU:0, one launch (start us, length us, event | category | flops | bytes accessed | tf_op | source)
XLA Modules:
  0.0 63.1 jit_solution(2063747692042525547)
XLA Ops:
  0.6 4.1 %send.1 = bf16[2048,384]{1,0:T(8,128)(2,1)} custom-call(s32[1]{0:T(128)} %bitcast.1.refs_0_, s32[2]{0:T(128)} %refs_2_.5, s32[8,256]{1,0:T(8,128)} %bitcast.15, bf16[512,768]{1,0:T(8,128)(2,1)} %refs_0_.3, bf16[3,192,768]{2,1,0:T(8,128)(2,1)} %bitcast.10), custom_call_target="tpu_custom_call" | custom-call | flops 1107296256 | bytes 1679372 | tf_op jit(solution)/shard_map/send/pallas_call | solution.py:62
  4.7 0.0 copy-start.2
  4.7 0.0 copy-start.4
  4.7 0.0 copy-start.1
  4.7 0.0 copy-start.5
  4.8 7.4 %all-to-all-start = ((bf16[8,256,384]{2,1,0:T(8,128)(2,1)}), bf16[8,256,384]{2,1,0:T(8,128)(2,1)}, u32[]{:S(2)}, u32[]{:S(2)}) async-start(bf16[8,256,384]{2,1,0:T(8,128)(2,1)} %bitcast.14), calls=%async_computation | async-start | bytes 3145728 | tf_op jit(solution)/shard_map/all_to_all | solution.py:395
  12.1 0.0 copy-start
  12.2 0.0 copy-done.2
  12.2 0.0 copy-done.4
  12.2 0.0 copy-start.3
  12.2 1.2 %copy-done.3 = bf16[3,768,192]{1,2,0:T(8,128)(2,1)S(1)} copy-done((bf16[3,768,192]{1,2,0:T(8,128)(2,1)S(1)}, bf16[3,768,192]{1,2,0:T(8,128)(2,1)}, u32[]{:S(2)}) %copy-start.3) | copy-done | bytes 884760
  13.4 1.7 %attn.1 = (f32[144,768]{1,0:T(8,128)S(1)}, bf16[144,768]{1,0:T(8,128)(2,1)S(1)}) custom-call(s32[1]{0:T(128)} %bitcast.refs_0_, bf16[256,768]{1,0:T(8,128)(2,1)S(1)} %copy-done.2, bf16[3,192,768]{2,1,0:T(8,128)(2,1)S(1)} %bitcast.9, bf16[192,768]{1,0:T(8,128)(2,1)S(1)} %copy-done.4), custom_call_target="tpu_custom_call" | custom-call | flops 301989888 | bytes 1572868 | tf_op jit(solution)/shard_map/attn/pallas_call | solution.py:62
  15.2 0.1 collective-permute-start
  15.2 1.5 %collective-permute-done.refs_1_ = bf16[144,768]{1,0:T(8,128)(2,1)S(1)} collective-permute-done((bf16[144,768]{1,0:T(8,128)(2,1)S(1)}, bf16[144,768]{1,0:T(8,128)(2,1)S(1)}, u32[]{:S(2)}, u32[]{:S(2)}) %collective-permute-start) | collective-permute-done | bytes 221216 | tf_op jit(solution)/shard_map/ppermute | solution.py:362
  16.8 1.6 %collective-permute-start.1 = (bf16[80,768]{1,0:T(8,128)(2,1)S(1)}, bf16[80,768]{1,0:T(8,128)(2,1)S(1)}, u32[]{:S(2)}, u32[]{:S(2)}) collective-permute-start(bf16[80,768]{1,0:T(8,128)(2,1)S(1)} %get-tuple-element.35), channel_id=1, source_target_pairs={{0,2},{1,3},{2,0},{3,1},{4,6},{5,7},{6,4},{7,5},{8,10},{9,11},{10,... | collective-permute-start | bytes 368648 | tf_op jit(solution)/shard_map/ppermute | solution.py:362
  18.3 3.8 %collective-permute-done.1.refs_6_ = bf16[80,768]{1,0:T(8,128)(2,1)S(1)} collective-permute-done((bf16[80,768]{1,0:T(8,128)(2,1)S(1)}, bf16[80,768]{1,0:T(8,128)(2,1)S(1)}, u32[]{:S(2)}, u32[]{:S(2)}) %collective-permute-start.1) | collective-permute-done | bytes 122912 | tf_op jit(solution)/shard_map/ppermute | solution.py:362
  22.2 0.0 copy-done.1
  22.2 0.0 copy-done.5
  22.2 0.0 copy-done
  22.2 0.7 %norm_one.1 = (bf16[80,768]{1,0:T(8,128)(2,1)S(1)}, bf16[16,768]{1,0:T(8,128)(2,1)S(1)}, f32[16,768]{1,0:T(8,128)S(1)}) custom-call(s32[1]{0:T(128)} %bitcast.refs_0_, bf16[256,768]{1,0:T(8,128)(2,1)S(1)} %copy-done.2, f32[2,768]{1,0:T(2,128)S(1)} %copy-done.5, bf16[768,768]{1,0:T(8,128)(2,1)S(1)} %copy-done, bf16[768,768]{1,0:T(8,128)(2,1)S(1)} %copy-done.1, ...), custom_call_target="tpu_custom_call" | custom-call | bytes 3127300 | tf_op jit(solution)/shard_map/norm_one/pallas_call | solution.py:62
  22.9 0.0 copy-start.8
  22.9 1.5 %collective-permute-start.2 = (bf16[80,768]{1,0:T(8,128)(2,1)S(1)}, bf16[80,768]{1,0:T(8,128)(2,1)S(1)}, u32[]{:S(2)}, u32[]{:S(2)}) collective-permute-start(bf16[80,768]{1,0:T(8,128)(2,1)S(1)} %get-tuple-element.38.refs_5_.refs_0_), channel_id=1, source_target_pairs={{0,2},{1,3},{2,0},{3,1},{4,6},{5,7},{6,4},{7,5},{8,10},{9,11},{10,... | collective-permute-start | bytes 368648 | tf_op jit(solution)/shard_map/ppermute | solution.py:362
  24.4 0.0 collective-permute-start.3
  24.4 3.4 %collective-permute-done.2.refs_6_ = bf16[80,768]{1,0:T(8,128)(2,1)S(1)} collective-permute-done((bf16[80,768]{1,0:T(8,128)(2,1)S(1)}, bf16[80,768]{1,0:T(8,128)(2,1)S(1)}, u32[]{:S(2)}, u32[]{:S(2)}) %collective-permute-start.2) | collective-permute-done | bytes 122912 | tf_op jit(solution)/shard_map/ppermute | solution.py:362
  27.8 0.0 collective-permute-start.4
  27.8 0.0 collective-permute-done.3.refs_7_
  27.8 1.3 %collective-permute-done.4.refs_8_ = bf16[80,768]{1,0:T(8,128)(2,1)S(1)} collective-permute-done((bf16[80,768]{1,0:T(8,128)(2,1)S(1)}, bf16[80,768]{1,0:T(8,128)(2,1)S(1)}, u32[]{:S(2)}, u32[]{:S(2)}) %collective-permute-start.4) | collective-permute-done | bytes 122912 | tf_op jit(solution)/shard_map/ppermute | solution.py:362
  29.1 0.9 %ffn.1 = (f32[128,768]{1,0:T(8,128)S(1)}, bf16[128,768]{1,0:T(8,128)(2,1)S(1)}, bf16[2,768]{1,0:T(2,128)(2,1)S(1)}) custom-call(bf16[768,768]{1,0:T(8,128)(2,1)S(1)} %copy-done, bf16[768,768]{1,0:T(8,128)(2,1)S(1)} %copy-done.1, f32[2,768]{1,0:T(2,128)S(1)} %copy-done.5, bf16[16,768]{1,0:T(8,128)(2,1)S(1)} %get-tuple-element.36.refs_3_, ...), custom_call_target="tpu_custom_call" | custom-call | flops 603979776 | bytes 2930688 | tf_op jit(solution)/shard_map/ffn/pallas_call | solution.py:62
  30.0 0.2 collective-permute-start.5
  30.3 0.0 copy-done.8
  30.3 0.0 copy-start.6
  30.3 4.2 %mask.1.refs_6_ = bf16[512,768]{1,0:T(8,128)(2,1)S(1)} custom-call(s32[16,512]{1,0:T(8,128)S(1)} %bitcast.13), custom_call_target="tpu_custom_call" | custom-call | flops 4000000000 | bytes 32768 | tf_op jit(solution)/shard_map/mask/pallas_call | solution.py:62
  34.5 0.0 copy-start.11
  34.5 3.0 %collective-permute-start.8 = (bf16[2,768]{1,0:T(2,128)(2,1)S(1)}, bf16[2,768]{1,0:T(2,128)(2,1)S(1)}, u32[]{:S(2)}, u32[]{:S(2)}) collective-permute-start(bf16[2,768]{1,0:T(2,128)(2,1)S(1)} %get-tuple-element.42.refs_8_), channel_id=1, source_target_pairs={{0,16},{1,21},{2,26},{3,31},{4,20},{5,17},{6,30},{7,27},{8,24},{9,... | collective-permute-start | bytes 9224 | tf_op jit(solution)/shard_map/ppermute | solution.py:432
  37.5 0.8 %collective-permute-start.7 = (bf16[2,768]{1,0:T(2,128)(2,1)S(1)}, bf16[2,768]{1,0:T(2,128)(2,1)S(1)}, u32[]{:S(2)}, u32[]{:S(2)}) collective-permute-start(bf16[2,768]{1,0:T(2,128)(2,1)S(1)} %get-tuple-element.42.refs_8_), channel_id=1, source_target_pairs={{1,5},{2,10},{3,15},{5,1},{6,14},{7,11},{9,13},{10,2},{11,7},{13,9... | collective-permute-start | bytes 9224 | tf_op jit(solution)/shard_map/ppermute | solution.py:432
  38.3 0.0 collective-permute-done.5.refs_1_
  38.4 0.0 copy-start.9
  38.4 0.0 copy-start.10
  38.4 3.7 %collective-permute-start.6 = (bf16[64,768]{1,0:T(8,128)(2,1)S(1)}, bf16[64,768]{1,0:T(8,128)(2,1)S(1)}, u32[]{:S(2)}, u32[]{:S(2)}) collective-permute-start(bf16[64,768]{1,0:T(8,128)(2,1)S(1)} %get-tuple-element.41), channel_id=1, source_target_pairs={{0,2},{1,3},{2,0},{3,1},{4,6},{5,7},{6,4},{7,5},{8,10},{9,11},{10,... | collective-permute-start | bytes 294920 | tf_op jit(solution)/shard_map/ppermute | solution.py:362
  42.2 0.0 copy-done.6
  42.2 0.0 copy-done.7
  42.2 0.9 %own.1 = (bf16[512,384]{1,0:T(8,128)(2,1)S(1)}, bf16[512,192]{1,0:T(8,128)(2,1)S(1)}) custom-call(bf16[512,768]{1,0:T(8,128)(2,1)S(1)} %copy-done.7, bf16[3,192,768]{2,1,0:T(8,128)(2,1)S(1)} %bitcast.11), custom_call_target="tpu_custom_call" | custom-call | flops 2000000000 | bytes 1671168 | tf_op jit(solution)/shard_map/own/pallas_call | solution.py:62
  43.0 0.0 copy-done.11
  43.0 6.3 %collective-permute-done.8.refs_1_ = bf16[2,768]{1,0:T(2,128)(2,1)S(1)} collective-permute-done((bf16[2,768]{1,0:T(2,128)(2,1)S(1)}, bf16[2,768]{1,0:T(2,128)(2,1)S(1)}, u32[]{:S(2)}, u32[]{:S(2)}) %collective-permute-start.8) | collective-permute-done | bytes 3104 | tf_op jit(solution)/shard_map/ppermute | solution.py:432
  49.4 0.0 collective-permute-done.7.refs_0_
  49.4 0.0 collective-permute-done.6.refs_3_
  49.4 0.2 norm_two.1.refs_9_
  49.6 0.1 collective-permute-start.9
  49.7 0.9 %collective-permute-start.12 = (bf16[16,768]{1,0:T(8,128)(2,1)S(1)}, bf16[16,768]{1,0:T(8,128)(2,1)S(1)}, u32[]{:S(2)}, u32[]{:S(2)}) collective-permute-start(bf16[16,768]{1,0:T(8,128)(2,1)S(1)} %pack.1.refs_13_), channel_id=1, source_target_pairs={{0,3},{1,2},{2,1},{3,0},{4,7},{5,6},{6,5},{7,4},{8,11},{9,10},{10,... | collective-permute-start | bytes 73736 | tf_op jit(solution)/shard_map/ppermute | solution.py:362
  50.6 1.2 %collective-permute-start.11 = (bf16[16,768]{1,0:T(8,128)(2,1)S(1)}, bf16[16,768]{1,0:T(8,128)(2,1)S(1)}, u32[]{:S(2)}, u32[]{:S(2)}) collective-permute-start(bf16[16,768]{1,0:T(8,128)(2,1)S(1)} %pack.1.refs_13_), channel_id=1, source_target_pairs={{0,2},{1,3},{2,0},{3,1},{4,6},{5,7},{6,4},{7,5},{8,10},{9,11},{10,... | collective-permute-start | bytes 73736 | tf_op jit(solution)/shard_map/ppermute | solution.py:362
  51.8 0.0 collective-permute-start.10
  51.9 0.5 collective-permute-start.13
  52.3 0.8 %collective-permute-done.12.refs_16_ = bf16[16,768]{1,0:T(8,128)(2,1)S(1)} collective-permute-done((bf16[16,768]{1,0:T(8,128)(2,1)S(1)}, bf16[16,768]{1,0:T(8,128)(2,1)S(1)}, u32[]{:S(2)}, u32[]{:S(2)}) %collective-permute-start.12) | collective-permute-done | bytes 24608 | tf_op jit(solution)/shard_map/ppermute | solution.py:362
  53.1 2.0 %collective-permute-done.11.refs_15_ = bf16[16,768]{1,0:T(8,128)(2,1)S(1)} collective-permute-done((bf16[16,768]{1,0:T(8,128)(2,1)S(1)}, bf16[16,768]{1,0:T(8,128)(2,1)S(1)}, u32[]{:S(2)}, u32[]{:S(2)}) %collective-permute-start.11) | collective-permute-done | bytes 24608 | tf_op jit(solution)/shard_map/ppermute | solution.py:362
  55.0 0.0 collective-permute-done.10.refs_14_
  55.0 0.0 collective-permute-done.9.refs_10_
  55.1 0.0 all-to-all-done
  55.1 0.1 collective-permute-start.14
  55.2 0.0 collective-permute-done.13.refs_11_
  55.2 1.2 %collective-permute-done.14.refs_12_ = bf16[64,768]{1,0:T(8,128)(2,1)S(1)} collective-permute-done((bf16[64,768]{1,0:T(8,128)(2,1)S(1)}, bf16[64,768]{1,0:T(8,128)(2,1)S(1)}, u32[]{:S(2)}, u32[]{:S(2)}) %collective-permute-start.14) | collective-permute-done | bytes 98336 | tf_op jit(solution)/shard_map/ppermute | solution.py:362
  56.4 0.0 copy-done.9
  56.4 0.0 copy-done.10
  56.4 1.1 %copy-done.12 = bf16[512,768]{1,0:T(8,128)(2,1)S(1)} copy-done((bf16[512,768]{1,0:T(8,128)(2,1)S(1)}, bf16[512,768]{1,0:T(8,128)(2,1)}, u32[]{:S(2)}) %copy-start.12) | copy-done | bytes 786456
  57.6 5.6 %graph.1 = (bf16[192,512]{1,0:T(8,128)(2,1)}, bf16[256,768]{1,0:T(8,128)(2,1)}) custom-call(s32[1]{0:T(128)} %bitcast.refs_0_, s32[4,6]{1,0:T(4,128)S(1)} %copy-done.9, s32[2]{0:T(128)S(1)} %copy-done.10, bf16[512,192]{1,0:T(8,128)(2,1)S(1)} %get-tuple-element.45.refs_3_, bf16[512,384]{1,0:T(8,128)(2,1)S(1)} %get-tuple-element.46.refs_4_, ...), custom_call_target="tpu_custom_call" | custom-call | flops 4000000000 | bytes 4328556 | tf_op jit(solution)/shard_map/graph/pallas_call | solution.py:62
  (5 shorter events, 0.1 us)
Async XLA Ops:
  4.7 7.5 %copy-start.2 = (bf16[256,768]{1,0:T(8,128)(2,1)S(1)}, bf16[256,768]{1,0:T(8,128)(2,1)}, u32[]{:S(2)}) copy-start(bf16[256,768]{1,0:T(8,128)(2,1)} %refs_1_.6) | copy-start | bytes 1179652
  4.7 7.5 %copy-start.4 = (bf16[192,768]{1,0:T(8,128)(2,1)S(1)}, bf16[192,768]{1,0:T(8,128)(2,1)}, u32[]{:S(2)}) copy-start(bf16[192,768]{1,0:T(8,128)(2,1)} %refs_3_.4) | copy-start | bytes 884740
  4.7 17.5 %copy-start.1 = (bf16[768,768]{1,0:T(8,128)(2,1)S(1)}, bf16[768,768]{1,0:T(8,128)(2,1)}, u32[]{:S(2)}) copy-start(bf16[768,768]{1,0:T(8,128)(2,1)} %refs_1_.7) | copy-start | bytes 3538948
  4.7 17.4 %copy-start.5 = (f32[2,768]{1,0:T(2,128)S(1)}, f32[2,768]{1,0:T(2,128)}, u32[]{:S(2)}) copy-start(f32[2,768]{1,0:T(2,128)} %refs_1_.8) | copy-start | bytes 18436
  4.8 50.3 %all-to-all-start = ((bf16[8,256,384]{2,1,0:T(8,128)(2,1)}), bf16[8,256,384]{2,1,0:T(8,128)(2,1)}, u32[]{:S(2)}, u32[]{:S(2)}) async-start(bf16[8,256,384]{2,1,0:T(8,128)(2,1)} %bitcast.14), calls=%async_computation | async-start | bytes 3145728 | tf_op jit(solution)/shard_map/all_to_all | solution.py:395
  12.1 10.0 %copy-start = (bf16[768,768]{1,0:T(8,128)(2,1)S(1)}, bf16[768,768]{1,0:T(8,128)(2,1)}, u32[]{:S(2)}) copy-start(bf16[768,768]{1,0:T(8,128)(2,1)} %refs_0_.2) | copy-start | bytes 3538948
  12.2 1.3 %copy-start.3 = (bf16[3,768,192]{1,2,0:T(8,128)(2,1)S(1)}, bf16[3,768,192]{1,2,0:T(8,128)(2,1)}, u32[]{:S(2)}) copy-start(bf16[3,768,192]{1,2,0:T(8,128)(2,1)} %param.13) | copy-start | bytes 2654212
  15.2 1.5 %collective-permute-start = (bf16[144,768]{1,0:T(8,128)(2,1)S(1)}, bf16[144,768]{1,0:T(8,128)(2,1)S(1)}, u32[]{:S(2)}, u32[]{:S(2)}) collective-permute-start(bf16[144,768]{1,0:T(8,128)(2,1)S(1)} %get-tuple-element.33), channel_id=1, source_target_pairs={{0,1},{1,0},{2,3},{3,2},{4,5},{5,4},{6,7},{7,6},{8,9},{9,8},{10,11... | collective-permute-start | bytes 663560 | tf_op jit(solution)/shard_map/ppermute | solution.py:362
  16.8 5.4 %collective-permute-start.1 = (bf16[80,768]{1,0:T(8,128)(2,1)S(1)}, bf16[80,768]{1,0:T(8,128)(2,1)S(1)}, u32[]{:S(2)}, u32[]{:S(2)}) collective-permute-start(bf16[80,768]{1,0:T(8,128)(2,1)S(1)} %get-tuple-element.35), channel_id=1, source_target_pairs={{0,2},{1,3},{2,0},{3,1},{4,6},{5,7},{6,4},{7,5},{8,10},{9,11},{10,... | collective-permute-start | bytes 368648 | tf_op jit(solution)/shard_map/ppermute | solution.py:362
  22.9 7.4 %copy-start.8 = (s32[512,16]{0,1:T(8,128)S(1)}, s32[512,16]{0,1:T(8,128)}, u32[]{:S(2)}) copy-start(s32[512,16]{0,1:T(8,128)} %param.23) | copy-start | bytes 98308
  22.9 4.9 %collective-permute-start.2 = (bf16[80,768]{1,0:T(8,128)(2,1)S(1)}, bf16[80,768]{1,0:T(8,128)(2,1)S(1)}, u32[]{:S(2)}, u32[]{:S(2)}) collective-permute-start(bf16[80,768]{1,0:T(8,128)(2,1)S(1)} %get-tuple-element.38.refs_5_.refs_0_), channel_id=1, source_target_pairs={{0,2},{1,3},{2,0},{3,1},{4,6},{5,7},{6,4},{7,5},{8,10},{9,11},{10,... | collective-permute-start | bytes 368648 | tf_op jit(solution)/shard_map/ppermute | solution.py:362
  24.4 3.4 %collective-permute-start.3 = (bf16[80,768]{1,0:T(8,128)(2,1)S(1)}, bf16[80,768]{1,0:T(8,128)(2,1)S(1)}, u32[]{:S(2)}, u32[]{:S(2)}) collective-permute-start(bf16[80,768]{1,0:T(8,128)(2,1)S(1)} %get-tuple-element.38.refs_5_.refs_0_), channel_id=1, source_target_pairs={{0,1},{1,0},{2,3},{3,2},{4,5},{5,4},{6,7},{7,6},{8,9},{9,8},{10,11... | collective-permute-start | bytes 368648 | tf_op jit(solution)/shard_map/ppermute | solution.py:362
  27.8 1.3 %collective-permute-start.4 = (bf16[80,768]{1,0:T(8,128)(2,1)S(1)}, bf16[80,768]{1,0:T(8,128)(2,1)S(1)}, u32[]{:S(2)}, u32[]{:S(2)}) collective-permute-start(bf16[80,768]{1,0:T(8,128)(2,1)S(1)} %collective-permute-done.2.refs_6_), channel_id=1, source_target_pairs={{0,1},{1,0},{2,3},{3,2},{4,5},{5,4},{6,7},{7,6},{8,9},{9,8},{10,11... | collective-permute-start | bytes 368648 | tf_op jit(solution)/shard_map/ppermute | solution.py:362
  30.0 8.3 %collective-permute-start.5 = (bf16[128,768]{1,0:T(8,128)(2,1)S(1)}, bf16[128,768]{1,0:T(8,128)(2,1)S(1)}, u32[]{:S(2)}, u32[]{:S(2)}) collective-permute-start(bf16[128,768]{1,0:T(8,128)(2,1)S(1)} %get-tuple-element.40), channel_id=1, source_target_pairs={{0,1},{1,0},{2,3},{3,2},{4,5},{5,4},{6,7},{7,6},{8,9},{9,8},{10,11... | collective-permute-start | bytes 589832 | tf_op jit(solution)/shard_map/ppermute | solution.py:362
  30.3 11.9 %copy-start.6 = (bf16[3,768,192]{1,2,0:T(8,128)(2,1)S(1)}, bf16[3,768,192]{1,2,0:T(8,128)(2,1)}, u32[]{:S(2)}) copy-start(bf16[3,768,192]{1,2,0:T(8,128)(2,1)} %param.19) | copy-start | bytes 2654212
  30.3 11.9 %copy-start.7 = (bf16[512,768]{1,0:T(8,128)(2,1)S(1)}, bf16[512,768]{1,0:T(8,128)(2,1)}, u32[]{:S(2)}) copy-start(bf16[512,768]{1,0:T(8,128)(2,1)} %refs_0_.3) | copy-start | bytes 2359300
  34.5 8.5 %copy-start.11 = (bf16[512,768]{1,0:T(8,128)(2,1)}, bf16[512,768]{1,0:T(8,128)(2,1)S(1)}, u32[]{:S(2)}) copy-start(bf16[512,768]{1,0:T(8,128)(2,1)S(1)} %mask.1.refs_6_) | copy-start | bytes 2359300
  34.5 14.8 %collective-permute-start.8 = (bf16[2,768]{1,0:T(2,128)(2,1)S(1)}, bf16[2,768]{1,0:T(2,128)(2,1)S(1)}, u32[]{:S(2)}, u32[]{:S(2)}) collective-permute-start(bf16[2,768]{1,0:T(2,128)(2,1)S(1)} %get-tuple-element.42.refs_8_), channel_id=1, source_target_pairs={{0,16},{1,21},{2,26},{3,31},{4,20},{5,17},{6,30},{7,27},{8,24},{9,... | collective-permute-start | bytes 9224 | tf_op jit(solution)/shard_map/ppermute | solution.py:432
  37.5 11.9 %collective-permute-start.7 = (bf16[2,768]{1,0:T(2,128)(2,1)S(1)}, bf16[2,768]{1,0:T(2,128)(2,1)S(1)}, u32[]{:S(2)}, u32[]{:S(2)}) collective-permute-start(bf16[2,768]{1,0:T(2,128)(2,1)S(1)} %get-tuple-element.42.refs_8_), channel_id=1, source_target_pairs={{1,5},{2,10},{3,15},{5,1},{6,14},{7,11},{9,13},{10,2},{11,7},{13,9... | collective-permute-start | bytes 9224 | tf_op jit(solution)/shard_map/ppermute | solution.py:432
  38.4 18.0 %copy-start.9 = (s32[4,6]{1,0:T(4,128)S(1)}, s32[4,6]{1,0:T(4,128)}, u32[]{:S(2)}) copy-start(s32[4,6]{1,0:T(4,128)} %refs_1_.9) | copy-start | bytes 292
  38.4 18.0 %copy-start.10 = (s32[2]{0:T(128)S(1)}, s32[2]{0:T(128)}, u32[]{:S(2)}) copy-start(s32[2]{0:T(128)} %refs_2_.5) | copy-start | bytes 28
  38.4 10.9 %collective-permute-start.6 = (bf16[64,768]{1,0:T(8,128)(2,1)S(1)}, bf16[64,768]{1,0:T(8,128)(2,1)S(1)}, u32[]{:S(2)}, u32[]{:S(2)}) collective-permute-start(bf16[64,768]{1,0:T(8,128)(2,1)S(1)} %get-tuple-element.41), channel_id=1, source_target_pairs={{0,2},{1,3},{2,0},{3,1},{4,6},{5,7},{6,4},{7,5},{8,10},{9,11},{10,... | collective-permute-start | bytes 294920 | tf_op jit(solution)/shard_map/ppermute | solution.py:362
  49.6 5.5 %collective-permute-start.9 = (bf16[64,768]{1,0:T(8,128)(2,1)S(1)}, bf16[64,768]{1,0:T(8,128)(2,1)S(1)}, u32[]{:S(2)}, u32[]{:S(2)}) collective-permute-start(bf16[64,768]{1,0:T(8,128)(2,1)S(1)} %norm_two.1.refs_9_), channel_id=1, source_target_pairs={{0,2},{1,3},{2,0},{3,1},{4,6},{5,7},{6,4},{7,5},{8,10},{9,11},{10,... | collective-permute-start | bytes 294920 | tf_op jit(solution)/shard_map/ppermute | solution.py:362
  49.7 3.4 %collective-permute-start.12 = (bf16[16,768]{1,0:T(8,128)(2,1)S(1)}, bf16[16,768]{1,0:T(8,128)(2,1)S(1)}, u32[]{:S(2)}, u32[]{:S(2)}) collective-permute-start(bf16[16,768]{1,0:T(8,128)(2,1)S(1)} %pack.1.refs_13_), channel_id=1, source_target_pairs={{0,3},{1,2},{2,1},{3,0},{4,7},{5,6},{6,5},{7,4},{8,11},{9,10},{10,... | collective-permute-start | bytes 73736 | tf_op jit(solution)/shard_map/ppermute | solution.py:362
  50.6 4.4 %collective-permute-start.11 = (bf16[16,768]{1,0:T(8,128)(2,1)S(1)}, bf16[16,768]{1,0:T(8,128)(2,1)S(1)}, u32[]{:S(2)}, u32[]{:S(2)}) collective-permute-start(bf16[16,768]{1,0:T(8,128)(2,1)S(1)} %pack.1.refs_13_), channel_id=1, source_target_pairs={{0,2},{1,3},{2,0},{3,1},{4,6},{5,7},{6,4},{7,5},{8,10},{9,11},{10,... | collective-permute-start | bytes 73736 | tf_op jit(solution)/shard_map/ppermute | solution.py:362
  51.8 3.2 %collective-permute-start.10 = (bf16[16,768]{1,0:T(8,128)(2,1)S(1)}, bf16[16,768]{1,0:T(8,128)(2,1)S(1)}, u32[]{:S(2)}, u32[]{:S(2)}) collective-permute-start(bf16[16,768]{1,0:T(8,128)(2,1)S(1)} %pack.1.refs_13_), channel_id=1, source_target_pairs={{0,1},{1,0},{2,3},{3,2},{4,5},{5,4},{6,7},{7,6},{8,9},{9,8},{10,11... | collective-permute-start | bytes 73736 | tf_op jit(solution)/shard_map/ppermute | solution.py:362
  51.9 3.3 %collective-permute-start.13 = (bf16[64,768]{1,0:T(8,128)(2,1)S(1)}, bf16[64,768]{1,0:T(8,128)(2,1)S(1)}, u32[]{:S(2)}, u32[]{:S(2)}) collective-permute-start(bf16[64,768]{1,0:T(8,128)(2,1)S(1)} %norm_two.1.refs_9_), channel_id=1, source_target_pairs={{0,1},{1,0},{2,3},{3,2},{4,5},{5,4},{6,7},{7,6},{8,9},{9,8},{10,11... | collective-permute-start | bytes 294920 | tf_op jit(solution)/shard_map/ppermute | solution.py:362
  55.1 1.4 %collective-permute-start.14 = (bf16[64,768]{1,0:T(8,128)(2,1)S(1)}, bf16[64,768]{1,0:T(8,128)(2,1)S(1)}, u32[]{:S(2)}, u32[]{:S(2)}) collective-permute-start(bf16[64,768]{1,0:T(8,128)(2,1)S(1)} %collective-permute-done.9.refs_10_), channel_id=1, source_target_pairs={{0,1},{1,0},{2,3},{3,2},{4,5},{5,4},{6,7},{7,6},{8,9},{9,8},{10,11... | collective-permute-start | bytes 294920 | tf_op jit(solution)/shard_map/ppermute | solution.py:362
  56.4 1.1 %copy-start.12 = (bf16[512,768]{1,0:T(8,128)(2,1)S(1)}, bf16[512,768]{1,0:T(8,128)(2,1)}, u32[]{:S(2)}) copy-start(bf16[512,768]{1,0:T(8,128)(2,1)} %copy-done.11) | copy-start | bytes 2359300

commit v13 on v11

--- a/solution.py
+++ b/solution.py
@@ -277,7 +277,7 @@
         rows = ref[...].astype(f32)
         for turn in range(firsts.shape[0] // per_part // members):
             for title in range(per_part):
-                place = (turn * members + (who_ref[0] ^ step)) * per_part + title
+                place = (turn * members + lax.rem(who_ref[0] ^ step, members)) * per_part + title
                 at = turn * per_part + title
                 firsts[pl.ds(place, 1), :] = rows[at : at + 1]
     firsts[0:per_part, :] = first_ref[...].astype(f32)
@@ -408,10 +408,14 @@
     )
     keep, give = halves(kept, swap(given, 1), PAD)
     part = swap(give, 2)
-    mask = call(
-        mask_kernel, shape((nodes, TPR * TILE), bf), (nbr_slots.T,), flops=4 * 10**9, name="mask"
-    )
-    part, mask = lax.optimization_barrier((part, mask))
+    kv, q = call(
+        own_kernel,
+        (shape((nodes, 2 * cols), bf), shape((nodes, cols), bf)),
+        (node_table, w_graph),
+        flops=2 * 10**9,
+        name="own",
+    )
+    part, kv, q = lax.optimization_barrier((part, kv, q))
     hidden, first_hidden, first_terms = call(
         norm_one_kernel,
         (shape((chunk + PAD, width), bf), shape((PAD, width), bf), shape((PAD, width), f32)),
@@ -431,36 +435,36 @@
         flops=4 * tok_rows * width * w_ffn_in.shape[1],
         name="ffn",
     )
-    turns = dp // mp
+    pair = 2
+    turns = dp // pair
     firsts = [
         lax.ppermute(
             first,
             ("dp", "mp"),
             [
-                (p * mp + m, (p ^ (turn * mp + m)) * mp + m)
+                (p * mp + m, (p ^ (turn * pair + m % pair)) * mp + m)
                 for p in range(dp)
                 for m in range(mp)
-                if turn or m
+                if turn or m % pair
             ],
         )
         for turn in range(turns)
     ]
     keep, give = halves(kept, swap(given, 1), 0)
+    give, slots = lax.optimization_barrier((give, nbr_slots))
     part = swap(give, 2)
-    kv, q = call(
-        own_kernel,
-        (shape((nodes, 2 * cols), bf), shape((nodes, cols), bf)),
-        (node_table, w_graph),
-        flops=2 * 10**9,
-        name="own",
-    )
-    part, firsts, kv, q = lax.optimization_barrier((part, firsts, kv, q))
+    mask = call(
+        mask_kernel, shape((nodes, TPR * TILE), bf), (slots.T,), flops=4 * 10**9, name="mask"
+    )
+    part, mask = lax.optimization_barrier((part, mask))
     done = call(
         norm_two_kernel, shape((chunk, width), bf), (hidden, gains, keep, part), name="norm_two"
     )
+    across = swap(done, 2)
+    across, firsts = lax.optimization_barrier((across, firsts))
     pack = call(pack_kernel, shape((tail_rows(turns * per_part), width), bf), firsts, name="pack")
-    packs = [pack] + [swap(pack, step) for step in range(1, mp)]
-    _, dones = gather(done)
+    packs = [pack, swap(pack, 1)]
+    dones = [done, across, swap(done, 1), swap(across, 1)]
     keys = nodes + dp * fetch
     graph_out, encoded = call(
         functools.partial(graph_kernel, whose),

time: 65.4 us -> 57.9 us (0.89)
  waiting for transfers between devices: 24.6 us -> 15.4 us
  starting transfers between devices: 18.6 us -> 21 us
  local copies, waits for them, and re-layouts: 3.71 us -> 3.01 us
    ppermute x2 -> x4, waiting for transfers between devices: 10.6 us -> 4.13 us  [local(): lax.ppermute(first, ('dp', 'mp'), [(p * mp + m, (p ^ turn * pair + m % pa...]
    ppermute x13 -> x11, waiting for transfers between devices: 14 us -> 11.3 us  [swap(): lax.ppermute(value, axis, [(i, i ^ step) for i in range(lax.axis_size(axi...]
    ppermute x2 -> x4, starting transfers between devices: 3.73 us -> 5.22 us  [local(): lax.ppermute(first, ('dp', 'mp'), [(p * mp + m, (p ^ turn * pair + m % pa...]
    ppermute x13 -> x11, starting transfers between devices: 7.48 us -> 8.34 us  [swap(): lax.ppermute(value, axis, [(i, i ^ step) for i in range(lax.axis_size(axi...]
    unnamed x30 -> x32, local copies, waits for them, and re-layouts: 3.71 us -> 3.01 us
  transfers between devices with their start and end apart: 16 -> 16, of which waited for: 7 -> 8; matrix products, arithmetic and copies ran while one was open for 0% -> 0% of each run, Pallas kernels for 13% -> 15%
where the time goes in v13:
time: 57.9 us; the launch traced here: 57.6 us
  starting transfers between devices  21 us (36%)
  Pallas kernels  17.4 us (30%)
  waiting for transfers between devices  15.4 us (27%)
  local copies, waits for them, and re-layouts  3.01 us (5%)
  between operations  0.87 us (2%)
    pallas_call x11, Pallas kernels, call(): pl.pallas_call(body, out_shape=outs, in_specs=specs, out_specs=jax.tree.m...  17.4 us
    ppermute x11, waiting for transfers between devices, swap(): lax.ppermute(value, axis, [(i, i ^ step) for i in range(lax.axis_size(axi...  11.3 us
    ppermute x11, starting transfers between devices, swap(): lax.ppermute(value, axis, [(i, i ^ step) for i in range(lax.axis_size(axi...  8.34 us
    all_to_all x1, starting transfers between devices, local(): lax.all_to_all(sent.reshape(dp, fetch, 2 * cols), 'dp', split_axis=0, con...  7.4 us
    ppermute x4, starting transfers between devices, local(): lax.ppermute(first, ('dp', 'mp'), [(p * mp + m, (p ^ turn * pair + m % pa...  5.22 us
    ppermute x4, waiting for transfers between devices, local(): lax.ppermute(first, ('dp', 'mp'), [(p * mp + m, (p ^ turn * pair + m % pa...  4.13 us
    unnamed x32, local copies, waits for them, and re-layouts  3.01 us
  transfers between devices with their start and end apart: 16, of which 8 were waited for; matrix products, arithmetic and copies ran while one was open for 0% of the time, Pallas kernels for 15%

profile of v13, /device:TPU:0, one launch (start us, length us, event | category | flops | bytes accessed | tf_op | source)
XLA Modules:
  0.0 57.6 jit_solution(5939175961171914649)
XLA Ops:
  0.6 4.1 %send.1 = bf16[2048,384]{1,0:T(8,128)(2,1)} custom-call(s32[1]{0:T(128)} %bitcast.1.refs_0_, s32[2]{0:T(128)} %refs_2_.5, s32[8,256]{1,0:T(8,128)} %bitcast.16, bf16[512,768]{1,0:T(8,128)(2,1)} %refs_0_.2, bf16[3,192,768]{2,1,0:T(8,128)(2,1)} %bitcast.11), custom_call_target="tpu_custom_call" | custom-call | flops 1107296256 | bytes 1679372 | tf_op jit(solution)/shard_map/send/pallas_call | solution.py:62
  4.7 0.0 copy-start.2
  4.7 0.0 copy-start.3
  4.7 0.0 copy-start.4
  4.7 7.4 %all-to-all-start = ((bf16[8,256,384]{2,1,0:T(8,128)(2,1)}), bf16[8,256,384]{2,1,0:T(8,128)(2,1)S(1)}, u32[]{:S(2)}, u32[]{:S(2)}) async-start(bf16[8,256,384]{2,1,0:T(8,128)(2,1)} %bitcast.15), calls=%async_computation | async-start | bytes 3145728 | tf_op jit(solution)/shard_map/all_to_all | solution.py:395
  12.1 0.0 copy-start.8
  12.2 0.0 copy-done.2
  12.2 0.0 copy-done.3
  12.2 0.0 copy-done.4
  12.2 1.7 %attn.1 = (f32[144,768]{1,0:T(8,128)S(1)}, bf16[144,768]{1,0:T(8,128)(2,1)S(1)}) custom-call(s32[1]{0:T(128)} %bitcast.refs_0_, bf16[256,768]{1,0:T(8,128)(2,1)S(1)} %copy-done.2, bf16[3,192,768]{2,1,0:T(8,128)(2,1)S(1)} %bitcast.10, bf16[192,768]{1,0:T(8,128)(2,1)S(1)} %copy-done.4), custom_call_target="tpu_custom_call" | custom-call | flops 301989888 | bytes 1572868 | tf_op jit(solution)/shard_map/attn/pallas_call | solution.py:62
  13.9 0.1 collective-permute-start
  14.0 1.5 %collective-permute-done.refs_1_ = bf16[144,768]{1,0:T(8,128)(2,1)S(1)} collective-permute-done((bf16[144,768]{1,0:T(8,128)(2,1)S(1)}, bf16[144,768]{1,0:T(8,128)(2,1)S(1)}, u32[]{:S(2)}, u32[]{:S(2)}) %collective-permute-start) | collective-permute-done | bytes 221216 | tf_op jit(solution)/shard_map/ppermute | solution.py:362
  15.5 0.0 copy-start
  15.5 0.0 copy-start.1
  15.5 0.0 copy-start.5
  15.5 1.6 %collective-permute-start.1 = (bf16[80,768]{1,0:T(8,128)(2,1)S(1)}, bf16[80,768]{1,0:T(8,128)(2,1)S(1)}, u32[]{:S(2)}, u32[]{:S(2)}) collective-permute-start(bf16[80,768]{1,0:T(8,128)(2,1)S(1)} %get-tuple-element.34), channel_id=1, source_target_pairs={{0,2},{1,3},{2,0},{3,1},{4,6},{5,7},{6,4},{7,5},{8,10},{9,11},{10,... | collective-permute-start | bytes 368648 | tf_op jit(solution)/shard_map/ppermute | solution.py:362
  17.1 0.0 copy-done.6
  17.1 0.0 copy-done.8
  17.1 0.9 %own.1 = (bf16[512,384]{1,0:T(8,128)(2,1)S(1)}, bf16[512,192]{1,0:T(8,128)(2,1)S(1)}) custom-call(bf16[512,768]{1,0:T(8,128)(2,1)S(1)} %copy-done.8, bf16[3,192,768]{2,1,0:T(8,128)(2,1)S(1)} %bitcast.12), custom_call_target="tpu_custom_call" | custom-call | flops 2000000000 | bytes 1671168 | tf_op jit(solution)/shard_map/own/pallas_call | solution.py:62
  18.0 0.0 copy-start.12
  18.0 3.0 %collective-permute-done.1.refs_6_ = bf16[80,768]{1,0:T(8,128)(2,1)S(1)} collective-permute-done((bf16[80,768]{1,0:T(8,128)(2,1)S(1)}, bf16[80,768]{1,0:T(8,128)(2,1)S(1)}, u32[]{:S(2)}, u32[]{:S(2)}) %collective-permute-start.1) | collective-permute-done | bytes 122912 | tf_op jit(solution)/shard_map/ppermute | solution.py:362
  21.0 0.0 copy-done
  21.0 0.0 copy-done.1
  21.0 0.0 copy-done.5
  21.0 0.7 %norm_one.1 = (bf16[80,768]{1,0:T(8,128)(2,1)S(1)}, bf16[16,768]{1,0:T(8,128)(2,1)S(1)}, f32[16,768]{1,0:T(8,128)S(1)}) custom-call(s32[1]{0:T(128)} %bitcast.refs_0_, bf16[256,768]{1,0:T(8,128)(2,1)S(1)} %copy-done.2, f32[2,768]{1,0:T(2,128)S(1)} %copy-done.5, bf16[768,768]{1,0:T(8,128)(2,1)S(1)} %copy-done, bf16[768,768]{1,0:T(8,128)(2,1)S(1)} %copy-done.1, ...), custom_call_target="tpu_custom_call" | custom-call | bytes 3127300 | tf_op jit(solution)/shard_map/norm_one/pallas_call | solution.py:62
  21.7 1.5 %collective-permute-start.2 = (bf16[80,768]{1,0:T(8,128)(2,1)S(1)}, bf16[80,768]{1,0:T(8,128)(2,1)S(1)}, u32[]{:S(2)}, u32[]{:S(2)}) collective-permute-start(bf16[80,768]{1,0:T(8,128)(2,1)S(1)} %get-tuple-element.43.refs_5_.refs_0_), channel_id=1, source_target_pairs={{0,2},{1,3},{2,0},{3,1},{4,6},{5,7},{6,4},{7,5},{8,10},{9,11},{10,... | collective-permute-start | bytes 368648 | tf_op jit(solution)/shard_map/ppermute | solution.py:362
  23.2 0.0 collective-permute-start.3
  23.2 3.4 %collective-permute-done.2.refs_6_ = bf16[80,768]{1,0:T(8,128)(2,1)S(1)} collective-permute-done((bf16[80,768]{1,0:T(8,128)(2,1)S(1)}, bf16[80,768]{1,0:T(8,128)(2,1)S(1)}, u32[]{:S(2)}, u32[]{:S(2)}) %collective-permute-start.2) | collective-permute-done | bytes 122912 | tf_op jit(solution)/shard_map/ppermute | solution.py:362
  26.6 0.0 collective-permute-start.4
  26.6 0.0 collective-permute-done.3.refs_7_
  26.6 1.3 %collective-permute-done.4.refs_8_ = bf16[80,768]{1,0:T(8,128)(2,1)S(1)} collective-permute-done((bf16[80,768]{1,0:T(8,128)(2,1)S(1)}, bf16[80,768]{1,0:T(8,128)(2,1)S(1)}, u32[]{:S(2)}, u32[]{:S(2)}) %collective-permute-start.4) | collective-permute-done | bytes 122912 | tf_op jit(solution)/shard_map/ppermute | solution.py:362
  27.9 0.0 copy-done.12
  27.9 0.9 %ffn.1 = (f32[128,768]{1,0:T(8,128)S(1)}, bf16[128,768]{1,0:T(8,128)(2,1)S(1)}, bf16[2,768]{1,0:T(2,128)(2,1)S(1)}) custom-call(bf16[768,768]{1,0:T(8,128)(2,1)S(1)} %copy-done, bf16[768,768]{1,0:T(8,128)(2,1)S(1)} %copy-done.1, f32[2,768]{1,0:T(2,128)S(1)} %copy-done.5, bf16[16,768]{1,0:T(8,128)(2,1)S(1)} %get-tuple-element.41.refs_3_, ...), custom_call_target="tpu_custom_call" | custom-call | flops 603979776 | bytes 2930688 | tf_op jit(solution)/shard_map/ffn/pallas_call | solution.py:62
  28.8 0.2 collective-permute-start.5
  29.0 1.3 %collective-permute-done.5.refs_1_ = bf16[128,768]{1,0:T(8,128)(2,1)S(1)} collective-permute-done((bf16[128,768]{1,0:T(8,128)(2,1)S(1)}, bf16[128,768]{1,0:T(8,128)(2,1)S(1)}, u32[]{:S(2)}, u32[]{:S(2)}) %collective-permute-start.5) | collective-permute-done | bytes 196640 | tf_op jit(solution)/shard_map/ppermute | solution.py:362
  30.3 0.1 half.3
  30.4 1.6 %collective-permute-start.6 = (bf16[64,768]{1,0:T(8,128)(2,1)S(1)}, bf16[64,768]{1,0:T(8,128)(2,1)S(1)}, u32[]{:S(2)}, u32[]{:S(2)}) collective-permute-start(bf16[64,768]{1,0:T(8,128)(2,1)S(1)} %get-tuple-element.47), channel_id=1, source_target_pairs={{0,2},{1,3},{2,0},{3,1},{4,6},{5,7},{6,4},{7,5},{8,10},{9,11},{10,... | collective-permute-start | bytes 294920 | tf_op jit(solution)/shard_map/ppermute | solution.py:362
  32.0 0.0 copy-done.9
  32.0 4.2 %mask.1.refs_6_ = bf16[512,768]{1,0:T(8,128)(2,1)S(1)} custom-call(s32[16,512]{1,0:T(8,128)S(1)} %bitcast.14), custom_call_target="tpu_custom_call" | custom-call | flops 4000000000 | bytes 32768 | tf_op jit(solution)/shard_map/mask/pallas_call | solution.py:62
  36.2 0.0 copy-start.14
  36.2 0.9 %copy-done.14 = bf16[512,768]{1,0:T(8,128)(2,1)} copy-done((bf16[512,768]{1,0:T(8,128)(2,1)}, bf16[512,768]{1,0:T(8,128)(2,1)S(1)}, u32[]{:S(2)}) %copy-start.14) | copy-done | bytes 786456
  37.1 0.0 collective-permute-done.6.refs_3_
  37.1 0.2 norm_two.1.refs_9_
  37.3 0.6 collective-permute-start.7
  37.9 3.8 %collective-permute-start.11 = (bf16[2,768]{1,0:T(2,128)(2,1)S(1)}, bf16[2,768]{1,0:T(2,128)(2,1)S(1)}, u32[]{:S(2)}, u32[]{:S(2)}) collective-permute-start(bf16[2,768]{1,0:T(2,128)(2,1)S(1)} %get-tuple-element.50.refs_8_), channel_id=1, source_target_pairs={{0,24},{1,29},{2,26},{3,31},{4,28},{5,25},{6,30},{7,27},{8,16},{9,... | collective-permute-start | bytes 9224 | tf_op jit(solution)/shard_map/ppermute | solution.py:441
  41.7 0.0 collective-permute-start.10
  41.7 0.6 %collective-permute-start.9 = (bf16[2,768]{1,0:T(2,128)(2,1)S(1)}, bf16[2,768]{1,0:T(2,128)(2,1)S(1)}, u32[]{:S(2)}, u32[]{:S(2)}) collective-permute-start(bf16[2,768]{1,0:T(2,128)(2,1)S(1)} %get-tuple-element.50.refs_8_), channel_id=1, source_target_pairs={{0,8},{1,13},{2,10},{3,15},{4,12},{5,9},{6,14},{7,11},{8,0},{9,5},... | collective-permute-start | bytes 9224 | tf_op jit(solution)/shard_map/ppermute | solution.py:441
  42.3 0.8 %collective-permute-start.8 = (bf16[2,768]{1,0:T(2,128)(2,1)S(1)}, bf16[2,768]{1,0:T(2,128)(2,1)S(1)}, u32[]{:S(2)}, u32[]{:S(2)}) collective-permute-start(bf16[2,768]{1,0:T(2,128)(2,1)S(1)} %get-tuple-element.50.refs_8_), channel_id=1, source_target_pairs={{1,5},{3,7},{5,1},{7,3},{9,13},{11,15},{13,9},{15,11},{17,21},{19,... | collective-permute-start | bytes 9224 | tf_op jit(solution)/shard_map/ppermute | solution.py:441
  43.1 0.3 collective-permute-done.11.refs_3_
  43.4 2.2 %collective-permute-start.12 = (bf16[64,768]{1,0:T(8,128)(2,1)S(1)}, bf16[64,768]{1,0:T(8,128)(2,1)S(1)}, u32[]{:S(2)}, u32[]{:S(2)}) collective-permute-start(bf16[64,768]{1,0:T(8,128)(2,1)S(1)} %norm_two.1.refs_9_), channel_id=1, source_target_pairs={{0,1},{1,0},{2,3},{3,2},{4,5},{5,4},{6,7},{7,6},{8,9},{9,8},{10,11... | collective-permute-start | bytes 294920 | tf_op jit(solution)/shard_map/ppermute | solution.py:362
  45.5 3.9 %collective-permute-done.10.refs_2_ = bf16[2,768]{1,0:T(2,128)(2,1)S(1)} collective-permute-done((bf16[2,768]{1,0:T(2,128)(2,1)S(1)}, bf16[2,768]{1,0:T(2,128)(2,1)S(1)}, u32[]{:S(2)}, u32[]{:S(2)}) %collective-permute-start.10) | collective-permute-done | bytes 3104 | tf_op jit(solution)/shard_map/ppermute | solution.py:441
  49.4 0.0 collective-permute-done.9.refs_1_
  49.4 0.0 collective-permute-done.8.refs_0_
  49.4 0.0 collective-permute-done.7.refs_10_
  49.4 0.1 collective-permute-start.13
  49.5 0.6 collective-permute-start.14
  50.1 0.0 collective-permute-done.12.refs_11_
  50.1 0.8 %collective-permute-done.14.refs_14_ = bf16[16,768]{1,0:T(8,128)(2,1)S(1)} collective-permute-done((bf16[16,768]{1,0:T(8,128)(2,1)S(1)}, bf16[16,768]{1,0:T(8,128)(2,1)S(1)}, u32[]{:S(2)}, u32[]{:S(2)}) %collective-permute-start.14) | collective-permute-done | bytes 24608 | tf_op jit(solution)/shard_map/ppermute | solution.py:362
  50.9 0.0 collective-permute-done.13.refs_12_
  50.9 0.0 all-to-all-done
  51.0 0.0 copy-start.13
  51.0 0.9 %copy-done.13 = bf16[512,192]{1,0:T(8,128)(2,1)S(1)} copy-done((bf16[512,192]{1,0:T(8,128)(2,1)S(1)}, bf16[512,192]{1,0:T(8,128)(2,1)}, u32[]{:S(2)}) %copy-start.13) | copy-done | bytes 196632
  51.9 1.1 %copy-done.15 = bf16[512,768]{1,0:T(8,128)(2,1)S(1)} copy-done((bf16[512,768]{1,0:T(8,128)(2,1)S(1)}, bf16[512,768]{1,0:T(8,128)(2,1)}, u32[]{:S(2)}) %copy-start.15) | copy-done | bytes 786456
  53.1 4.5 %graph.1 = (bf16[192,512]{1,0:T(8,128)(2,1)}, bf16[256,768]{1,0:T(8,128)(2,1)}) custom-call(s32[1]{0:T(128)} %bitcast.refs_0_, s32[4,6]{1,0:T(4,128)S(1)} %copy-done.10, s32[2]{0:T(128)S(1)} %copy-done.11, bf16[512,192]{1,0:T(8,128)(2,1)S(1)} %copy-done.13, bf16[512,384]{1,0:T(8,128)(2,1)S(1)} %get-tuple-element.38.refs_4_, ...), custom_call_target="tpu_custom_call" | custom-call | flops 4000000000 | bytes 4279404 | tf_op jit(solution)/shard_map/graph/pallas_call | solution.py:62
  (11 shorter events, 0.1 us)
Async XLA Ops:
  4.7 7.5 %copy-start.2 = (bf16[256,768]{1,0:T(8,128)(2,1)S(1)}, bf16[256,768]{1,0:T(8,128)(2,1)}, u32[]{:S(2)}) copy-start(bf16[256,768]{1,0:T(8,128)(2,1)} %refs_1_.6) | copy-start | bytes 1179652
  4.7 7.4 %copy-start.3 = (bf16[3,768,192]{1,2,0:T(8,128)(2,1)S(1)}, bf16[3,768,192]{1,2,0:T(8,128)(2,1)}, u32[]{:S(2)}) copy-start(bf16[3,768,192]{1,2,0:T(8,128)(2,1)} %param.13) | copy-start | bytes 2654212
  4.7 7.4 %copy-start.4 = (bf16[192,768]{1,0:T(8,128)(2,1)S(1)}, bf16[192,768]{1,0:T(8,128)(2,1)}, u32[]{:S(2)}) copy-start(bf16[192,768]{1,0:T(8,128)(2,1)} %refs_3_.4) | copy-start | bytes 884740
  4.7 46.2 %all-to-all-start = ((bf16[8,256,384]{2,1,0:T(8,128)(2,1)}), bf16[8,256,384]{2,1,0:T(8,128)(2,1)S(1)}, u32[]{:S(2)}, u32[]{:S(2)}) async-start(bf16[8,256,384]{2,1,0:T(8,128)(2,1)} %bitcast.15), calls=%async_computation | async-start | bytes 3145728 | tf_op jit(solution)/shard_map/all_to_all | solution.py:395
  12.1 5.0 %copy-start.6 = (bf16[3,768,192]{1,2,0:T(8,128)(2,1)S(1)}, bf16[3,768,192]{1,2,0:T(8,128)(2,1)}, u32[]{:S(2)}) copy-start(bf16[3,768,192]{1,2,0:T(8,128)(2,1)} %param.19) | copy-start | bytes 2654212
  12.1 5.0 %copy-start.8 = (bf16[512,768]{1,0:T(8,128)(2,1)S(1)}, bf16[512,768]{1,0:T(8,128)(2,1)}, u32[]{:S(2)}) copy-start(bf16[512,768]{1,0:T(8,128)(2,1)} %refs_0_.2) | copy-start | bytes 2359300
  13.9 1.5 %collective-permute-start = (bf16[144,768]{1,0:T(8,128)(2,1)S(1)}, bf16[144,768]{1,0:T(8,128)(2,1)S(1)}, u32[]{:S(2)}, u32[]{:S(2)}) collective-permute-start(bf16[144,768]{1,0:T(8,128)(2,1)S(1)} %get-tuple-element.33), channel_id=1, source_target_pairs={{0,1},{1,0},{2,3},{3,2},{4,5},{5,4},{6,7},{7,6},{8,9},{9,8},{10,11... | collective-permute-start | bytes 663560 | tf_op jit(solution)/shard_map/ppermute | solution.py:362
  15.5 5.5 %copy-start = (bf16[768,768]{1,0:T(8,128)(2,1)S(1)}, bf16[768,768]{1,0:T(8,128)(2,1)}, u32[]{:S(2)}) copy-start(bf16[768,768]{1,0:T(8,128)(2,1)} %refs_0_.3) | copy-start | bytes 3538948
  15.5 5.5 %copy-start.1 = (bf16[768,768]{1,0:T(8,128)(2,1)S(1)}, bf16[768,768]{1,0:T(8,128)(2,1)}, u32[]{:S(2)}) copy-start(bf16[768,768]{1,0:T(8,128)(2,1)} %refs_1_.7) | copy-start | bytes 3538948
  15.5 5.4 %copy-start.5 = (f32[2,768]{1,0:T(2,128)S(1)}, f32[2,768]{1,0:T(2,128)}, u32[]{:S(2)}) copy-start(f32[2,768]{1,0:T(2,128)} %refs_1_.8) | copy-start | bytes 18436
  15.5 5.4 %collective-permute-start.1 = (bf16[80,768]{1,0:T(8,128)(2,1)S(1)}, bf16[80,768]{1,0:T(8,128)(2,1)S(1)}, u32[]{:S(2)}, u32[]{:S(2)}) collective-permute-start(bf16[80,768]{1,0:T(8,128)(2,1)S(1)} %get-tuple-element.34), channel_id=1, source_target_pairs={{0,2},{1,3},{2,0},{3,1},{4,6},{5,7},{6,4},{7,5},{8,10},{9,11},{10,... | collective-permute-start | bytes 368648 | tf_op jit(solution)/shard_map/ppermute | solution.py:362
  18.0 9.9 %copy-start.12 = (bf16[512,192]{1,0:T(8,128)(2,1)}, bf16[512,192]{1,0:T(8,128)(2,1)S(1)}, u32[]{:S(2)}) copy-start(bf16[512,192]{1,0:T(8,128)(2,1)S(1)} %get-tuple-element.37.refs_3_) | copy-start | bytes 589828
  21.7 4.9 %collective-permute-start.2 = (bf16[80,768]{1,0:T(8,128)(2,1)S(1)}, bf16[80,768]{1,0:T(8,128)(2,1)S(1)}, u32[]{:S(2)}, u32[]{:S(2)}) collective-permute-start(bf16[80,768]{1,0:T(8,128)(2,1)S(1)} %get-tuple-element.43.refs_5_.refs_0_), channel_id=1, source_target_pairs={{0,2},{1,3},{2,0},{3,1},{4,6},{5,7},{6,4},{7,5},{8,10},{9,11},{10,... | collective-permute-start | bytes 368648 | tf_op jit(solution)/shard_map/ppermute | solution.py:362
  23.2 3.4 %collective-permute-start.3 = (bf16[80,768]{1,0:T(8,128)(2,1)S(1)}, bf16[80,768]{1,0:T(8,128)(2,1)S(1)}, u32[]{:S(2)}, u32[]{:S(2)}) collective-permute-start(bf16[80,768]{1,0:T(8,128)(2,1)S(1)} %get-tuple-element.43.refs_5_.refs_0_), channel_id=1, source_target_pairs={{0,1},{1,0},{2,3},{3,2},{4,5},{5,4},{6,7},{7,6},{8,9},{9,8},{10,11... | collective-permute-start | bytes 368648 | tf_op jit(solution)/shard_map/ppermute | solution.py:362
  26.6 1.3 %collective-permute-start.4 = (bf16[80,768]{1,0:T(8,128)(2,1)S(1)}, bf16[80,768]{1,0:T(8,128)(2,1)S(1)}, u32[]{:S(2)}, u32[]{:S(2)}) collective-permute-start(bf16[80,768]{1,0:T(8,128)(2,1)S(1)} %collective-permute-done.2.refs_6_), channel_id=1, source_target_pairs={{0,1},{1,0},{2,3},{3,2},{4,5},{5,4},{6,7},{7,6},{8,9},{9,8},{10,11... | collective-permute-start | bytes 368648 | tf_op jit(solution)/shard_map/ppermute | solution.py:362
  27.9 4.1 %copy-start.9 = (s32[512,16]{0,1:T(8,128)S(1)}, s32[512,16]{0,1:T(8,128)}, u32[]{:S(2)}) copy-start(s32[512,16]{0,1:T(8,128)} %param.23) | copy-start | bytes 98308
  28.8 1.5 %collective-permute-start.5 = (bf16[128,768]{1,0:T(8,128)(2,1)S(1)}, bf16[128,768]{1,0:T(8,128)(2,1)S(1)}, u32[]{:S(2)}, u32[]{:S(2)}) collective-permute-start(bf16[128,768]{1,0:T(8,128)(2,1)S(1)} %get-tuple-element.45), channel_id=1, source_target_pairs={{0,1},{1,0},{2,3},{3,2},{4,5},{5,4},{6,7},{7,6},{8,9},{9,8},{10,11... | collective-permute-start | bytes 589832 | tf_op jit(solution)/shard_map/ppermute | solution.py:362
  30.4 6.7 %collective-permute-start.6 = (bf16[64,768]{1,0:T(8,128)(2,1)S(1)}, bf16[64,768]{1,0:T(8,128)(2,1)S(1)}, u32[]{:S(2)}, u32[]{:S(2)}) collective-permute-start(bf16[64,768]{1,0:T(8,128)(2,1)S(1)} %get-tuple-element.47), channel_id=1, source_target_pairs={{0,2},{1,3},{2,0},{3,1},{4,6},{5,7},{6,4},{7,5},{8,10},{9,11},{10,... | collective-permute-start | bytes 294920 | tf_op jit(solution)/shard_map/ppermute | solution.py:362
  32.0 19.0 %copy-start.7 = (bf16[3,768,192]{1,2,0:T(8,128)(2,1)S(1)}, bf16[3,768,192]{1,2,0:T(8,128)(2,1)}, u32[]{:S(2)}) copy-start(bf16[3,768,192]{1,2,0:T(8,128)(2,1)} %param.19) | copy-start | bytes 2654212
  32.0 19.0 %copy-start.10 = (s32[4,6]{1,0:T(4,128)S(1)}, s32[4,6]{1,0:T(4,128)}, u32[]{:S(2)}) copy-start(s32[4,6]{1,0:T(4,128)} %refs_1_.9) | copy-start | bytes 292
  32.0 19.0 %copy-start.11 = (s32[2]{0:T(128)S(1)}, s32[2]{0:T(128)}, u32[]{:S(2)}) copy-start(s32[2]{0:T(128)} %refs_2_.5) | copy-start | bytes 28
  36.2 0.9 %copy-start.14 = (bf16[512,768]{1,0:T(8,128)(2,1)}, bf16[512,768]{1,0:T(8,128)(2,1)S(1)}, u32[]{:S(2)}) copy-start(bf16[512,768]{1,0:T(8,128)(2,1)S(1)} %mask.1.refs_6_) | copy-start | bytes 2359300
  37.3 12.1 %collective-permute-start.7 = (bf16[64,768]{1,0:T(8,128)(2,1)S(1)}, bf16[64,768]{1,0:T(8,128)(2,1)S(1)}, u32[]{:S(2)}, u32[]{:S(2)}) collective-permute-start(bf16[64,768]{1,0:T(8,128)(2,1)S(1)} %norm_two.1.refs_9_), channel_id=1, source_target_pairs={{0,2},{1,3},{2,0},{3,1},{4,6},{5,7},{6,4},{7,5},{8,10},{9,11},{10,... | collective-permute-start | bytes 294920 | tf_op jit(solution)/shard_map/ppermute | solution.py:362
  37.9 5.5 %collective-permute-start.11 = (bf16[2,768]{1,0:T(2,128)(2,1)S(1)}, bf16[2,768]{1,0:T(2,128)(2,1)S(1)}, u32[]{:S(2)}, u32[]{:S(2)}) collective-permute-start(bf16[2,768]{1,0:T(2,128)(2,1)S(1)} %get-tuple-element.50.refs_8_), channel_id=1, source_target_pairs={{0,24},{1,29},{2,26},{3,31},{4,28},{5,25},{6,30},{7,27},{8,16},{9,... | collective-permute-start | bytes 9224 | tf_op jit(solution)/shard_map/ppermute | solution.py:441
  41.7 7.7 %collective-permute-start.10 = (bf16[2,768]{1,0:T(2,128)(2,1)S(1)}, bf16[2,768]{1,0:T(2,128)(2,1)S(1)}, u32[]{:S(2)}, u32[]{:S(2)}) collective-permute-start(bf16[2,768]{1,0:T(2,128)(2,1)S(1)} %get-tuple-element.50.refs_8_), channel_id=1, source_target_pairs={{0,16},{1,21},{2,18},{3,23},{4,20},{5,17},{6,22},{7,19},{8,24},{9,... | collective-permute-start | bytes 9224 | tf_op jit(solution)/shard_map/ppermute | solution.py:441
  41.7 7.7 %collective-permute-start.9 = (bf16[2,768]{1,0:T(2,128)(2,1)S(1)}, bf16[2,768]{1,0:T(2,128)(2,1)S(1)}, u32[]{:S(2)}, u32[]{:S(2)}) collective-permute-start(bf16[2,768]{1,0:T(2,128)(2,1)S(1)} %get-tuple-element.50.refs_8_), channel_id=1, source_target_pairs={{0,8},{1,13},{2,10},{3,15},{4,12},{5,9},{6,14},{7,11},{8,0},{9,5},... | collective-permute-start | bytes 9224 | tf_op jit(solution)/shard_map/ppermute | solution.py:441
  42.3 7.1 %collective-permute-start.8 = (bf16[2,768]{1,0:T(2,128)(2,1)S(1)}, bf16[2,768]{1,0:T(2,128)(2,1)S(1)}, u32[]{:S(2)}, u32[]{:S(2)}) collective-permute-start(bf16[2,768]{1,0:T(2,128)(2,1)S(1)} %get-tuple-element.50.refs_8_), channel_id=1, source_target_pairs={{1,5},{3,7},{5,1},{7,3},{9,13},{11,15},{13,9},{15,11},{17,21},{19,... | collective-permute-start | bytes 9224 | tf_op jit(solution)/shard_map/ppermute | solution.py:441
  43.4 6.7 %collective-permute-start.12 = (bf16[64,768]{1,0:T(8,128)(2,1)S(1)}, bf16[64,768]{1,0:T(8,128)(2,1)S(1)}, u32[]{:S(2)}, u32[]{:S(2)}) collective-permute-start(bf16[64,768]{1,0:T(8,128)(2,1)S(1)} %norm_two.1.refs_9_), channel_id=1, source_target_pairs={{0,1},{1,0},{2,3},{3,2},{4,5},{5,4},{6,7},{7,6},{8,9},{9,8},{10,11... | collective-permute-start | bytes 294920 | tf_op jit(solution)/shard_map/ppermute | solution.py:362
  49.4 1.5 %collective-permute-start.13 = (bf16[64,768]{1,0:T(8,128)(2,1)S(1)}, bf16[64,768]{1,0:T(8,128)(2,1)S(1)}, u32[]{:S(2)}, u32[]{:S(2)}) collective-permute-start(bf16[64,768]{1,0:T(8,128)(2,1)S(1)} %collective-permute-done.7.refs_10_), channel_id=1, source_target_pairs={{0,1},{1,0},{2,3},{3,2},{4,5},{5,4},{6,7},{7,6},{8,9},{9,8},{10,11... | collective-permute-start | bytes 294920 | tf_op jit(solution)/shard_map/ppermute | solution.py:362
  49.5 1.4 %collective-permute-start.14 = (bf16[16,768]{1,0:T(8,128)(2,1)S(1)}, bf16[16,768]{1,0:T(8,128)(2,1)S(1)}, u32[]{:S(2)}, u32[]{:S(2)}) collective-permute-start(bf16[16,768]{1,0:T(8,128)(2,1)S(1)} %pack.1.refs_13_), channel_id=1, source_target_pairs={{0,1},{1,0},{2,3},{3,2},{4,5},{5,4},{6,7},{7,6},{8,9},{9,8},{10,11... | collective-permute-start | bytes 73736 | tf_op jit(solution)/shard_map/ppermute | solution.py:362
  51.0 1.0 %copy-start.13 = (bf16[512,192]{1,0:T(8,128)(2,1)S(1)}, bf16[512,192]{1,0:T(8,128)(2,1)}, u32[]{:S(2)}) copy-start(bf16[512,192]{1,0:T(8,128)(2,1)} %copy-done.12) | copy-start | bytes 589828
  51.9 1.1 %copy-start.15 = (bf16[512,768]{1,0:T(8,128)(2,1)S(1)}, bf16[512,768]{1,0:T(8,128)(2,1)}, u32[]{:S(2)}) copy-start(bf16[512,768]{1,0:T(8,128)(2,1)} %copy-done.14) | copy-start | bytes 2359300

commit v14 on v13

--- a/solution.py
+++ b/solution.py
@@ -31,6 +31,7 @@
     args,
     smem=(),
     hbm=(),
+    pieces=None,
     scalars=(),
     scratch=(),
     out_specs=None,
@@ -42,20 +43,28 @@
     nbytes = sum(a.size * a.dtype.itemsize for a in args)
     space = [pltpu.SMEM if i in scalars else pltpu.VMEM for i in hbm]
     buffers = [kind(args[i].shape, args[i].dtype) for kind, i in zip(space, hbm)]
-    sems = [pltpu.SemaphoreType.DMA((len(hbm),))] if hbm else []
+    spans = {i: (pieces or {}).get(i, ((0, args[i].shape[0]),)) for i in hbm}
+    sems = [pltpu.SemaphoreType.DMA((len(spans[i]),)) for i in hbm]
 
     def body(*refs):
         ins, rest = list(refs[:count]), refs[count:]
         kept, moved = rest[: out_count + own], rest[out_count + own :]
         moves = {}
         for j, i in enumerate(hbm):
-            moves[i] = pltpu.make_async_copy(ins[i], moved[j], moved[-1].at[j])
-            moves[i].start()
+            moves[i] = []
+            for k, (start, size) in enumerate(spans[i]):
+                at = pl.ds(start, size)
+                move = pltpu.make_async_copy(
+                    ins[i].at[at], moved[j].at[at], moved[len(hbm) + j].at[k]
+                )
+                move.start()
+                moves[i].append(move)
             ins[i] = moved[j]
 
         def ready(*wanted):
             for i in wanted:
-                moves[i].wait()
+                for move in moves[i]:
+                    move.wait()
 
         kernel(ready, *ins, *kept)
 
@@ -385,7 +394,8 @@
         shape((dp * fetch, 2 * cols), bf),
         (me, title_nodes, send_ids[0], node_table, w_graph),
         smem=(0,),
-        hbm=(4, 3, 2, 1),
+        hbm=(2, 3, 4, 1),
+        pieces={3: [(i, nodes // 4) for i in range(0, nodes, nodes // 4)], 4: [(1, 1), (2, 1)]},
         scalars=(1,),
         out_specs=HBM,
         scratch=[pltpu.VMEM((dp * fetch, 2 * cols), bf), pltpu.SemaphoreType.DMA((dp,))],
@@ -461,7 +471,7 @@
         norm_two_kernel, shape((chunk, width), bf), (hidden, gains, keep, part), name="norm_two"
     )
     across = swap(done, 2)
-    across, firsts = lax.optimization_barrier((across, firsts))
+    across, firsts, far = lax.optimization_barrier((across, firsts, far))
     pack = call(pack_kernel, shape((tail_rows(turns * per_part), width), bf), firsts, name="pack")
     packs = [pack, swap(pack, 1)]
     dones = [done, across, swap(done, 1), swap(across, 1)]

time: 57.9 us -> 57 us (0.984)
  local copies, waits for them, and re-layouts: 3.01 us -> 2.07 us
    unnamed x32 -> x28, local copies, waits for them, and re-layouts: 3.01 us -> 2.07 us
where the time goes in v14:
time: 57 us; the launch traced here: 56.7 us
  starting transfers between devices  21 us (37%)
  Pallas kernels  17.4 us (31%)
  waiting for transfers between devices  15.4 us (27%)
  local copies, waits for them, and re-layouts  2.07 us (4%)
  between operations  0.86 us (2%)
    pallas_call x11, Pallas kernels, call(): pl.pallas_call(body, out_shape=outs, in_specs=specs, out_specs=jax.tree.m...  17.4 us
    ppermute x11, waiting for transfers between devices, swap(): lax.ppermute(value, axis, [(i, i ^ step) for i in range(lax.axis_size(axi...  11.3 us
    ppermute x11, starting transfers between devices, swap(): lax.ppermute(value, axis, [(i, i ^ step) for i in range(lax.axis_size(axi...  8.34 us
    all_to_all x1, starting transfers between devices, local(): lax.all_to_all(sent.reshape(dp, fetch, 2 * cols), 'dp', split_axis=0, con...  7.4 us
    ppermute x4, starting transfers between devices, local(): lax.ppermute(first, ('dp', 'mp'), [(p * mp + m, (p ^ turn * pair + m % pa...  5.22 us
    ppermute x4, waiting for transfers between devices, local(): lax.ppermute(first, ('dp', 'mp'), [(p * mp + m, (p ^ turn * pair + m % pa...  4.12 us
    unnamed x28, local copies, waits for them, and re-layouts  2.07 us
  transfers between devices with their start and end apart: 16, of which 8 were waited for; matrix products, arithmetic and copies ran while one was open for 0% of the time, Pallas kernels for 15%

profile of v14, /device:TPU:0, one launch (start us, length us, event | category | flops | bytes accessed | tf_op | source)
XLA Modules:
  0.0 56.7 jit_solution(3491360873254228504)
XLA Ops:
  0.6 4.1 %send.1 = bf16[2048,384]{1,0:T(8,128)(2,1)} custom-call(s32[1]{0:T(128)} %bitcast.1.refs_0_, s32[2]{0:T(128)} %refs_2_.5, s32[8,256]{1,0:T(8,128)} %bitcast.16, bf16[512,768]{1,0:T(8,128)(2,1)} %refs_0_.2, bf16[3,192,768]{2,1,0:T(8,128)(2,1)} %bitcast.11), custom_call_target="tpu_custom_call" | custom-call | flops 1107296256 | bytes 1679372 | tf_op jit(solution)/shard_map/send/pallas_call | solution.py:71
  4.7 0.0 copy-start.2
  4.8 0.0 copy-start.3
  4.8 0.0 copy-start.4
  4.8 7.4 %all-to-all-start = ((bf16[8,256,384]{2,1,0:T(8,128)(2,1)}), bf16[8,256,384]{2,1,0:T(8,128)(2,1)S(1)}, u32[]{:S(2)}, u32[]{:S(2)}) async-start(bf16[8,256,384]{2,1,0:T(8,128)(2,1)} %bitcast.15), calls=%async_computation | async-start | bytes 3145728 | tf_op jit(solution)/shard_map/all_to_all | solution.py:405
  12.2 0.0 copy-start.8
  12.2 0.0 copy-done.2
  12.2 0.0 copy-done.3
  12.2 0.0 copy-done.4
  12.2 1.7 %attn.1 = (f32[144,768]{1,0:T(8,128)S(1)}, bf16[144,768]{1,0:T(8,128)(2,1)S(1)}) custom-call(s32[1]{0:T(128)} %bitcast.refs_0_, bf16[256,768]{1,0:T(8,128)(2,1)S(1)} %copy-done.2, bf16[3,192,768]{2,1,0:T(8,128)(2,1)S(1)} %bitcast.10, bf16[192,768]{1,0:T(8,128)(2,1)S(1)} %copy-done.4), custom_call_target="tpu_custom_call" | custom-call | flops 301989888 | bytes 1572868 | tf_op jit(solution)/shard_map/attn/pallas_call | solution.py:71
  14.0 0.1 collective-permute-start
  14.0 1.5 %collective-permute-done.refs_1_ = bf16[144,768]{1,0:T(8,128)(2,1)S(1)} collective-permute-done((bf16[144,768]{1,0:T(8,128)(2,1)S(1)}, bf16[144,768]{1,0:T(8,128)(2,1)S(1)}, u32[]{:S(2)}, u32[]{:S(2)}) %collective-permute-start) | collective-permute-done | bytes 221216 | tf_op jit(solution)/shard_map/ppermute | solution.py:371
  15.5 0.0 copy-start
  15.6 0.0 copy-start.1
  15.6 0.0 copy-start.5
  15.6 1.6 %collective-permute-start.1 = (bf16[80,768]{1,0:T(8,128)(2,1)S(1)}, bf16[80,768]{1,0:T(8,128)(2,1)S(1)}, u32[]{:S(2)}, u32[]{:S(2)}) collective-permute-start(bf16[80,768]{1,0:T(8,128)(2,1)S(1)} %get-tuple-element.35), channel_id=1, source_target_pairs={{0,2},{1,3},{2,0},{3,1},{4,6},{5,7},{6,4},{7,5},{8,10},{9,11},{10,... | collective-permute-start | bytes 368648 | tf_op jit(solution)/shard_map/ppermute | solution.py:371
  17.2 0.0 copy-done.6
  17.2 0.0 copy-done.8
  17.2 0.9 %own.1 = (bf16[512,384]{1,0:T(8,128)(2,1)S(1)}, bf16[512,192]{1,0:T(8,128)(2,1)S(1)}) custom-call(bf16[512,768]{1,0:T(8,128)(2,1)S(1)} %copy-done.8, bf16[3,192,768]{2,1,0:T(8,128)(2,1)S(1)} %bitcast.12), custom_call_target="tpu_custom_call" | custom-call | flops 2000000000 | bytes 1671168 | tf_op jit(solution)/shard_map/own/pallas_call | solution.py:71
  18.0 3.0 %collective-permute-done.1.refs_6_ = bf16[80,768]{1,0:T(8,128)(2,1)S(1)} collective-permute-done((bf16[80,768]{1,0:T(8,128)(2,1)S(1)}, bf16[80,768]{1,0:T(8,128)(2,1)S(1)}, u32[]{:S(2)}, u32[]{:S(2)}) %collective-permute-start.1) | collective-permute-done | bytes 122912 | tf_op jit(solution)/shard_map/ppermute | solution.py:371
  21.0 0.0 copy-done
  21.0 0.0 copy-done.1
  21.0 0.0 copy-done.5
  21.0 0.7 %norm_one.1 = (bf16[80,768]{1,0:T(8,128)(2,1)S(1)}, bf16[16,768]{1,0:T(8,128)(2,1)S(1)}, f32[16,768]{1,0:T(8,128)S(1)}) custom-call(s32[1]{0:T(128)} %bitcast.refs_0_, bf16[256,768]{1,0:T(8,128)(2,1)S(1)} %copy-done.2, f32[2,768]{1,0:T(2,128)S(1)} %copy-done.5, bf16[768,768]{1,0:T(8,128)(2,1)S(1)} %copy-done, bf16[768,768]{1,0:T(8,128)(2,1)S(1)} %copy-done.1, ...), custom_call_target="tpu_custom_call" | custom-call | bytes 3127300 | tf_op jit(solution)/shard_map/norm_one/pallas_call | solution.py:71
  21.7 1.5 %collective-permute-start.2 = (bf16[80,768]{1,0:T(8,128)(2,1)S(1)}, bf16[80,768]{1,0:T(8,128)(2,1)S(1)}, u32[]{:S(2)}, u32[]{:S(2)}) collective-permute-start(bf16[80,768]{1,0:T(8,128)(2,1)S(1)} %get-tuple-element.44.refs_5_.refs_0_), channel_id=1, source_target_pairs={{0,2},{1,3},{2,0},{3,1},{4,6},{5,7},{6,4},{7,5},{8,10},{9,11},{10,... | collective-permute-start | bytes 368648 | tf_op jit(solution)/shard_map/ppermute | solution.py:371
  23.2 0.0 collective-permute-start.3
  23.2 3.4 %collective-permute-done.2.refs_6_ = bf16[80,768]{1,0:T(8,128)(2,1)S(1)} collective-permute-done((bf16[80,768]{1,0:T(8,128)(2,1)S(1)}, bf16[80,768]{1,0:T(8,128)(2,1)S(1)}, u32[]{:S(2)}, u32[]{:S(2)}) %collective-permute-start.2) | collective-permute-done | bytes 122912 | tf_op jit(solution)/shard_map/ppermute | solution.py:371
  26.6 0.0 collective-permute-start.4
  26.6 0.0 collective-permute-done.3.refs_7_
  26.6 1.3 %collective-permute-done.4.refs_8_ = bf16[80,768]{1,0:T(8,128)(2,1)S(1)} collective-permute-done((bf16[80,768]{1,0:T(8,128)(2,1)S(1)}, bf16[80,768]{1,0:T(8,128)(2,1)S(1)}, u32[]{:S(2)}, u32[]{:S(2)}) %collective-permute-start.4) | collective-permute-done | bytes 122912 | tf_op jit(solution)/shard_map/ppermute | solution.py:371
  27.9 0.9 %ffn.1 = (f32[128,768]{1,0:T(8,128)S(1)}, bf16[128,768]{1,0:T(8,128)(2,1)S(1)}, bf16[2,768]{1,0:T(2,128)(2,1)S(1)}) custom-call(bf16[768,768]{1,0:T(8,128)(2,1)S(1)} %copy-done, bf16[768,768]{1,0:T(8,128)(2,1)S(1)} %copy-done.1, f32[2,768]{1,0:T(2,128)S(1)} %copy-done.5, bf16[16,768]{1,0:T(8,128)(2,1)S(1)} %get-tuple-element.42.refs_3_, ...), custom_call_target="tpu_custom_call" | custom-call | flops 603979776 | bytes 2930688 | tf_op jit(solution)/shard_map/ffn/pallas_call | solution.py:71
  28.9 0.2 collective-permute-start.5
  29.1 1.3 %collective-permute-done.5.refs_1_ = bf16[128,768]{1,0:T(8,128)(2,1)S(1)} collective-permute-done((bf16[128,768]{1,0:T(8,128)(2,1)S(1)}, bf16[128,768]{1,0:T(8,128)(2,1)S(1)}, u32[]{:S(2)}, u32[]{:S(2)}) %collective-permute-start.5) | collective-permute-done | bytes 196640 | tf_op jit(solution)/shard_map/ppermute | solution.py:371
  30.4 0.1 half.3
  30.4 1.6 %collective-permute-start.6 = (bf16[64,768]{1,0:T(8,128)(2,1)S(1)}, bf16[64,768]{1,0:T(8,128)(2,1)S(1)}, u32[]{:S(2)}, u32[]{:S(2)}) collective-permute-start(bf16[64,768]{1,0:T(8,128)(2,1)S(1)} %get-tuple-element.48), channel_id=1, source_target_pairs={{0,2},{1,3},{2,0},{3,1},{4,6},{5,7},{6,4},{7,5},{8,10},{9,11},{10,... | collective-permute-start | bytes 294920 | tf_op jit(solution)/shard_map/ppermute | solution.py:371
  32.0 0.0 copy-done.9
  32.0 4.2 %mask.1.refs_6_ = bf16[512,768]{1,0:T(8,128)(2,1)S(1)} custom-call(s32[16,512]{1,0:T(8,128)S(1)} %bitcast.14), custom_call_target="tpu_custom_call" | custom-call | flops 4000000000 | bytes 32768 | tf_op jit(solution)/shard_map/mask/pallas_call | solution.py:71
  36.3 0.0 copy-start.12
  36.3 0.9 %copy-done.12 = bf16[512,768]{1,0:T(8,128)(2,1)} copy-done((bf16[512,768]{1,0:T(8,128)(2,1)}, bf16[512,768]{1,0:T(8,128)(2,1)S(1)}, u32[]{:S(2)}) %copy-start.12) | copy-done | bytes 786456
  37.2 0.0 collective-permute-done.6.refs_3_
  37.2 0.2 norm_two.1.refs_9_
  37.4 0.6 %collective-permute-start.7 = (bf16[64,768]{1,0:T(8,128)(2,1)S(1)}, bf16[64,768]{1,0:T(8,128)(2,1)S(1)}, u32[]{:S(2)}, u32[]{:S(2)}) collective-permute-start(bf16[64,768]{1,0:T(8,128)(2,1)S(1)} %norm_two.1.refs_9_), channel_id=1, source_target_pairs={{0,2},{1,3},{2,0},{3,1},{4,6},{5,7},{6,4},{7,5},{8,10},{9,11},{10,... | collective-permute-start | bytes 294920 | tf_op jit(solution)/shard_map/ppermute | solution.py:371
  38.0 3.8 %collective-permute-start.11 = (bf16[2,768]{1,0:T(2,128)(2,1)S(1)}, bf16[2,768]{1,0:T(2,128)(2,1)S(1)}, u32[]{:S(2)}, u32[]{:S(2)}) collective-permute-start(bf16[2,768]{1,0:T(2,128)(2,1)S(1)} %get-tuple-element.53.refs_8_), channel_id=1, source_target_pairs={{0,24},{1,29},{2,26},{3,31},{4,28},{5,25},{6,30},{7,27},{8,16},{9,... | collective-permute-start | bytes 9224 | tf_op jit(solution)/shard_map/ppermute | solution.py:451
  41.8 0.0 collective-permute-start.10
  41.8 0.6 %collective-permute-start.9 = (bf16[2,768]{1,0:T(2,128)(2,1)S(1)}, bf16[2,768]{1,0:T(2,128)(2,1)S(1)}, u32[]{:S(2)}, u32[]{:S(2)}) collective-permute-start(bf16[2,768]{1,0:T(2,128)(2,1)S(1)} %get-tuple-element.53.refs_8_), channel_id=1, source_target_pairs={{0,8},{1,13},{2,10},{3,15},{4,12},{5,9},{6,14},{7,11},{8,0},{9,5},... | collective-permute-start | bytes 9224 | tf_op jit(solution)/shard_map/ppermute | solution.py:451
  42.3 0.8 %collective-permute-start.8 = (bf16[2,768]{1,0:T(2,128)(2,1)S(1)}, bf16[2,768]{1,0:T(2,128)(2,1)S(1)}, u32[]{:S(2)}, u32[]{:S(2)}) collective-permute-start(bf16[2,768]{1,0:T(2,128)(2,1)S(1)} %get-tuple-element.53.refs_8_), channel_id=1, source_target_pairs={{1,5},{3,7},{5,1},{7,3},{9,13},{11,15},{13,9},{15,11},{17,21},{19,... | collective-permute-start | bytes 9224 | tf_op jit(solution)/shard_map/ppermute | solution.py:451
  43.2 0.3 collective-permute-done.11.refs_3_
  43.5 2.2 %collective-permute-start.12 = (bf16[64,768]{1,0:T(8,128)(2,1)S(1)}, bf16[64,768]{1,0:T(8,128)(2,1)S(1)}, u32[]{:S(2)}, u32[]{:S(2)}) collective-permute-start(bf16[64,768]{1,0:T(8,128)(2,1)S(1)} %norm_two.1.refs_9_), channel_id=1, source_target_pairs={{0,1},{1,0},{2,3},{3,2},{4,5},{5,4},{6,7},{7,6},{8,9},{9,8},{10,11... | collective-permute-start | bytes 294920 | tf_op jit(solution)/shard_map/ppermute | solution.py:371
  45.6 3.8 %collective-permute-done.10.refs_2_ = bf16[2,768]{1,0:T(2,128)(2,1)S(1)} collective-permute-done((bf16[2,768]{1,0:T(2,128)(2,1)S(1)}, bf16[2,768]{1,0:T(2,128)(2,1)S(1)}, u32[]{:S(2)}, u32[]{:S(2)}) %collective-permute-start.10) | collective-permute-done | bytes 3104 | tf_op jit(solution)/shard_map/ppermute | solution.py:451
  49.5 0.0 collective-permute-done.9.refs_1_
  49.5 0.0 collective-permute-done.8.refs_0_
  49.5 0.0 collective-permute-done.7.refs_10_
  49.5 0.0 all-to-all-done
  49.5 0.1 collective-permute-start.13
  49.6 0.6 collective-permute-start.14
  50.1 0.0 collective-permute-done.12.refs_11_
  50.1 0.8 %collective-permute-done.14.refs_14_ = bf16[16,768]{1,0:T(8,128)(2,1)S(1)} collective-permute-done((bf16[16,768]{1,0:T(8,128)(2,1)S(1)}, bf16[16,768]{1,0:T(8,128)(2,1)S(1)}, u32[]{:S(2)}, u32[]{:S(2)}) %collective-permute-start.14) | collective-permute-done | bytes 24608 | tf_op jit(solution)/shard_map/ppermute | solution.py:371
  51.0 0.0 collective-permute-done.13.refs_12_
  51.0 0.0 copy-done.7
  51.0 0.0 copy-done.10
  51.0 0.0 copy-done.11
  51.0 0.0 copy-start.13
  51.0 1.1 %copy-done.13 = bf16[512,768]{1,0:T(8,128)(2,1)S(1)} copy-done((bf16[512,768]{1,0:T(8,128)(2,1)S(1)}, bf16[512,768]{1,0:T(8,128)(2,1)}, u32[]{:S(2)}) %copy-start.13) | copy-done | bytes 786456
  52.1 4.5 %graph.1 = (bf16[192,512]{1,0:T(8,128)(2,1)}, bf16[256,768]{1,0:T(8,128)(2,1)}) custom-call(s32[1]{0:T(128)} %bitcast.refs_0_, s32[4,6]{1,0:T(4,128)S(1)} %copy-done.10, s32[2]{0:T(128)S(1)} %copy-done.11, bf16[512,192]{1,0:T(8,128)(2,1)S(1)} %get-tuple-element.38.refs_3_, bf16[512,384]{1,0:T(8,128)(2,1)S(1)} %get-tuple-element.39.refs_4_, ...), custom_call_target="tpu_custom_call" | custom-call | flops 4000000000 | bytes 4279404 | tf_op jit(solution)/shard_map/graph/pallas_call | solution.py:71
  (7 shorter events, 0.1 us)
Async XLA Ops:
  4.7 7.5 %copy-start.2 = (bf16[256,768]{1,0:T(8,128)(2,1)S(1)}, bf16[256,768]{1,0:T(8,128)(2,1)}, u32[]{:S(2)}) copy-start(bf16[256,768]{1,0:T(8,128)(2,1)} %refs_1_.6) | copy-start | bytes 1179652
  4.8 7.5 %copy-start.3 = (bf16[3,768,192]{1,2,0:T(8,128)(2,1)S(1)}, bf16[3,768,192]{1,2,0:T(8,128)(2,1)}, u32[]{:S(2)}) copy-start(bf16[3,768,192]{1,2,0:T(8,128)(2,1)} %param.13) | copy-start | bytes 2654212
  4.8 7.5 %copy-start.4 = (bf16[192,768]{1,0:T(8,128)(2,1)S(1)}, bf16[192,768]{1,0:T(8,128)(2,1)}, u32[]{:S(2)}) copy-start(bf16[192,768]{1,0:T(8,128)(2,1)} %refs_3_.4) | copy-start | bytes 884740
  4.8 44.7 %all-to-all-start = ((bf16[8,256,384]{2,1,0:T(8,128)(2,1)}), bf16[8,256,384]{2,1,0:T(8,128)(2,1)S(1)}, u32[]{:S(2)}, u32[]{:S(2)}) async-start(bf16[8,256,384]{2,1,0:T(8,128)(2,1)} %bitcast.15), calls=%async_computation | async-start | bytes 3145728 | tf_op jit(solution)/shard_map/all_to_all | solution.py:405
  12.2 5.0 %copy-start.6 = (bf16[3,768,192]{1,2,0:T(8,128)(2,1)S(1)}, bf16[3,768,192]{1,2,0:T(8,128)(2,1)}, u32[]{:S(2)}) copy-start(bf16[3,768,192]{1,2,0:T(8,128)(2,1)} %param.19) | copy-start | bytes 2654212
  12.2 5.0 %copy-start.8 = (bf16[512,768]{1,0:T(8,128)(2,1)S(1)}, bf16[512,768]{1,0:T(8,128)(2,1)}, u32[]{:S(2)}) copy-start(bf16[512,768]{1,0:T(8,128)(2,1)} %refs_0_.2) | copy-start | bytes 2359300
  14.0 1.5 %collective-permute-start = (bf16[144,768]{1,0:T(8,128)(2,1)S(1)}, bf16[144,768]{1,0:T(8,128)(2,1)S(1)}, u32[]{:S(2)}, u32[]{:S(2)}) collective-permute-start(bf16[144,768]{1,0:T(8,128)(2,1)S(1)} %get-tuple-element.34), channel_id=1, source_target_pairs={{0,1},{1,0},{2,3},{3,2},{4,5},{5,4},{6,7},{7,6},{8,9},{9,8},{10,11... | collective-permute-start | bytes 663560 | tf_op jit(solution)/shard_map/ppermute | solution.py:371
  15.5 5.5 %copy-start = (bf16[768,768]{1,0:T(8,128)(2,1)S(1)}, bf16[768,768]{1,0:T(8,128)(2,1)}, u32[]{:S(2)}) copy-start(bf16[768,768]{1,0:T(8,128)(2,1)} %refs_0_.3) | copy-start | bytes 3538948
  15.6 5.5 %copy-start.1 = (bf16[768,768]{1,0:T(8,128)(2,1)S(1)}, bf16[768,768]{1,0:T(8,128)(2,1)}, u32[]{:S(2)}) copy-start(bf16[768,768]{1,0:T(8,128)(2,1)} %refs_1_.7) | copy-start | bytes 3538948
  15.6 5.4 %copy-start.5 = (f32[2,768]{1,0:T(2,128)S(1)}, f32[2,768]{1,0:T(2,128)}, u32[]{:S(2)}) copy-start(f32[2,768]{1,0:T(2,128)} %refs_1_.8) | copy-start | bytes 18436
  15.6 5.4 %collective-permute-start.1 = (bf16[80,768]{1,0:T(8,128)(2,1)S(1)}, bf16[80,768]{1,0:T(8,128)(2,1)S(1)}, u32[]{:S(2)}, u32[]{:S(2)}) collective-permute-start(bf16[80,768]{1,0:T(8,128)(2,1)S(1)} %get-tuple-element.35), channel_id=1, source_target_pairs={{0,2},{1,3},{2,0},{3,1},{4,6},{5,7},{6,4},{7,5},{8,10},{9,11},{10,... | collective-permute-start | bytes 368648 | tf_op jit(solution)/shard_map/ppermute | solution.py:371
  21.7 4.9 %collective-permute-start.2 = (bf16[80,768]{1,0:T(8,128)(2,1)S(1)}, bf16[80,768]{1,0:T(8,128)(2,1)S(1)}, u32[]{:S(2)}, u32[]{:S(2)}) collective-permute-start(bf16[80,768]{1,0:T(8,128)(2,1)S(1)} %get-tuple-element.44.refs_5_.refs_0_), channel_id=1, source_target_pairs={{0,2},{1,3},{2,0},{3,1},{4,6},{5,7},{6,4},{7,5},{8,10},{9,11},{10,... | collective-permute-start | bytes 368648 | tf_op jit(solution)/shard_map/ppermute | solution.py:371
  23.2 3.4 %collective-permute-start.3 = (bf16[80,768]{1,0:T(8,128)(2,1)S(1)}, bf16[80,768]{1,0:T(8,128)(2,1)S(1)}, u32[]{:S(2)}, u32[]{:S(2)}) collective-permute-start(bf16[80,768]{1,0:T(8,128)(2,1)S(1)} %get-tuple-element.44.refs_5_.refs_0_), channel_id=1, source_target_pairs={{0,1},{1,0},{2,3},{3,2},{4,5},{5,4},{6,7},{7,6},{8,9},{9,8},{10,11... | collective-permute-start | bytes 368648 | tf_op jit(solution)/shard_map/ppermute | solution.py:371
  26.6 1.3 %collective-permute-start.4 = (bf16[80,768]{1,0:T(8,128)(2,1)S(1)}, bf16[80,768]{1,0:T(8,128)(2,1)S(1)}, u32[]{:S(2)}, u32[]{:S(2)}) collective-permute-start(bf16[80,768]{1,0:T(8,128)(2,1)S(1)} %collective-permute-done.2.refs_6_), channel_id=1, source_target_pairs={{0,1},{1,0},{2,3},{3,2},{4,5},{5,4},{6,7},{7,6},{8,9},{9,8},{10,11... | collective-permute-start | bytes 368648 | tf_op jit(solution)/shard_map/ppermute | solution.py:371
  27.9 4.1 %copy-start.9 = (s32[512,16]{0,1:T(8,128)S(1)}, s32[512,16]{0,1:T(8,128)}, u32[]{:S(2)}) copy-start(s32[512,16]{0,1:T(8,128)} %param.23) | copy-start | bytes 98308
  28.9 1.5 %collective-permute-start.5 = (bf16[128,768]{1,0:T(8,128)(2,1)S(1)}, bf16[128,768]{1,0:T(8,128)(2,1)S(1)}, u32[]{:S(2)}, u32[]{:S(2)}) collective-permute-start(bf16[128,768]{1,0:T(8,128)(2,1)S(1)} %get-tuple-element.46), channel_id=1, source_target_pairs={{0,1},{1,0},{2,3},{3,2},{4,5},{5,4},{6,7},{7,6},{8,9},{9,8},{10,11... | collective-permute-start | bytes 589832 | tf_op jit(solution)/shard_map/ppermute | solution.py:371
  30.4 6.7 %collective-permute-start.6 = (bf16[64,768]{1,0:T(8,128)(2,1)S(1)}, bf16[64,768]{1,0:T(8,128)(2,1)S(1)}, u32[]{:S(2)}, u32[]{:S(2)}) collective-permute-start(bf16[64,768]{1,0:T(8,128)(2,1)S(1)} %get-tuple-element.48), channel_id=1, source_target_pairs={{0,2},{1,3},{2,0},{3,1},{4,6},{5,7},{6,4},{7,5},{8,10},{9,11},{10,... | collective-permute-start | bytes 294920 | tf_op jit(solution)/shard_map/ppermute | solution.py:371
  32.0 19.0 %copy-start.7 = (bf16[3,768,192]{1,2,0:T(8,128)(2,1)S(1)}, bf16[3,768,192]{1,2,0:T(8,128)(2,1)}, u32[]{:S(2)}) copy-start(bf16[3,768,192]{1,2,0:T(8,128)(2,1)} %param.19) | copy-start | bytes 2654212
  32.0 19.0 %copy-start.10 = (s32[4,6]{1,0:T(4,128)S(1)}, s32[4,6]{1,0:T(4,128)}, u32[]{:S(2)}) copy-start(s32[4,6]{1,0:T(4,128)} %refs_1_.9) | copy-start | bytes 292
  32.0 19.0 %copy-start.11 = (s32[2]{0:T(128)S(1)}, s32[2]{0:T(128)}, u32[]{:S(2)}) copy-start(s32[2]{0:T(128)} %refs_2_.5) | copy-start | bytes 28
  36.3 0.9 %copy-start.12 = (bf16[512,768]{1,0:T(8,128)(2,1)}, bf16[512,768]{1,0:T(8,128)(2,1)S(1)}, u32[]{:S(2)}) copy-start(bf16[512,768]{1,0:T(8,128)(2,1)S(1)} %mask.1.refs_6_) | copy-start | bytes 2359300
  37.4 12.1 %collective-permute-start.7 = (bf16[64,768]{1,0:T(8,128)(2,1)S(1)}, bf16[64,768]{1,0:T(8,128)(2,1)S(1)}, u32[]{:S(2)}, u32[]{:S(2)}) collective-permute-start(bf16[64,768]{1,0:T(8,128)(2,1)S(1)} %norm_two.1.refs_9_), channel_id=1, source_target_pairs={{0,2},{1,3},{2,0},{3,1},{4,6},{5,7},{6,4},{7,5},{8,10},{9,11},{10,... | collective-permute-start | bytes 294920 | tf_op jit(solution)/shard_map/ppermute | solution.py:371
  38.0 5.5 %collective-permute-start.11 = (bf16[2,768]{1,0:T(2,128)(2,1)S(1)}, bf16[2,768]{1,0:T(2,128)(2,1)S(1)}, u32[]{:S(2)}, u32[]{:S(2)}) collective-permute-start(bf16[2,768]{1,0:T(2,128)(2,1)S(1)} %get-tuple-element.53.refs_8_), channel_id=1, source_target_pairs={{0,24},{1,29},{2,26},{3,31},{4,28},{5,25},{6,30},{7,27},{8,16},{9,... | collective-permute-start | bytes 9224 | tf_op jit(solution)/shard_map/ppermute | solution.py:451
  41.8 7.7 %collective-permute-start.10 = (bf16[2,768]{1,0:T(2,128)(2,1)S(1)}, bf16[2,768]{1,0:T(2,128)(2,1)S(1)}, u32[]{:S(2)}, u32[]{:S(2)}) collective-permute-start(bf16[2,768]{1,0:T(2,128)(2,1)S(1)} %get-tuple-element.53.refs_8_), channel_id=1, source_target_pairs={{0,16},{1,21},{2,18},{3,23},{4,20},{5,17},{6,22},{7,19},{8,24},{9,... | collective-permute-start | bytes 9224 | tf_op jit(solution)/shard_map/ppermute | solution.py:451
  41.8 7.7 %collective-permute-start.9 = (bf16[2,768]{1,0:T(2,128)(2,1)S(1)}, bf16[2,768]{1,0:T(2,128)(2,1)S(1)}, u32[]{:S(2)}, u32[]{:S(2)}) collective-permute-start(bf16[2,768]{1,0:T(2,128)(2,1)S(1)} %get-tuple-element.53.refs_8_), channel_id=1, source_target_pairs={{0,8},{1,13},{2,10},{3,15},{4,12},{5,9},{6,14},{7,11},{8,0},{9,5},... | collective-permute-start | bytes 9224 | tf_op jit(solution)/shard_map/ppermute | solution.py:451
  42.3 7.1 %collective-permute-start.8 = (bf16[2,768]{1,0:T(2,128)(2,1)S(1)}, bf16[2,768]{1,0:T(2,128)(2,1)S(1)}, u32[]{:S(2)}, u32[]{:S(2)}) collective-permute-start(bf16[2,768]{1,0:T(2,128)(2,1)S(1)} %get-tuple-element.53.refs_8_), channel_id=1, source_target_pairs={{1,5},{3,7},{5,1},{7,3},{9,13},{11,15},{13,9},{15,11},{17,21},{19,... | collective-permute-start | bytes 9224 | tf_op jit(solution)/shard_map/ppermute | solution.py:451
  43.5 6.7 %collective-permute-start.12 = (bf16[64,768]{1,0:T(8,128)(2,1)S(1)}, bf16[64,768]{1,0:T(8,128)(2,1)S(1)}, u32[]{:S(2)}, u32[]{:S(2)}) collective-permute-start(bf16[64,768]{1,0:T(8,128)(2,1)S(1)} %norm_two.1.refs_9_), channel_id=1, source_target_pairs={{0,1},{1,0},{2,3},{3,2},{4,5},{5,4},{6,7},{7,6},{8,9},{9,8},{10,11... | collective-permute-start | bytes 294920 | tf_op jit(solution)/shard_map/ppermute | solution.py:371
  49.5 1.5 %collective-permute-start.13 = (bf16[64,768]{1,0:T(8,128)(2,1)S(1)}, bf16[64,768]{1,0:T(8,128)(2,1)S(1)}, u32[]{:S(2)}, u32[]{:S(2)}) collective-permute-start(bf16[64,768]{1,0:T(8,128)(2,1)S(1)} %collective-permute-done.7.refs_10_), channel_id=1, source_target_pairs={{0,1},{1,0},{2,3},{3,2},{4,5},{5,4},{6,7},{7,6},{8,9},{9,8},{10,11... | collective-permute-start | bytes 294920 | tf_op jit(solution)/shard_map/ppermute | solution.py:371
  49.6 1.4 %collective-permute-start.14 = (bf16[16,768]{1,0:T(8,128)(2,1)S(1)}, bf16[16,768]{1,0:T(8,128)(2,1)S(1)}, u32[]{:S(2)}, u32[]{:S(2)}) collective-permute-start(bf16[16,768]{1,0:T(8,128)(2,1)S(1)} %pack.1.refs_13_), channel_id=1, source_target_pairs={{0,1},{1,0},{2,3},{3,2},{4,5},{5,4},{6,7},{7,6},{8,9},{9,8},{10,11... | collective-permute-start | bytes 73736 | tf_op jit(solution)/shard_map/ppermute | solution.py:371
  51.0 1.1 %copy-start.13 = (bf16[512,768]{1,0:T(8,128)(2,1)S(1)}, bf16[512,768]{1,0:T(8,128)(2,1)}, u32[]{:S(2)}) copy-start(bf16[512,768]{1,0:T(8,128)(2,1)} %copy-done.12) | copy-start | bytes 2359300

commit v15 on v14

--- a/solution.py
+++ b/solution.py
@@ -21,6 +21,7 @@
 SMEM = pl.BlockSpec(memory_space=pltpu.SMEM)
 HBM = pl.BlockSpec(memory_space=pltpu.HBM)
 PAD = 16
+LANES = 128
 NT = (((1,), (1,)), ((), ()))
 TN = (((0,), (0,)), ((), ()))
 
@@ -126,13 +127,21 @@
     table = table_ref[...]
     kv = jnp.concatenate([dot_nt(table, w_ref[1]), dot_nt(table, w_ref[2])], axis=1).astype(bf)
     moves = []
-    for part in range(ids.shape[1]):
-        picked = ids[:, part : part + 1]
-        rows = mark(dot(one_hot(picked, nodes), kv), picked, at_ref, me_ref[0] ^ part)
-        at = pl.ds(part * fetch, fetch)
-        rows_ref[at, :] = rows.astype(bf)
-        moves.append(pltpu.make_async_copy(rows_ref.at[at, :], sent_ref.at[at, :], sems.at[part]))
-        moves[-1].start()
+    parts = ids.shape[1]
+    group = min(parts, max(1, 1024 // fetch))
+    for start in range(0, parts, group):
+        picks = [ids[:, part : part + 1] for part in range(start, start + group)]
+        rows = dot(one_hot(jnp.concatenate(picks, axis=0), nodes), kv)
+        for j, picked in enumerate(picks):
+            part = start + j
+            mine = rows[j * fetch : (j + 1) * fetch]
+            at = pl.ds(part * fetch, fetch)
+            lead = mark(mine[:, :LANES], picked, at_ref, me_ref[0] ^ part)
+            rows_ref[at, :LANES] = lead.astype(bf)
+            rows_ref[at, LANES:] = mine[:, LANES:].astype(bf)
+            move = pltpu.make_async_copy(rows_ref.at[at, :], sent_ref.at[at, :], sems.at[part])
+            move.start()
+            moves.append(move)
     for move in moves:
         move.wait()
 
@@ -146,6 +155,10 @@
         for edge in range(DEG):
             edges = edges | (lanes == slots[:, edge : edge + 1])
         mask_ref[tile * TILE : (tile + 1) * TILE, :] = jnp.where(edges, 1.0, 0.0).astype(bf)
+
+
+def bias_kernel(ready, mask_ref, bias_ref):
+    bias_ref[...] = jnp.where(mask_ref[...].astype(f32) > 0.5, 0.0, -jnp.inf)
 
 
 def attn_kernel(ready, who_ref, titles_ref, w_in_ref, w_out_ref, *refs):
@@ -270,7 +283,7 @@
 
 
 def graph_kernel(
-    whose, ready, who_ref, cols_ref, at_ref, q_ref, kv_ref, w_ref, mask_ref, far_ref, first_ref, *refs
+    whose, ready, who_ref, cols_ref, at_ref, q_ref, kv_ref, w_ref, bias_ref, far_ref, first_ref, *refs
 ):
     *packs, out_ref, encoded_ref, k_all, v_all, firsts = refs
     dones, packs = packs[: len(whose)], packs[len(whose) :]
@@ -328,9 +341,8 @@
         keys = jnp.concatenate([k_all[pl.ds(start, TILE), :] for start in starts], axis=0)
         values = jnp.concatenate([v_all[pl.ds(start, TILE), :] for start in starts], axis=0)
         scores = dot_nt(stacked, keys) * (1.0 / GHD**0.5)
-        mask = mask_ref[tile * TILE : (tile + 1) * TILE, :].astype(f32)
-        mask = jnp.concatenate([mask] * heads, axis=0) > 0.5
-        masked = jnp.where(mask, scores, -jnp.inf)
+        bias = bias_ref[tile * TILE : (tile + 1) * TILE, :]
+        masked = scores + jnp.concatenate([bias] * heads, axis=0)
         expo = jnp.exp(masked - jnp.max(masked, axis=-1, keepdims=True))
         scale = 1.0 / jnp.sum(expo, axis=-1, keepdims=True)
         mixed = dot(expo.astype(bf), values) * scale
@@ -473,13 +485,15 @@
     across = swap(done, 2)
     across, firsts, far = lax.optimization_barrier((across, firsts, far))
     pack = call(pack_kernel, shape((tail_rows(turns * per_part), width), bf), firsts, name="pack")
+    mask, pack = lax.optimization_barrier((mask, pack))
     packs = [pack, swap(pack, 1)]
+    bias = call(bias_kernel, shape(mask.shape, f32), (mask,), flops=10**9, name="bias")
     dones = [done, across, swap(done, 1), swap(across, 1)]
     keys = nodes + dp * fetch
     graph_out, encoded = call(
         functools.partial(graph_kernel, whose),
         (shape((cols, nodes), bf), shape((tok_rows, width), bf)),
-        (who, tile_cols, title_nodes, q, kv, w_graph, mask, far, first, *dones, *packs),
+        (who, tile_cols, title_nodes, q, kv, w_graph, bias, far, first, *dones, *packs),
         smem=(0, 1, 2),
         scratch=[
             pltpu.VMEM((keys, cols), bf),

time: 57 us -> 56.2 us (0.986)
  waiting for transfers between devices: 15.4 us -> 18.5 us
  starting transfers between devices: 21 us -> 18.9 us
  local copies, waits for them, and re-layouts: 2.07 us -> 0.07 us
    ppermute x4, waiting for transfers between devices: 4.12 us -> 7.04 us  [local(): lax.ppermute(first, ('dp', 'mp'), [(p * mp + m, (p ^ turn * pair + m % pa...]
    ppermute x11, starting transfers between devices: 8.34 us -> 6.29 us  [swap(): lax.ppermute(value, axis, [(i, i ^ step) for i in range(lax.axis_size(axi...]
    unnamed x28 -> x24, local copies, waits for them, and re-layouts: 2.07 us -> 0.07 us
    pallas_call x11 -> x12, Pallas kernels: 17.4 us -> 17.6 us  [call(): pl.pallas_call(body, out_shape=outs, in_specs=specs, out_specs=jax.tree.m...]
  transfers between devices with their start and end apart: 16 -> 16, of which waited for: 8 -> 8; matrix products, arithmetic and copies ran while one was open for 0% -> 0% of each run, Pallas kernels for 15% -> 16%
where the time goes in v15:
time: 56.2 us; the launch traced here: 56 us
  starting transfers between devices  18.9 us (34%)
  waiting for transfers between devices  18.5 us (33%)
  Pallas kernels  17.6 us (31%)
  between operations  0.88 us (2%)
    pallas_call x12, Pallas kernels, call(): pl.pallas_call(body, out_shape=outs, in_specs=specs, out_specs=jax.tree.m...  17.6 us
    ppermute x11, waiting for transfers between devices, swap(): lax.ppermute(value, axis, [(i, i ^ step) for i in range(lax.axis_size(axi...  11.4 us
    all_to_all x1, starting transfers between devices, local(): lax.all_to_all(sent.reshape(dp, fetch, 2 * cols), 'dp', split_axis=0, con...  7.4 us
    ppermute x4, waiting for transfers between devices, local(): lax.ppermute(first, ('dp', 'mp'), [(p * mp + m, (p ^ turn * pair + m % pa...  7.04 us
    ppermute x11, starting transfers between devices, swap(): lax.ppermute(value, axis, [(i, i ^ step) for i in range(lax.axis_size(axi...  6.29 us
    ppermute x4, starting transfers between devices, local(): lax.ppermute(first, ('dp', 'mp'), [(p * mp + m, (p ^ turn * pair + m % pa...  5.26 us
  transfers between devices with their start and end apart: 16, of which 8 were waited for; matrix products, arithmetic and copies ran while one was open for 0% of the time, Pallas kernels for 16%

profile of v15, /device:TPU:0, one launch (start us, length us, event | category | flops | bytes accessed | tf_op | source)
XLA Modules:
  0.0 56.0 jit_solution(6618771936823933387)
XLA Ops:
  0.6 4.1 %send.1 = bf16[2048,384]{1,0:T(8,128)(2,1)} custom-call(s32[1]{0:T(128)} %bitcast.1.refs_0_, s32[2]{0:T(128)} %refs_2_.5, s32[8,256]{1,0:T(8,128)} %bitcast.16, bf16[512,768]{1,0:T(8,128)(2,1)} %refs_0_.2, bf16[3,192,768]{2,1,0:T(8,128)(2,1)} %bitcast.11), custom_call_target="tpu_custom_call" | custom-call | flops 1107296256 | bytes 1679372 | tf_op jit(solution)/shard_map/send/pallas_call | solution.py:72
  4.8 0.0 copy-start.2
  4.8 0.0 copy-start.3
  4.8 0.0 copy-start.4
  4.8 7.4 %all-to-all-start = ((bf16[8,256,384]{2,1,0:T(8,128)(2,1)}), bf16[8,256,384]{2,1,0:T(8,128)(2,1)S(1)}, u32[]{:S(2)}, u32[]{:S(2)}) async-start(bf16[8,256,384]{2,1,0:T(8,128)(2,1)} %bitcast.15), calls=%async_computation | async-start | bytes 3145728 | tf_op jit(solution)/shard_map/all_to_all | solution.py:417
  12.2 0.0 copy-start.8
  12.2 0.0 copy-done.2
  12.2 0.0 copy-done.3
  12.2 0.0 copy-done.4
  12.2 1.7 %attn.1 = (f32[144,768]{1,0:T(8,128)S(1)}, bf16[144,768]{1,0:T(8,128)(2,1)S(1)}) custom-call(s32[1]{0:T(128)} %bitcast.refs_0_, bf16[256,768]{1,0:T(8,128)(2,1)S(1)} %copy-done.2, bf16[3,192,768]{2,1,0:T(8,128)(2,1)S(1)} %bitcast.10, bf16[192,768]{1,0:T(8,128)(2,1)S(1)} %copy-done.4), custom_call_target="tpu_custom_call" | custom-call | flops 301989888 | bytes 1572868 | tf_op jit(solution)/shard_map/attn/pallas_call | solution.py:72
  14.0 0.1 collective-permute-start
  14.0 1.5 %collective-permute-done.refs_1_ = bf16[144,768]{1,0:T(8,128)(2,1)S(1)} collective-permute-done((bf16[144,768]{1,0:T(8,128)(2,1)S(1)}, bf16[144,768]{1,0:T(8,128)(2,1)S(1)}, u32[]{:S(2)}, u32[]{:S(2)}) %collective-permute-start) | collective-permute-done | bytes 221216 | tf_op jit(solution)/shard_map/ppermute | solution.py:383
  15.6 0.0 copy-start
  15.6 0.0 copy-start.1
  15.6 0.0 copy-start.5
  15.6 1.6 %collective-permute-start.1 = (bf16[80,768]{1,0:T(8,128)(2,1)S(1)}, bf16[80,768]{1,0:T(8,128)(2,1)S(1)}, u32[]{:S(2)}, u32[]{:S(2)}) collective-permute-start(bf16[80,768]{1,0:T(8,128)(2,1)S(1)} %get-tuple-element.37), channel_id=1, source_target_pairs={{0,2},{1,3},{2,0},{3,1},{4,6},{5,7},{6,4},{7,5},{8,10},{9,11},{10,... | collective-permute-start | bytes 368648 | tf_op jit(solution)/shard_map/ppermute | solution.py:383
  17.2 0.0 copy-done.6
  17.2 0.0 copy-done.8
  17.2 0.9 %own.1 = (bf16[512,384]{1,0:T(8,128)(2,1)S(1)}, bf16[512,192]{1,0:T(8,128)(2,1)S(1)}) custom-call(bf16[512,768]{1,0:T(8,128)(2,1)S(1)} %copy-done.8, bf16[3,192,768]{2,1,0:T(8,128)(2,1)S(1)} %bitcast.12), custom_call_target="tpu_custom_call" | custom-call | flops 2000000000 | bytes 1671168 | tf_op jit(solution)/shard_map/own/pallas_call | solution.py:72
  18.0 3.0 %collective-permute-done.1.refs_6_ = bf16[80,768]{1,0:T(8,128)(2,1)S(1)} collective-permute-done((bf16[80,768]{1,0:T(8,128)(2,1)S(1)}, bf16[80,768]{1,0:T(8,128)(2,1)S(1)}, u32[]{:S(2)}, u32[]{:S(2)}) %collective-permute-start.1) | collective-permute-done | bytes 122912 | tf_op jit(solution)/shard_map/ppermute | solution.py:383
  21.0 0.0 copy-done
  21.0 0.0 copy-done.1
  21.0 0.0 copy-done.5
  21.0 0.7 %norm_one.1 = (bf16[80,768]{1,0:T(8,128)(2,1)S(1)}, bf16[16,768]{1,0:T(8,128)(2,1)S(1)}, f32[16,768]{1,0:T(8,128)S(1)}) custom-call(s32[1]{0:T(128)} %bitcast.refs_0_, bf16[256,768]{1,0:T(8,128)(2,1)S(1)} %copy-done.2, f32[2,768]{1,0:T(2,128)S(1)} %copy-done.5, bf16[768,768]{1,0:T(8,128)(2,1)S(1)} %copy-done, bf16[768,768]{1,0:T(8,128)(2,1)S(1)} %copy-done.1, ...), custom_call_target="tpu_custom_call" | custom-call | bytes 3127300 | tf_op jit(solution)/shard_map/norm_one/pallas_call | solution.py:72
  21.7 1.5 %collective-permute-start.2 = (bf16[80,768]{1,0:T(8,128)(2,1)S(1)}, bf16[80,768]{1,0:T(8,128)(2,1)S(1)}, u32[]{:S(2)}, u32[]{:S(2)}) collective-permute-start(bf16[80,768]{1,0:T(8,128)(2,1)S(1)} %get-tuple-element.46.refs_5_.refs_0_), channel_id=1, source_target_pairs={{0,2},{1,3},{2,0},{3,1},{4,6},{5,7},{6,4},{7,5},{8,10},{9,11},{10,... | collective-permute-start | bytes 368648 | tf_op jit(solution)/shard_map/ppermute | solution.py:383
  23.3 0.0 collective-permute-start.3
  23.3 3.4 %collective-permute-done.2.refs_6_ = bf16[80,768]{1,0:T(8,128)(2,1)S(1)} collective-permute-done((bf16[80,768]{1,0:T(8,128)(2,1)S(1)}, bf16[80,768]{1,0:T(8,128)(2,1)S(1)}, u32[]{:S(2)}, u32[]{:S(2)}) %collective-permute-start.2) | collective-permute-done | bytes 122912 | tf_op jit(solution)/shard_map/ppermute | solution.py:383
  26.6 0.0 collective-permute-start.4
  26.6 0.0 collective-permute-done.3.refs_7_
  26.6 1.3 %collective-permute-done.4.refs_8_ = bf16[80,768]{1,0:T(8,128)(2,1)S(1)} collective-permute-done((bf16[80,768]{1,0:T(8,128)(2,1)S(1)}, bf16[80,768]{1,0:T(8,128)(2,1)S(1)}, u32[]{:S(2)}, u32[]{:S(2)}) %collective-permute-start.4) | collective-permute-done | bytes 122912 | tf_op jit(solution)/shard_map/ppermute | solution.py:383
  28.0 0.9 %ffn.1 = (f32[128,768]{1,0:T(8,128)S(1)}, bf16[128,768]{1,0:T(8,128)(2,1)S(1)}, bf16[2,768]{1,0:T(2,128)(2,1)S(1)}) custom-call(bf16[768,768]{1,0:T(8,128)(2,1)S(1)} %copy-done, bf16[768,768]{1,0:T(8,128)(2,1)S(1)} %copy-done.1, f32[2,768]{1,0:T(2,128)S(1)} %copy-done.5, bf16[16,768]{1,0:T(8,128)(2,1)S(1)} %get-tuple-element.44.refs_3_, ...), custom_call_target="tpu_custom_call" | custom-call | flops 603979776 | bytes 2930688 | tf_op jit(solution)/shard_map/ffn/pallas_call | solution.py:72
  28.9 0.2 collective-permute-start.5
  29.1 1.3 %collective-permute-done.5.refs_1_ = bf16[128,768]{1,0:T(8,128)(2,1)S(1)} collective-permute-done((bf16[128,768]{1,0:T(8,128)(2,1)S(1)}, bf16[128,768]{1,0:T(8,128)(2,1)S(1)}, u32[]{:S(2)}, u32[]{:S(2)}) %collective-permute-start.5) | collective-permute-done | bytes 196640 | tf_op jit(solution)/shard_map/ppermute | solution.py:383
  30.4 0.1 half.3
  30.4 1.6 %collective-permute-start.6 = (bf16[64,768]{1,0:T(8,128)(2,1)S(1)}, bf16[64,768]{1,0:T(8,128)(2,1)S(1)}, u32[]{:S(2)}, u32[]{:S(2)}) collective-permute-start(bf16[64,768]{1,0:T(8,128)(2,1)S(1)} %get-tuple-element.50), channel_id=1, source_target_pairs={{0,2},{1,3},{2,0},{3,1},{4,6},{5,7},{6,4},{7,5},{8,10},{9,11},{10,... | collective-permute-start | bytes 294920 | tf_op jit(solution)/shard_map/ppermute | solution.py:383
  32.0 0.0 copy-done.9
  32.0 4.2 %mask.1.refs_0_ = bf16[512,768]{1,0:T(8,128)(2,1)S(1)} custom-call(s32[16,512]{1,0:T(8,128)S(1)} %bitcast.14), custom_call_target="tpu_custom_call" | custom-call | flops 4000000000 | bytes 32768 | tf_op jit(solution)/shard_map/mask/pallas_call | solution.py:72
  36.3 0.0 collective-permute-done.6.refs_3_
  36.3 0.2 norm_two.1.refs_9_
  36.5 0.6 %collective-permute-start.7 = (bf16[64,768]{1,0:T(8,128)(2,1)S(1)}, bf16[64,768]{1,0:T(8,128)(2,1)S(1)}, u32[]{:S(2)}, u32[]{:S(2)}) collective-permute-start(bf16[64,768]{1,0:T(8,128)(2,1)S(1)} %norm_two.1.refs_9_), channel_id=1, source_target_pairs={{0,2},{1,3},{2,0},{3,1},{4,6},{5,7},{6,4},{7,5},{8,10},{9,11},{10,... | collective-permute-start | bytes 294920 | tf_op jit(solution)/shard_map/ppermute | solution.py:383
  37.1 2.9 %collective-permute-start.10 = (bf16[2,768]{1,0:T(2,128)(2,1)S(1)}, bf16[2,768]{1,0:T(2,128)(2,1)S(1)}, u32[]{:S(2)}, u32[]{:S(2)}) collective-permute-start(bf16[2,768]{1,0:T(2,128)(2,1)S(1)} %get-tuple-element.55.refs_8_), channel_id=1, source_target_pairs={{0,16},{1,21},{2,18},{3,23},{4,20},{5,17},{6,22},{7,19},{8,24},{9,... | collective-permute-start | bytes 9224 | tf_op jit(solution)/shard_map/ppermute | solution.py:463
  40.1 1.5 %collective-permute-start.11 = (bf16[2,768]{1,0:T(2,128)(2,1)S(1)}, bf16[2,768]{1,0:T(2,128)(2,1)S(1)}, u32[]{:S(2)}, u32[]{:S(2)}) collective-permute-start(bf16[2,768]{1,0:T(2,128)(2,1)S(1)} %get-tuple-element.55.refs_8_), channel_id=1, source_target_pairs={{0,24},{1,29},{2,26},{3,31},{4,28},{5,25},{6,30},{7,27},{8,16},{9,... | collective-permute-start | bytes 9224 | tf_op jit(solution)/shard_map/ppermute | solution.py:463
  41.5 0.8 %collective-permute-start.8 = (bf16[2,768]{1,0:T(2,128)(2,1)S(1)}, bf16[2,768]{1,0:T(2,128)(2,1)S(1)}, u32[]{:S(2)}, u32[]{:S(2)}) collective-permute-start(bf16[2,768]{1,0:T(2,128)(2,1)S(1)} %get-tuple-element.55.refs_8_), channel_id=1, source_target_pairs={{1,5},{3,7},{5,1},{7,3},{9,13},{11,15},{13,9},{15,11},{17,21},{19,... | collective-permute-start | bytes 9224 | tf_op jit(solution)/shard_map/ppermute | solution.py:463
  42.3 0.1 collective-permute-start.9
  42.4 7.0 %collective-permute-done.10.refs_2_ = bf16[2,768]{1,0:T(2,128)(2,1)S(1)} collective-permute-done((bf16[2,768]{1,0:T(2,128)(2,1)S(1)}, bf16[2,768]{1,0:T(2,128)(2,1)S(1)}, u32[]{:S(2)}, u32[]{:S(2)}) %collective-permute-start.10) | collective-permute-done | bytes 3104 | tf_op jit(solution)/shard_map/ppermute | solution.py:463
  49.5 0.0 collective-permute-start.12
  49.5 0.0 collective-permute-done.11.refs_3_
  49.5 0.0 collective-permute-done.8.refs_0_
  49.5 0.0 collective-permute-done.9.refs_1_
  49.5 0.0 collective-permute-done.7.refs_10_
  49.5 0.0 all-to-all-done
  49.5 0.6 %collective-permute-start.13 = (bf16[64,768]{1,0:T(8,128)(2,1)S(1)}, bf16[64,768]{1,0:T(8,128)(2,1)S(1)}, u32[]{:S(2)}, u32[]{:S(2)}) collective-permute-start(bf16[64,768]{1,0:T(8,128)(2,1)S(1)} %collective-permute-done.7.refs_10_), channel_id=1, source_target_pairs={{0,1},{1,0},{2,3},{3,2},{4,5},{5,4},{6,7},{7,6},{8,9},{9,8},{10,11... | collective-permute-start | bytes 294920 | tf_op jit(solution)/shard_map/ppermute | solution.py:383
  50.1 0.0 copy-start.7
  50.1 0.0 copy-start.10
  50.1 0.0 copy-start.11
  50.1 0.1 collective-permute-start.14
  50.2 0.2 bias.1.refs_6_
  50.4 0.4 collective-permute-done.12.refs_11_
  50.8 0.6 %collective-permute-done.14.refs_14_ = bf16[16,768]{1,0:T(8,128)(2,1)S(1)} collective-permute-done((bf16[16,768]{1,0:T(8,128)(2,1)S(1)}, bf16[16,768]{1,0:T(8,128)(2,1)S(1)}, u32[]{:S(2)}, u32[]{:S(2)}) %collective-permute-start.14) | collective-permute-done | bytes 24608 | tf_op jit(solution)/shard_map/ppermute | solution.py:383
  51.4 0.0 collective-permute-done.13.refs_12_
  51.4 0.0 copy-done.7
  51.4 0.0 copy-done.10
  51.4 0.0 copy-done.11
  51.4 4.6 %graph.1 = (bf16[192,512]{1,0:T(8,128)(2,1)}, bf16[256,768]{1,0:T(8,128)(2,1)}) custom-call(s32[1]{0:T(128)} %bitcast.refs_0_, s32[4,6]{1,0:T(4,128)S(1)} %copy-done.10, s32[2]{0:T(128)S(1)} %copy-done.11, bf16[512,192]{1,0:T(8,128)(2,1)S(1)} %get-tuple-element.40.refs_3_, bf16[512,384]{1,0:T(8,128)(2,1)S(1)} %get-tuple-element.41.refs_4_, ...), custom_call_target="tpu_custom_call" | custom-call | flops 4000000000 | bytes 5065836 | tf_op jit(solution)/shard_map/graph/pallas_call | solution.py:72
  (4 shorter events, 0.1 us)
Async XLA Ops:
  4.8 7.5 %copy-start.2 = (bf16[256,768]{1,0:T(8,128)(2,1)S(1)}, bf16[256,768]{1,0:T(8,128)(2,1)}, u32[]{:S(2)}) copy-start(bf16[256,768]{1,0:T(8,128)(2,1)} %refs_1_.6) | copy-start | bytes 1179652
  4.8 7.5 %copy-start.3 = (bf16[3,768,192]{1,2,0:T(8,128)(2,1)S(1)}, bf16[3,768,192]{1,2,0:T(8,128)(2,1)}, u32[]{:S(2)}) copy-start(bf16[3,768,192]{1,2,0:T(8,128)(2,1)} %param.13) | copy-start | bytes 2654212
  4.8 7.4 %copy-start.4 = (bf16[192,768]{1,0:T(8,128)(2,1)S(1)}, bf16[192,768]{1,0:T(8,128)(2,1)}, u32[]{:S(2)}) copy-start(bf16[192,768]{1,0:T(8,128)(2,1)} %refs_3_.4) | copy-start | bytes 884740
  4.8 44.7 %all-to-all-start = ((bf16[8,256,384]{2,1,0:T(8,128)(2,1)}), bf16[8,256,384]{2,1,0:T(8,128)(2,1)S(1)}, u32[]{:S(2)}, u32[]{:S(2)}) async-start(bf16[8,256,384]{2,1,0:T(8,128)(2,1)} %bitcast.15), calls=%async_computation | async-start | bytes 3145728 | tf_op jit(solution)/shard_map/all_to_all | solution.py:417
  12.2 5.0 %copy-start.6 = (bf16[3,768,192]{1,2,0:T(8,128)(2,1)S(1)}, bf16[3,768,192]{1,2,0:T(8,128)(2,1)}, u32[]{:S(2)}) copy-start(bf16[3,768,192]{1,2,0:T(8,128)(2,1)} %param.19) | copy-start | bytes 2654212
  12.2 5.0 %copy-start.8 = (bf16[512,768]{1,0:T(8,128)(2,1)S(1)}, bf16[512,768]{1,0:T(8,128)(2,1)}, u32[]{:S(2)}) copy-start(bf16[512,768]{1,0:T(8,128)(2,1)} %refs_0_.2) | copy-start | bytes 2359300
  14.0 1.5 %collective-permute-start = (bf16[144,768]{1,0:T(8,128)(2,1)S(1)}, bf16[144,768]{1,0:T(8,128)(2,1)S(1)}, u32[]{:S(2)}, u32[]{:S(2)}) collective-permute-start(bf16[144,768]{1,0:T(8,128)(2,1)S(1)} %get-tuple-element.36), channel_id=1, source_target_pairs={{0,1},{1,0},{2,3},{3,2},{4,5},{5,4},{6,7},{7,6},{8,9},{9,8},{10,11... | collective-permute-start | bytes 663560 | tf_op jit(solution)/shard_map/ppermute | solution.py:383
  15.6 5.5 %copy-start = (bf16[768,768]{1,0:T(8,128)(2,1)S(1)}, bf16[768,768]{1,0:T(8,128)(2,1)}, u32[]{:S(2)}) copy-start(bf16[768,768]{1,0:T(8,128)(2,1)} %refs_0_.3) | copy-start | bytes 3538948
  15.6 5.5 %copy-start.1 = (bf16[768,768]{1,0:T(8,128)(2,1)S(1)}, bf16[768,768]{1,0:T(8,128)(2,1)}, u32[]{:S(2)}) copy-start(bf16[768,768]{1,0:T(8,128)(2,1)} %refs_1_.7) | copy-start | bytes 3538948
  15.6 5.4 %copy-start.5 = (f32[2,768]{1,0:T(2,128)S(1)}, f32[2,768]{1,0:T(2,128)}, u32[]{:S(2)}) copy-start(f32[2,768]{1,0:T(2,128)} %refs_1_.8) | copy-start | bytes 18436
  15.6 5.4 %collective-permute-start.1 = (bf16[80,768]{1,0:T(8,128)(2,1)S(1)}, bf16[80,768]{1,0:T(8,128)(2,1)S(1)}, u32[]{:S(2)}, u32[]{:S(2)}) collective-permute-start(bf16[80,768]{1,0:T(8,128)(2,1)S(1)} %get-tuple-element.37), channel_id=1, source_target_pairs={{0,2},{1,3},{2,0},{3,1},{4,6},{5,7},{6,4},{7,5},{8,10},{9,11},{10,... | collective-permute-start | bytes 368648 | tf_op jit(solution)/shard_map/ppermute | solution.py:383
  21.7 4.9 %collective-permute-start.2 = (bf16[80,768]{1,0:T(8,128)(2,1)S(1)}, bf16[80,768]{1,0:T(8,128)(2,1)S(1)}, u32[]{:S(2)}, u32[]{:S(2)}) collective-permute-start(bf16[80,768]{1,0:T(8,128)(2,1)S(1)} %get-tuple-element.46.refs_5_.refs_0_), channel_id=1, source_target_pairs={{0,2},{1,3},{2,0},{3,1},{4,6},{5,7},{6,4},{7,5},{8,10},{9,11},{10,... | collective-permute-start | bytes 368648 | tf_op jit(solution)/shard_map/ppermute | solution.py:383
  23.3 3.4 %collective-permute-start.3 = (bf16[80,768]{1,0:T(8,128)(2,1)S(1)}, bf16[80,768]{1,0:T(8,128)(2,1)S(1)}, u32[]{:S(2)}, u32[]{:S(2)}) collective-permute-start(bf16[80,768]{1,0:T(8,128)(2,1)S(1)} %get-tuple-element.46.refs_5_.refs_0_), channel_id=1, source_target_pairs={{0,1},{1,0},{2,3},{3,2},{4,5},{5,4},{6,7},{7,6},{8,9},{9,8},{10,11... | collective-permute-start | bytes 368648 | tf_op jit(solution)/shard_map/ppermute | solution.py:383
  26.6 1.3 %collective-permute-start.4 = (bf16[80,768]{1,0:T(8,128)(2,1)S(1)}, bf16[80,768]{1,0:T(8,128)(2,1)S(1)}, u32[]{:S(2)}, u32[]{:S(2)}) collective-permute-start(bf16[80,768]{1,0:T(8,128)(2,1)S(1)} %collective-permute-done.2.refs_6_), channel_id=1, source_target_pairs={{0,1},{1,0},{2,3},{3,2},{4,5},{5,4},{6,7},{7,6},{8,9},{9,8},{10,11... | collective-permute-start | bytes 368648 | tf_op jit(solution)/shard_map/ppermute | solution.py:383
  27.9 4.1 %copy-start.9 = (s32[512,16]{0,1:T(8,128)S(1)}, s32[512,16]{0,1:T(8,128)}, u32[]{:S(2)}) copy-start(s32[512,16]{0,1:T(8,128)} %param.23) | copy-start | bytes 98308
  28.9 1.5 %collective-permute-start.5 = (bf16[128,768]{1,0:T(8,128)(2,1)S(1)}, bf16[128,768]{1,0:T(8,128)(2,1)S(1)}, u32[]{:S(2)}, u32[]{:S(2)}) collective-permute-start(bf16[128,768]{1,0:T(8,128)(2,1)S(1)} %get-tuple-element.48), channel_id=1, source_target_pairs={{0,1},{1,0},{2,3},{3,2},{4,5},{5,4},{6,7},{7,6},{8,9},{9,8},{10,11... | collective-permute-start | bytes 589832 | tf_op jit(solution)/shard_map/ppermute | solution.py:383
  30.4 5.8 %collective-permute-start.6 = (bf16[64,768]{1,0:T(8,128)(2,1)S(1)}, bf16[64,768]{1,0:T(8,128)(2,1)S(1)}, u32[]{:S(2)}, u32[]{:S(2)}) collective-permute-start(bf16[64,768]{1,0:T(8,128)(2,1)S(1)} %get-tuple-element.50), channel_id=1, source_target_pairs={{0,2},{1,3},{2,0},{3,1},{4,6},{5,7},{6,4},{7,5},{8,10},{9,11},{10,... | collective-permute-start | bytes 294920 | tf_op jit(solution)/shard_map/ppermute | solution.py:383
  36.5 13.0 %collective-permute-start.7 = (bf16[64,768]{1,0:T(8,128)(2,1)S(1)}, bf16[64,768]{1,0:T(8,128)(2,1)S(1)}, u32[]{:S(2)}, u32[]{:S(2)}) collective-permute-start(bf16[64,768]{1,0:T(8,128)(2,1)S(1)} %norm_two.1.refs_9_), channel_id=1, source_target_pairs={{0,2},{1,3},{2,0},{3,1},{4,6},{5,7},{6,4},{7,5},{8,10},{9,11},{10,... | collective-permute-start | bytes 294920 | tf_op jit(solution)/shard_map/ppermute | solution.py:383
  37.1 12.3 %collective-permute-start.10 = (bf16[2,768]{1,0:T(2,128)(2,1)S(1)}, bf16[2,768]{1,0:T(2,128)(2,1)S(1)}, u32[]{:S(2)}, u32[]{:S(2)}) collective-permute-start(bf16[2,768]{1,0:T(2,128)(2,1)S(1)} %get-tuple-element.55.refs_8_), channel_id=1, source_target_pairs={{0,16},{1,21},{2,18},{3,23},{4,20},{5,17},{6,22},{7,19},{8,24},{9,... | collective-permute-start | bytes 9224 | tf_op jit(solution)/shard_map/ppermute | solution.py:463
  40.1 9.4 %collective-permute-start.11 = (bf16[2,768]{1,0:T(2,128)(2,1)S(1)}, bf16[2,768]{1,0:T(2,128)(2,1)S(1)}, u32[]{:S(2)}, u32[]{:S(2)}) collective-permute-start(bf16[2,768]{1,0:T(2,128)(2,1)S(1)} %get-tuple-element.55.refs_8_), channel_id=1, source_target_pairs={{0,24},{1,29},{2,26},{3,31},{4,28},{5,25},{6,30},{7,27},{8,16},{9,... | collective-permute-start | bytes 9224 | tf_op jit(solution)/shard_map/ppermute | solution.py:463
  41.5 8.0 %collective-permute-start.8 = (bf16[2,768]{1,0:T(2,128)(2,1)S(1)}, bf16[2,768]{1,0:T(2,128)(2,1)S(1)}, u32[]{:S(2)}, u32[]{:S(2)}) collective-permute-start(bf16[2,768]{1,0:T(2,128)(2,1)S(1)} %get-tuple-element.55.refs_8_), channel_id=1, source_target_pairs={{1,5},{3,7},{5,1},{7,3},{9,13},{11,15},{13,9},{15,11},{17,21},{19,... | collective-permute-start | bytes 9224 | tf_op jit(solution)/shard_map/ppermute | solution.py:463
  42.3 7.1 %collective-permute-start.9 = (bf16[2,768]{1,0:T(2,128)(2,1)S(1)}, bf16[2,768]{1,0:T(2,128)(2,1)S(1)}, u32[]{:S(2)}, u32[]{:S(2)}) collective-permute-start(bf16[2,768]{1,0:T(2,128)(2,1)S(1)} %get-tuple-element.55.refs_8_), channel_id=1, source_target_pairs={{0,8},{1,13},{2,10},{3,15},{4,12},{5,9},{6,14},{7,11},{8,0},{9,5},... | collective-permute-start | bytes 9224 | tf_op jit(solution)/shard_map/ppermute | solution.py:463
  49.5 1.3 %collective-permute-start.12 = (bf16[64,768]{1,0:T(8,128)(2,1)S(1)}, bf16[64,768]{1,0:T(8,128)(2,1)S(1)}, u32[]{:S(2)}, u32[]{:S(2)}) collective-permute-start(bf16[64,768]{1,0:T(8,128)(2,1)S(1)} %norm_two.1.refs_9_), channel_id=1, source_target_pairs={{0,1},{1,0},{2,3},{3,2},{4,5},{5,4},{6,7},{7,6},{8,9},{9,8},{10,11... | collective-permute-start | bytes 294920 | tf_op jit(solution)/shard_map/ppermute | solution.py:383
  49.5 1.9 %collective-permute-start.13 = (bf16[64,768]{1,0:T(8,128)(2,1)S(1)}, bf16[64,768]{1,0:T(8,128)(2,1)S(1)}, u32[]{:S(2)}, u32[]{:S(2)}) collective-permute-start(bf16[64,768]{1,0:T(8,128)(2,1)S(1)} %collective-permute-done.7.refs_10_), channel_id=1, source_target_pairs={{0,1},{1,0},{2,3},{3,2},{4,5},{5,4},{6,7},{7,6},{8,9},{9,8},{10,11... | collective-permute-start | bytes 294920 | tf_op jit(solution)/shard_map/ppermute | solution.py:383
  50.1 1.3 %copy-start.7 = (bf16[3,768,192]{1,2,0:T(8,128)(2,1)S(1)}, bf16[3,768,192]{1,2,0:T(8,128)(2,1)}, u32[]{:S(2)}) copy-start(bf16[3,768,192]{1,2,0:T(8,128)(2,1)} %param.19) | copy-start | bytes 2654212
  50.1 1.3 %copy-start.10 = (s32[4,6]{1,0:T(4,128)S(1)}, s32[4,6]{1,0:T(4,128)}, u32[]{:S(2)}) copy-start(s32[4,6]{1,0:T(4,128)} %refs_1_.9) | copy-start | bytes 292
  50.1 1.3 %copy-start.11 = (s32[2]{0:T(128)S(1)}, s32[2]{0:T(128)}, u32[]{:S(2)}) copy-start(s32[2]{0:T(128)} %refs_2_.5) | copy-start | bytes 28
  50.1 1.3 %collective-permute-start.14 = (bf16[16,768]{1,0:T(8,128)(2,1)S(1)}, bf16[16,768]{1,0:T(8,128)(2,1)S(1)}, u32[]{:S(2)}, u32[]{:S(2)}) collective-permute-start(bf16[16,768]{1,0:T(8,128)(2,1)S(1)} %pack.1.refs_13_), channel_id=1, source_target_pairs={{0,1},{1,0},{2,3},{3,2},{4,5},{5,4},{6,7},{7,6},{8,9},{9,8},{10,11... | collective-permute-start | bytes 73736 | tf_op jit(solution)/shard_map/ppermute | solution.py:383

commit v16 on v15

--- a/solution.py
+++ b/solution.py
@@ -128,7 +128,7 @@
     kv = jnp.concatenate([dot_nt(table, w_ref[1]), dot_nt(table, w_ref[2])], axis=1).astype(bf)
     moves = []
     parts = ids.shape[1]
-    group = min(parts, max(1, 1024 // fetch))
+    group = min(parts, max(1, 512 // fetch))
     for start in range(0, parts, group):
         picks = [ids[:, part : part + 1] for part in range(start, start + group)]
         rows = dot(one_hot(jnp.concatenate(picks, axis=0), nodes), kv)
@@ -485,7 +485,7 @@
     across = swap(done, 2)
     across, firsts, far = lax.optimization_barrier((across, firsts, far))
     pack = call(pack_kernel, shape((tail_rows(turns * per_part), width), bf), firsts, name="pack")
-    mask, pack = lax.optimization_barrier((mask, pack))
+    mask, pack, across = lax.optimization_barrier((mask, pack, across))
     packs = [pack, swap(pack, 1)]
     bias = call(bias_kernel, shape(mask.shape, f32), (mask,), flops=10**9, name="bias")
     dones = [done, across, swap(done, 1), swap(across, 1)]

time: 56.2 us -> 56.1 us (level)
  no operation moved by 1% of the time
where the time goes in v16:
time: 56.1 us; the launch traced here: 55.9 us
  starting transfers between devices  18.9 us (34%)
  waiting for transfers between devices  18.4 us (33%)
  Pallas kernels  17.6 us (31%)
  between operations  0.89 us (2%)
    pallas_call x12, Pallas kernels, call(): pl.pallas_call(body, out_shape=outs, in_specs=specs, out_specs=jax.tree.m...  17.6 us
    ppermute x11, waiting for transfers between devices, swap(): lax.ppermute(value, axis, [(i, i ^ step) for i in range(lax.axis_size(axi...  11.4 us
    all_to_all x1, starting transfers between devices, local(): lax.all_to_all(sent.reshape(dp, fetch, 2 * cols), 'dp', split_axis=0, con...  7.4 us
    ppermute x4, waiting for transfers between devices, local(): lax.ppermute(first, ('dp', 'mp'), [(p * mp + m, (p ^ turn * pair + m % pa...  7.04 us
    ppermute x11, starting transfers between devices, swap(): lax.ppermute(value, axis, [(i, i ^ step) for i in range(lax.axis_size(axi...  6.28 us
    ppermute x4, starting transfers between devices, local(): lax.ppermute(first, ('dp', 'mp'), [(p * mp + m, (p ^ turn * pair + m % pa...  5.26 us
  transfers between devices with their start and end apart: 16, of which 8 were waited for; matrix products, arithmetic and copies ran while one was open for 0% of the time, Pallas kernels for 16%

profile of v16, /device:TPU:0, one launch (start us, length us, event | category | flops | bytes accessed | tf_op | source)
XLA Modules:
  0.0 55.9 jit_solution(388099152936728956)
XLA Ops:
  0.6 4.1 %send.1 = bf16[2048,384]{1,0:T(8,128)(2,1)} custom-call(s32[1]{0:T(128)} %bitcast.1.refs_0_, s32[2]{0:T(128)} %refs_2_.5, s32[8,256]{1,0:T(8,128)} %bitcast.16, bf16[512,768]{1,0:T(8,128)(2,1)} %refs_0_.2, bf16[3,192,768]{2,1,0:T(8,128)(2,1)} %bitcast.11), custom_call_target="tpu_custom_call" | custom-call | flops 1107296256 | bytes 1679372 | tf_op jit(solution)/shard_map/send/pallas_call | solution.py:72
  4.7 0.0 copy-start.2
  4.7 0.0 copy-start.3
  4.7 0.0 copy-start.4
  4.8 7.4 %all-to-all-start = ((bf16[8,256,384]{2,1,0:T(8,128)(2,1)}), bf16[8,256,384]{2,1,0:T(8,128)(2,1)S(1)}, u32[]{:S(2)}, u32[]{:S(2)}) async-start(bf16[8,256,384]{2,1,0:T(8,128)(2,1)} %bitcast.15), calls=%async_computation | async-start | bytes 3145728 | tf_op jit(solution)/shard_map/all_to_all | solution.py:417
  12.2 0.0 copy-start.8
  12.2 0.0 copy-done.2
  12.2 0.0 copy-done.3
  12.2 0.0 copy-done.4
  12.2 1.7 %attn.1 = (f32[144,768]{1,0:T(8,128)S(1)}, bf16[144,768]{1,0:T(8,128)(2,1)S(1)}) custom-call(s32[1]{0:T(128)} %bitcast.refs_0_, bf16[256,768]{1,0:T(8,128)(2,1)S(1)} %copy-done.2, bf16[3,192,768]{2,1,0:T(8,128)(2,1)S(1)} %bitcast.10, bf16[192,768]{1,0:T(8,128)(2,1)S(1)} %copy-done.4), custom_call_target="tpu_custom_call" | custom-call | flops 301989888 | bytes 1572868 | tf_op jit(solution)/shard_map/attn/pallas_call | solution.py:72
  13.9 0.1 collective-permute-start
  14.0 1.5 %collective-permute-done.refs_1_ = bf16[144,768]{1,0:T(8,128)(2,1)S(1)} collective-permute-done((bf16[144,768]{1,0:T(8,128)(2,1)S(1)}, bf16[144,768]{1,0:T(8,128)(2,1)S(1)}, u32[]{:S(2)}, u32[]{:S(2)}) %collective-permute-start) | collective-permute-done | bytes 221216 | tf_op jit(solution)/shard_map/ppermute | solution.py:383
  15.5 0.0 copy-start
  15.5 0.0 copy-start.1
  15.5 0.0 copy-start.5
  15.6 1.6 %collective-permute-start.1 = (bf16[80,768]{1,0:T(8,128)(2,1)S(1)}, bf16[80,768]{1,0:T(8,128)(2,1)S(1)}, u32[]{:S(2)}, u32[]{:S(2)}) collective-permute-start(bf16[80,768]{1,0:T(8,128)(2,1)S(1)} %get-tuple-element.38), channel_id=1, source_target_pairs={{0,2},{1,3},{2,0},{3,1},{4,6},{5,7},{6,4},{7,5},{8,10},{9,11},{10,... | collective-permute-start | bytes 368648 | tf_op jit(solution)/shard_map/ppermute | solution.py:383
  17.1 0.0 copy-done.6
  17.1 0.0 copy-done.8
  17.1 0.9 %own.1 = (bf16[512,384]{1,0:T(8,128)(2,1)S(1)}, bf16[512,192]{1,0:T(8,128)(2,1)S(1)}) custom-call(bf16[512,768]{1,0:T(8,128)(2,1)S(1)} %copy-done.8, bf16[3,192,768]{2,1,0:T(8,128)(2,1)S(1)} %bitcast.12), custom_call_target="tpu_custom_call" | custom-call | flops 2000000000 | bytes 1671168 | tf_op jit(solution)/shard_map/own/pallas_call | solution.py:72
  18.0 3.0 %collective-permute-done.1.refs_6_ = bf16[80,768]{1,0:T(8,128)(2,1)S(1)} collective-permute-done((bf16[80,768]{1,0:T(8,128)(2,1)S(1)}, bf16[80,768]{1,0:T(8,128)(2,1)S(1)}, u32[]{:S(2)}, u32[]{:S(2)}) %collective-permute-start.1) | collective-permute-done | bytes 122912 | tf_op jit(solution)/shard_map/ppermute | solution.py:383
  21.0 0.0 copy-done
  21.0 0.0 copy-done.1
  21.0 0.0 copy-done.5
  21.0 0.7 %norm_one.1 = (bf16[80,768]{1,0:T(8,128)(2,1)S(1)}, bf16[16,768]{1,0:T(8,128)(2,1)S(1)}, f32[16,768]{1,0:T(8,128)S(1)}) custom-call(s32[1]{0:T(128)} %bitcast.refs_0_, bf16[256,768]{1,0:T(8,128)(2,1)S(1)} %copy-done.2, f32[2,768]{1,0:T(2,128)S(1)} %copy-done.5, bf16[768,768]{1,0:T(8,128)(2,1)S(1)} %copy-done, bf16[768,768]{1,0:T(8,128)(2,1)S(1)} %copy-done.1, ...), custom_call_target="tpu_custom_call" | custom-call | bytes 3127300 | tf_op jit(solution)/shard_map/norm_one/pallas_call | solution.py:72
  21.7 1.5 %collective-permute-start.2 = (bf16[80,768]{1,0:T(8,128)(2,1)S(1)}, bf16[80,768]{1,0:T(8,128)(2,1)S(1)}, u32[]{:S(2)}, u32[]{:S(2)}) collective-permute-start(bf16[80,768]{1,0:T(8,128)(2,1)S(1)} %get-tuple-element.47.refs_5_.refs_0_), channel_id=1, source_target_pairs={{0,2},{1,3},{2,0},{3,1},{4,6},{5,7},{6,4},{7,5},{8,10},{9,11},{10,... | collective-permute-start | bytes 368648 | tf_op jit(solution)/shard_map/ppermute | solution.py:383
  23.2 0.0 collective-permute-start.3
  23.2 3.4 %collective-permute-done.2.refs_6_ = bf16[80,768]{1,0:T(8,128)(2,1)S(1)} collective-permute-done((bf16[80,768]{1,0:T(8,128)(2,1)S(1)}, bf16[80,768]{1,0:T(8,128)(2,1)S(1)}, u32[]{:S(2)}, u32[]{:S(2)}) %collective-permute-start.2) | collective-permute-done | bytes 122912 | tf_op jit(solution)/shard_map/ppermute | solution.py:383
  26.6 0.0 collective-permute-start.4
  26.6 0.0 collective-permute-done.3.refs_7_
  26.6 1.3 %collective-permute-done.4.refs_8_ = bf16[80,768]{1,0:T(8,128)(2,1)S(1)} collective-permute-done((bf16[80,768]{1,0:T(8,128)(2,1)S(1)}, bf16[80,768]{1,0:T(8,128)(2,1)S(1)}, u32[]{:S(2)}, u32[]{:S(2)}) %collective-permute-start.4) | collective-permute-done | bytes 122912 | tf_op jit(solution)/shard_map/ppermute | solution.py:383
  27.9 0.9 %ffn.1 = (f32[128,768]{1,0:T(8,128)S(1)}, bf16[128,768]{1,0:T(8,128)(2,1)S(1)}, bf16[2,768]{1,0:T(2,128)(2,1)S(1)}) custom-call(bf16[768,768]{1,0:T(8,128)(2,1)S(1)} %copy-done, bf16[768,768]{1,0:T(8,128)(2,1)S(1)} %copy-done.1, f32[2,768]{1,0:T(2,128)S(1)} %copy-done.5, bf16[16,768]{1,0:T(8,128)(2,1)S(1)} %get-tuple-element.45.refs_3_, ...), custom_call_target="tpu_custom_call" | custom-call | flops 603979776 | bytes 2930688 | tf_op jit(solution)/shard_map/ffn/pallas_call | solution.py:72
  28.8 0.2 collective-permute-start.5
  29.1 1.3 %collective-permute-done.5.refs_1_ = bf16[128,768]{1,0:T(8,128)(2,1)S(1)} collective-permute-done((bf16[128,768]{1,0:T(8,128)(2,1)S(1)}, bf16[128,768]{1,0:T(8,128)(2,1)S(1)}, u32[]{:S(2)}, u32[]{:S(2)}) %collective-permute-start.5) | collective-permute-done | bytes 196640 | tf_op jit(solution)/shard_map/ppermute | solution.py:383
  30.3 0.1 half.3
  30.4 1.6 %collective-permute-start.6 = (bf16[64,768]{1,0:T(8,128)(2,1)S(1)}, bf16[64,768]{1,0:T(8,128)(2,1)S(1)}, u32[]{:S(2)}, u32[]{:S(2)}) collective-permute-start(bf16[64,768]{1,0:T(8,128)(2,1)S(1)} %get-tuple-element.51), channel_id=1, source_target_pairs={{0,2},{1,3},{2,0},{3,1},{4,6},{5,7},{6,4},{7,5},{8,10},{9,11},{10,... | collective-permute-start | bytes 294920 | tf_op jit(solution)/shard_map/ppermute | solution.py:383
  32.0 0.0 copy-done.9
  32.0 4.2 %mask.1.refs_0_ = bf16[512,768]{1,0:T(8,128)(2,1)S(1)} custom-call(s32[16,512]{1,0:T(8,128)S(1)} %bitcast.14), custom_call_target="tpu_custom_call" | custom-call | flops 4000000000 | bytes 32768 | tf_op jit(solution)/shard_map/mask/pallas_call | solution.py:72
  36.2 0.0 collective-permute-done.6.refs_3_
  36.2 0.2 norm_two.1.refs_9_
  36.5 0.6 %collective-permute-start.7 = (bf16[64,768]{1,0:T(8,128)(2,1)S(1)}, bf16[64,768]{1,0:T(8,128)(2,1)S(1)}, u32[]{:S(2)}, u32[]{:S(2)}) collective-permute-start(bf16[64,768]{1,0:T(8,128)(2,1)S(1)} %norm_two.1.refs_9_), channel_id=1, source_target_pairs={{0,2},{1,3},{2,0},{3,1},{4,6},{5,7},{6,4},{7,5},{8,10},{9,11},{10,... | collective-permute-start | bytes 294920 | tf_op jit(solution)/shard_map/ppermute | solution.py:383
  37.1 2.9 %collective-permute-start.10 = (bf16[2,768]{1,0:T(2,128)(2,1)S(1)}, bf16[2,768]{1,0:T(2,128)(2,1)S(1)}, u32[]{:S(2)}, u32[]{:S(2)}) collective-permute-start(bf16[2,768]{1,0:T(2,128)(2,1)S(1)} %get-tuple-element.56.refs_8_), channel_id=1, source_target_pairs={{0,16},{1,21},{2,18},{3,23},{4,20},{5,17},{6,22},{7,19},{8,24},{9,... | collective-permute-start | bytes 9224 | tf_op jit(solution)/shard_map/ppermute | solution.py:463
  40.0 1.5 %collective-permute-start.11 = (bf16[2,768]{1,0:T(2,128)(2,1)S(1)}, bf16[2,768]{1,0:T(2,128)(2,1)S(1)}, u32[]{:S(2)}, u32[]{:S(2)}) collective-permute-start(bf16[2,768]{1,0:T(2,128)(2,1)S(1)} %get-tuple-element.56.refs_8_), channel_id=1, source_target_pairs={{0,24},{1,29},{2,26},{3,31},{4,28},{5,25},{6,30},{7,27},{8,16},{9,... | collective-permute-start | bytes 9224 | tf_op jit(solution)/shard_map/ppermute | solution.py:463
  41.5 0.8 %collective-permute-start.8 = (bf16[2,768]{1,0:T(2,128)(2,1)S(1)}, bf16[2,768]{1,0:T(2,128)(2,1)S(1)}, u32[]{:S(2)}, u32[]{:S(2)}) collective-permute-start(bf16[2,768]{1,0:T(2,128)(2,1)S(1)} %get-tuple-element.56.refs_8_), channel_id=1, source_target_pairs={{1,5},{3,7},{5,1},{7,3},{9,13},{11,15},{13,9},{15,11},{17,21},{19,... | collective-permute-start | bytes 9224 | tf_op jit(solution)/shard_map/ppermute | solution.py:463
  42.3 0.1 collective-permute-start.9
  42.4 7.0 %collective-permute-done.10.refs_2_ = bf16[2,768]{1,0:T(2,128)(2,1)S(1)} collective-permute-done((bf16[2,768]{1,0:T(2,128)(2,1)S(1)}, bf16[2,768]{1,0:T(2,128)(2,1)S(1)}, u32[]{:S(2)}, u32[]{:S(2)}) %collective-permute-start.10) | collective-permute-done | bytes 3104 | tf_op jit(solution)/shard_map/ppermute | solution.py:463
  49.4 0.0 collective-permute-start.12
  49.4 0.0 collective-permute-done.11.refs_3_
  49.4 0.0 collective-permute-done.8.refs_0_
  49.4 0.0 collective-permute-done.9.refs_1_
  49.4 0.0 collective-permute-done.7.refs_10_
  49.5 0.0 all-to-all-done
  49.5 0.0 copy-start.7
  49.5 0.0 copy-start.10
  49.5 0.0 copy-start.11
  49.5 0.6 %collective-permute-start.13 = (bf16[64,768]{1,0:T(8,128)(2,1)S(1)}, bf16[64,768]{1,0:T(8,128)(2,1)S(1)}, u32[]{:S(2)}, u32[]{:S(2)}) collective-permute-start(bf16[64,768]{1,0:T(8,128)(2,1)S(1)} %collective-permute-done.7.refs_10_), channel_id=1, source_target_pairs={{0,1},{1,0},{2,3},{3,2},{4,5},{5,4},{6,7},{7,6},{8,9},{9,8},{10,11... | collective-permute-start | bytes 294920 | tf_op jit(solution)/shard_map/ppermute | solution.py:383
  50.1 0.1 collective-permute-start.14
  50.2 0.2 bias.1.refs_6_
  50.3 0.4 collective-permute-done.12.refs_11_
  50.7 0.6 %collective-permute-done.14.refs_14_ = bf16[16,768]{1,0:T(8,128)(2,1)S(1)} collective-permute-done((bf16[16,768]{1,0:T(8,128)(2,1)S(1)}, bf16[16,768]{1,0:T(8,128)(2,1)S(1)}, u32[]{:S(2)}, u32[]{:S(2)}) %collective-permute-start.14) | collective-permute-done | bytes 24608 | tf_op jit(solution)/shard_map/ppermute | solution.py:383
  51.3 0.0 collective-permute-done.13.refs_12_
  51.3 0.0 copy-done.7
  51.3 0.0 copy-done.10
  51.3 0.0 copy-done.11
  51.3 4.6 %graph.1 = (bf16[192,512]{1,0:T(8,128)(2,1)}, bf16[256,768]{1,0:T(8,128)(2,1)}) custom-call(s32[1]{0:T(128)} %bitcast.refs_0_, s32[4,6]{1,0:T(4,128)S(1)} %copy-done.10, s32[2]{0:T(128)S(1)} %copy-done.11, bf16[512,192]{1,0:T(8,128)(2,1)S(1)} %get-tuple-element.41.refs_3_, bf16[512,384]{1,0:T(8,128)(2,1)S(1)} %get-tuple-element.42.refs_4_, ...), custom_call_target="tpu_custom_call" | custom-call | flops 4000000000 | bytes 5065836 | tf_op jit(solution)/shard_map/graph/pallas_call | solution.py:72
  (4 shorter events, 0.1 us)
Async XLA Ops:
  4.7 7.5 %copy-start.2 = (bf16[256,768]{1,0:T(8,128)(2,1)S(1)}, bf16[256,768]{1,0:T(8,128)(2,1)}, u32[]{:S(2)}) copy-start(bf16[256,768]{1,0:T(8,128)(2,1)} %refs_1_.6) | copy-start | bytes 1179652
  4.7 7.5 %copy-start.3 = (bf16[3,768,192]{1,2,0:T(8,128)(2,1)S(1)}, bf16[3,768,192]{1,2,0:T(8,128)(2,1)}, u32[]{:S(2)}) copy-start(bf16[3,768,192]{1,2,0:T(8,128)(2,1)} %param.13) | copy-start | bytes 2654212
  4.7 7.4 %copy-start.4 = (bf16[192,768]{1,0:T(8,128)(2,1)S(1)}, bf16[192,768]{1,0:T(8,128)(2,1)}, u32[]{:S(2)}) copy-start(bf16[192,768]{1,0:T(8,128)(2,1)} %refs_3_.4) | copy-start | bytes 884740
  4.8 44.7 %all-to-all-start = ((bf16[8,256,384]{2,1,0:T(8,128)(2,1)}), bf16[8,256,384]{2,1,0:T(8,128)(2,1)S(1)}, u32[]{:S(2)}, u32[]{:S(2)}) async-start(bf16[8,256,384]{2,1,0:T(8,128)(2,1)} %bitcast.15), calls=%async_computation | async-start | bytes 3145728 | tf_op jit(solution)/shard_map/all_to_all | solution.py:417
  12.2 5.0 %copy-start.6 = (bf16[3,768,192]{1,2,0:T(8,128)(2,1)S(1)}, bf16[3,768,192]{1,2,0:T(8,128)(2,1)}, u32[]{:S(2)}) copy-start(bf16[3,768,192]{1,2,0:T(8,128)(2,1)} %param.19) | copy-start | bytes 2654212
  12.2 5.0 %copy-start.8 = (bf16[512,768]{1,0:T(8,128)(2,1)S(1)}, bf16[512,768]{1,0:T(8,128)(2,1)}, u32[]{:S(2)}) copy-start(bf16[512,768]{1,0:T(8,128)(2,1)} %refs_0_.2) | copy-start | bytes 2359300
  13.9 1.5 %collective-permute-start = (bf16[144,768]{1,0:T(8,128)(2,1)S(1)}, bf16[144,768]{1,0:T(8,128)(2,1)S(1)}, u32[]{:S(2)}, u32[]{:S(2)}) collective-permute-start(bf16[144,768]{1,0:T(8,128)(2,1)S(1)} %get-tuple-element.37), channel_id=1, source_target_pairs={{0,1},{1,0},{2,3},{3,2},{4,5},{5,4},{6,7},{7,6},{8,9},{9,8},{10,11... | collective-permute-start | bytes 663560 | tf_op jit(solution)/shard_map/ppermute | solution.py:383
  15.5 5.5 %copy-start = (bf16[768,768]{1,0:T(8,128)(2,1)S(1)}, bf16[768,768]{1,0:T(8,128)(2,1)}, u32[]{:S(2)}) copy-start(bf16[768,768]{1,0:T(8,128)(2,1)} %refs_0_.3) | copy-start | bytes 3538948
  15.5 5.5 %copy-start.1 = (bf16[768,768]{1,0:T(8,128)(2,1)S(1)}, bf16[768,768]{1,0:T(8,128)(2,1)}, u32[]{:S(2)}) copy-start(bf16[768,768]{1,0:T(8,128)(2,1)} %refs_1_.7) | copy-start | bytes 3538948
  15.5 5.4 %copy-start.5 = (f32[2,768]{1,0:T(2,128)S(1)}, f32[2,768]{1,0:T(2,128)}, u32[]{:S(2)}) copy-start(f32[2,768]{1,0:T(2,128)} %refs_1_.8) | copy-start | bytes 18436
  15.6 5.4 %collective-permute-start.1 = (bf16[80,768]{1,0:T(8,128)(2,1)S(1)}, bf16[80,768]{1,0:T(8,128)(2,1)S(1)}, u32[]{:S(2)}, u32[]{:S(2)}) collective-permute-start(bf16[80,768]{1,0:T(8,128)(2,1)S(1)} %get-tuple-element.38), channel_id=1, source_target_pairs={{0,2},{1,3},{2,0},{3,1},{4,6},{5,7},{6,4},{7,5},{8,10},{9,11},{10,... | collective-permute-start | bytes 368648 | tf_op jit(solution)/shard_map/ppermute | solution.py:383
  21.7 4.9 %collective-permute-start.2 = (bf16[80,768]{1,0:T(8,128)(2,1)S(1)}, bf16[80,768]{1,0:T(8,128)(2,1)S(1)}, u32[]{:S(2)}, u32[]{:S(2)}) collective-permute-start(bf16[80,768]{1,0:T(8,128)(2,1)S(1)} %get-tuple-element.47.refs_5_.refs_0_), channel_id=1, source_target_pairs={{0,2},{1,3},{2,0},{3,1},{4,6},{5,7},{6,4},{7,5},{8,10},{9,11},{10,... | collective-permute-start | bytes 368648 | tf_op jit(solution)/shard_map/ppermute | solution.py:383
  23.2 3.4 %collective-permute-start.3 = (bf16[80,768]{1,0:T(8,128)(2,1)S(1)}, bf16[80,768]{1,0:T(8,128)(2,1)S(1)}, u32[]{:S(2)}, u32[]{:S(2)}) collective-permute-start(bf16[80,768]{1,0:T(8,128)(2,1)S(1)} %get-tuple-element.47.refs_5_.refs_0_), channel_id=1, source_target_pairs={{0,1},{1,0},{2,3},{3,2},{4,5},{5,4},{6,7},{7,6},{8,9},{9,8},{10,11... | collective-permute-start | bytes 368648 | tf_op jit(solution)/shard_map/ppermute | solution.py:383
  26.6 1.3 %collective-permute-start.4 = (bf16[80,768]{1,0:T(8,128)(2,1)S(1)}, bf16[80,768]{1,0:T(8,128)(2,1)S(1)}, u32[]{:S(2)}, u32[]{:S(2)}) collective-permute-start(bf16[80,768]{1,0:T(8,128)(2,1)S(1)} %collective-permute-done.2.refs_6_), channel_id=1, source_target_pairs={{0,1},{1,0},{2,3},{3,2},{4,5},{5,4},{6,7},{7,6},{8,9},{9,8},{10,11... | collective-permute-start | bytes 368648 | tf_op jit(solution)/shard_map/ppermute | solution.py:383
  27.9 4.1 %copy-start.9 = (s32[512,16]{0,1:T(8,128)S(1)}, s32[512,16]{0,1:T(8,128)}, u32[]{:S(2)}) copy-start(s32[512,16]{0,1:T(8,128)} %param.23) | copy-start | bytes 98308
  28.8 1.5 %collective-permute-start.5 = (bf16[128,768]{1,0:T(8,128)(2,1)S(1)}, bf16[128,768]{1,0:T(8,128)(2,1)S(1)}, u32[]{:S(2)}, u32[]{:S(2)}) collective-permute-start(bf16[128,768]{1,0:T(8,128)(2,1)S(1)} %get-tuple-element.49), channel_id=1, source_target_pairs={{0,1},{1,0},{2,3},{3,2},{4,5},{5,4},{6,7},{7,6},{8,9},{9,8},{10,11... | collective-permute-start | bytes 589832 | tf_op jit(solution)/shard_map/ppermute | solution.py:383
  30.4 5.8 %collective-permute-start.6 = (bf16[64,768]{1,0:T(8,128)(2,1)S(1)}, bf16[64,768]{1,0:T(8,128)(2,1)S(1)}, u32[]{:S(2)}, u32[]{:S(2)}) collective-permute-start(bf16[64,768]{1,0:T(8,128)(2,1)S(1)} %get-tuple-element.51), channel_id=1, source_target_pairs={{0,2},{1,3},{2,0},{3,1},{4,6},{5,7},{6,4},{7,5},{8,10},{9,11},{10,... | collective-permute-start | bytes 294920 | tf_op jit(solution)/shard_map/ppermute | solution.py:383
  36.5 13.0 %collective-permute-start.7 = (bf16[64,768]{1,0:T(8,128)(2,1)S(1)}, bf16[64,768]{1,0:T(8,128)(2,1)S(1)}, u32[]{:S(2)}, u32[]{:S(2)}) collective-permute-start(bf16[64,768]{1,0:T(8,128)(2,1)S(1)} %norm_two.1.refs_9_), channel_id=1, source_target_pairs={{0,2},{1,3},{2,0},{3,1},{4,6},{5,7},{6,4},{7,5},{8,10},{9,11},{10,... | collective-permute-start | bytes 294920 | tf_op jit(solution)/shard_map/ppermute | solution.py:383
  37.1 12.3 %collective-permute-start.10 = (bf16[2,768]{1,0:T(2,128)(2,1)S(1)}, bf16[2,768]{1,0:T(2,128)(2,1)S(1)}, u32[]{:S(2)}, u32[]{:S(2)}) collective-permute-start(bf16[2,768]{1,0:T(2,128)(2,1)S(1)} %get-tuple-element.56.refs_8_), channel_id=1, source_target_pairs={{0,16},{1,21},{2,18},{3,23},{4,20},{5,17},{6,22},{7,19},{8,24},{9,... | collective-permute-start | bytes 9224 | tf_op jit(solution)/shard_map/ppermute | solution.py:463
  40.0 9.4 %collective-permute-start.11 = (bf16[2,768]{1,0:T(2,128)(2,1)S(1)}, bf16[2,768]{1,0:T(2,128)(2,1)S(1)}, u32[]{:S(2)}, u32[]{:S(2)}) collective-permute-start(bf16[2,768]{1,0:T(2,128)(2,1)S(1)} %get-tuple-element.56.refs_8_), channel_id=1, source_target_pairs={{0,24},{1,29},{2,26},{3,31},{4,28},{5,25},{6,30},{7,27},{8,16},{9,... | collective-permute-start | bytes 9224 | tf_op jit(solution)/shard_map/ppermute | solution.py:463
  41.5 8.0 %collective-permute-start.8 = (bf16[2,768]{1,0:T(2,128)(2,1)S(1)}, bf16[2,768]{1,0:T(2,128)(2,1)S(1)}, u32[]{:S(2)}, u32[]{:S(2)}) collective-permute-start(bf16[2,768]{1,0:T(2,128)(2,1)S(1)} %get-tuple-element.56.refs_8_), channel_id=1, source_target_pairs={{1,5},{3,7},{5,1},{7,3},{9,13},{11,15},{13,9},{15,11},{17,21},{19,... | collective-permute-start | bytes 9224 | tf_op jit(solution)/shard_map/ppermute | solution.py:463
  42.3 7.1 %collective-permute-start.9 = (bf16[2,768]{1,0:T(2,128)(2,1)S(1)}, bf16[2,768]{1,0:T(2,128)(2,1)S(1)}, u32[]{:S(2)}, u32[]{:S(2)}) collective-permute-start(bf16[2,768]{1,0:T(2,128)(2,1)S(1)} %get-tuple-element.56.refs_8_), channel_id=1, source_target_pairs={{0,8},{1,13},{2,10},{3,15},{4,12},{5,9},{6,14},{7,11},{8,0},{9,5},... | collective-permute-start | bytes 9224 | tf_op jit(solution)/shard_map/ppermute | solution.py:463
  49.4 1.3 %collective-permute-start.12 = (bf16[64,768]{1,0:T(8,128)(2,1)S(1)}, bf16[64,768]{1,0:T(8,128)(2,1)S(1)}, u32[]{:S(2)}, u32[]{:S(2)}) collective-permute-start(bf16[64,768]{1,0:T(8,128)(2,1)S(1)} %norm_two.1.refs_9_), channel_id=1, source_target_pairs={{0,1},{1,0},{2,3},{3,2},{4,5},{5,4},{6,7},{7,6},{8,9},{9,8},{10,11... | collective-permute-start | bytes 294920 | tf_op jit(solution)/shard_map/ppermute | solution.py:383
  49.5 1.8 %copy-start.7 = (bf16[3,768,192]{1,2,0:T(8,128)(2,1)S(1)}, bf16[3,768,192]{1,2,0:T(8,128)(2,1)}, u32[]{:S(2)}) copy-start(bf16[3,768,192]{1,2,0:T(8,128)(2,1)} %param.19) | copy-start | bytes 2654212
  49.5 1.8 %copy-start.10 = (s32[4,6]{1,0:T(4,128)S(1)}, s32[4,6]{1,0:T(4,128)}, u32[]{:S(2)}) copy-start(s32[4,6]{1,0:T(4,128)} %refs_1_.9) | copy-start | bytes 292
  49.5 1.8 %copy-start.11 = (s32[2]{0:T(128)S(1)}, s32[2]{0:T(128)}, u32[]{:S(2)}) copy-start(s32[2]{0:T(128)} %refs_2_.5) | copy-start | bytes 28
  49.5 1.8 %collective-permute-start.13 = (bf16[64,768]{1,0:T(8,128)(2,1)S(1)}, bf16[64,768]{1,0:T(8,128)(2,1)S(1)}, u32[]{:S(2)}, u32[]{:S(2)}) collective-permute-start(bf16[64,768]{1,0:T(8,128)(2,1)S(1)} %collective-permute-done.7.refs_10_), channel_id=1, source_target_pairs={{0,1},{1,0},{2,3},{3,2},{4,5},{5,4},{6,7},{7,6},{8,9},{9,8},{10,11... | collective-permute-start | bytes 294920 | tf_op jit(solution)/shard_map/ppermute | solution.py:383
  50.1 1.2 %collective-permute-start.14 = (bf16[16,768]{1,0:T(8,128)(2,1)S(1)}, bf16[16,768]{1,0:T(8,128)(2,1)S(1)}, u32[]{:S(2)}, u32[]{:S(2)}) collective-permute-start(bf16[16,768]{1,0:T(8,128)(2,1)S(1)} %pack.1.refs_13_), channel_id=1, source_target_pairs={{0,1},{1,0},{2,3},{3,2},{4,5},{5,4},{6,7},{7,6},{8,9},{9,8},{10,11... | collective-permute-start | bytes 73736 | tf_op jit(solution)/shard_map/ppermute | solution.py:383

commit v17 on v15

--- a/solution.py
+++ b/solution.py
@@ -22,6 +22,7 @@
 HBM = pl.BlockSpec(memory_space=pltpu.HBM)
 PAD = 16
 LANES = 128
+FIX = 256
 NT = (((1,), (1,)), ((), ()))
 TN = (((0,), (0,)), ((), ()))
 
@@ -316,13 +317,13 @@
         rows = rows.astype(bf)
         k_all[span, :] = rows[:, :cols]
         v_all[span, :] = rows[:, cols:]
-    lanes = lax.broadcasted_iota(jnp.int32, (TILE, first_kv.shape[0]), 1).astype(f32)
-    for tile in range(far_ref.shape[0] // TILE):
-        rows = far_ref[tile * TILE : (tile + 1) * TILE, :].astype(f32)
+    lanes = lax.broadcasted_iota(jnp.int32, (FIX, first_kv.shape[0]), 1).astype(f32)
+    for tile in range(far_ref.shape[0] // FIX):
+        rows = far_ref[tile * FIX : (tile + 1) * FIX, :].astype(f32)
         code = jnp.where(rows[:, 0:1] != rows[:, 0:1], rows[:, 1:2], -1.0)
         hot = jnp.where(lanes == code, 1.0, 0.0).astype(bf)
         fixed = jnp.where(code >= 0.0, dot(hot, first_kv), rows).astype(bf)
-        span = slice(nodes + tile * TILE, nodes + (tile + 1) * TILE)
+        span = slice(nodes + tile * FIX, nodes + (tile + 1) * FIX)
         k_all[span, :] = fixed[:, :cols]
         v_all[span, :] = fixed[:, cols:]
 

time: 56.2 us -> 56.1 us (level)
  no operation moved by 1% of the time
where the time goes in v17:
time: 56.1 us; the launch traced here: 55.9 us
  starting transfers between devices  18.9 us (34%)
  waiting for transfers between devices  18.5 us (33%)
  Pallas kernels  17.5 us (31%)
  between operations  0.88 us (2%)
    pallas_call x12, Pallas kernels, call(): pl.pallas_call(body, out_shape=outs, in_specs=specs, out_specs=jax.tree.m...  17.5 us
    ppermute x11, waiting for transfers between devices, swap(): lax.ppermute(value, axis, [(i, i ^ step) for i in range(lax.axis_size(axi...  11.4 us
    all_to_all x1, starting transfers between devices, local(): lax.all_to_all(sent.reshape(dp, fetch, 2 * cols), 'dp', split_axis=0, con...  7.4 us
    ppermute x4, waiting for transfers between devices, local(): lax.ppermute(first, ('dp', 'mp'), [(p * mp + m, (p ^ turn * pair + m % pa...  7.04 us
    ppermute x11, starting transfers between devices, swap(): lax.ppermute(value, axis, [(i, i ^ step) for i in range(lax.axis_size(axi...  6.29 us
    ppermute x4, starting transfers between devices, local(): lax.ppermute(first, ('dp', 'mp'), [(p * mp + m, (p ^ turn * pair + m % pa...  5.26 us
  transfers between devices with their start and end apart: 16, of which 8 were waited for; matrix products, arithmetic and copies ran while one was open for 0% of the time, Pallas kernels for 16%

profile of v17, /device:TPU:0, one launch (start us, length us, event | category | flops | bytes accessed | tf_op | source)
XLA Modules:
  0.0 55.9 jit_solution(6233176184800450002)
XLA Ops:
  0.6 4.1 %send.1 = bf16[2048,384]{1,0:T(8,128)(2,1)} custom-call(s32[1]{0:T(128)} %bitcast.1.refs_0_, s32[2]{0:T(128)} %refs_2_.5, s32[8,256]{1,0:T(8,128)} %bitcast.16, bf16[512,768]{1,0:T(8,128)(2,1)} %refs_0_.2, bf16[3,192,768]{2,1,0:T(8,128)(2,1)} %bitcast.11), custom_call_target="tpu_custom_call" | custom-call | flops 1107296256 | bytes 1679372 | tf_op jit(solution)/shard_map/send/pallas_call | solution.py:73
  4.8 0.0 copy-start.2
  4.8 0.0 copy-start.3
  4.8 0.0 copy-start.4
  4.8 7.4 %all-to-all-start = ((bf16[8,256,384]{2,1,0:T(8,128)(2,1)}), bf16[8,256,384]{2,1,0:T(8,128)(2,1)S(1)}, u32[]{:S(2)}, u32[]{:S(2)}) async-start(bf16[8,256,384]{2,1,0:T(8,128)(2,1)} %bitcast.15), calls=%async_computation | async-start | bytes 3145728 | tf_op jit(solution)/shard_map/all_to_all | solution.py:418
  12.2 0.0 copy-start.8
  12.2 0.0 copy-done.2
  12.2 0.0 copy-done.3
  12.2 0.0 copy-done.4
  12.2 1.7 %attn.1 = (f32[144,768]{1,0:T(8,128)S(1)}, bf16[144,768]{1,0:T(8,128)(2,1)S(1)}) custom-call(s32[1]{0:T(128)} %bitcast.refs_0_, bf16[256,768]{1,0:T(8,128)(2,1)S(1)} %copy-done.2, bf16[3,192,768]{2,1,0:T(8,128)(2,1)S(1)} %bitcast.10, bf16[192,768]{1,0:T(8,128)(2,1)S(1)} %copy-done.4), custom_call_target="tpu_custom_call" | custom-call | flops 301989888 | bytes 1572868 | tf_op jit(solution)/shard_map/attn/pallas_call | solution.py:73
  14.0 0.1 collective-permute-start
  14.0 1.5 %collective-permute-done.refs_1_ = bf16[144,768]{1,0:T(8,128)(2,1)S(1)} collective-permute-done((bf16[144,768]{1,0:T(8,128)(2,1)S(1)}, bf16[144,768]{1,0:T(8,128)(2,1)S(1)}, u32[]{:S(2)}, u32[]{:S(2)}) %collective-permute-start) | collective-permute-done | bytes 221216 | tf_op jit(solution)/shard_map/ppermute | solution.py:384
  15.6 0.0 copy-start
  15.6 0.0 copy-start.1
  15.6 0.0 copy-start.5
  15.6 1.6 %collective-permute-start.1 = (bf16[80,768]{1,0:T(8,128)(2,1)S(1)}, bf16[80,768]{1,0:T(8,128)(2,1)S(1)}, u32[]{:S(2)}, u32[]{:S(2)}) collective-permute-start(bf16[80,768]{1,0:T(8,128)(2,1)S(1)} %get-tuple-element.37), channel_id=1, source_target_pairs={{0,2},{1,3},{2,0},{3,1},{4,6},{5,7},{6,4},{7,5},{8,10},{9,11},{10,... | collective-permute-start | bytes 368648 | tf_op jit(solution)/shard_map/ppermute | solution.py:384
  17.2 0.0 copy-done.6
  17.2 0.0 copy-done.8
  17.2 0.9 %own.1 = (bf16[512,384]{1,0:T(8,128)(2,1)S(1)}, bf16[512,192]{1,0:T(8,128)(2,1)S(1)}) custom-call(bf16[512,768]{1,0:T(8,128)(2,1)S(1)} %copy-done.8, bf16[3,192,768]{2,1,0:T(8,128)(2,1)S(1)} %bitcast.12), custom_call_target="tpu_custom_call" | custom-call | flops 2000000000 | bytes 1671168 | tf_op jit(solution)/shard_map/own/pallas_call | solution.py:73
  18.0 3.0 %collective-permute-done.1.refs_6_ = bf16[80,768]{1,0:T(8,128)(2,1)S(1)} collective-permute-done((bf16[80,768]{1,0:T(8,128)(2,1)S(1)}, bf16[80,768]{1,0:T(8,128)(2,1)S(1)}, u32[]{:S(2)}, u32[]{:S(2)}) %collective-permute-start.1) | collective-permute-done | bytes 122912 | tf_op jit(solution)/shard_map/ppermute | solution.py:384
  21.0 0.0 copy-done
  21.0 0.0 copy-done.1
  21.0 0.0 copy-done.5
  21.0 0.7 %norm_one.1 = (bf16[80,768]{1,0:T(8,128)(2,1)S(1)}, bf16[16,768]{1,0:T(8,128)(2,1)S(1)}, f32[16,768]{1,0:T(8,128)S(1)}) custom-call(s32[1]{0:T(128)} %bitcast.refs_0_, bf16[256,768]{1,0:T(8,128)(2,1)S(1)} %copy-done.2, f32[2,768]{1,0:T(2,128)S(1)} %copy-done.5, bf16[768,768]{1,0:T(8,128)(2,1)S(1)} %copy-done, bf16[768,768]{1,0:T(8,128)(2,1)S(1)} %copy-done.1, ...), custom_call_target="tpu_custom_call" | custom-call | bytes 3127300 | tf_op jit(solution)/shard_map/norm_one/pallas_call | solution.py:73
  21.7 1.5 %collective-permute-start.2 = (bf16[80,768]{1,0:T(8,128)(2,1)S(1)}, bf16[80,768]{1,0:T(8,128)(2,1)S(1)}, u32[]{:S(2)}, u32[]{:S(2)}) collective-permute-start(bf16[80,768]{1,0:T(8,128)(2,1)S(1)} %get-tuple-element.46.refs_5_.refs_0_), channel_id=1, source_target_pairs={{0,2},{1,3},{2,0},{3,1},{4,6},{5,7},{6,4},{7,5},{8,10},{9,11},{10,... | collective-permute-start | bytes 368648 | tf_op jit(solution)/shard_map/ppermute | solution.py:384
  23.3 0.0 collective-permute-start.3
  23.3 3.4 %collective-permute-done.2.refs_6_ = bf16[80,768]{1,0:T(8,128)(2,1)S(1)} collective-permute-done((bf16[80,768]{1,0:T(8,128)(2,1)S(1)}, bf16[80,768]{1,0:T(8,128)(2,1)S(1)}, u32[]{:S(2)}, u32[]{:S(2)}) %collective-permute-start.2) | collective-permute-done | bytes 122912 | tf_op jit(solution)/shard_map/ppermute | solution.py:384
  26.6 0.0 collective-permute-start.4
  26.6 0.0 collective-permute-done.3.refs_7_
  26.6 1.3 %collective-permute-done.4.refs_8_ = bf16[80,768]{1,0:T(8,128)(2,1)S(1)} collective-permute-done((bf16[80,768]{1,0:T(8,128)(2,1)S(1)}, bf16[80,768]{1,0:T(8,128)(2,1)S(1)}, u32[]{:S(2)}, u32[]{:S(2)}) %collective-permute-start.4) | collective-permute-done | bytes 122912 | tf_op jit(solution)/shard_map/ppermute | solution.py:384
  28.0 0.9 %ffn.1 = (f32[128,768]{1,0:T(8,128)S(1)}, bf16[128,768]{1,0:T(8,128)(2,1)S(1)}, bf16[2,768]{1,0:T(2,128)(2,1)S(1)}) custom-call(bf16[768,768]{1,0:T(8,128)(2,1)S(1)} %copy-done, bf16[768,768]{1,0:T(8,128)(2,1)S(1)} %copy-done.1, f32[2,768]{1,0:T(2,128)S(1)} %copy-done.5, bf16[16,768]{1,0:T(8,128)(2,1)S(1)} %get-tuple-element.44.refs_3_, ...), custom_call_target="tpu_custom_call" | custom-call | flops 603979776 | bytes 2930688 | tf_op jit(solution)/shard_map/ffn/pallas_call | solution.py:73
  28.9 0.2 collective-permute-start.5
  29.1 1.3 %collective-permute-done.5.refs_1_ = bf16[128,768]{1,0:T(8,128)(2,1)S(1)} collective-permute-done((bf16[128,768]{1,0:T(8,128)(2,1)S(1)}, bf16[128,768]{1,0:T(8,128)(2,1)S(1)}, u32[]{:S(2)}, u32[]{:S(2)}) %collective-permute-start.5) | collective-permute-done | bytes 196640 | tf_op jit(solution)/shard_map/ppermute | solution.py:384
  30.4 0.1 half.3
  30.4 1.6 %collective-permute-start.6 = (bf16[64,768]{1,0:T(8,128)(2,1)S(1)}, bf16[64,768]{1,0:T(8,128)(2,1)S(1)}, u32[]{:S(2)}, u32[]{:S(2)}) collective-permute-start(bf16[64,768]{1,0:T(8,128)(2,1)S(1)} %get-tuple-element.50), channel_id=1, source_target_pairs={{0,2},{1,3},{2,0},{3,1},{4,6},{5,7},{6,4},{7,5},{8,10},{9,11},{10,... | collective-permute-start | bytes 294920 | tf_op jit(solution)/shard_map/ppermute | solution.py:384
  32.0 0.0 copy-done.9
  32.0 4.2 %mask.1.refs_0_ = bf16[512,768]{1,0:T(8,128)(2,1)S(1)} custom-call(s32[16,512]{1,0:T(8,128)S(1)} %bitcast.14), custom_call_target="tpu_custom_call" | custom-call | flops 4000000000 | bytes 32768 | tf_op jit(solution)/shard_map/mask/pallas_call | solution.py:73
  36.3 0.0 collective-permute-done.6.refs_3_
  36.3 0.2 norm_two.1.refs_9_
  36.5 0.6 %collective-permute-start.7 = (bf16[64,768]{1,0:T(8,128)(2,1)S(1)}, bf16[64,768]{1,0:T(8,128)(2,1)S(1)}, u32[]{:S(2)}, u32[]{:S(2)}) collective-permute-start(bf16[64,768]{1,0:T(8,128)(2,1)S(1)} %norm_two.1.refs_9_), channel_id=1, source_target_pairs={{0,2},{1,3},{2,0},{3,1},{4,6},{5,7},{6,4},{7,5},{8,10},{9,11},{10,... | collective-permute-start | bytes 294920 | tf_op jit(solution)/shard_map/ppermute | solution.py:384
  37.1 2.9 %collective-permute-start.10 = (bf16[2,768]{1,0:T(2,128)(2,1)S(1)}, bf16[2,768]{1,0:T(2,128)(2,1)S(1)}, u32[]{:S(2)}, u32[]{:S(2)}) collective-permute-start(bf16[2,768]{1,0:T(2,128)(2,1)S(1)} %get-tuple-element.55.refs_8_), channel_id=1, source_target_pairs={{0,16},{1,21},{2,18},{3,23},{4,20},{5,17},{6,22},{7,19},{8,24},{9,... | collective-permute-start | bytes 9224 | tf_op jit(solution)/shard_map/ppermute | solution.py:464
  40.1 1.5 %collective-permute-start.11 = (bf16[2,768]{1,0:T(2,128)(2,1)S(1)}, bf16[2,768]{1,0:T(2,128)(2,1)S(1)}, u32[]{:S(2)}, u32[]{:S(2)}) collective-permute-start(bf16[2,768]{1,0:T(2,128)(2,1)S(1)} %get-tuple-element.55.refs_8_), channel_id=1, source_target_pairs={{0,24},{1,29},{2,26},{3,31},{4,28},{5,25},{6,30},{7,27},{8,16},{9,... | collective-permute-start | bytes 9224 | tf_op jit(solution)/shard_map/ppermute | solution.py:464
  41.5 0.8 %collective-permute-start.8 = (bf16[2,768]{1,0:T(2,128)(2,1)S(1)}, bf16[2,768]{1,0:T(2,128)(2,1)S(1)}, u32[]{:S(2)}, u32[]{:S(2)}) collective-permute-start(bf16[2,768]{1,0:T(2,128)(2,1)S(1)} %get-tuple-element.55.refs_8_), channel_id=1, source_target_pairs={{1,5},{3,7},{5,1},{7,3},{9,13},{11,15},{13,9},{15,11},{17,21},{19,... | collective-permute-start | bytes 9224 | tf_op jit(solution)/shard_map/ppermute | solution.py:464
  42.3 0.1 collective-permute-start.9
  42.4 7.0 %collective-permute-done.10.refs_2_ = bf16[2,768]{1,0:T(2,128)(2,1)S(1)} collective-permute-done((bf16[2,768]{1,0:T(2,128)(2,1)S(1)}, bf16[2,768]{1,0:T(2,128)(2,1)S(1)}, u32[]{:S(2)}, u32[]{:S(2)}) %collective-permute-start.10) | collective-permute-done | bytes 3104 | tf_op jit(solution)/shard_map/ppermute | solution.py:464
  49.5 0.0 collective-permute-start.12
  49.5 0.0 collective-permute-done.11.refs_3_
  49.5 0.0 collective-permute-done.8.refs_0_
  49.5 0.0 collective-permute-done.9.refs_1_
  49.5 0.0 collective-permute-done.7.refs_10_
  49.5 0.0 all-to-all-done
  49.5 0.6 %collective-permute-start.13 = (bf16[64,768]{1,0:T(8,128)(2,1)S(1)}, bf16[64,768]{1,0:T(8,128)(2,1)S(1)}, u32[]{:S(2)}, u32[]{:S(2)}) collective-permute-start(bf16[64,768]{1,0:T(8,128)(2,1)S(1)} %collective-permute-done.7.refs_10_), channel_id=1, source_target_pairs={{0,1},{1,0},{2,3},{3,2},{4,5},{5,4},{6,7},{7,6},{8,9},{9,8},{10,11... | collective-permute-start | bytes 294920 | tf_op jit(solution)/shard_map/ppermute | solution.py:384
  50.1 0.0 copy-start.7
  50.1 0.0 copy-start.10
  50.1 0.0 copy-start.11
  50.1 0.1 collective-permute-start.14
  50.2 0.2 bias.1.refs_6_
  50.4 0.4 collective-permute-done.12.refs_11_
  50.8 0.6 %collective-permute-done.14.refs_14_ = bf16[16,768]{1,0:T(8,128)(2,1)S(1)} collective-permute-done((bf16[16,768]{1,0:T(8,128)(2,1)S(1)}, bf16[16,768]{1,0:T(8,128)(2,1)S(1)}, u32[]{:S(2)}, u32[]{:S(2)}) %collective-permute-start.14) | collective-permute-done | bytes 24608 | tf_op jit(solution)/shard_map/ppermute | solution.py:384
  51.4 0.0 collective-permute-done.13.refs_12_
  51.4 0.0 copy-done.7
  51.4 0.0 copy-done.10
  51.4 0.0 copy-done.11
  51.4 4.5 %graph.1 = (bf16[192,512]{1,0:T(8,128)(2,1)}, bf16[256,768]{1,0:T(8,128)(2,1)}) custom-call(s32[1]{0:T(128)} %bitcast.refs_0_, s32[4,6]{1,0:T(4,128)S(1)} %copy-done.10, s32[2]{0:T(128)S(1)} %copy-done.11, bf16[512,192]{1,0:T(8,128)(2,1)S(1)} %get-tuple-element.40.refs_3_, bf16[512,384]{1,0:T(8,128)(2,1)S(1)} %get-tuple-element.41.refs_4_, ...), custom_call_target="tpu_custom_call" | custom-call | flops 4000000000 | bytes 5065836 | tf_op jit(solution)/shard_map/graph/pallas_call | solution.py:73
  (4 shorter events, 0.1 us)
Async XLA Ops:
  4.8 7.5 %copy-start.2 = (bf16[256,768]{1,0:T(8,128)(2,1)S(1)}, bf16[256,768]{1,0:T(8,128)(2,1)}, u32[]{:S(2)}) copy-start(bf16[256,768]{1,0:T(8,128)(2,1)} %refs_1_.6) | copy-start | bytes 1179652
  4.8 7.5 %copy-start.3 = (bf16[3,768,192]{1,2,0:T(8,128)(2,1)S(1)}, bf16[3,768,192]{1,2,0:T(8,128)(2,1)}, u32[]{:S(2)}) copy-start(bf16[3,768,192]{1,2,0:T(8,128)(2,1)} %param.13) | copy-start | bytes 2654212
  4.8 7.4 %copy-start.4 = (bf16[192,768]{1,0:T(8,128)(2,1)S(1)}, bf16[192,768]{1,0:T(8,128)(2,1)}, u32[]{:S(2)}) copy-start(bf16[192,768]{1,0:T(8,128)(2,1)} %refs_3_.4) | copy-start | bytes 884740
  4.8 44.7 %all-to-all-start = ((bf16[8,256,384]{2,1,0:T(8,128)(2,1)}), bf16[8,256,384]{2,1,0:T(8,128)(2,1)S(1)}, u32[]{:S(2)}, u32[]{:S(2)}) async-start(bf16[8,256,384]{2,1,0:T(8,128)(2,1)} %bitcast.15), calls=%async_computation | async-start | bytes 3145728 | tf_op jit(solution)/shard_map/all_to_all | solution.py:418
  12.2 5.0 %copy-start.6 = (bf16[3,768,192]{1,2,0:T(8,128)(2,1)S(1)}, bf16[3,768,192]{1,2,0:T(8,128)(2,1)}, u32[]{:S(2)}) copy-start(bf16[3,768,192]{1,2,0:T(8,128)(2,1)} %param.19) | copy-start | bytes 2654212
  12.2 5.0 %copy-start.8 = (bf16[512,768]{1,0:T(8,128)(2,1)S(1)}, bf16[512,768]{1,0:T(8,128)(2,1)}, u32[]{:S(2)}) copy-start(bf16[512,768]{1,0:T(8,128)(2,1)} %refs_0_.2) | copy-start | bytes 2359300
  14.0 1.5 %collective-permute-start = (bf16[144,768]{1,0:T(8,128)(2,1)S(1)}, bf16[144,768]{1,0:T(8,128)(2,1)S(1)}, u32[]{:S(2)}, u32[]{:S(2)}) collective-permute-start(bf16[144,768]{1,0:T(8,128)(2,1)S(1)} %get-tuple-element.36), channel_id=1, source_target_pairs={{0,1},{1,0},{2,3},{3,2},{4,5},{5,4},{6,7},{7,6},{8,9},{9,8},{10,11... | collective-permute-start | bytes 663560 | tf_op jit(solution)/shard_map/ppermute | solution.py:384
  15.6 5.5 %copy-start = (bf16[768,768]{1,0:T(8,128)(2,1)S(1)}, bf16[768,768]{1,0:T(8,128)(2,1)}, u32[]{:S(2)}) copy-start(bf16[768,768]{1,0:T(8,128)(2,1)} %refs_0_.3) | copy-start | bytes 3538948
  15.6 5.5 %copy-start.1 = (bf16[768,768]{1,0:T(8,128)(2,1)S(1)}, bf16[768,768]{1,0:T(8,128)(2,1)}, u32[]{:S(2)}) copy-start(bf16[768,768]{1,0:T(8,128)(2,1)} %refs_1_.7) | copy-start | bytes 3538948
  15.6 5.4 %copy-start.5 = (f32[2,768]{1,0:T(2,128)S(1)}, f32[2,768]{1,0:T(2,128)}, u32[]{:S(2)}) copy-start(f32[2,768]{1,0:T(2,128)} %refs_1_.8) | copy-start | bytes 18436
  15.6 5.4 %collective-permute-start.1 = (bf16[80,768]{1,0:T(8,128)(2,1)S(1)}, bf16[80,768]{1,0:T(8,128)(2,1)S(1)}, u32[]{:S(2)}, u32[]{:S(2)}) collective-permute-start(bf16[80,768]{1,0:T(8,128)(2,1)S(1)} %get-tuple-element.37), channel_id=1, source_target_pairs={{0,2},{1,3},{2,0},{3,1},{4,6},{5,7},{6,4},{7,5},{8,10},{9,11},{10,... | collective-permute-start | bytes 368648 | tf_op jit(solution)/shard_map/ppermute | solution.py:384
  21.7 4.9 %collective-permute-start.2 = (bf16[80,768]{1,0:T(8,128)(2,1)S(1)}, bf16[80,768]{1,0:T(8,128)(2,1)S(1)}, u32[]{:S(2)}, u32[]{:S(2)}) collective-permute-start(bf16[80,768]{1,0:T(8,128)(2,1)S(1)} %get-tuple-element.46.refs_5_.refs_0_), channel_id=1, source_target_pairs={{0,2},{1,3},{2,0},{3,1},{4,6},{5,7},{6,4},{7,5},{8,10},{9,11},{10,... | collective-permute-start | bytes 368648 | tf_op jit(solution)/shard_map/ppermute | solution.py:384
  23.3 3.4 %collective-permute-start.3 = (bf16[80,768]{1,0:T(8,128)(2,1)S(1)}, bf16[80,768]{1,0:T(8,128)(2,1)S(1)}, u32[]{:S(2)}, u32[]{:S(2)}) collective-permute-start(bf16[80,768]{1,0:T(8,128)(2,1)S(1)} %get-tuple-element.46.refs_5_.refs_0_), channel_id=1, source_target_pairs={{0,1},{1,0},{2,3},{3,2},{4,5},{5,4},{6,7},{7,6},{8,9},{9,8},{10,11... | collective-permute-start | bytes 368648 | tf_op jit(solution)/shard_map/ppermute | solution.py:384
  26.6 1.3 %collective-permute-start.4 = (bf16[80,768]{1,0:T(8,128)(2,1)S(1)}, bf16[80,768]{1,0:T(8,128)(2,1)S(1)}, u32[]{:S(2)}, u32[]{:S(2)}) collective-permute-start(bf16[80,768]{1,0:T(8,128)(2,1)S(1)} %collective-permute-done.2.refs_6_), channel_id=1, source_target_pairs={{0,1},{1,0},{2,3},{3,2},{4,5},{5,4},{6,7},{7,6},{8,9},{9,8},{10,11... | collective-permute-start | bytes 368648 | tf_op jit(solution)/shard_map/ppermute | solution.py:384
  27.9 4.1 %copy-start.9 = (s32[512,16]{0,1:T(8,128)S(1)}, s32[512,16]{0,1:T(8,128)}, u32[]{:S(2)}) copy-start(s32[512,16]{0,1:T(8,128)} %param.23) | copy-start | bytes 98308
  28.9 1.5 %collective-permute-start.5 = (bf16[128,768]{1,0:T(8,128)(2,1)S(1)}, bf16[128,768]{1,0:T(8,128)(2,1)S(1)}, u32[]{:S(2)}, u32[]{:S(2)}) collective-permute-start(bf16[128,768]{1,0:T(8,128)(2,1)S(1)} %get-tuple-element.48), channel_id=1, source_target_pairs={{0,1},{1,0},{2,3},{3,2},{4,5},{5,4},{6,7},{7,6},{8,9},{9,8},{10,11... | collective-permute-start | bytes 589832 | tf_op jit(solution)/shard_map/ppermute | solution.py:384
  30.4 5.8 %collective-permute-start.6 = (bf16[64,768]{1,0:T(8,128)(2,1)S(1)}, bf16[64,768]{1,0:T(8,128)(2,1)S(1)}, u32[]{:S(2)}, u32[]{:S(2)}) collective-permute-start(bf16[64,768]{1,0:T(8,128)(2,1)S(1)} %get-tuple-element.50), channel_id=1, source_target_pairs={{0,2},{1,3},{2,0},{3,1},{4,6},{5,7},{6,4},{7,5},{8,10},{9,11},{10,... | collective-permute-start | bytes 294920 | tf_op jit(solution)/shard_map/ppermute | solution.py:384
  36.5 13.0 %collective-permute-start.7 = (bf16[64,768]{1,0:T(8,128)(2,1)S(1)}, bf16[64,768]{1,0:T(8,128)(2,1)S(1)}, u32[]{:S(2)}, u32[]{:S(2)}) collective-permute-start(bf16[64,768]{1,0:T(8,128)(2,1)S(1)} %norm_two.1.refs_9_), channel_id=1, source_target_pairs={{0,2},{1,3},{2,0},{3,1},{4,6},{5,7},{6,4},{7,5},{8,10},{9,11},{10,... | collective-permute-start | bytes 294920 | tf_op jit(solution)/shard_map/ppermute | solution.py:384
  37.1 12.3 %collective-permute-start.10 = (bf16[2,768]{1,0:T(2,128)(2,1)S(1)}, bf16[2,768]{1,0:T(2,128)(2,1)S(1)}, u32[]{:S(2)}, u32[]{:S(2)}) collective-permute-start(bf16[2,768]{1,0:T(2,128)(2,1)S(1)} %get-tuple-element.55.refs_8_), channel_id=1, source_target_pairs={{0,16},{1,21},{2,18},{3,23},{4,20},{5,17},{6,22},{7,19},{8,24},{9,... | collective-permute-start | bytes 9224 | tf_op jit(solution)/shard_map/ppermute | solution.py:464
  40.1 9.4 %collective-permute-start.11 = (bf16[2,768]{1,0:T(2,128)(2,1)S(1)}, bf16[2,768]{1,0:T(2,128)(2,1)S(1)}, u32[]{:S(2)}, u32[]{:S(2)}) collective-permute-start(bf16[2,768]{1,0:T(2,128)(2,1)S(1)} %get-tuple-element.55.refs_8_), channel_id=1, source_target_pairs={{0,24},{1,29},{2,26},{3,31},{4,28},{5,25},{6,30},{7,27},{8,16},{9,... | collective-permute-start | bytes 9224 | tf_op jit(solution)/shard_map/ppermute | solution.py:464
  41.5 8.0 %collective-permute-start.8 = (bf16[2,768]{1,0:T(2,128)(2,1)S(1)}, bf16[2,768]{1,0:T(2,128)(2,1)S(1)}, u32[]{:S(2)}, u32[]{:S(2)}) collective-permute-start(bf16[2,768]{1,0:T(2,128)(2,1)S(1)} %get-tuple-element.55.refs_8_), channel_id=1, source_target_pairs={{1,5},{3,7},{5,1},{7,3},{9,13},{11,15},{13,9},{15,11},{17,21},{19,... | collective-permute-start | bytes 9224 | tf_op jit(solution)/shard_map/ppermute | solution.py:464
  42.3 7.1 %collective-permute-start.9 = (bf16[2,768]{1,0:T(2,128)(2,1)S(1)}, bf16[2,768]{1,0:T(2,128)(2,1)S(1)}, u32[]{:S(2)}, u32[]{:S(2)}) collective-permute-start(bf16[2,768]{1,0:T(2,128)(2,1)S(1)} %get-tuple-element.55.refs_8_), channel_id=1, source_target_pairs={{0,8},{1,13},{2,10},{3,15},{4,12},{5,9},{6,14},{7,11},{8,0},{9,5},... | collective-permute-start | bytes 9224 | tf_op jit(solution)/shard_map/ppermute | solution.py:464
  49.5 1.3 %collective-permute-start.12 = (bf16[64,768]{1,0:T(8,128)(2,1)S(1)}, bf16[64,768]{1,0:T(8,128)(2,1)S(1)}, u32[]{:S(2)}, u32[]{:S(2)}) collective-permute-start(bf16[64,768]{1,0:T(8,128)(2,1)S(1)} %norm_two.1.refs_9_), channel_id=1, source_target_pairs={{0,1},{1,0},{2,3},{3,2},{4,5},{5,4},{6,7},{7,6},{8,9},{9,8},{10,11... | collective-permute-start | bytes 294920 | tf_op jit(solution)/shard_map/ppermute | solution.py:384
  49.5 1.9 %collective-permute-start.13 = (bf16[64,768]{1,0:T(8,128)(2,1)S(1)}, bf16[64,768]{1,0:T(8,128)(2,1)S(1)}, u32[]{:S(2)}, u32[]{:S(2)}) collective-permute-start(bf16[64,768]{1,0:T(8,128)(2,1)S(1)} %collective-permute-done.7.refs_10_), channel_id=1, source_target_pairs={{0,1},{1,0},{2,3},{3,2},{4,5},{5,4},{6,7},{7,6},{8,9},{9,8},{10,11... | collective-permute-start | bytes 294920 | tf_op jit(solution)/shard_map/ppermute | solution.py:384
  50.1 1.3 %copy-start.7 = (bf16[3,768,192]{1,2,0:T(8,128)(2,1)S(1)}, bf16[3,768,192]{1,2,0:T(8,128)(2,1)}, u32[]{:S(2)}) copy-start(bf16[3,768,192]{1,2,0:T(8,128)(2,1)} %param.19) | copy-start | bytes 2654212
  50.1 1.3 %copy-start.10 = (s32[4,6]{1,0:T(4,128)S(1)}, s32[4,6]{1,0:T(4,128)}, u32[]{:S(2)}) copy-start(s32[4,6]{1,0:T(4,128)} %refs_1_.9) | copy-start | bytes 292
  50.1 1.3 %copy-start.11 = (s32[2]{0:T(128)S(1)}, s32[2]{0:T(128)}, u32[]{:S(2)}) copy-start(s32[2]{0:T(128)} %refs_2_.5) | copy-start | bytes 28
  50.1 1.3 %collective-permute-start.14 = (bf16[16,768]{1,0:T(8,128)(2,1)S(1)}, bf16[16,768]{1,0:T(8,128)(2,1)S(1)}, u32[]{:S(2)}, u32[]{:S(2)}) collective-permute-start(bf16[16,768]{1,0:T(8,128)(2,1)S(1)} %pack.1.refs_13_), channel_id=1, source_target_pairs={{0,1},{1,0},{2,3},{3,2},{4,5},{5,4},{6,7},{7,6},{8,9},{9,8},{10,11... | collective-permute-start | bytes 73736 | tf_op jit(solution)/shard_map/ppermute | solution.py:384

commit v18 on v15

--- a/solution.py
+++ b/solution.py
@@ -275,7 +275,7 @@
     table = table_ref[...]
     kv_ref[:, :cols] = dot_nt(table, w_ref[1]).astype(bf)
     kv_ref[:, cols:] = dot_nt(table, w_ref[2]).astype(bf)
-    q_ref[...] = dot_nt(table, w_ref[0]).astype(bf)
+    q_ref[...] = (dot_nt(table, w_ref[0]) * (1.0 / GHD**0.5)).astype(bf)
 
 
 def tail_rows(count):
@@ -305,7 +305,7 @@
     firsts[0:per_part, :] = first_ref[...].astype(f32)
     first = firsts[...].astype(bf)
     first_kv = jnp.concatenate([dot_nt(first, w_ref[1]), dot_nt(first, w_ref[2])], axis=1).astype(bf)
-    first_q = dot_nt(first, w_ref[0])
+    first_q = dot_nt(first, w_ref[0]) * (1.0 / GHD**0.5)
     for tile in range(row_tiles):
         span = slice(tile * TILE, (tile + 1) * TILE)
         rows = kv_ref[span, :].astype(f32)
@@ -340,7 +340,7 @@
         starts = [pl.multiple_of(cols_ref[tile, c] * TILE, TILE) for c in range(TPR)]
         keys = jnp.concatenate([k_all[pl.ds(start, TILE), :] for start in starts], axis=0)
         values = jnp.concatenate([v_all[pl.ds(start, TILE), :] for start in starts], axis=0)
-        scores = dot_nt(stacked, keys) * (1.0 / GHD**0.5)
+        scores = dot_nt(stacked, keys)
         bias = bias_ref[tile * TILE : (tile + 1) * TILE, :]
         masked = scores + jnp.concatenate([bias] * heads, axis=0)
         expo = jnp.exp(masked - jnp.max(masked, axis=-1, keepdims=True))

time: 56.2 us -> 56.2 us (level)
  no operation moved by 1% of the time
where the time goes in v18:
time: 56.2 us; the launch traced here: 56 us
  starting transfers between devices  18.9 us (34%)
  waiting for transfers between devices  18.5 us (33%)
  Pallas kernels  17.6 us (31%)
  between operations  0.88 us (2%)
    pallas_call x12, Pallas kernels, call(): pl.pallas_call(body, out_shape=outs, in_specs=specs, out_specs=jax.tree.m...  17.6 us
    ppermute x11, waiting for transfers between devices, swap(): lax.ppermute(value, axis, [(i, i ^ step) for i in range(lax.axis_size(axi...  11.4 us
    all_to_all x1, starting transfers between devices, local(): lax.all_to_all(sent.reshape(dp, fetch, 2 * cols), 'dp', split_axis=0, con...  7.4 us
    ppermute x4, waiting for transfers between devices, local(): lax.ppermute(first, ('dp', 'mp'), [(p * mp + m, (p ^ turn * pair + m % pa...  7.04 us
    ppermute x11, starting transfers between devices, swap(): lax.ppermute(value, axis, [(i, i ^ step) for i in range(lax.axis_size(axi...  6.29 us
    ppermute x4, starting transfers between devices, local(): lax.ppermute(first, ('dp', 'mp'), [(p * mp + m, (p ^ turn * pair + m % pa...  5.26 us
  transfers between devices with their start and end apart: 16, of which 8 were waited for; matrix products, arithmetic and copies ran while one was open for 0% of the time, Pallas kernels for 16%

profile of v18, /device:TPU:0, one launch (start us, length us, event | category | flops | bytes accessed | tf_op | source)
XLA Modules:
  0.0 56.0 jit_solution(17210167636893482207)
XLA Ops:
  0.6 4.1 %send.1 = bf16[2048,384]{1,0:T(8,128)(2,1)} custom-call(s32[1]{0:T(128)} %bitcast.1.refs_0_, s32[2]{0:T(128)} %refs_2_.5, s32[8,256]{1,0:T(8,128)} %bitcast.16, bf16[512,768]{1,0:T(8,128)(2,1)} %refs_0_.2, bf16[3,192,768]{2,1,0:T(8,128)(2,1)} %bitcast.11), custom_call_target="tpu_custom_call" | custom-call | flops 1107296256 | bytes 1679372 | tf_op jit(solution)/shard_map/send/pallas_call | solution.py:72
  4.8 0.0 copy-start.2
  4.8 0.0 copy-start.3
  4.8 0.0 copy-start.4
  4.8 7.4 %all-to-all-start = ((bf16[8,256,384]{2,1,0:T(8,128)(2,1)}), bf16[8,256,384]{2,1,0:T(8,128)(2,1)S(1)}, u32[]{:S(2)}, u32[]{:S(2)}) async-start(bf16[8,256,384]{2,1,0:T(8,128)(2,1)} %bitcast.15), calls=%async_computation | async-start | bytes 3145728 | tf_op jit(solution)/shard_map/all_to_all | solution.py:417
  12.2 0.0 copy-start.8
  12.2 0.0 copy-done.2
  12.2 0.0 copy-done.3
  12.2 0.0 copy-done.4
  12.2 1.7 %attn.1 = (f32[144,768]{1,0:T(8,128)S(1)}, bf16[144,768]{1,0:T(8,128)(2,1)S(1)}) custom-call(s32[1]{0:T(128)} %bitcast.refs_0_, bf16[256,768]{1,0:T(8,128)(2,1)S(1)} %copy-done.2, bf16[3,192,768]{2,1,0:T(8,128)(2,1)S(1)} %bitcast.10, bf16[192,768]{1,0:T(8,128)(2,1)S(1)} %copy-done.4), custom_call_target="tpu_custom_call" | custom-call | flops 301989888 | bytes 1572868 | tf_op jit(solution)/shard_map/attn/pallas_call | solution.py:72
  14.0 0.1 collective-permute-start
  14.0 1.5 %collective-permute-done.refs_1_ = bf16[144,768]{1,0:T(8,128)(2,1)S(1)} collective-permute-done((bf16[144,768]{1,0:T(8,128)(2,1)S(1)}, bf16[144,768]{1,0:T(8,128)(2,1)S(1)}, u32[]{:S(2)}, u32[]{:S(2)}) %collective-permute-start) | collective-permute-done | bytes 221216 | tf_op jit(solution)/shard_map/ppermute | solution.py:383
  15.6 0.0 copy-start
  15.6 0.0 copy-start.1
  15.6 0.0 copy-start.5
  15.6 1.6 %collective-permute-start.1 = (bf16[80,768]{1,0:T(8,128)(2,1)S(1)}, bf16[80,768]{1,0:T(8,128)(2,1)S(1)}, u32[]{:S(2)}, u32[]{:S(2)}) collective-permute-start(bf16[80,768]{1,0:T(8,128)(2,1)S(1)} %get-tuple-element.37), channel_id=1, source_target_pairs={{0,2},{1,3},{2,0},{3,1},{4,6},{5,7},{6,4},{7,5},{8,10},{9,11},{10,... | collective-permute-start | bytes 368648 | tf_op jit(solution)/shard_map/ppermute | solution.py:383
  17.2 0.0 copy-done.6
  17.2 0.0 copy-done.8
  17.2 0.9 %own.1 = (bf16[512,384]{1,0:T(8,128)(2,1)S(1)}, bf16[512,192]{1,0:T(8,128)(2,1)S(1)}) custom-call(bf16[512,768]{1,0:T(8,128)(2,1)S(1)} %copy-done.8, bf16[3,192,768]{2,1,0:T(8,128)(2,1)S(1)} %bitcast.12), custom_call_target="tpu_custom_call" | custom-call | flops 2000000000 | bytes 1671168 | tf_op jit(solution)/shard_map/own/pallas_call | solution.py:72
  18.0 3.0 %collective-permute-done.1.refs_6_ = bf16[80,768]{1,0:T(8,128)(2,1)S(1)} collective-permute-done((bf16[80,768]{1,0:T(8,128)(2,1)S(1)}, bf16[80,768]{1,0:T(8,128)(2,1)S(1)}, u32[]{:S(2)}, u32[]{:S(2)}) %collective-permute-start.1) | collective-permute-done | bytes 122912 | tf_op jit(solution)/shard_map/ppermute | solution.py:383
  21.0 0.0 copy-done
  21.0 0.0 copy-done.1
  21.0 0.0 copy-done.5
  21.0 0.7 %norm_one.1 = (bf16[80,768]{1,0:T(8,128)(2,1)S(1)}, bf16[16,768]{1,0:T(8,128)(2,1)S(1)}, f32[16,768]{1,0:T(8,128)S(1)}) custom-call(s32[1]{0:T(128)} %bitcast.refs_0_, bf16[256,768]{1,0:T(8,128)(2,1)S(1)} %copy-done.2, f32[2,768]{1,0:T(2,128)S(1)} %copy-done.5, bf16[768,768]{1,0:T(8,128)(2,1)S(1)} %copy-done, bf16[768,768]{1,0:T(8,128)(2,1)S(1)} %copy-done.1, ...), custom_call_target="tpu_custom_call" | custom-call | bytes 3127300 | tf_op jit(solution)/shard_map/norm_one/pallas_call | solution.py:72
  21.7 1.5 %collective-permute-start.2 = (bf16[80,768]{1,0:T(8,128)(2,1)S(1)}, bf16[80,768]{1,0:T(8,128)(2,1)S(1)}, u32[]{:S(2)}, u32[]{:S(2)}) collective-permute-start(bf16[80,768]{1,0:T(8,128)(2,1)S(1)} %get-tuple-element.46.refs_5_.refs_0_), channel_id=1, source_target_pairs={{0,2},{1,3},{2,0},{3,1},{4,6},{5,7},{6,4},{7,5},{8,10},{9,11},{10,... | collective-permute-start | bytes 368648 | tf_op jit(solution)/shard_map/ppermute | solution.py:383
  23.3 0.0 collective-permute-start.3
  23.3 3.4 %collective-permute-done.2.refs_6_ = bf16[80,768]{1,0:T(8,128)(2,1)S(1)} collective-permute-done((bf16[80,768]{1,0:T(8,128)(2,1)S(1)}, bf16[80,768]{1,0:T(8,128)(2,1)S(1)}, u32[]{:S(2)}, u32[]{:S(2)}) %collective-permute-start.2) | collective-permute-done | bytes 122912 | tf_op jit(solution)/shard_map/ppermute | solution.py:383
  26.6 0.0 collective-permute-start.4
  26.6 0.0 collective-permute-done.3.refs_7_
  26.6 1.3 %collective-permute-done.4.refs_8_ = bf16[80,768]{1,0:T(8,128)(2,1)S(1)} collective-permute-done((bf16[80,768]{1,0:T(8,128)(2,1)S(1)}, bf16[80,768]{1,0:T(8,128)(2,1)S(1)}, u32[]{:S(2)}, u32[]{:S(2)}) %collective-permute-start.4) | collective-permute-done | bytes 122912 | tf_op jit(solution)/shard_map/ppermute | solution.py:383
  28.0 0.9 %ffn.1 = (f32[128,768]{1,0:T(8,128)S(1)}, bf16[128,768]{1,0:T(8,128)(2,1)S(1)}, bf16[2,768]{1,0:T(2,128)(2,1)S(1)}) custom-call(bf16[768,768]{1,0:T(8,128)(2,1)S(1)} %copy-done, bf16[768,768]{1,0:T(8,128)(2,1)S(1)} %copy-done.1, f32[2,768]{1,0:T(2,128)S(1)} %copy-done.5, bf16[16,768]{1,0:T(8,128)(2,1)S(1)} %get-tuple-element.44.refs_3_, ...), custom_call_target="tpu_custom_call" | custom-call | flops 603979776 | bytes 2930688 | tf_op jit(solution)/shard_map/ffn/pallas_call | solution.py:72
  28.9 0.2 collective-permute-start.5
  29.1 1.3 %collective-permute-done.5.refs_1_ = bf16[128,768]{1,0:T(8,128)(2,1)S(1)} collective-permute-done((bf16[128,768]{1,0:T(8,128)(2,1)S(1)}, bf16[128,768]{1,0:T(8,128)(2,1)S(1)}, u32[]{:S(2)}, u32[]{:S(2)}) %collective-permute-start.5) | collective-permute-done | bytes 196640 | tf_op jit(solution)/shard_map/ppermute | solution.py:383
  30.4 0.1 half.3
  30.4 1.6 %collective-permute-start.6 = (bf16[64,768]{1,0:T(8,128)(2,1)S(1)}, bf16[64,768]{1,0:T(8,128)(2,1)S(1)}, u32[]{:S(2)}, u32[]{:S(2)}) collective-permute-start(bf16[64,768]{1,0:T(8,128)(2,1)S(1)} %get-tuple-element.50), channel_id=1, source_target_pairs={{0,2},{1,3},{2,0},{3,1},{4,6},{5,7},{6,4},{7,5},{8,10},{9,11},{10,... | collective-permute-start | bytes 294920 | tf_op jit(solution)/shard_map/ppermute | solution.py:383
  32.0 0.0 copy-done.9
  32.0 4.2 %mask.1.refs_0_ = bf16[512,768]{1,0:T(8,128)(2,1)S(1)} custom-call(s32[16,512]{1,0:T(8,128)S(1)} %bitcast.14), custom_call_target="tpu_custom_call" | custom-call | flops 4000000000 | bytes 32768 | tf_op jit(solution)/shard_map/mask/pallas_call | solution.py:72
  36.3 0.0 collective-permute-done.6.refs_3_
  36.3 0.2 norm_two.1.refs_9_
  36.5 0.6 %collective-permute-start.7 = (bf16[64,768]{1,0:T(8,128)(2,1)S(1)}, bf16[64,768]{1,0:T(8,128)(2,1)S(1)}, u32[]{:S(2)}, u32[]{:S(2)}) collective-permute-start(bf16[64,768]{1,0:T(8,128)(2,1)S(1)} %norm_two.1.refs_9_), channel_id=1, source_target_pairs={{0,2},{1,3},{2,0},{3,1},{4,6},{5,7},{6,4},{7,5},{8,10},{9,11},{10,... | collective-permute-start | bytes 294920 | tf_op jit(solution)/shard_map/ppermute | solution.py:383
  37.1 2.9 %collective-permute-start.10 = (bf16[2,768]{1,0:T(2,128)(2,1)S(1)}, bf16[2,768]{1,0:T(2,128)(2,1)S(1)}, u32[]{:S(2)}, u32[]{:S(2)}) collective-permute-start(bf16[2,768]{1,0:T(2,128)(2,1)S(1)} %get-tuple-element.55.refs_8_), channel_id=1, source_target_pairs={{0,16},{1,21},{2,18},{3,23},{4,20},{5,17},{6,22},{7,19},{8,24},{9,... | collective-permute-start | bytes 9224 | tf_op jit(solution)/shard_map/ppermute | solution.py:463
  40.1 1.5 %collective-permute-start.11 = (bf16[2,768]{1,0:T(2,128)(2,1)S(1)}, bf16[2,768]{1,0:T(2,128)(2,1)S(1)}, u32[]{:S(2)}, u32[]{:S(2)}) collective-permute-start(bf16[2,768]{1,0:T(2,128)(2,1)S(1)} %get-tuple-element.55.refs_8_), channel_id=1, source_target_pairs={{0,24},{1,29},{2,26},{3,31},{4,28},{5,25},{6,30},{7,27},{8,16},{9,... | collective-permute-start | bytes 9224 | tf_op jit(solution)/shard_map/ppermute | solution.py:463
  41.5 0.8 %collective-permute-start.8 = (bf16[2,768]{1,0:T(2,128)(2,1)S(1)}, bf16[2,768]{1,0:T(2,128)(2,1)S(1)}, u32[]{:S(2)}, u32[]{:S(2)}) collective-permute-start(bf16[2,768]{1,0:T(2,128)(2,1)S(1)} %get-tuple-element.55.refs_8_), channel_id=1, source_target_pairs={{1,5},{3,7},{5,1},{7,3},{9,13},{11,15},{13,9},{15,11},{17,21},{19,... | collective-permute-start | bytes 9224 | tf_op jit(solution)/shard_map/ppermute | solution.py:463
  42.3 0.1 collective-permute-start.9
  42.4 7.0 %collective-permute-done.10.refs_2_ = bf16[2,768]{1,0:T(2,128)(2,1)S(1)} collective-permute-done((bf16[2,768]{1,0:T(2,128)(2,1)S(1)}, bf16[2,768]{1,0:T(2,128)(2,1)S(1)}, u32[]{:S(2)}, u32[]{:S(2)}) %collective-permute-start.10) | collective-permute-done | bytes 3104 | tf_op jit(solution)/shard_map/ppermute | solution.py:463
  49.5 0.0 collective-permute-start.12
  49.5 0.0 collective-permute-done.11.refs_3_
  49.5 0.0 collective-permute-done.8.refs_0_
  49.5 0.0 collective-permute-done.9.refs_1_
  49.5 0.0 collective-permute-done.7.refs_10_
  49.5 0.0 all-to-all-done
  49.5 0.6 %collective-permute-start.13 = (bf16[64,768]{1,0:T(8,128)(2,1)S(1)}, bf16[64,768]{1,0:T(8,128)(2,1)S(1)}, u32[]{:S(2)}, u32[]{:S(2)}) collective-permute-start(bf16[64,768]{1,0:T(8,128)(2,1)S(1)} %collective-permute-done.7.refs_10_), channel_id=1, source_target_pairs={{0,1},{1,0},{2,3},{3,2},{4,5},{5,4},{6,7},{7,6},{8,9},{9,8},{10,11... | collective-permute-start | bytes 294920 | tf_op jit(solution)/shard_map/ppermute | solution.py:383
  50.1 0.0 copy-start.7
  50.1 0.0 copy-start.10
  50.1 0.0 copy-start.11
  50.1 0.1 collective-permute-start.14
  50.2 0.2 bias.1.refs_6_
  50.4 0.4 collective-permute-done.12.refs_11_
  50.8 0.6 %collective-permute-done.14.refs_14_ = bf16[16,768]{1,0:T(8,128)(2,1)S(1)} collective-permute-done((bf16[16,768]{1,0:T(8,128)(2,1)S(1)}, bf16[16,768]{1,0:T(8,128)(2,1)S(1)}, u32[]{:S(2)}, u32[]{:S(2)}) %collective-permute-start.14) | collective-permute-done | bytes 24608 | tf_op jit(solution)/shard_map/ppermute | solution.py:383
  51.4 0.0 collective-permute-done.13.refs_12_
  51.4 0.0 copy-done.7
  51.4 0.0 copy-done.10
  51.4 0.0 copy-done.11
  51.4 4.5 %graph.1 = (bf16[192,512]{1,0:T(8,128)(2,1)}, bf16[256,768]{1,0:T(8,128)(2,1)}) custom-call(s32[1]{0:T(128)} %bitcast.refs_0_, s32[4,6]{1,0:T(4,128)S(1)} %copy-done.10, s32[2]{0:T(128)S(1)} %copy-done.11, bf16[512,192]{1,0:T(8,128)(2,1)S(1)} %get-tuple-element.40.refs_3_, bf16[512,384]{1,0:T(8,128)(2,1)S(1)} %get-tuple-element.41.refs_4_, ...), custom_call_target="tpu_custom_call" | custom-call | flops 4000000000 | bytes 5065836 | tf_op jit(solution)/shard_map/graph/pallas_call | solution.py:72
  (4 shorter events, 0.1 us)
Async XLA Ops:
  4.8 7.5 %copy-start.2 = (bf16[256,768]{1,0:T(8,128)(2,1)S(1)}, bf16[256,768]{1,0:T(8,128)(2,1)}, u32[]{:S(2)}) copy-start(bf16[256,768]{1,0:T(8,128)(2,1)} %refs_1_.6) | copy-start | bytes 1179652
  4.8 7.5 %copy-start.3 = (bf16[3,768,192]{1,2,0:T(8,128)(2,1)S(1)}, bf16[3,768,192]{1,2,0:T(8,128)(2,1)}, u32[]{:S(2)}) copy-start(bf16[3,768,192]{1,2,0:T(8,128)(2,1)} %param.13) | copy-start | bytes 2654212
  4.8 7.4 %copy-start.4 = (bf16[192,768]{1,0:T(8,128)(2,1)S(1)}, bf16[192,768]{1,0:T(8,128)(2,1)}, u32[]{:S(2)}) copy-start(bf16[192,768]{1,0:T(8,128)(2,1)} %refs_3_.4) | copy-start | bytes 884740
  4.8 44.7 %all-to-all-start = ((bf16[8,256,384]{2,1,0:T(8,128)(2,1)}), bf16[8,256,384]{2,1,0:T(8,128)(2,1)S(1)}, u32[]{:S(2)}, u32[]{:S(2)}) async-start(bf16[8,256,384]{2,1,0:T(8,128)(2,1)} %bitcast.15), calls=%async_computation | async-start | bytes 3145728 | tf_op jit(solution)/shard_map/all_to_all | solution.py:417
  12.2 5.0 %copy-start.6 = (bf16[3,768,192]{1,2,0:T(8,128)(2,1)S(1)}, bf16[3,768,192]{1,2,0:T(8,128)(2,1)}, u32[]{:S(2)}) copy-start(bf16[3,768,192]{1,2,0:T(8,128)(2,1)} %param.19) | copy-start | bytes 2654212
  12.2 5.0 %copy-start.8 = (bf16[512,768]{1,0:T(8,128)(2,1)S(1)}, bf16[512,768]{1,0:T(8,128)(2,1)}, u32[]{:S(2)}) copy-start(bf16[512,768]{1,0:T(8,128)(2,1)} %refs_0_.2) | copy-start | bytes 2359300
  14.0 1.5 %collective-permute-start = (bf16[144,768]{1,0:T(8,128)(2,1)S(1)}, bf16[144,768]{1,0:T(8,128)(2,1)S(1)}, u32[]{:S(2)}, u32[]{:S(2)}) collective-permute-start(bf16[144,768]{1,0:T(8,128)(2,1)S(1)} %get-tuple-element.36), channel_id=1, source_target_pairs={{0,1},{1,0},{2,3},{3,2},{4,5},{5,4},{6,7},{7,6},{8,9},{9,8},{10,11... | collective-permute-start | bytes 663560 | tf_op jit(solution)/shard_map/ppermute | solution.py:383
  15.6 5.5 %copy-start = (bf16[768,768]{1,0:T(8,128)(2,1)S(1)}, bf16[768,768]{1,0:T(8,128)(2,1)}, u32[]{:S(2)}) copy-start(bf16[768,768]{1,0:T(8,128)(2,1)} %refs_0_.3) | copy-start | bytes 3538948
  15.6 5.5 %copy-start.1 = (bf16[768,768]{1,0:T(8,128)(2,1)S(1)}, bf16[768,768]{1,0:T(8,128)(2,1)}, u32[]{:S(2)}) copy-start(bf16[768,768]{1,0:T(8,128)(2,1)} %refs_1_.7) | copy-start | bytes 3538948
  15.6 5.4 %copy-start.5 = (f32[2,768]{1,0:T(2,128)S(1)}, f32[2,768]{1,0:T(2,128)}, u32[]{:S(2)}) copy-start(f32[2,768]{1,0:T(2,128)} %refs_1_.8) | copy-start | bytes 18436
  15.6 5.4 %collective-permute-start.1 = (bf16[80,768]{1,0:T(8,128)(2,1)S(1)}, bf16[80,768]{1,0:T(8,128)(2,1)S(1)}, u32[]{:S(2)}, u32[]{:S(2)}) collective-permute-start(bf16[80,768]{1,0:T(8,128)(2,1)S(1)} %get-tuple-element.37), channel_id=1, source_target_pairs={{0,2},{1,3},{2,0},{3,1},{4,6},{5,7},{6,4},{7,5},{8,10},{9,11},{10,... | collective-permute-start | bytes 368648 | tf_op jit(solution)/shard_map/ppermute | solution.py:383
  21.7 4.9 %collective-permute-start.2 = (bf16[80,768]{1,0:T(8,128)(2,1)S(1)}, bf16[80,768]{1,0:T(8,128)(2,1)S(1)}, u32[]{:S(2)}, u32[]{:S(2)}) collective-permute-start(bf16[80,768]{1,0:T(8,128)(2,1)S(1)} %get-tuple-element.46.refs_5_.refs_0_), channel_id=1, source_target_pairs={{0,2},{1,3},{2,0},{3,1},{4,6},{5,7},{6,4},{7,5},{8,10},{9,11},{10,... | collective-permute-start | bytes 368648 | tf_op jit(solution)/shard_map/ppermute | solution.py:383
  23.3 3.4 %collective-permute-start.3 = (bf16[80,768]{1,0:T(8,128)(2,1)S(1)}, bf16[80,768]{1,0:T(8,128)(2,1)S(1)}, u32[]{:S(2)}, u32[]{:S(2)}) collective-permute-start(bf16[80,768]{1,0:T(8,128)(2,1)S(1)} %get-tuple-element.46.refs_5_.refs_0_), channel_id=1, source_target_pairs={{0,1},{1,0},{2,3},{3,2},{4,5},{5,4},{6,7},{7,6},{8,9},{9,8},{10,11... | collective-permute-start | bytes 368648 | tf_op jit(solution)/shard_map/ppermute | solution.py:383
  26.6 1.3 %collective-permute-start.4 = (bf16[80,768]{1,0:T(8,128)(2,1)S(1)}, bf16[80,768]{1,0:T(8,128)(2,1)S(1)}, u32[]{:S(2)}, u32[]{:S(2)}) collective-permute-start(bf16[80,768]{1,0:T(8,128)(2,1)S(1)} %collective-permute-done.2.refs_6_), channel_id=1, source_target_pairs={{0,1},{1,0},{2,3},{3,2},{4,5},{5,4},{6,7},{7,6},{8,9},{9,8},{10,11... | collective-permute-start | bytes 368648 | tf_op jit(solution)/shard_map/ppermute | solution.py:383
  27.9 4.1 %copy-start.9 = (s32[512,16]{0,1:T(8,128)S(1)}, s32[512,16]{0,1:T(8,128)}, u32[]{:S(2)}) copy-start(s32[512,16]{0,1:T(8,128)} %param.23) | copy-start | bytes 98308
  28.9 1.5 %collective-permute-start.5 = (bf16[128,768]{1,0:T(8,128)(2,1)S(1)}, bf16[128,768]{1,0:T(8,128)(2,1)S(1)}, u32[]{:S(2)}, u32[]{:S(2)}) collective-permute-start(bf16[128,768]{1,0:T(8,128)(2,1)S(1)} %get-tuple-element.48), channel_id=1, source_target_pairs={{0,1},{1,0},{2,3},{3,2},{4,5},{5,4},{6,7},{7,6},{8,9},{9,8},{10,11... | collective-permute-start | bytes 589832 | tf_op jit(solution)/shard_map/ppermute | solution.py:383
  30.4 5.8 %collective-permute-start.6 = (bf16[64,768]{1,0:T(8,128)(2,1)S(1)}, bf16[64,768]{1,0:T(8,128)(2,1)S(1)}, u32[]{:S(2)}, u32[]{:S(2)}) collective-permute-start(bf16[64,768]{1,0:T(8,128)(2,1)S(1)} %get-tuple-element.50), channel_id=1, source_target_pairs={{0,2},{1,3},{2,0},{3,1},{4,6},{5,7},{6,4},{7,5},{8,10},{9,11},{10,... | collective-permute-start | bytes 294920 | tf_op jit(solution)/shard_map/ppermute | solution.py:383
  36.5 13.0 %collective-permute-start.7 = (bf16[64,768]{1,0:T(8,128)(2,1)S(1)}, bf16[64,768]{1,0:T(8,128)(2,1)S(1)}, u32[]{:S(2)}, u32[]{:S(2)}) collective-permute-start(bf16[64,768]{1,0:T(8,128)(2,1)S(1)} %norm_two.1.refs_9_), channel_id=1, source_target_pairs={{0,2},{1,3},{2,0},{3,1},{4,6},{5,7},{6,4},{7,5},{8,10},{9,11},{10,... | collective-permute-start | bytes 294920 | tf_op jit(solution)/shard_map/ppermute | solution.py:383
  37.1 12.3 %collective-permute-start.10 = (bf16[2,768]{1,0:T(2,128)(2,1)S(1)}, bf16[2,768]{1,0:T(2,128)(2,1)S(1)}, u32[]{:S(2)}, u32[]{:S(2)}) collective-permute-start(bf16[2,768]{1,0:T(2,128)(2,1)S(1)} %get-tuple-element.55.refs_8_), channel_id=1, source_target_pairs={{0,16},{1,21},{2,18},{3,23},{4,20},{5,17},{6,22},{7,19},{8,24},{9,... | collective-permute-start | bytes 9224 | tf_op jit(solution)/shard_map/ppermute | solution.py:463
  40.1 9.4 %collective-permute-start.11 = (bf16[2,768]{1,0:T(2,128)(2,1)S(1)}, bf16[2,768]{1,0:T(2,128)(2,1)S(1)}, u32[]{:S(2)}, u32[]{:S(2)}) collective-permute-start(bf16[2,768]{1,0:T(2,128)(2,1)S(1)} %get-tuple-element.55.refs_8_), channel_id=1, source_target_pairs={{0,24},{1,29},{2,26},{3,31},{4,28},{5,25},{6,30},{7,27},{8,16},{9,... | collective-permute-start | bytes 9224 | tf_op jit(solution)/shard_map/ppermute | solution.py:463
  41.5 8.0 %collective-permute-start.8 = (bf16[2,768]{1,0:T(2,128)(2,1)S(1)}, bf16[2,768]{1,0:T(2,128)(2,1)S(1)}, u32[]{:S(2)}, u32[]{:S(2)}) collective-permute-start(bf16[2,768]{1,0:T(2,128)(2,1)S(1)} %get-tuple-element.55.refs_8_), channel_id=1, source_target_pairs={{1,5},{3,7},{5,1},{7,3},{9,13},{11,15},{13,9},{15,11},{17,21},{19,... | collective-permute-start | bytes 9224 | tf_op jit(solution)/shard_map/ppermute | solution.py:463
  42.3 7.1 %collective-permute-start.9 = (bf16[2,768]{1,0:T(2,128)(2,1)S(1)}, bf16[2,768]{1,0:T(2,128)(2,1)S(1)}, u32[]{:S(2)}, u32[]{:S(2)}) collective-permute-start(bf16[2,768]{1,0:T(2,128)(2,1)S(1)} %get-tuple-element.55.refs_8_), channel_id=1, source_target_pairs={{0,8},{1,13},{2,10},{3,15},{4,12},{5,9},{6,14},{7,11},{8,0},{9,5},... | collective-permute-start | bytes 9224 | tf_op jit(solution)/shard_map/ppermute | solution.py:463
  49.5 1.3 %collective-permute-start.12 = (bf16[64,768]{1,0:T(8,128)(2,1)S(1)}, bf16[64,768]{1,0:T(8,128)(2,1)S(1)}, u32[]{:S(2)}, u32[]{:S(2)}) collective-permute-start(bf16[64,768]{1,0:T(8,128)(2,1)S(1)} %norm_two.1.refs_9_), channel_id=1, source_target_pairs={{0,1},{1,0},{2,3},{3,2},{4,5},{5,4},{6,7},{7,6},{8,9},{9,8},{10,11... | collective-permute-start | bytes 294920 | tf_op jit(solution)/shard_map/ppermute | solution.py:383
  49.5 1.9 %collective-permute-start.13 = (bf16[64,768]{1,0:T(8,128)(2,1)S(1)}, bf16[64,768]{1,0:T(8,128)(2,1)S(1)}, u32[]{:S(2)}, u32[]{:S(2)}) collective-permute-start(bf16[64,768]{1,0:T(8,128)(2,1)S(1)} %collective-permute-done.7.refs_10_), channel_id=1, source_target_pairs={{0,1},{1,0},{2,3},{3,2},{4,5},{5,4},{6,7},{7,6},{8,9},{9,8},{10,11... | collective-permute-start | bytes 294920 | tf_op jit(solution)/shard_map/ppermute | solution.py:383
  50.1 1.3 %copy-start.7 = (bf16[3,768,192]{1,2,0:T(8,128)(2,1)S(1)}, bf16[3,768,192]{1,2,0:T(8,128)(2,1)}, u32[]{:S(2)}) copy-start(bf16[3,768,192]{1,2,0:T(8,128)(2,1)} %param.19) | copy-start | bytes 2654212
  50.1 1.3 %copy-start.10 = (s32[4,6]{1,0:T(4,128)S(1)}, s32[4,6]{1,0:T(4,128)}, u32[]{:S(2)}) copy-start(s32[4,6]{1,0:T(4,128)} %refs_1_.9) | copy-start | bytes 292
  50.1 1.3 %copy-start.11 = (s32[2]{0:T(128)S(1)}, s32[2]{0:T(128)}, u32[]{:S(2)}) copy-start(s32[2]{0:T(128)} %refs_2_.5) | copy-start | bytes 28
  50.1 1.3 %collective-permute-start.14 = (bf16[16,768]{1,0:T(8,128)(2,1)S(1)}, bf16[16,768]{1,0:T(8,128)(2,1)S(1)}, u32[]{:S(2)}, u32[]{:S(2)}) collective-permute-start(bf16[16,768]{1,0:T(8,128)(2,1)S(1)} %pack.1.refs_13_), channel_id=1, source_target_pairs={{0,1},{1,0},{2,3},{3,2},{4,5},{5,4},{6,7},{7,6},{8,9},{9,8},{10,11... | collective-permute-start | bytes 73736 | tf_op jit(solution)/shard_map/ppermute | solution.py:383
